TPU v7x, 32 devices: a whole 2x2x4 slice. The times are simulated.
32 devices in a mesh: req: 8 (over y, x, core), row: 4 (over z).
Axes of the slice: x: 2, y: 2, z: 4, core: 2. Of those that a mesh axis runs over, the one named last changes fastest.
Arguments:
- hidden_in: bfloat16 [8, 512, 2304], P('req', 'row'), may hold values from -30 to 30
- cache_len: int32 [8], P('req'), may hold values from 64 to 512, as said below
- new_count: int32 [8], P('req'), may hold values from 128 to 512, as said below
- key_cache: bfloat16 [8, 512, 2304], P('req', 'row'), may hold values from -150 to 150
- value_cache: bfloat16 [8, 512, 2304], P('req', 'row'), may hold values from -6 to 6
- attn_gain: float32 [2304], replicated, may hold values from 0.1 to 1.9
- w_query: bfloat16 [2304, 2304], P('req', 'row'), may hold values from -0.125 to 0.125
- w_key: bfloat16 [2304, 2304], P('req', 'row'), may hold values from -0.125 to 0.125
- w_value: bfloat16 [2304, 2304], P('req', 'row'), may hold values from -0.125 to 0.125
- w_out: bfloat16 [2304, 2304], P('row', 'req'), may hold values from -0.125 to 0.125
- final_gain: float32 [2304], replicated, may hold values from 0.1 to 1.9
- head_weight: bfloat16 [2304, 122880], P(None, ('req', 'row')), may hold values from -60 to 60
Outputs:
- layer_out: bfloat16 [8, 512, 2304], P('req', 'row')
- logprobs: float32 [8, 122880], P(None, ('req', 'row'))
Inputs may be any that keep to these rules, and one draw needn't show every extreme that they name: `cache_len`: exactly 1 request, chosen at random, hold between 448 and 512 cached tokens, one of them exactly 512; every other request holds between 64 and 128. `new_count`: one request brings exactly 512 live tokens.
All inputs are finite; a program needn't handle non-finite values.
Results may differ from a plain program's by a relative error of at most 0.0075.
Values may be sent and summed in bfloat16 or wider, within the bound.
No kernel may reach another device: no remote copies, remote signals or barrier semaphores. Data moves between devices by JAX's collectives and lax.ppermute only.
A program may use at most 128 MiB of HBM per device.

v0:
```python
import jax
import jax.numpy as jnp
from jax import lax
from jax.sharding import PartitionSpec as P

HEAD_DIM = 64


EPSILON = 1e-05
KEY_BLOCK = 256


def rms_scale(values, gain_vec):
    return (
        values * lax.rsqrt(jnp.mean(values * values, axis=-1, keepdims=True) + EPSILON) * gain_vec
    )


def rotate(vectors, places):
    half_dim = vectors.shape[-1] // 2
    frequency = 10000.0 ** (-jnp.arange(half_dim).astype(jnp.float32) / half_dim)
    angles = places.astype(jnp.float32)[:, None] * frequency[None, :]
    cosine = jnp.cos(angles)[:, None, :]
    sine_part = jnp.sin(angles)[:, None, :]
    first_half = vectors[..., :half_dim]
    second_half = vectors[..., half_dim:]
    return jnp.concatenate(
        [
            first_half * cosine - second_half * sine_part,
            second_half * cosine + first_half * sine_part,
        ],
        axis=-1,
    )


def empty_state(head_count, query_len, head_dim):
    return (
        jnp.full((head_count, query_len), -jnp.inf, jnp.float32),
        jnp.zeros((head_count, query_len), jnp.float32),
        jnp.zeros((head_count, query_len, head_dim), jnp.float32),
    )


def absorb(state, queries, keys_block, values_block, allowed, scale_factor):
    run_max, run_total, run_acc = state
    scores = (
        jnp.einsum("cgd,kgd->gck", queries, keys_block, preferred_element_type=jnp.float32)
        * scale_factor
    )
    scores = jnp.where(allowed[None], scores, -jnp.inf)
    new_max = jnp.maximum(run_max, jnp.max(scores, axis=-1))
    exp_scores = jnp.exp(scores - new_max[..., None])
    rescale = jnp.exp(run_max - new_max)
    new_total = run_total * rescale + jnp.sum(exp_scores, axis=-1)
    weights = exp_scores.astype(jnp.bfloat16)
    new_acc = run_acc * rescale[..., None] + jnp.einsum(
        "gck,kgd->gcd", weights, values_block, preferred_element_type=jnp.float32
    )
    return (new_max, new_total, new_acc)


def key_pass(state, queries, keys_all, values_all, live_keys, causal, scale_factor):
    query_len = queries.shape[0]
    block_len = min(KEY_BLOCK, keys_all.shape[0])
    blocks_live = (live_keys + block_len - 1) // block_len
    query_pos = jnp.arange(query_len)

    def advance(index, carried):
        offset = index * block_len
        keys_block = lax.dynamic_slice_in_dim(keys_all, offset, block_len, 0)
        values_block = lax.dynamic_slice_in_dim(values_all, offset, block_len, 0)
        key_pos = offset + jnp.arange(block_len)
        allowed = key_pos[None, :] < live_keys
        if causal:
            allowed = allowed & (key_pos[None, :] <= query_pos[:, None])
        allowed = jnp.broadcast_to(allowed, (query_len, block_len))
        return absorb(carried, queries, keys_block, values_block, allowed, scale_factor)

    return lax.fori_loop(0, blocks_live, advance, state)


def on_device(
    hidden_in,
    cache_len,
    new_count,
    key_cache,
    value_cache,
    attn_gain,
    w_query,
    w_key,
    w_value,
    w_out,
    final_gain,
    head_weight,
):
    row_index = lax.axis_index("row")
    inputs = hidden_in[0]
    local_rows = inputs.shape[0]
    head_dim = HEAD_DIM
    scale_factor = head_dim ** (-0.5)
    length = cache_len[0]
    fresh_count = new_count[0]
    normed = rms_scale(inputs.astype(jnp.float32), attn_gain).astype(jnp.bfloat16)
    span_rows = lax.all_gather(normed, "row", axis=0, tiled=True)
    span_len = span_rows.shape[0]
    local_width = w_query.shape[1]
    pieces = (
        lax.all_gather(w_query, "req", axis=0, tiled=True),
        lax.all_gather(w_key, "req", axis=0, tiled=True),
        lax.all_gather(w_value, "req", axis=0, tiled=True),
    )
    raw_query, raw_key, raw_value = tuple(
        (
            jnp.dot(span_rows, piece_part, preferred_element_type=jnp.float32)
            for piece_part in pieces
        )
    )
    groups = local_width // head_dim
    places = length + jnp.arange(span_len, dtype=jnp.int32)
    queries = rotate(raw_query.reshape(span_len, groups, head_dim), places).astype(jnp.bfloat16)
    fresh_keys = rotate(raw_key.reshape(span_len, groups, head_dim), places).astype(jnp.bfloat16)
    fresh_values = raw_value.astype(jnp.bfloat16).reshape(span_len, groups, head_dim)
    span_state = key_pass(
        empty_state(groups, span_len, head_dim),
        queries,
        fresh_keys,
        fresh_values,
        fresh_count,
        True,
        scale_factor,
    )
    cache_keys, cache_values = (
        lax.all_to_all(key_cache[0], "row", split_axis=1, concat_axis=0, tiled=True),
        lax.all_to_all(value_cache[0], "row", split_axis=1, concat_axis=0, tiled=True),
    )
    cap_len = cache_keys.shape[0]
    joint_max, joint_total, joint_acc = key_pass(
        span_state,
        queries,
        cache_keys.reshape(cap_len, groups, head_dim),
        cache_values.reshape(cap_len, groups, head_dim),
        length,
        False,
        scale_factor,
    )
    attended = (joint_acc / joint_total[..., None]).astype(jnp.bfloat16)
    attended = jnp.transpose(attended, (1, 0, 2)).reshape(span_len, local_width)
    partial_out = jnp.dot(
        attended,
        lax.all_gather(w_out, "req", axis=1, tiled=True),
        preferred_element_type=jnp.float32,
    )
    own_rows = lax.psum_scatter(
        partial_out.astype(jnp.bfloat16), "row", scatter_dimension=0, tiled=True
    ).astype(jnp.float32)
    layer_rows = (own_rows + inputs.astype(jnp.float32)).astype(jnp.bfloat16)
    local_index = fresh_count - 1 - row_index * local_rows
    is_owner = (local_index >= 0) & (local_index < local_rows)
    picked = lax.dynamic_slice_in_dim(layer_rows, jnp.clip(local_index, 0, local_rows - 1), 1, 0)
    final_rows = rms_scale(picked.astype(jnp.float32), final_gain).astype(jnp.bfloat16)
    final_rows = jnp.where(is_owner, final_rows, jnp.zeros_like(final_rows))
    owner_rows = lax.psum(final_rows.astype(jnp.float32).astype(jnp.bfloat16), "row")
    last_table = lax.all_gather(owner_rows, "req", axis=0, tiled=True)
    logits = jnp.dot(last_table, head_weight, preferred_element_type=jnp.float32)
    row_max = lax.pmax(jnp.max(logits, axis=1), ("req", "row"))
    row_total = lax.psum(jnp.sum(jnp.exp(logits - row_max[:, None]), axis=1), ("req", "row"))
    logprobs = logits - row_max[:, None] - jnp.log(row_total)[:, None]
    return (layer_rows[None], logprobs)


def solution(mesh):
    placed = (
        P("req", "row", None),
        P("req"),
        P("req"),
        P("req", "row", None),
        P("req", "row", None),
        P(),
        P("req", "row"),
        P("req", "row"),
        P("req", "row"),
        P("row", "req"),
        P(),
        P(None, ("req", "row")),
    )
    return jax.shard_map(
        on_device,
        mesh=mesh,
        in_specs=placed,
        out_specs=(P("req", "row", None), P(None, ("req", "row"))),
        check_vma=False,
    )
```

profile of v0, /device:TPU:0, one launch (start us, length us, event | category | flops | bytes accessed | tf_op | source)
XLA Modules:
  0.0 391.2 jit_solution(181319088362210290)
XLA Ops:
  7.2 1.3 fusion.41
  8.6 2.1 fusion.43
  10.8 0.7 all-gather.9.cloned.1.call-update
  11.5 0.7 all-gather.11.cloned.1.call-update
  12.2 0.5 all-gather.13.cloned.1.call-update
  12.8 1.1 copy.30
  13.8 6.3 %all-to-all-start = ((bf16[128,4,576]{0,2,1:T(8,128)(2,1)}), bf16[128,4,576]{0,2,1:T(8,128)(2,1)S(1)}, u32[]{:S(2)}, u32[]{:S(2)}) async-start(bf16[128,4,576]{0,2,1:T(8,128)(2,1)} %bitcast.8), calls=%async_computation | async-start | bytes 1179648 | tf_op jit(solution)/shard_map/all_to_all | solution.py:133
  20.1 1.0 copy.32
  21.2 30.8 %all-to-all-done = bf16[128,4,576]{0,2,1:T(8,128)(2,1)S(1)} async-done(((bf16[128,4,576]{0,2,1:T(8,128)(2,1)}), bf16[128,4,576]{0,2,1:T(8,128)(2,1)S(1)}, u32[]{:S(2)}, u32[]{:S(2)}) %all-to-all-start) | async-done | bytes 589856 | tf_op jit(solution)/shard_map/all_to_all | solution.py:133
  52.0 3.8 all-to-all-start.1
  55.8 0.6 all-gather.15.cloned.1.call-update
  57.8 0.3 multiply_cosine_fusion
  58.1 0.5 copy.31
  58.6 0.2 reshape.180
  58.8 24.4 %all-to-all-done.1 = bf16[128,4,576]{0,2,1:T(8,128)(2,1)S(1)} async-done(((bf16[128,4,576]{0,2,1:T(8,128)(2,1)}), bf16[128,4,576]{0,2,1:T(8,128)(2,1)S(1)}, u32[]{:S(2)}, u32[]{:S(2)}) %all-to-all-start.1) | async-done | bytes 589856 | tf_op jit(solution)/shard_map/all_to_all | solution.py:134
  83.2 0.5 copy.33
  83.6 0.2 reshape.181
  83.9 3.2 all-gather.7.cloned.1.call-done
  87.1 32.6 %all-gather.9.cloned.1.call-done = bf16[2304,576]{1,0:T(8,128)(2,1)} async-done(((bf16[288,576]{1,0:T(8,128)(2,1)}), bf16[2304,576]{1,0:T(8,128)(2,1)}) %all-gather.9.cloned.1.call-update) | async-done | bytes 2654224 | tf_op jit(solution)/shard_map/all_gather | solution.py:109
  119.6 4.1 %fusion.49 = f32[512,576]{0,1:T(8,128)S(1)} fusion(bf16[512,2304]{1,0:T(8,128)(2,1)} %all-gather.7.cloned.1.call-done, bf16[2304,576]{1,0:T(8,128)(2,1)} %all-gather.9.cloned.1.call-done), kind=kOutput, calls=%fused_computation.76 | convolution fusion | flops 1358954496 | bytes 6193152 | tf_op jit(solution)/shard_map/dot_general | solution.py:114
  123.8 29.3 %all-gather.11.cloned.1.call-done = bf16[2304,576]{1,0:T(8,128)(2,1)} async-done(((bf16[288,576]{1,0:T(8,128)(2,1)}), bf16[2304,576]{1,0:T(8,128)(2,1)}) %all-gather.11.cloned.1.call-update) | async-done | bytes 2654224 | tf_op jit(solution)/shard_map/all_gather | solution.py:108
  153.0 4.1 %fusion.50 = f32[512,576]{0,1:T(8,128)S(1)} fusion(bf16[512,2304]{1,0:T(8,128)(2,1)} %all-gather.7.cloned.1.call-done, bf16[2304,576]{1,0:T(8,128)(2,1)} %all-gather.11.cloned.1.call-done), kind=kOutput, calls=%fused_computation.77 | convolution fusion | flops 1358954496 | bytes 6193152 | tf_op jit(solution)/shard_map/dot_general | solution.py:114
  157.2 0.4 subtract_convert_fusion
  157.6 0.9 pad_maximum_fusion
  158.5 27.8 %all-gather.13.cloned.1.call-done = bf16[2304,576]{1,0:T(8,128)(2,1)} async-done(((bf16[288,576]{1,0:T(8,128)(2,1)}), bf16[2304,576]{1,0:T(8,128)(2,1)}) %all-gather.13.cloned.1.call-update) | async-done | bytes 2654224 | tf_op jit(solution)/shard_map/all_gather | solution.py:110
  186.3 5.0 %convolution_convert_fusion.1 = bf16[512,576]{0,1:T(8,128)(2,1)} fusion(bf16[512,2304]{1,0:T(8,128)(2,1)} %all-gather.7.cloned.1.call-done, bf16[2304,576]{1,0:T(8,128)(2,1)} %all-gather.13.cloned.1.call-done), kind=kOutput, calls=%fused_computation.51 | convolution fusion | flops 1359249408 | bytes 5603328 | tf_op jit(solution)/shard_map/dot_general | solution.py:114
  191.4 5.3 %while.30 = (s32[]{:T(128)}, f32[9,512]{1,0:T(8,128)S(1)}, f32[9,512]{1,0:T(8,128)S(1)}, f32[9,512,64]{1,2,0:T(8,128)S(1)}, s32[]{:T(128)}, /*index=5*/s32[]{:T(...) while((s32[]{:T(128)}, f32[9,512]{1,0:T(8,128)S(1)}, ...), condition=%wide.region_4.5_spmd.clone, body=%wide.region_1.4_spmd.clone.sunk | while | flops 315827968 | bytes 20904668 | solution.py:79
  191.5 0.7 broadcast_compare_fusion.2
  192.3 1.9 fusion.83
  194.2 1.0 fusion.84
  195.3 1.5 fusion.85
  196.8 4.4 %while.29 = (s32[]{:T(128)}, f32[9,512]{1,0:T(8,128)S(1)}, f32[9,512]{1,0:T(8,128)S(1)}, f32[9,512,64]{1,2,0:T(8,128)S(1)}, s32[]{:T(128)}, /*index=5*/s32[]{:T(...) while((s32[]{:T(128)}, f32[9,512]{1,0:T(8,128)S(1)}, ...), condition=%wide.region_8.9_spmd, body=%wide.region_5.8_spmd.sunk | while | flops 315565568 | bytes 18020028 | solution.py:79
  197.0 0.7 add_compare_fusion.2
  197.6 1.1 bitcast_reduce_fusion.2
  198.8 1.0 fusion.77
  199.8 1.3 fusion.78
  201.4 18.2 %all-gather.15.cloned.1.call-done = bf16[576,2304]{0,1:T(8,128)(2,1)} async-done(((bf16[576,288]{0,1:T(8,128)(2,1)}), bf16[576,2304]{0,1:T(8,128)(2,1)}) %all-gather.15.cloned.1.call-update) | async-done | bytes 2654224 | tf_op jit(solution)/shard_map/all_gather | solution.py:150
  219.6 5.4 %convolution_convert_fusion = bf16[512,2304]{1,0:T(8,128)(2,1)} fusion(bf16[512,576]{0,1:T(8,128)(2,1)S(1)} %bitcast.88, bf16[576,2304]{0,1:T(8,128)(2,1)} %all-gather.15.cloned.1.call-done), kind=kOutput, calls=%fused_computation.47 | convolution fusion | flops 1360134144 | bytes 5603328 | tf_op jit(solution)/shard_map/dot_general | solution.py:148
  225.0 48.2 %reduce-scatter.2.cloned.1.call-done = bf16[128,2304]{1,0:T(8,128)(2,1)} async-done(((bf16[512,2304]{1,0:T(8,128)(2,1)}), bf16[128,2304]{1,0:T(8,128)(2,1)}) %reduce-scatter.2.cloned.1.call-update) | async-done | bytes 589840 | tf_op jit(solution)/shard_map/reduce_scatter | solution.py:153
  273.2 1.2 fusion.44
  274.4 0.7 multiply_reduce_fusion
  275.8 10.3 %psum.14 = bf16[1,2304]{1,0:T(2,128)(2,1)S(1)} all-reduce(bf16[1,2304]{1,0:T(2,128)(2,1)S(1)} %broadcast_select_fusion), channel_id=1, replica_groups=mesh['req'=8,'row'=4] {'row'}, use_global_device_ids=true, to_apply=%region_11.12 | all-reduce | flops 2304 | bytes 9216 | tf_op jit(solution)/shard_map/psum | solution.py:162
  286.2 9.4 %all-gather = bf16[8,1,2304]{2,1,0:T(2,128)(2,1)S(1)} all-gather(bf16[1,1,2304]{2,1,0:T(2,128)(2,1)S(1)} %bitcast.89), channel_id=1, replica_groups=mesh['req'=8,'row'=4] {'req'}, dimensions={0}, use_global_device_ids=true | all-gather | bytes 41472 | tf_op jit(solution)/shard_map/all_gather | solution.py:163
  295.6 8.5 %fusion.48 = (f32[8]{0:T(128)S(1)}, f32[8,3840]{1,0:T(8,128)S(1)}) fusion(bf16[2304,3840]{1,0:T(8,128)(2,1)} %param.27, bf16[8,1,2304]{2,1,0:T(2,128)(2,1)S(1)} %all-gather), kind=kOutput, calls=%fused_computation.75 | convolution fusion | flops 141588480 | bytes 17854496 | tf_op jit(solution)/shard_map/dot_general | solution.py:164
  304.1 37.8 %pmax.7 = f32[8]{0:T(128)S(1)} all-reduce(f32[8]{0:T(128)S(1)} %get-tuple-element.184), channel_id=1, replica_groups=mesh['req'=8,'row'=4] {'req','row'}, use_global_device_ids=true, to_apply=%region_13.14 | all-reduce | flops 8 | bytes 64 | tf_op jit(solution)/shard_map/pmax | solution.py:165
  342.0 0.2 exponential_reduce_fusion
  342.2 41.4 %psum.15 = f32[8]{0:T(128)S(1)} all-reduce(f32[8]{0:T(128)S(1)} %exponential_reduce_fusion), channel_id=1, replica_groups=mesh['req'=8,'row'=4] {'req','row'}, use_global_device_ids=true, to_apply=%region_15.16 | all-reduce | flops 8 | bytes 64 | tf_op jit(solution)/shard_map/psum | solution.py:166
  383.6 0.7 subtract_subtract_fusion
  (37 shorter events, 0.9 us)
Async XLA Ops:
  7.2 5.6 %copy-start.3 = (bf16[1,128,2304]{2,1,0:T(8,128)(2,1)S(1)}, bf16[1,128,2304]{2,1,0:T(8,128)(2,1)}, u32[]{:S(2)}) copy-start(bf16[1,128,2304]{2,1,0:T(8,128)(2,1)} %param.19) | copy-start | bytes 1769476
  7.2 13.0 %copy-start.4 = (bf16[1,128,2304]{2,1,0:T(8,128)(2,1)S(1)}, bf16[1,128,2304]{2,1,0:T(8,128)(2,1)}, u32[]{:S(2)}) copy-start(bf16[1,128,2304]{2,1,0:T(8,128)(2,1)} %param.20) | copy-start | bytes 1769476
  7.2 79.9 %all-gather.7.cloned.1.call-start = ((), (), s32[]{:S(2)}) async-start(), calls=%async_computation.3 | async-start | bytes 2949120 | tf_op jit(solution)/shard_map/all_gather | solution.py:104
  10.7 108.9 %all-gather.9.cloned.1.call-start = ((), (), s32[]{:S(2)}) async-start(), calls=%async_computation.4 | async-start | bytes 3317760 | tf_op jit(solution)/shard_map/all_gather | solution.py:109
  11.5 141.6 %all-gather.11.cloned.1.call-start = ((), (), s32[]{:S(2)}) async-start(), calls=%async_computation.5 | async-start | bytes 3317760 | tf_op jit(solution)/shard_map/all_gather | solution.py:108
  12.2 174.1 %all-gather.13.cloned.1.call-start = ((), (), s32[]{:S(2)}) async-start(), calls=%async_computation.6 | async-start | bytes 3317760 | tf_op jit(solution)/shard_map/all_gather | solution.py:110
  13.8 38.2 %all-to-all-start = ((bf16[128,4,576]{0,2,1:T(8,128)(2,1)}), bf16[128,4,576]{0,2,1:T(8,128)(2,1)S(1)}, u32[]{:S(2)}, u32[]{:S(2)}) async-start(bf16[128,4,576]{0,2,1:T(8,128)(2,1)} %bitcast.8), calls=%async_computation | async-start | bytes 1179648 | tf_op jit(solution)/shard_map/all_to_all | solution.py:133
  52.0 31.2 %all-to-all-start.1 = ((bf16[128,4,576]{0,2,1:T(8,128)(2,1)}), bf16[128,4,576]{0,2,1:T(8,128)(2,1)S(1)}, u32[]{:S(2)}, u32[]{:S(2)}) async-start(bf16[128,4,576]{0,2,1:T(8,128)(2,1)} %bitcast.10), calls=%async_computation.1 | async-start | bytes 1179648 | tf_op jit(solution)/shard_map/all_to_all | solution.py:134
  55.8 163.8 %all-gather.15.cloned.1.call-start = ((), (), s32[]{:S(2)}) async-start(), calls=%async_computation.7 | async-start | bytes 3317760 | tf_op jit(solution)/shard_map/all_gather | solution.py:150
  56.4 216.8 %reduce-scatter.2.cloned.1.call-start = ((), (), s32[]{:S(2)}) async-start(), calls=%async_computation.8 | async-start | bytes 2949120 | tf_op jit(solution)/shard_map/reduce_scatter | solution.py:153
  194.2 1.1 copy-start.1
  219.6 53.6 %copy-start = (bf16[1,128,2304]{2,1,0:T(8,128)(2,1)S(1)}, bf16[1,128,2304]{2,1,0:T(8,128)(2,1)}, u32[]{:S(2)}) copy-start(bf16[1,128,2304]{2,1,0:T(8,128)(2,1)} %param.16) | copy-start | bytes 1769476
  225.0 50.8 %copy-start.5 = (f32[2304]{0:T(1024)S(1)}, f32[2304]{0:T(1024)}, u32[]{:S(2)}) copy-start(f32[2304]{0:T(1024)} %param.26) | copy-start | bytes 27652
  274.4 29.7 %copy-start.2 = (bf16[128,2304]{1,0:T(8,128)(2,1)}, bf16[128,2304]{1,0:T(8,128)(2,1)S(1)}, u32[]{:S(2)}) copy-start(bf16[128,2304]{1,0:T(8,128)(2,1)S(1)} %fusion.44) | copy-start | bytes 1769476
Sparse Core Ops, SparseCore 0:
  10.8 76.1 all-gather.6
  88.9 30.6 all-gather.8
  121.5 31.4 all-gather.10
  154.8 31.4 all-gather.12
  188.0 31.4 all-gather.14
  225.1 48.0 reduce-scatter.1
where the time goes:
time: 392 us; the launch traced here: 391 us
  waiting for transfers between devices  217 us (55%)
  blocking collectives  99 us (25%)
  matrix products  32.9 us (8%)
  between operations  16.3 us (4%)
  other arithmetic  11.6 us (3%)
  starting transfers between devices  10.3 us (3%)
    reduce_scatter x1, waiting for transfers between devices, on_device(): lax.psum_scatter(partial_out.astype(jnp.bfloat16), 'row', scatter_dimensi...  48.2 us
    psum x1, blocking collectives, on_device(): lax.psum(jnp.sum(jnp.exp(logits - row_max[:, None]), axis=1), ('req', 'ro...  41.4 us
    pmax x1, blocking collectives, on_device(): row_max = lax.pmax(jnp.max(logits, axis=1), ('req', 'row'))  37.8 us
    all_gather x1, waiting for transfers between devices, on_device(): lax.all_gather(w_key, 'req', axis=0, tiled=True)  32.6 us
    all_to_all x1, waiting for transfers between devices, on_device(): lax.all_to_all(key_cache[0], 'row', split_axis=1, concat_axis=0, tiled=True)  30.8 us
    all_gather x1, waiting for transfers between devices, on_device(): lax.all_gather(w_query, 'req', axis=0, tiled=True)  29.3 us
    all_gather x1, waiting for transfers between devices, on_device(): lax.all_gather(w_value, 'req', axis=0, tiled=True)  27.8 us
    all_to_all x1, waiting for transfers between devices, on_device(): lax.all_to_all(value_cache[0], 'row', split_axis=1, concat_axis=0, tiled=...  24.4 us
  transfers between devices with their start and end apart: 8, of which 8 were waited for; matrix products, arithmetic and copies ran while one was open for 7% of the time, Pallas kernels for 0%

commit v1 on v0

v1 whole, which is shorter than its diff:
```python
import functools

import jax
import jax.numpy as jnp
from jax import lax
from jax.experimental import pallas as pl
from jax.experimental.pallas import tpu as pltpu
from jax.sharding import PartitionSpec as P

HEAD_DIM = 64
EPSILON = 1e-05
VMEM_LIMIT = 56 * 1024 * 1024
ANY = pl.BlockSpec(memory_space=pl.ANY)
SMEM = pl.BlockSpec(memory_space=pltpu.SMEM)
VMEM = pl.BlockSpec(memory_space=pltpu.VMEM)


def rms_scale(values, gain_vec):
    return (
        values * lax.rsqrt(jnp.mean(values * values, axis=-1, keepdims=True) + EPSILON) * gain_vec
    )


def rotary_tables(places):
    half_dim = HEAD_DIM // 2
    frequency = 10000.0 ** (-jnp.arange(half_dim).astype(jnp.float32) / half_dim)
    angles = places.astype(jnp.float32)[:, None] * frequency[None, :]
    cosine, sine = jnp.cos(angles), jnp.sin(angles)
    return (
        jnp.concatenate([cosine] * 4, axis=1),
        jnp.concatenate([-sine, sine, -sine, sine], axis=1),
    )


def up_pairs(size, hop, first=0):
    return [(i, i + hop) for i in range(first, size - hop)]


def down_pairs(size, hop, last=None):
    last = size - 1 if last is None else last
    return [(i, i - hop) for i in range(hop, last + 1)]


def xor_pairs(size, bit):
    return [(i, i ^ bit) for i in range(size)]


def gather_line(block, size):
    ups, downs = [], []
    up, down = block, block
    for step in range(1, size):
        up = lax.ppermute(up, "row", up_pairs(size, 1, step - 1))
        down = lax.ppermute(down, "row", down_pairs(size, 1, size - step))
        ups.append(up)
        downs.append(down)
    return ups, downs


def exchange_line(pieces_for, size):
    me = lax.axis_index("row")
    ups, downs = [], []
    for hop in range(1, size):
        up = pieces_for(jnp.minimum(me + hop, size - 1))
        down = pieces_for(jnp.maximum(me - hop, 0))
        ups.append(lax.ppermute(up, "row", up_pairs(size, hop)))
        downs.append(lax.ppermute(down, "row", down_pairs(size, hop)))
    return ups, downs


def gather_weights(block, size):
    rows = block.shape[0]
    if size != 8:
        whole = lax.all_gather(block, "req", axis=0, tiled=True)
        return [(whole, None, 0, rows * size)]
    half = rows // 2
    from_x = lax.ppermute(block, "req", xor_pairs(size, 2))
    from_y = lax.ppermute(block, "req", xor_pairs(size, 4))
    from_c = lax.ppermute(block, "req", xor_pairs(size, 1))
    diag_a = lax.ppermute(from_y[:half], "req", xor_pairs(size, 2))
    diag_b = lax.ppermute(from_x[half:], "req", xor_pairs(size, 4))
    pieces = [
        (block, 0, 0, rows),
        (from_x, 2, 0, rows),
        (from_y, 4, 0, rows),
        (diag_a, 6, 0, half),
        (diag_b, 6, half, half),
        (from_c, 1, 0, rows),
    ]
    for array, mask, first, count in pieces[1:5]:
        pieces.append((lax.ppermute(array, "req", xor_pairs(size, 1)), mask ^ 1, first, count))
    return pieces


def weight_copies(refs, layout, target, sems, me_req, block_rows):
    copies = []
    for index, (ref, (mask, first, count)) in enumerate(zip(refs, layout)):
        if mask is None:
            start = 0
        else:
            start = pl.multiple_of(jnp.bitwise_xor(me_req, mask) * block_rows + first, 16)
        copies.append(pltpu.make_async_copy(ref, target.at[pl.ds(start, count), :], sems.at[index]))
    return copies


def start_line_copies(own, ups, downs, target, sems, me_row, rows):
    size = len(ups) + 1
    waits = []
    own_copy = pltpu.make_async_copy(own, target.at[pl.ds(me_row * rows, rows), :], sems.at[0])
    own_copy.start()
    waits.append(own_copy)
    for hop in range(1, size):
        index = lax.rem(me_row - hop + size, size)
        place = target.at[pl.ds(pl.multiple_of(index * rows, rows), rows), :]
        below = pltpu.make_async_copy(ups[hop - 1], place, sems.at[hop])
        above = pltpu.make_async_copy(downs[size - hop - 1], place, sems.at[hop])

        @pl.when(me_row >= hop)
        def _(below=below):
            below.start()

        @pl.when(me_row < hop)
        def _(above=above):
            above.start()

        waits.append(below)
    return waits


def qkv_kernel(size, layout, block_rows, scalars, *refs):
    pieces = len(layout)
    own, ups, downs = refs[0], refs[1:size], refs[size : 2 * size - 1]
    weights = refs[2 * size - 1 : 2 * size - 1 + pieces]
    cos_ref, sin_ref, qk_ref, v_ref, x_scr, w_scr, x_sems, w_sems = refs[2 * size - 1 + pieces :]
    rows = own.shape[0]
    copies = weight_copies(weights, layout, w_scr, w_sems, scalars[1], block_rows)
    for copy in copies:
        copy.start()
    waits = start_line_copies(own, ups, downs, x_scr, x_sems, scalars[0], rows)
    for copy in waits + copies:
        copy.wait()
    span = x_scr.shape[0]
    width = v_ref.shape[1]
    lane = lax.broadcasted_iota(jnp.int32, (span, 128), 1)
    first_half = lax.rem(lane, HEAD_DIM) < HEAD_DIM // 2
    cosine, sine = cos_ref[...], sin_ref[...]
    x = x_scr[...]
    for tile in range(0, 2 * width, 256):
        stop = min(tile + 256, 2 * width)
        raw = jnp.dot(x, w_scr[:, tile:stop], preferred_element_type=jnp.float32)
        for at in range(tile, stop, 128):
            part = raw[:, at - tile : at - tile + 128]
            half = HEAD_DIM // 2
            swapped = jnp.where(
                first_half, pltpu.roll(part, 128 - half, 1), pltpu.roll(part, half, 1)
            )
            turned = part * cosine + swapped * sine
            if at + 128 <= width:
                turned = turned * (HEAD_DIM**-0.5)
            elif at < width:
                turned = jnp.where(lane < width - at, turned * (HEAD_DIM**-0.5), turned)
            qk_ref[:, at : at + 128] = turned.astype(jnp.bfloat16)
    for tile in range(0, width, 256):
        stop = min(tile + 256, width)
        v_ref[:, tile:stop] = jnp.dot(
            x, w_scr[:, 2 * width + tile : 2 * width + stop], preferred_element_type=jnp.float32
        ).astype(jnp.bfloat16)


def attend_block(q, k_new, v_new, k_old, v_old, limit_new, length):
    nt = (((1,), (1,)), ((), ()))
    s_new = lax.dot_general(q, k_new, nt, preferred_element_type=jnp.float32)
    s_old = lax.dot_general(q, k_old, nt, preferred_element_type=jnp.float32)
    pos_new = lax.broadcasted_iota(jnp.int32, s_new.shape, 1)
    pos_old = lax.broadcasted_iota(jnp.int32, s_old.shape, 1)
    s_new = jnp.where(pos_new < limit_new, s_new, -jnp.inf)
    s_old = jnp.where(pos_old < length, s_old, -jnp.inf)
    top = jnp.maximum(
        jnp.max(s_new, axis=1, keepdims=True), jnp.max(s_old, axis=1, keepdims=True)
    )
    e_new = jnp.exp(s_new - top)
    e_old = jnp.exp(s_old - top)
    total = jnp.sum(e_new, axis=1, keepdims=True) + jnp.sum(e_old, axis=1, keepdims=True)
    summed = jnp.dot(e_new.astype(jnp.bfloat16), v_new, preferred_element_type=jnp.float32)
    summed += jnp.dot(e_old.astype(jnp.bfloat16), v_old, preferred_element_type=jnp.float32)
    return summed / total


def attention_kernel(size, layout, block_rows, scalars, *refs):
    pieces = len(layout)
    own, ups, downs = refs[0], refs[1:size], refs[size : 2 * size - 1]
    weights = refs[2 * size - 1 : 2 * size - 1 + pieces]
    qk_ref, v_ref, out_ref, old_scr, w_scr, att_scr, x_sems, w_sems = refs[2 * size - 1 + pieces :]
    rows = own.shape[0]
    half_rows = rows // 2
    copies = weight_copies(weights, layout, w_scr, w_sems, scalars[1], block_rows)
    waits = start_line_copies(own, ups, downs, old_scr, x_sems, scalars[0], rows)
    for copy in copies:
        copy.start()
    for copy in waits:
        copy.wait()
    span, width = v_ref.shape
    length, count = scalars[2], scalars[3]
    heads = width // HEAD_DIM
    block = min(256, span)

    def attend(live):
        lane = lax.broadcasted_iota(jnp.int32, (block, 128), 1)
        left = lane < HEAD_DIM
        for at in range(0, heads, 2):
            lo = at * HEAD_DIM
            hi = min(lo + 128, width)
            k_at = width + HEAD_DIM + lo if hi - lo == 128 else width
            k_old = jnp.concatenate(
                [old_scr[i * rows : i * rows + half_rows, lo:hi] for i in range(live)], axis=0
            )
            v_old = jnp.concatenate(
                [old_scr[i * rows + half_rows : (i + 1) * rows, lo:hi] for i in range(live)], axis=0
            )
            for begin in range(0, span, block):
                q = qk_ref[begin : begin + block, lo:hi]
                k_new = qk_ref[0 : begin + block, k_at : k_at + hi - lo]
                v_new = v_ref[0 : begin + block, lo:hi]
                row = begin + lax.broadcasted_iota(jnp.int32, (block, 1), 0)
                limit = jnp.minimum(row + 1, count)
                if hi - lo == 128:
                    zero = jnp.zeros_like(q)
                    even = attend_block(
                        jnp.where(left, q, zero), k_new, v_new, k_old, v_old, limit, length
                    )
                    odd = attend_block(
                        jnp.where(left, zero, q), k_new, v_new, k_old, v_old, limit, length
                    )
                    both = jnp.where(left, even, odd)
                else:
                    both = attend_block(q, k_new, v_new, k_old, v_old, limit, length)
                att_scr[begin : begin + block, lo:hi] = both.astype(jnp.bfloat16)

    @pl.when(length <= half_rows)
    def _():
        attend(1)

    @pl.when(length > half_rows)
    def _():
        attend(size)

    for copy in copies:
        copy.wait()
    attended = att_scr[...]
    for tile in range(0, out_ref.shape[1], 256):
        out_ref[:, tile : tile + 256] = lax.dot_general(
            attended,
            w_scr[tile : tile + 256, :],
            (((1,), (1,)), ((), ())),
            preferred_element_type=jnp.float32,
        ).astype(jnp.bfloat16)


def scatter_line(chunks, size):
    me = lax.axis_index("row")

    def own_part(index):
        return lax.dynamic_index_in_dim(chunks, jnp.clip(index, 0, size - 1), 0, keepdims=False)

    up, down = own_part(me + size - 1), own_part(me - size + 1)
    for step in range(1, size):
        up = lax.ppermute(up, "row", [(i, i + 1) for i in range(step)])
        down = lax.ppermute(down, "row", [(i, i - 1) for i in range(size - step, size)])
        if step < size - 1:
            up = (
                up.astype(jnp.float32) + own_part(me + size - 1 - step).astype(jnp.float32)
            ).astype(jnp.bfloat16)
            down = (
                down.astype(jnp.float32) + own_part(me - size + 1 + step).astype(jnp.float32)
            ).astype(jnp.bfloat16)
    return up.astype(jnp.float32) + down.astype(jnp.float32) + own_part(me).astype(jnp.float32)


def butterfly(value, axis, size, combine):
    bit = 1
    while bit < size:
        value = combine(value, lax.ppermute(value, axis, xor_pairs(size, bit)))
        bit *= 2
    return value


def merge_stats(one, other):
    top = jnp.maximum(one[0], other[0])
    total = one[1] * jnp.exp(one[0] - top) + other[1] * jnp.exp(other[0] - top)
    return jnp.stack([top, total])


def on_device(
    n_req,
    n_row,
    hidden_in,
    cache_len,
    new_count,
    key_cache,
    value_cache,
    attn_gain,
    w_query,
    w_key,
    w_value,
    w_out,
    final_gain,
    head_weight,
):
    me_row = lax.axis_index("row")
    me_req = lax.axis_index("req")
    inputs = hidden_in[0]
    rows, model = inputs.shape
    span = rows * n_row
    block_rows, width = w_query.shape
    length, count = cache_len[0], new_count[0]
    scalars = jnp.stack([me_row, me_req, length, count]).astype(jnp.int32)
    params = pltpu.CompilerParams(vmem_limit_bytes=VMEM_LIMIT)

    normed = rms_scale(inputs.astype(jnp.float32), attn_gain).astype(jnp.bfloat16)
    last = width - width % 128
    joined = jnp.concatenate([w_query, w_key[:, last:], w_key[:, :last], w_value], axis=1)
    x_ups, x_downs = gather_line(normed, n_row)
    w_pieces = gather_weights(joined, n_req)
    out_pieces = gather_weights(w_out.T, n_req)

    def cache_for(owner):
        return jnp.concatenate(
            [
                lax.dynamic_slice_in_dim(key_cache[0], owner * width, width, 1),
                lax.dynamic_slice_in_dim(value_cache[0], owner * width, width, 1),
            ],
            axis=0,
        )

    old_ups, old_downs = exchange_line(cache_for, n_row)
    cosine, sine = rotary_tables(length + jnp.arange(span, dtype=jnp.int32))

    w_layout = tuple(piece[1:] for piece in w_pieces)
    queries_keys, values = pl.pallas_call(
        functools.partial(qkv_kernel, n_row, w_layout, block_rows),
        out_shape=(
            jax.ShapeDtypeStruct((span, 2 * width), jnp.bfloat16),
            jax.ShapeDtypeStruct((span, width), jnp.bfloat16),
        ),
        in_specs=[SMEM] + [ANY] * (2 * n_row - 1 + len(w_pieces)) + [VMEM] * 2,
        out_specs=(VMEM, VMEM),
        scratch_shapes=[
            pltpu.VMEM((span, model), jnp.bfloat16),
            pltpu.VMEM((model, 3 * width), jnp.bfloat16),
            pltpu.SemaphoreType.DMA((n_row,)),
            pltpu.SemaphoreType.DMA((len(w_pieces),)),
        ],
        compiler_params=params,
        cost_estimate=pl.CostEstimate(
            flops=6 * span * model * width, bytes_accessed=14 * 2**20, transcendentals=0
        ),
        name="qkv",
    )(scalars, normed, *x_ups, *x_downs, *[piece[0] for piece in w_pieces], cosine, sine)

    out_layout = tuple(piece[1:] for piece in out_pieces)
    partial = pl.pallas_call(
        functools.partial(attention_kernel, n_row, out_layout, block_rows),
        out_shape=jax.ShapeDtypeStruct((span, model), jnp.bfloat16),
        in_specs=[SMEM] + [ANY] * (2 * n_row - 1 + len(out_pieces)) + [VMEM] * 2,
        out_specs=VMEM,
        scratch_shapes=[
            pltpu.VMEM((2 * key_cache.shape[1] * n_row, width), jnp.bfloat16),
            pltpu.VMEM((model, width), jnp.bfloat16),
            pltpu.VMEM((span, width), jnp.bfloat16),
            pltpu.SemaphoreType.DMA((n_row,)),
            pltpu.SemaphoreType.DMA((len(out_pieces),)),
        ],
        compiler_params=params,
        cost_estimate=pl.CostEstimate(
            flops=8 * span * model * width, bytes_accessed=14 * 2**20, transcendentals=0
        ),
        name="attention",
    )(
        scalars,
        cache_for(me_row),
        *old_ups,
        *old_downs,
        *[piece[0] for piece in out_pieces],
        queries_keys,
        values,
    )

    local_index = count - 1 - me_row * rows
    is_owner = (local_index >= 0) & (local_index < rows)
    residual = lax.dynamic_slice_in_dim(inputs, jnp.clip(local_index, 0, rows - 1), 1, 0)
    last_row = lax.dynamic_slice_in_dim(partial, count - 1, 1, 0).astype(jnp.float32)
    last_row += jnp.where(is_owner, residual.astype(jnp.float32), 0.0)
    last_row = butterfly(last_row, "row", n_row, jnp.add).astype(jnp.bfloat16)
    final_row = rms_scale(last_row.astype(jnp.float32), final_gain).astype(jnp.bfloat16)
    table = jnp.where(jnp.arange(n_req)[:, None] == me_req, final_row, jnp.zeros_like(final_row))
    table = butterfly(table, "req", n_req, jnp.add)
    logits = jnp.dot(table, head_weight, preferred_element_type=jnp.float32)
    top = jnp.max(logits, axis=1)
    stats = jnp.stack([top, jnp.sum(jnp.exp(logits - top[:, None]), axis=1)])
    stats = butterfly(stats, "req", n_req, merge_stats)
    stats = butterfly(stats, "row", n_row, merge_stats)
    logprobs = logits - stats[0][:, None] - jnp.log(stats[1])[:, None]

    own_rows = scatter_line(partial.reshape(n_row, rows, model), n_row)
    layer_rows = (own_rows + inputs.astype(jnp.float32)).astype(jnp.bfloat16)
    return (layer_rows[None], logprobs)


def solution(mesh):
    placed = (
        P("req", "row", None),
        P("req"),
        P("req"),
        P("req", "row", None),
        P("req", "row", None),
        P(),
        P("req", "row"),
        P("req", "row"),
        P("req", "row"),
        P("row", "req"),
        P(),
        P(None, ("req", "row")),
    )
    return jax.shard_map(
        functools.partial(on_device, mesh.shape["req"], mesh.shape["row"]),
        mesh=mesh,
        in_specs=placed,
        out_specs=(P("req", "row", None), P(None, ("req", "row"))),
        check_vma=False,
    )
```

time: 392 us -> 226 us (0.58)
  waiting for transfers between devices: 217 us -> 79 us
  blocking collectives: 99 us -> 0 us
  starting transfers between devices: 10.3 us -> 81.1 us
  Pallas kernels: 0 us -> 24.9 us
  matrix products: 32.9 us -> 8.54 us
  between operations: 16.3 us -> 3.22 us
  local copies, waits for them, and re-layouts: 3.68 us -> 15.6 us
    all_gather x5 -> x0, waiting for transfers between devices: 111 us -> none  [the longest x1 32.6 us: on_device(): lax.all_gather(w_key, 'req', axis=0, tiled=True)]
    ppermute x0 -> x46, starting transfers between devices: none -> 81.1 us  [the longest x10 27.8 us: butterfly(): value = combine(value, lax.ppermute(value, axis, xor_pairs(size, bit)))]
    ppermute x0 -> x46, waiting for transfers between devices: none -> 79 us  [the longest x10 19.8 us: butterfly(): value = combine(value, lax.ppermute(value, axis, xor_pairs(size, bit)))]
    all_to_all x2 -> x0, waiting for transfers between devices: 55.2 us -> none  [the longest x1 30.8 us: on_device(): lax.all_to_all(key_cache[0], 'row', split_axis=1, concat_axis=0, tiled=True)]
    psum x2 -> x0, blocking collectives: 51.8 us -> none  [the longest x1 41.4 us: on_device(): lax.psum(jnp.sum(jnp.exp(logits - row_max[:, None]), axis=1), ('req', 'ro...]
    reduce_scatter x1 -> x0, waiting for transfers between devices: 48.2 us -> none  [on_device(): lax.psum_scatter(partial_out.astype(jnp.bfloat16), 'row', scatter_dimensi...]
    pmax x1 -> x0, blocking collectives: 37.8 us -> none  [on_device(): row_max = lax.pmax(jnp.max(logits, axis=1), ('req', 'row'))]
    pallas_call x0 -> x2, Pallas kernels: none -> 24.9 us  [the longest x1 13.8 us: on_device(): pl.pallas_call(functools.partial(attention_kernel, n_row, out_layout, blo...]
  transfers between devices with their start and end apart: 8 -> 46, of which waited for: 8 -> 18; matrix products, arithmetic and copies ran while one was open for 7% -> 10% of each run, Pallas kernels for 0% -> 5%
where the time goes in v1:
time: 226 us
  starting transfers between devices  81.1 us (36%)
  waiting for transfers between devices  79 us (35%)
  Pallas kernels  24.9 us (11%)
  local copies, waits for them, and re-layouts  15.6 us (7%)
  other arithmetic  13.7 us (6%)
  matrix products  8.54 us (4%)
  between operations  3.22 us (1%)
    ppermute x10, starting transfers between devices, butterfly(): value = combine(value, lax.ppermute(value, axis, xor_pairs(size, bit)))  27.8 us
    ppermute x10, waiting for transfers between devices, butterfly(): value = combine(value, lax.ppermute(value, axis, xor_pairs(size, bit)))  19.8 us
    ppermute x3, waiting for transfers between devices, gather_line(): down = lax.ppermute(down, 'row', down_pairs(size, 1, size - step))  17.8 us
    pallas_call x1, Pallas kernels, on_device(): pl.pallas_call(functools.partial(attention_kernel, n_row, out_layout, blo...  13.8 us
    ppermute x3, starting transfers between devices, exchange_line(): ups.append(lax.ppermute(up, 'row', up_pairs(size, hop)))  12 us
    ppermute x3, waiting for transfers between devices, exchange_line(): downs.append(lax.ppermute(down, 'row', down_pairs(size, hop)))  12 us
    pallas_call x1, Pallas kernels, on_device(): pl.pallas_call(functools.partial(qkv_kernel, n_row, w_layout, block_rows)...  11.1 us
    ppermute x2, waiting for transfers between devices, gather_weights(): from_x = lax.ppermute(block, 'req', xor_pairs(size, 2))  9.55 us
  transfers between devices with their start and end apart: 46, of which 18 were waited for; matrix products, arithmetic and copies ran while one was open for 10% of the time, Pallas kernels for 5%

profile of v1, /device:TPU:0, one launch (start us, length us, event | category | flops | bytes accessed | tf_op | source)
XLA Modules:
  0.0 226.0 jit_solution(14190082033249732363)
XLA Ops:
  0.6 3.1 %dynamic-slice_bitcast_fusion.2 = (bf16[128,576]{1,0:T(8,128)(2,1)S(1)}, bf16[128,576]{1,0:T(8,128)(2,1)S(1)}, bf16[128,576]{1,0:T(8,128)(2,1)S(1)}, bf16[128,57...) fusion(bf16[1,128,2304]{2,1,0:T(8,128)(2,1)} %param.16, ...), kind=kLoop, calls=%fused_computation.30 | loop fusion | bytes 4128796 | tf_op jit(solution)/shard_map/dynamic_slice | solution.py:329
  5.1 1.4 collective-permute-start.5
  6.6 1.3 collective-permute-start.3
  7.9 7.9 %collective-permute-start.2 = (bf16[256,576]{1,0:T(8,128)(2,1)S(1)}, bf16[256,576]{1,0:T(8,128)(2,1)S(1)}, u32[]{:S(2)}, u32[]{:S(2)}) collective-permute-start(bf16[256,576]{1,0:T(8,128)(2,1)S(1)} %pad_maximum_fusion.3), channel_id=1, source_target_pairs={{0,3},{4,7},{8,11},{12,15},{16,19},{20,23},{24,27},{28,31}} | collective-permute-start | bytes 884744 | tf_op jit(solution)/shard_map/ppermute | solution.py:65
  16.6 2.0 collective-permute-start.1
  19.6 11.9 %collective-permute-done.4.refs_5_ = bf16[256,576]{1,0:T(8,128)(2,1)S(1)} collective-permute-done((bf16[256,576]{1,0:T(8,128)(2,1)S(1)}, bf16[256,576]{1,0:T(8,128)(2,1)S(1)}, u32[]{:S(2)}, u32[]{:S(2)}) %collective-permute-start.4) | collective-permute-done | bytes 294944 | tf_op jit(solution)/shard_map/ppermute | solution.py:66
  31.6 2.0 collective-permute-start
  34.3 2.5 %collective-permute-start.7 = (bf16[288,576]{1,0:T(8,128)(2,1)}, bf16[288,576]{1,0:T(8,128)(2,1)}, u32[]{:S(2)}, u32[]{:S(2)}) collective-permute-start(bf16[288,576]{1,0:T(8,128)(2,1)} %bitcast.16.refs_7_), channel_id=1, source_target_pairs={{0,16},{4,20},{8,24},{12,28},{16,0},{20,4},{24,8},{28,12},{1,17},{... | collective-permute-start | bytes 995336 | tf_op jit(solution)/shard_map/ppermute | solution.py:77
  37.1 3.9 %collective-permute-start.15 = (bf16[128,2304]{1,0:T(8,128)(2,1)S(1)}, bf16[128,2304]{1,0:T(8,128)(2,1)}, u32[]{:S(2)}, u32[]{:S(2)}) collective-permute-start(bf16[128,2304]{1,0:T(8,128)(2,1)S(1)} %fusion.2.refs_0_), channel_id=1, source_target_pairs={{0,1},{1,2},{2,3},{4,5},{5,6},{6,7},{8,9},{9,10},{10,11},{12,13},{... | collective-permute-start | bytes 1769480 | tf_op jit(solution)/shard_map/ppermute | solution.py:52
  41.0 2.3 %collective-permute-start.6 = (bf16[288,576]{1,0:T(8,128)(2,1)}, bf16[288,576]{1,0:T(8,128)(2,1)}, u32[]{:S(2)}, u32[]{:S(2)}) collective-permute-start(bf16[288,576]{1,0:T(8,128)(2,1)} %bitcast.16.refs_7_), channel_id=1, source_target_pairs={{0,8},{4,12},{8,0},{12,4},{16,24},{20,28},{24,16},{28,20},{1,9},{5... | collective-permute-start | bytes 995336 | tf_op jit(solution)/shard_map/ppermute | solution.py:76
  43.4 2.0 concatenate.37.refs_7_
  45.4 1.6 collective-permute-start.22
  49.0 4.2 %collective-permute-done.6.refs_8_ = bf16[288,576]{1,0:T(8,128)(2,1)} collective-permute-done((bf16[288,576]{1,0:T(8,128)(2,1)}, bf16[288,576]{1,0:T(8,128)(2,1)}, u32[]{:S(2)}, u32[]{:S(2)}) %collective-permute-start.6) | collective-permute-done | bytes 331808 | tf_op jit(solution)/shard_map/ppermute | solution.py:76
  53.2 1.5 collective-permute-start.16
  54.7 8.5 %collective-permute-done.18.refs_4_ = bf16[128,2304]{1,0:T(8,128)(2,1)S(1)} collective-permute-done((bf16[128,2304]{1,0:T(8,128)(2,1)S(1)}, bf16[128,2304]{1,0:T(8,128)(2,1)S(1)}, u32[]{:S(2)}, u32[]{:S(2)}) %collective-permute-start.18) | collective-permute-done | bytes 589856 | tf_op jit(solution)/shard_map/ppermute | solution.py:53
  66.3 2.6 %collective-permute-done.22.refs_9_ = bf16[288,1728]{1,0:T(8,128)(2,1)} collective-permute-done((bf16[288,1728]{1,0:T(8,128)(2,1)S(1)}, bf16[288,1728]{1,0:T(8,128)(2,1)}, u32[]{:S(2)}, u32[]{:S(2)}) %collective-permute-start.22) | collective-permute-done | bytes 995360 | tf_op jit(solution)/shard_map/ppermute | solution.py:77
  69.9 5.4 %collective-permute-done.21.refs_8_ = bf16[288,1728]{1,0:T(8,128)(2,1)} collective-permute-done((bf16[288,1728]{1,0:T(8,128)(2,1)S(1)}, bf16[288,1728]{1,0:T(8,128)(2,1)}, u32[]{:S(2)}, u32[]{:S(2)}) %collective-permute-start.21) | collective-permute-done | bytes 995360 | tf_op jit(solution)/shard_map/ppermute | solution.py:76
  75.3 1.9 collective-permute-start.9
  77.2 1.5 collective-permute-start.17
  80.8 1.6 collective-permute-start.23
  82.4 2.1 collective-permute-start.24
  88.2 2.2 collective-permute-done.23.refs_10_
  96.2 9.4 %collective-permute-done.20.refs_6_ = bf16[128,2304]{1,0:T(8,128)(2,1)S(1)} collective-permute-done((bf16[128,2304]{1,0:T(8,128)(2,1)}, bf16[128,2304]{1,0:T(8,128)(2,1)S(1)}, u32[]{:S(2)}, u32[]{:S(2)}) %collective-permute-start.20) | collective-permute-done | bytes 589856 | tf_op jit(solution)/shard_map/ppermute | solution.py:53
  107.1 11.1 %qkv.1 = (bf16[512,1152]{1,0:T(8,128)(2,1)}, bf16[512,576]{1,0:T(8,128)(2,1)}) custom-call(s32[4]{0:T(128)} %pad_add_fusion.scalars, bf16[128,2304]{1,0:T(8,128)(2,1)} %copy-done.3, bf16[128,2304]{1,0:T(8,128)(2,1)} %collective-permute-done.15.refs_1_, bf16[128,2304]{1,0:T(8,128)(2,1)} %collective-permute-done.16.refs_2_, ...), custom_call_target="tpu_custom_call" | custom-call | flops 4076863488 | bytes 14680064 | tf_op jit(solution)/shard_map/qkv/pallas_call | solution.py:338
  119.4 13.8 %attention.1 = bf16[512,2304]{1,0:T(8,128)(2,1)} custom-call(s32[4]{0:T(128)} %pad_add_fusion.scalars, bf16[256,576]{1,0:T(8,128)(2,1)} %pad_maximum_fusion.refs_0_, bf16[256,576]{1,0:T(8,128)(2,1)} %collective-permute-done.refs_1_, bf16[256,576]{1,0:T(8,128)(2,1)} %collective-permute-done.1.refs_2_, bf16[256,576]{1,0:T(8,128)(2,1)} %copy-done.19, ...), custom_call_target="tpu_custom_call" | custom-call | flops 5435817984 | bytes 14680064 | tf_op jit(solution)/shard_map/attention/pallas_call | solution.py:360
  134.0 3.6 %collective-permute-done.36 = f32[1,2304]{1,0:T(1,128)S(1)} collective-permute-done((f32[1,2304]{1,0:T(1,128)S(1)}, f32[1,2304]{1,0:T(1,128)S(1)}, u32[]{:S(2)}, u32[]{:S(2)}) %collective-permute-start.36) | collective-permute-done | bytes 9248 | tf_op jit(solution)/shard_map/ppermute | solution.py:281
  137.8 4.5 %collective-permute-done.37 = f32[1,2304]{1,0:T(1,128)S(1)} collective-permute-done((f32[1,2304]{1,0:T(1,128)S(1)}, f32[1,2304]{1,0:T(1,128)S(1)}, u32[]{:S(2)}, u32[]{:S(2)}) %collective-permute-start.37) | collective-permute-done | bytes 9248 | tf_op jit(solution)/shard_map/ppermute | solution.py:281
  145.1 1.7 collective-permute-start.39
  146.8 2.3 %collective-permute-done.39 = bf16[8,2304]{1,0:T(8,128)(2,1)S(1)} collective-permute-done((bf16[8,2304]{1,0:T(8,128)(2,1)S(1)}, bf16[8,2304]{1,0:T(8,128)(2,1)S(1)}, u32[]{:S(2)}, u32[]{:S(2)}) %collective-permute-start.39) | collective-permute-done | bytes 36896 | tf_op jit(solution)/shard_map/ppermute | solution.py:281
  149.1 2.6 %collective-permute-start.40 = (bf16[8,2304]{1,0:T(8,128)(2,1)S(1)}, bf16[8,2304]{1,0:T(8,128)(2,1)S(1)}, u32[]{:S(2)}, u32[]{:S(2)}) collective-permute-start(bf16[8,2304]{1,0:T(8,128)(2,1)S(1)} %fusion.32), channel_id=1, source_target_pairs={{0,16},{4,20},{8,24},{12,28},{16,0},{20,4},{24,8},{28,12},{1,17},{... | collective-permute-start | bytes 110600 | tf_op jit(solution)/shard_map/ppermute | solution.py:281
  151.7 2.3 %dynamic-slice_bitcast_fusion.1 = (bf16[128,2304]{1,0:T(8,128)(2,1)}, bf16[128,2304]{1,0:T(8,128)(2,1)}) fusion(bf16[4,128,2304]{2,1,0:T(8,128)(2,1)} %bitcast.167, s32[]{:T(128)S(6)} %min.37, s32[]{:T(128)S(6)} %min.40), kind=kLoop, calls=%fused_computation.18 | loop fusion | bytes 2359304 | tf_op jit(solution)/shard_map/jit(dynamic_index_in_dim)/squeeze | solution.py:262
  154.0 2.9 %collective-permute-start.30 = (bf16[128,2304]{1,0:T(8,128)(2,1)}, bf16[128,2304]{1,0:T(8,128)(2,1)}, u32[]{:S(2)}, u32[]{:S(2)}) collective-permute-start(bf16[128,2304]{1,0:T(8,128)(2,1)} %get-tuple-element.18), channel_id=1, source_target_pairs={{0,1},{4,5},{8,9},{12,13},{16,17},{20,21},{24,25},{28,29}} | collective-permute-start | bytes 1769480 | tf_op jit(solution)/shard_map/ppermute | solution.py:266
  156.9 8.5 %fusion.30 = (f32[8]{0:T(128)S(1)}, f32[8,3840]{1,0:T(8,128)S(1)}) fusion(bf16[2304,3840]{1,0:T(8,128)(2,1)} %param.23, bf16[8,2304]{1,0:T(8,128)(2,1)S(1)} %fusion.32, bf16[8,2304]{1,0:T(8,128)(2,1)S(1)} %collective-permute-done.40), kind=kOutput, calls=%fused_computation.104 | convolution fusion | flops 141606912 | bytes 17891360 | tf_op jit(solution)/shard_map/dot_general | solution.py:396
  165.8 1.5 collective-permute-start.33
  167.3 2.1 collective-permute-start.42
  169.4 1.5 collective-permute-done.42
  171.1 3.5 %collective-permute-done.43 = f32[2,8]{1,0:T(2,128)S(1)} collective-permute-done((f32[2,8]{1,0:T(2,128)S(1)}, f32[2,8]{1,0:T(2,128)S(1)}, u32[]{:S(2)}, u32[]{:S(2)}) %collective-permute-start.43) | collective-permute-done | bytes 96 | tf_op jit(solution)/shard_map/ppermute | solution.py:281
  174.7 2.5 %fusion.7 = (bf16[128,2304]{1,0:T(8,128)(2,1)}, bf16[128,2304]{1,0:T(8,128)(2,1)}) fusion(bf16[128,2304]{1,0:T(8,128)(2,1)} %collective-permute-done.30, bf16[4,128,2304]{2,1,0:T(8,128)(2,1)S(1)} %bitcast.168, s32[]{:T(128)S(6)} %min.38, s32[]{:T(128)S(6)} %min.41, bf16[128,2304]{1,0:T(8,128)(2,1)} %collective-permute-done.33), kind=kLoop, calls=%fused_computation.15 | loop fusion | flops 2359296 | bytes 3538952 | tf_op jit(solution)/shard_map/convert_element_type | solution.py:271
  177.2 2.2 collective-permute-start.31
  179.3 1.5 collective-permute-start.34
  180.8 8.0 %collective-permute-start.44 = (f32[2,8]{1,0:T(2,128)S(1)}, f32[2,8]{1,0:T(2,128)S(1)}, u32[]{:S(2)}, u32[]{:S(2)}) collective-permute-start(f32[2,8]{1,0:T(2,128)S(1)} %pad_maximum_fusion.12), channel_id=1, source_target_pairs={{0,1},{1,0},{2,3},{3,2},{4,5},{5,4},{6,7},{7,6},{8,9},{9,8},{10,11... | collective-permute-start | bytes 200 | tf_op jit(solution)/shard_map/ppermute | solution.py:281
  188.8 1.5 collective-permute-done.44
  190.4 13.1 %collective-permute-start.45 = (f32[2,8]{1,0:T(2,128)S(1)}, f32[2,8]{1,0:T(2,128)S(1)}, u32[]{:S(2)}, u32[]{:S(2)}) collective-permute-start(f32[2,8]{1,0:T(2,128)S(1)} %pad_maximum_fusion.13), channel_id=1, source_target_pairs={{0,2},{1,3},{2,0},{3,1},{4,6},{5,7},{6,4},{7,5},{8,10},{9,11},{10,... | collective-permute-start | bytes 200 | tf_op jit(solution)/shard_map/ppermute | solution.py:281
  203.5 1.5 collective-permute-done.45
  205.1 1.5 fusion.6
  206.6 1.5 collective-permute-start.32
  210.2 8.8 %collective-permute-done.32 = bf16[128,2304]{1,0:T(8,128)(2,1)S(1)} collective-permute-done((bf16[128,2304]{1,0:T(8,128)(2,1)S(1)}, bf16[128,2304]{1,0:T(8,128)(2,1)S(1)}, u32[]{:S(2)}, u32[]{:S(2)}) %collective-permute-start.32) | collective-permute-done | bytes 589856 | tf_op jit(solution)/shard_map/ppermute | solution.py:266
  219.0 5.8 %collective-permute-done.35 = bf16[128,2304]{1,0:T(8,128)(2,1)S(1)} collective-permute-done((bf16[128,2304]{1,0:T(8,128)(2,1)S(1)}, bf16[128,2304]{1,0:T(8,128)(2,1)S(1)}, u32[]{:S(2)}, u32[]{:S(2)}) %collective-permute-start.35) | collective-permute-done | bytes 589856 | tf_op jit(solution)/shard_map/ppermute | solution.py:267
  (148 shorter events, 30.0 us)
Async XLA Ops:
  3.8 27.8 %collective-permute-start.4 = (bf16[256,576]{1,0:T(8,128)(2,1)S(1)}, bf16[256,576]{1,0:T(8,128)(2,1)S(1)}, u32[]{:S(2)}, u32[]{:S(2)}) collective-permute-start(bf16[256,576]{1,0:T(8,128)(2,1)S(1)} %pad_maximum_fusion.5), channel_id=1, source_target_pairs={{2,0},{3,1},{6,4},{7,5},{10,8},{11,9},{14,12},{15,13},{18,16},{19,... | collective-permute-start | bytes 884744 | tf_op jit(solution)/shard_map/ppermute | solution.py:66
  5.1 28.5 %collective-permute-start.5 = (bf16[256,576]{1,0:T(8,128)(2,1)S(1)}, bf16[256,576]{1,0:T(8,128)(2,1)S(1)}, u32[]{:S(2)}, u32[]{:S(2)}) collective-permute-start(bf16[256,576]{1,0:T(8,128)(2,1)S(1)} %pad_maximum_fusion.6), channel_id=1, source_target_pairs={{3,0},{7,4},{11,8},{15,12},{19,16},{23,20},{27,24},{31,28}} | collective-permute-start | bytes 884744 | tf_op jit(solution)/shard_map/ppermute | solution.py:66
  6.6 30.5 %collective-permute-start.3 = (bf16[256,576]{1,0:T(8,128)(2,1)S(1)}, bf16[256,576]{1,0:T(8,128)(2,1)S(1)}, u32[]{:S(2)}, u32[]{:S(2)}) collective-permute-start(bf16[256,576]{1,0:T(8,128)(2,1)S(1)} %pad_maximum_fusion.4), channel_id=1, source_target_pairs={{1,0},{2,1},{3,2},{5,4},{6,5},{7,6},{9,8},{10,9},{11,10},{13,12},{... | collective-permute-start | bytes 884744 | tf_op jit(solution)/shard_map/ppermute | solution.py:66
  7.9 29.0 %copy-start.5 = (f32[2304]{0:T(1024)S(1)}, f32[2304]{0:T(1024)}, u32[]{:S(2)}) copy-start(f32[2304]{0:T(1024)} %param.17) | copy-start | bytes 27652
  7.9 33.1 %collective-permute-start.2 = (bf16[256,576]{1,0:T(8,128)(2,1)S(1)}, bf16[256,576]{1,0:T(8,128)(2,1)S(1)}, u32[]{:S(2)}, u32[]{:S(2)}) collective-permute-start(bf16[256,576]{1,0:T(8,128)(2,1)S(1)} %pad_maximum_fusion.3), channel_id=1, source_target_pairs={{0,3},{4,7},{8,11},{12,15},{16,19},{20,23},{24,27},{28,31}} | collective-permute-start | bytes 884744 | tf_op jit(solution)/shard_map/ppermute | solution.py:65
  16.6 28.8 %collective-permute-start.1 = (bf16[256,576]{1,0:T(8,128)(2,1)}, bf16[256,576]{1,0:T(8,128)(2,1)}, u32[]{:S(2)}, u32[]{:S(2)}) collective-permute-start(bf16[256,576]{1,0:T(8,128)(2,1)} %pad_maximum_fusion.2), channel_id=1, source_target_pairs={{0,2},{1,3},{4,6},{5,7},{8,10},{9,11},{12,14},{13,15},{16,18},{17,... | collective-permute-start | bytes 884744 | tf_op jit(solution)/shard_map/ppermute | solution.py:65
  31.6 15.5 %collective-permute-start = (bf16[256,576]{1,0:T(8,128)(2,1)}, bf16[256,576]{1,0:T(8,128)(2,1)}, u32[]{:S(2)}, u32[]{:S(2)}) collective-permute-start(bf16[256,576]{1,0:T(8,128)(2,1)} %pad_maximum_fusion.1), channel_id=1, source_target_pairs={{0,1},{1,2},{2,3},{4,5},{5,6},{6,7},{8,9},{9,10},{10,11},{12,13},{... | collective-permute-start | bytes 884744 | tf_op jit(solution)/shard_map/ppermute | solution.py:65
  34.3 13.4 %collective-permute-start.7 = (bf16[288,576]{1,0:T(8,128)(2,1)}, bf16[288,576]{1,0:T(8,128)(2,1)}, u32[]{:S(2)}, u32[]{:S(2)}) collective-permute-start(bf16[288,576]{1,0:T(8,128)(2,1)} %bitcast.16.refs_7_), channel_id=1, source_target_pairs={{0,16},{4,20},{8,24},{12,28},{16,0},{20,4},{24,8},{28,12},{1,17},{... | collective-permute-start | bytes 995336 | tf_op jit(solution)/shard_map/ppermute | solution.py:77
  37.1 16.0 %collective-permute-start.15 = (bf16[128,2304]{1,0:T(8,128)(2,1)S(1)}, bf16[128,2304]{1,0:T(8,128)(2,1)}, u32[]{:S(2)}, u32[]{:S(2)}) collective-permute-start(bf16[128,2304]{1,0:T(8,128)(2,1)S(1)} %fusion.2.refs_0_), channel_id=1, source_target_pairs={{0,1},{1,2},{2,3},{4,5},{5,6},{6,7},{8,9},{9,10},{10,11},{12,13},{... | collective-permute-start | bytes 1769480 | tf_op jit(solution)/shard_map/ppermute | solution.py:52
  41.0 12.1 %collective-permute-start.6 = (bf16[288,576]{1,0:T(8,128)(2,1)}, bf16[288,576]{1,0:T(8,128)(2,1)}, u32[]{:S(2)}, u32[]{:S(2)}) collective-permute-start(bf16[288,576]{1,0:T(8,128)(2,1)} %bitcast.16.refs_7_), channel_id=1, source_target_pairs={{0,8},{4,12},{8,0},{12,4},{16,24},{20,28},{24,16},{28,20},{1,9},{5... | collective-permute-start | bytes 995336 | tf_op jit(solution)/shard_map/ppermute | solution.py:76
  45.4 35.4 %copy-start.2 = (bf16[288,1728]{1,0:T(8,128)(2,1)}, bf16[288,1728]{1,0:T(8,128)(2,1)S(1)}, u32[]{:S(2)}) copy-start(bf16[288,1728]{1,0:T(8,128)(2,1)S(1)} %concatenate.37.refs_7_) | copy-start | bytes 2985988
  45.4 23.5 %collective-permute-start.22 = (bf16[288,1728]{1,0:T(8,128)(2,1)S(1)}, bf16[288,1728]{1,0:T(8,128)(2,1)}, u32[]{:S(2)}, u32[]{:S(2)}) collective-permute-start(bf16[288,1728]{1,0:T(8,128)(2,1)S(1)} %concatenate.37.refs_7_), channel_id=1, source_target_pairs={{0,16},{4,20},{8,24},{12,28},{16,0},{20,4},{24,8},{28,12},{1,17},{... | collective-permute-start | bytes 2985992 | tf_op jit(solution)/shard_map/ppermute | solution.py:77
  47.0 28.3 %collective-permute-start.21 = (bf16[288,1728]{1,0:T(8,128)(2,1)S(1)}, bf16[288,1728]{1,0:T(8,128)(2,1)}, u32[]{:S(2)}, u32[]{:S(2)}) collective-permute-start(bf16[288,1728]{1,0:T(8,128)(2,1)S(1)} %concatenate.37.refs_7_), channel_id=1, source_target_pairs={{0,8},{4,12},{8,0},{12,4},{16,24},{20,28},{24,16},{28,20},{1,9},{5... | collective-permute-start | bytes 2985992 | tf_op jit(solution)/shard_map/ppermute | solution.py:76
  47.7 15.4 %collective-permute-start.18 = (bf16[128,2304]{1,0:T(8,128)(2,1)S(1)}, bf16[128,2304]{1,0:T(8,128)(2,1)S(1)}, u32[]{:S(2)}, u32[]{:S(2)}) collective-permute-start(bf16[128,2304]{1,0:T(8,128)(2,1)S(1)} %fusion.2.refs_0_), channel_id=1, source_target_pairs={{1,0},{2,1},{3,2},{5,4},{6,5},{7,6},{9,8},{10,9},{11,10},{13,12},{... | collective-permute-start | bytes 1769480 | tf_op jit(solution)/shard_map/ppermute | solution.py:53
  53.2 31.3 %collective-permute-start.25 = (bf16[288,1728]{1,0:T(8,128)(2,1)S(1)}, bf16[288,1728]{1,0:T(8,128)(2,1)S(1)}, u32[]{:S(2)}, u32[]{:S(2)}) collective-permute-start(bf16[288,1728]{1,0:T(8,128)(2,1)S(1)} %concatenate.37.refs_7_), channel_id=1, source_target_pairs={{0,4},{4,0},{8,12},{12,8},{16,20},{20,16},{24,28},{28,24},{1,5},{5... | collective-permute-start | bytes 2985992 | tf_op jit(solution)/shard_map/ppermute | solution.py:78
  53.2 24.0 %collective-permute-start.16 = (bf16[128,2304]{1,0:T(8,128)(2,1)}, bf16[128,2304]{1,0:T(8,128)(2,1)}, u32[]{:S(2)}, u32[]{:S(2)}) collective-permute-start(bf16[128,2304]{1,0:T(8,128)(2,1)} %collective-permute-done.15.refs_1_), channel_id=1, source_target_pairs={{1,2},{2,3},{5,6},{6,7},{9,10},{10,11},{13,14},{14,15},{17,18},{18... | collective-permute-start | bytes 1769480 | tf_op jit(solution)/shard_map/ppermute | solution.py:52
  63.2 22.3 %collective-permute-start.19 = (bf16[128,2304]{1,0:T(8,128)(2,1)S(1)}, bf16[128,2304]{1,0:T(8,128)(2,1)S(1)}, u32[]{:S(2)}, u32[]{:S(2)}) collective-permute-start(bf16[128,2304]{1,0:T(8,128)(2,1)S(1)} %collective-permute-done.18.refs_4_), channel_id=1, source_target_pairs={{1,0},{2,1},{5,4},{6,5},{9,8},{10,9},{13,12},{14,13},{17,16},{18,1... | collective-permute-start | bytes 1769480 | tf_op jit(solution)/shard_map/ppermute | solution.py:53
  68.9 11.9 %collective-permute-start.8 = (bf16[144,576]{1,0:T(8,128)(2,1)S(1)}, bf16[144,576]{1,0:T(8,128)(2,1)S(1)}, u32[]{:S(2)}, u32[]{:S(2)}) collective-permute-start(bf16[144,576]{1,0:T(8,128)(2,1)S(1)} %slice.69), channel_id=1, source_target_pairs={{0,8},{4,12},{8,0},{12,4},{16,24},{20,28},{24,16},{28,20},{1,9},{5... | collective-permute-start | bytes 497672 | tf_op jit(solution)/shard_map/ppermute | solution.py:79
  75.3 7.1 %collective-permute-start.9 = (bf16[144,576]{1,0:T(8,128)(2,1)S(1)}, bf16[144,576]{1,0:T(8,128)(2,1)S(1)}, u32[]{:S(2)}, u32[]{:S(2)}) collective-permute-start(bf16[144,576]{1,0:T(8,128)(2,1)S(1)} %slice.70), channel_id=1, source_target_pairs={{0,16},{4,20},{8,24},{12,28},{16,0},{20,4},{24,8},{28,12},{1,17},{... | collective-permute-start | bytes 497672 | tf_op jit(solution)/shard_map/ppermute | solution.py:80
  77.2 14.8 %collective-permute-start.17 = (bf16[128,2304]{1,0:T(8,128)(2,1)}, bf16[128,2304]{1,0:T(8,128)(2,1)}, u32[]{:S(2)}, u32[]{:S(2)}) collective-permute-start(bf16[128,2304]{1,0:T(8,128)(2,1)} %collective-permute-done.16.refs_2_), channel_id=1, source_target_pairs={{2,3},{6,7},{10,11},{14,15},{18,19},{22,23},{26,27},{30,31}} | collective-permute-start | bytes 1769480 | tf_op jit(solution)/shard_map/ppermute | solution.py:52
  80.8 9.5 %collective-permute-start.23 = (bf16[144,1728]{1,0:T(8,128)(2,1)S(1)}, bf16[144,1728]{1,0:T(8,128)(2,1)}, u32[]{:S(2)}, u32[]{:S(2)}) collective-permute-start(bf16[144,1728]{1,0:T(8,128)(2,1)S(1)} %slice.71), channel_id=1, source_target_pairs={{0,8},{4,12},{8,0},{12,4},{16,24},{20,28},{24,16},{28,20},{1,9},{5... | collective-permute-start | bytes 1493000 | tf_op jit(solution)/shard_map/ppermute | solution.py:79
  82.4 9.6 %collective-permute-start.24 = (bf16[144,1728]{1,0:T(8,128)(2,1)S(1)}, bf16[144,1728]{1,0:T(8,128)(2,1)}, u32[]{:S(2)}, u32[]{:S(2)}) collective-permute-start(bf16[144,1728]{1,0:T(8,128)(2,1)S(1)} %slice.72), channel_id=1, source_target_pairs={{0,16},{4,20},{8,24},{12,28},{16,0},{20,4},{24,8},{28,12},{1,17},{... | collective-permute-start | bytes 1493000 | tf_op jit(solution)/shard_map/ppermute | solution.py:80
  85.5 20.7 %collective-permute-start.26 = (bf16[288,1728]{1,0:T(8,128)(2,1)}, bf16[288,1728]{1,0:T(8,128)(2,1)S(1)}, u32[]{:S(2)}, u32[]{:S(2)}) collective-permute-start(bf16[288,1728]{1,0:T(8,128)(2,1)} %collective-permute-done.21.refs_8_), channel_id=1, source_target_pairs={{0,4},{4,0},{8,12},{12,8},{16,20},{20,16},{24,28},{28,24},{1,5},{5... | collective-permute-start | bytes 2985992 | tf_op jit(solution)/shard_map/ppermute | solution.py:90
  86.4 20.3 %collective-permute-start.27 = (bf16[288,1728]{1,0:T(8,128)(2,1)}, bf16[288,1728]{1,0:T(8,128)(2,1)}, u32[]{:S(2)}, u32[]{:S(2)}) collective-permute-start(bf16[288,1728]{1,0:T(8,128)(2,1)} %collective-permute-done.22.refs_9_), channel_id=1, source_target_pairs={{0,4},{4,0},{8,12},{12,8},{16,20},{20,16},{24,28},{28,24},{1,5},{5... | collective-permute-start | bytes 2985992 | tf_op jit(solution)/shard_map/ppermute | solution.py:90
  90.4 15.2 %collective-permute-start.20 = (bf16[128,2304]{1,0:T(8,128)(2,1)}, bf16[128,2304]{1,0:T(8,128)(2,1)S(1)}, u32[]{:S(2)}, u32[]{:S(2)}) collective-permute-start(bf16[128,2304]{1,0:T(8,128)(2,1)} %copy-done.10), channel_id=1, source_target_pairs={{1,0},{5,4},{9,8},{13,12},{17,16},{21,20},{25,24},{29,28}} | collective-permute-start | bytes 1769480 | tf_op jit(solution)/shard_map/ppermute | solution.py:53
  92.0 13.6 %collective-permute-start.28 = (bf16[144,1728]{1,0:T(8,128)(2,1)}, bf16[144,1728]{1,0:T(8,128)(2,1)S(1)}, u32[]{:S(2)}, u32[]{:S(2)}) collective-permute-start(bf16[144,1728]{1,0:T(8,128)(2,1)} %collective-permute-done.23.refs_10_), channel_id=1, source_target_pairs={{0,4},{4,0},{8,12},{12,8},{16,20},{20,16},{24,28},{28,24},{1,5},{5... | collective-permute-start | bytes 1493000 | tf_op jit(solution)/shard_map/ppermute | solution.py:90
  92.0 14.1 %collective-permute-start.29 = (bf16[144,1728]{1,0:T(8,128)(2,1)}, bf16[144,1728]{1,0:T(8,128)(2,1)}, u32[]{:S(2)}, u32[]{:S(2)}) collective-permute-start(bf16[144,1728]{1,0:T(8,128)(2,1)} %collective-permute-done.24.refs_11_), channel_id=1, source_target_pairs={{0,4},{4,0},{8,12},{12,8},{16,20},{20,16},{24,28},{28,24},{1,5},{5... | collective-permute-start | bytes 1493000 | tf_op jit(solution)/shard_map/ppermute | solution.py:90
  105.6 12.7 %collective-permute-start.10 = (bf16[288,576]{1,0:T(8,128)(2,1)}, bf16[288,576]{1,0:T(8,128)(2,1)S(1)}, u32[]{:S(2)}, u32[]{:S(2)}) collective-permute-start(bf16[288,576]{1,0:T(8,128)(2,1)} %bitcast.16.refs_7_), channel_id=1, source_target_pairs={{0,4},{4,0},{8,12},{12,8},{16,20},{20,16},{24,28},{28,24},{1,5},{5... | collective-permute-start | bytes 995336 | tf_op jit(solution)/shard_map/ppermute | solution.py:78
  105.6 12.7 %collective-permute-start.11 = (bf16[288,576]{1,0:T(8,128)(2,1)}, bf16[288,576]{1,0:T(8,128)(2,1)S(1)}, u32[]{:S(2)}, u32[]{:S(2)}) collective-permute-start(bf16[288,576]{1,0:T(8,128)(2,1)} %collective-permute-done.6.refs_8_), channel_id=1, source_target_pairs={{0,4},{4,0},{8,12},{12,8},{16,20},{20,16},{24,28},{28,24},{1,5},{5... | collective-permute-start | bytes 995336 | tf_op jit(solution)/shard_map/ppermute | solution.py:90
  106.1 12.2 %collective-permute-start.12 = (bf16[288,576]{1,0:T(8,128)(2,1)}, bf16[288,576]{1,0:T(8,128)(2,1)S(1)}, u32[]{:S(2)}, u32[]{:S(2)}) collective-permute-start(bf16[288,576]{1,0:T(8,128)(2,1)} %collective-permute-done.7.refs_9_), channel_id=1, source_target_pairs={{0,4},{4,0},{8,12},{12,8},{16,20},{20,16},{24,28},{28,24},{1,5},{5... | collective-permute-start | bytes 995336 | tf_op jit(solution)/shard_map/ppermute | solution.py:90
  106.2 12.1 %collective-permute-start.13 = (bf16[144,576]{1,0:T(8,128)(2,1)S(1)}, bf16[144,576]{1,0:T(8,128)(2,1)S(1)}, u32[]{:S(2)}, u32[]{:S(2)}) collective-permute-start(bf16[144,576]{1,0:T(8,128)(2,1)S(1)} %copy-done.21), channel_id=1, source_target_pairs={{0,4},{4,0},{8,12},{12,8},{16,20},{20,16},{24,28},{28,24},{1,5},{5... | collective-permute-start | bytes 497672 | tf_op jit(solution)/shard_map/ppermute | solution.py:90
  106.7 11.6 %collective-permute-start.14 = (bf16[144,576]{1,0:T(8,128)(2,1)S(1)}, bf16[144,576]{1,0:T(8,128)(2,1)S(1)}, u32[]{:S(2)}, u32[]{:S(2)}) collective-permute-start(bf16[144,576]{1,0:T(8,128)(2,1)S(1)} %copy-done.23), channel_id=1, source_target_pairs={{0,4},{4,0},{8,12},{12,8},{16,20},{20,16},{24,28},{28,24},{1,5},{5... | collective-permute-start | bytes 497672 | tf_op jit(solution)/shard_map/ppermute | solution.py:90
  134.0 3.7 %collective-permute-start.36 = (f32[1,2304]{1,0:T(1,128)S(1)}, f32[1,2304]{1,0:T(1,128)S(1)}, u32[]{:S(2)}, u32[]{:S(2)}) collective-permute-start(f32[1,2304]{1,0:T(1,128)S(1)} %fusion.13), channel_id=1, source_target_pairs={{0,1},{1,0},{2,3},{3,2},{4,5},{5,4},{6,7},{7,6},{8,9},{9,8},{10,11... | collective-permute-start | bytes 27656 | tf_op jit(solution)/shard_map/ppermute | solution.py:281
  137.7 4.6 %collective-permute-start.37 = (f32[1,2304]{1,0:T(1,128)S(1)}, f32[1,2304]{1,0:T(1,128)S(1)}, u32[]{:S(2)}, u32[]{:S(2)}) collective-permute-start(f32[1,2304]{1,0:T(1,128)S(1)} %add.228), channel_id=1, source_target_pairs={{0,2},{1,3},{2,0},{3,1},{4,6},{5,7},{6,4},{7,5},{8,10},{9,11},{10,... | collective-permute-start | bytes 27656 | tf_op jit(solution)/shard_map/ppermute | solution.py:281
  143.8 1.2 collective-permute-start.38
  145.1 4.0 %collective-permute-start.39 = (bf16[8,2304]{1,0:T(8,128)(2,1)S(1)}, bf16[8,2304]{1,0:T(8,128)(2,1)S(1)}, u32[]{:S(2)}, u32[]{:S(2)}) collective-permute-start(bf16[8,2304]{1,0:T(8,128)(2,1)S(1)} %fusion.14), channel_id=1, source_target_pairs={{0,8},{4,12},{8,0},{12,4},{16,24},{20,28},{24,16},{28,20},{1,9},{5... | collective-permute-start | bytes 110600 | tf_op jit(solution)/shard_map/ppermute | solution.py:281
  149.1 7.8 %collective-permute-start.40 = (bf16[8,2304]{1,0:T(8,128)(2,1)S(1)}, bf16[8,2304]{1,0:T(8,128)(2,1)S(1)}, u32[]{:S(2)}, u32[]{:S(2)}) collective-permute-start(bf16[8,2304]{1,0:T(8,128)(2,1)S(1)} %fusion.32), channel_id=1, source_target_pairs={{0,16},{4,20},{8,24},{12,28},{16,0},{20,4},{24,8},{28,12},{1,17},{... | collective-permute-start | bytes 110600 | tf_op jit(solution)/shard_map/ppermute | solution.py:281
  154.0 20.6 %collective-permute-start.30 = (bf16[128,2304]{1,0:T(8,128)(2,1)}, bf16[128,2304]{1,0:T(8,128)(2,1)}, u32[]{:S(2)}, u32[]{:S(2)}) collective-permute-start(bf16[128,2304]{1,0:T(8,128)(2,1)} %get-tuple-element.18), channel_id=1, source_target_pairs={{0,1},{4,5},{8,9},{12,13},{16,17},{20,21},{24,25},{28,29}} | collective-permute-start | bytes 1769480 | tf_op jit(solution)/shard_map/ppermute | solution.py:266
  165.7 1.6 collective-permute-start.41
  165.8 8.9 %collective-permute-start.33 = (bf16[128,2304]{1,0:T(8,128)(2,1)}, bf16[128,2304]{1,0:T(8,128)(2,1)}, u32[]{:S(2)}, u32[]{:S(2)}) collective-permute-start(bf16[128,2304]{1,0:T(8,128)(2,1)} %get-tuple-element.19), channel_id=1, source_target_pairs={{3,2},{7,6},{11,10},{15,14},{19,18},{23,22},{27,26},{31,30}} | collective-permute-start | bytes 1769480 | tf_op jit(solution)/shard_map/ppermute | solution.py:267
  167.3 3.6 %collective-permute-start.42 = (f32[2,8]{1,0:T(2,128)S(1)}, f32[2,8]{1,0:T(2,128)S(1)}, u32[]{:S(2)}, u32[]{:S(2)}) collective-permute-start(f32[2,8]{1,0:T(2,128)S(1)} %pad_maximum_fusion.10), channel_id=1, source_target_pairs={{0,8},{4,12},{8,0},{12,4},{16,24},{20,28},{24,16},{28,20},{1,9},{5... | collective-permute-start | bytes 200 | tf_op jit(solution)/shard_map/ppermute | solution.py:281
  171.0 3.6 %collective-permute-start.43 = (f32[2,8]{1,0:T(2,128)S(1)}, f32[2,8]{1,0:T(2,128)S(1)}, u32[]{:S(2)}, u32[]{:S(2)}) collective-permute-start(f32[2,8]{1,0:T(2,128)S(1)} %pad_maximum_fusion.11), channel_id=1, source_target_pairs={{0,16},{4,20},{8,24},{12,28},{16,0},{20,4},{24,8},{28,12},{1,17},{... | collective-permute-start | bytes 200 | tf_op jit(solution)/shard_map/ppermute | solution.py:281
  177.2 27.9 %collective-permute-start.31 = (bf16[128,2304]{1,0:T(8,128)(2,1)}, bf16[128,2304]{1,0:T(8,128)(2,1)}, u32[]{:S(2)}, u32[]{:S(2)}) collective-permute-start(bf16[128,2304]{1,0:T(8,128)(2,1)} %get-tuple-element.16), channel_id=1, source_target_pairs={{0,1},{1,2},{4,5},{5,6},{8,9},{9,10},{12,13},{13,14},{16,17},{17,1... | collective-permute-start | bytes 1769480 | tf_op jit(solution)/shard_map/ppermute | solution.py:266
  179.3 25.8 %collective-permute-start.34 = (bf16[128,2304]{1,0:T(8,128)(2,1)}, bf16[128,2304]{1,0:T(8,128)(2,1)}, u32[]{:S(2)}, u32[]{:S(2)}) collective-permute-start(bf16[128,2304]{1,0:T(8,128)(2,1)} %get-tuple-element.17), channel_id=1, source_target_pairs={{2,1},{3,2},{6,5},{7,6},{10,9},{11,10},{14,13},{15,14},{18,17},{19... | collective-permute-start | bytes 1769480 | tf_op jit(solution)/shard_map/ppermute | solution.py:267
  180.8 9.5 %collective-permute-start.44 = (f32[2,8]{1,0:T(2,128)S(1)}, f32[2,8]{1,0:T(2,128)S(1)}, u32[]{:S(2)}, u32[]{:S(2)}) collective-permute-start(f32[2,8]{1,0:T(2,128)S(1)} %pad_maximum_fusion.12), channel_id=1, source_target_pairs={{0,1},{1,0},{2,3},{3,2},{4,5},{5,4},{6,7},{7,6},{8,9},{9,8},{10,11... | collective-permute-start | bytes 200 | tf_op jit(solution)/shard_map/ppermute | solution.py:281
  190.4 14.7 %collective-permute-start.45 = (f32[2,8]{1,0:T(2,128)S(1)}, f32[2,8]{1,0:T(2,128)S(1)}, u32[]{:S(2)}, u32[]{:S(2)}) collective-permute-start(f32[2,8]{1,0:T(2,128)S(1)} %pad_maximum_fusion.13), channel_id=1, source_target_pairs={{0,2},{1,3},{2,0},{3,1},{4,6},{5,7},{6,4},{7,5},{8,10},{9,11},{10,... | collective-permute-start | bytes 200 | tf_op jit(solution)/shard_map/ppermute | solution.py:281
  206.6 12.3 %collective-permute-start.32 = (bf16[128,2304]{1,0:T(8,128)(2,1)S(1)}, bf16[128,2304]{1,0:T(8,128)(2,1)S(1)}, u32[]{:S(2)}, u32[]{:S(2)}) collective-permute-start(bf16[128,2304]{1,0:T(8,128)(2,1)S(1)} %get-tuple-element.14), channel_id=1, source_target_pairs={{0,1},{1,2},{2,3},{4,5},{5,6},{6,7},{8,9},{9,10},{10,11},{12,13},{... | collective-permute-start | bytes 1769480 | tf_op jit(solution)/shard_map/ppermute | solution.py:266
  208.1 16.7 %collective-permute-start.35 = (bf16[128,2304]{1,0:T(8,128)(2,1)S(1)}, bf16[128,2304]{1,0:T(8,128)(2,1)S(1)}, u32[]{:S(2)}, u32[]{:S(2)}) collective-permute-start(bf16[128,2304]{1,0:T(8,128)(2,1)S(1)} %get-tuple-element.15), channel_id=1, source_target_pairs={{1,0},{2,1},{3,2},{5,4},{6,5},{7,6},{9,8},{10,9},{11,10},{13,12},{... | collective-permute-start | bytes 1769480 | tf_op jit(solution)/shard_map/ppermute | solution.py:267
  (26 other events, 214.0 us)

commit v2 on v1

v2 whole, which is shorter than its diff:
```python
import functools

import jax
import jax.numpy as jnp
from jax import lax
from jax.experimental import pallas as pl
from jax.experimental.pallas import tpu as pltpu
from jax.sharding import PartitionSpec as P

HEAD_DIM = 64
EPSILON = 1e-05
ANY = pl.BlockSpec(memory_space=pl.ANY)
SMEM = pl.BlockSpec(memory_space=pltpu.SMEM)
VMEM = pl.BlockSpec(memory_space=pltpu.VMEM)


def rms_scale(values, gain_vec):
    return (
        values * lax.rsqrt(jnp.mean(values * values, axis=-1, keepdims=True) + EPSILON) * gain_vec
    )


def rotary_tables(places):
    half_dim = HEAD_DIM // 2
    frequency = 10000.0 ** (-jnp.arange(half_dim).astype(jnp.float32) / half_dim)
    angles = places.astype(jnp.float32)[:, None] * frequency[None, :]
    cosine, sine = jnp.cos(angles), jnp.sin(angles)
    return (
        jnp.concatenate([cosine] * 4, axis=1),
        jnp.concatenate([-sine, sine, -sine, sine], axis=1),
    )


def up_pairs(size, hop, first=0):
    return [(i, i + hop) for i in range(first, size - hop)]


def down_pairs(size, hop, last=None):
    last = size - 1 if last is None else last
    return [(i, i - hop) for i in range(hop, last + 1)]


def xor_pairs(size, bit):
    return [(i, i ^ bit) for i in range(size)]


def after(value, *earlier):
    return lax.optimization_barrier((value, *earlier))[0]


def gather_line(block, size):
    ups, downs = [], []
    up, down = block, block
    for step in range(1, size):
        up = lax.ppermute(up, "row", up_pairs(size, 1, step - 1))
        down = lax.ppermute(down, "row", down_pairs(size, 1, size - step))
        up, down = lax.optimization_barrier((up, down))
        ups.append(up)
        downs.append(down)
    return ups, downs


def gather_weights(block, size, *earlier):
    rows = block.shape[0]
    if size != 8:
        whole = lax.all_gather(block, "req", axis=0, tiled=True)
        return [(whole, None, 0, rows * size)]
    half = rows // 2
    from_x = lax.ppermute(block, "req", xor_pairs(size, 2))
    from_y = lax.ppermute(block, "req", xor_pairs(size, 4))
    block, from_x, from_y, *_ = lax.optimization_barrier((block, from_x, from_y, *earlier))
    from_c = lax.ppermute(block, "req", xor_pairs(size, 1))
    half_x, half_y = lax.optimization_barrier((from_x[half:], from_y[:half]))
    diag_a = lax.ppermute(half_y, "req", xor_pairs(size, 2))
    diag_b = lax.ppermute(half_x, "req", xor_pairs(size, 4))
    pieces = [
        (block, 0, 0, rows),
        (from_x, 2, 0, rows),
        (from_y, 4, 0, rows),
        (diag_a, 6, 0, half),
        (diag_b, 6, half, half),
        (from_c, 1, 0, rows),
    ]
    for array, mask, first, count in pieces[1:5]:
        pieces.append((lax.ppermute(array, "req", xor_pairs(size, 1)), mask ^ 1, first, count))
    return pieces


def weight_copies(refs, layout, target, sems, me_req, block_rows):
    copies = []
    for index, (ref, (mask, first, count)) in enumerate(zip(refs, layout)):
        if mask is None:
            start = 0
        else:
            start = pl.multiple_of(jnp.bitwise_xor(me_req, mask) * block_rows + first, 16)
        copies.append(pltpu.make_async_copy(ref, target.at[pl.ds(start, count), :], sems.at[index]))
    return copies


def start_line_copies(own, ups, downs, target, sems, me_row, rows):
    size = len(ups) + 1
    waits = []
    own_copy = pltpu.make_async_copy(own, target.at[pl.ds(me_row * rows, rows), :], sems.at[0])
    own_copy.start()
    waits.append(own_copy)
    for hop in range(1, size):
        index = lax.rem(me_row - hop + size, size)
        place = target.at[pl.ds(pl.multiple_of(index * rows, rows), rows), :]
        below = pltpu.make_async_copy(ups[hop - 1], place, sems.at[hop])
        above = pltpu.make_async_copy(downs[size - hop - 1], place, sems.at[hop])

        @pl.when(me_row >= hop)
        def _(below=below):
            below.start()

        @pl.when(me_row < hop)
        def _(above=above):
            above.start()

        waits.append(below)
    return waits


def qkv_kernel(size, layout, block_rows, scalars, *refs):
    pieces = len(layout)
    own, ups, downs = refs[0], refs[1:size], refs[size : 2 * size - 1]
    weights = refs[2 * size - 1 : 2 * size - 1 + pieces]
    cos_ref, sin_ref, out_ref, x_scr, w_scr, x_sems, w_sems = refs[2 * size - 1 + pieces :]
    rows = own.shape[0]
    copies = weight_copies(weights, layout, w_scr, w_sems, scalars[1], block_rows)
    for copy in copies:
        copy.start()
    waits = start_line_copies(own, ups, downs, x_scr, x_sems, scalars[0], rows)
    for copy in waits + copies:
        copy.wait()
    span = x_scr.shape[0]
    total = out_ref.shape[1]
    width = total // 3
    half = HEAD_DIM // 2
    lane = lax.broadcasted_iota(jnp.int32, (span, 128), 1)
    first_half = lax.rem(lane, HEAD_DIM) < half
    cosine, sine = cos_ref[...], sin_ref[...]
    x = x_scr[...]
    for tile in range(0, total, 256):
        end = min(tile + 256, total)
        raw = jnp.dot(x, w_scr[:, tile:end], preferred_element_type=jnp.float32)
        for at in range(tile, end, 128):
            stop = min(at + 128, end)
            part = raw[:, at - tile : stop - tile]
            if at < 2 * width:
                swapped = jnp.where(
                    first_half, pltpu.roll(part, 128 - half, 1), pltpu.roll(part, half, 1)
                )
                part = part * cosine + swapped * sine
                if stop <= width:
                    part = part * (HEAD_DIM**-0.5)
                elif at < width:
                    part = jnp.where(lane < width - at, part * (HEAD_DIM**-0.5), part)
            out_ref[:, at:stop] = part.astype(jnp.bfloat16)


def attend_block(q, k_new, v_new, k_old, v_old, limit_new, length):
    nt = (((1,), (1,)), ((), ()))
    s_new = lax.dot_general(q, k_new, nt, preferred_element_type=jnp.float32)
    s_old = lax.dot_general(q, k_old, nt, preferred_element_type=jnp.float32)
    pos_new = lax.broadcasted_iota(jnp.int32, s_new.shape, 1)
    pos_old = lax.broadcasted_iota(jnp.int32, s_old.shape, 1)
    s_new = jnp.where(pos_new < limit_new, s_new, -jnp.inf)
    s_old = jnp.where(pos_old < length, s_old, -jnp.inf)
    top = jnp.maximum(
        jnp.max(s_new, axis=1, keepdims=True), jnp.max(s_old, axis=1, keepdims=True)
    )
    e_new = jnp.exp(s_new - top)
    e_old = jnp.exp(s_old - top)
    total = jnp.sum(e_new, axis=1, keepdims=True) + jnp.sum(e_old, axis=1, keepdims=True)
    summed = jnp.dot(e_new.astype(jnp.bfloat16), v_new, preferred_element_type=jnp.float32)
    summed += jnp.dot(e_old.astype(jnp.bfloat16), v_old, preferred_element_type=jnp.float32)
    return summed / total


def attention_kernel(size, scalars, *refs):
    blocks = refs[:size]
    qkv_ref, keep_ref, send_ref, last_ref, old_scr, att_scr, sems = refs[size:]
    rows = blocks[0].shape[0]
    half_rows = rows // 2
    me_row, length, count = scalars[0], scalars[2], scalars[3]
    waits = []
    for mask in range(size):
        index = jnp.bitwise_xor(me_row, mask)
        place = old_scr.at[pl.ds(pl.multiple_of(index * rows, rows), rows), :]
        waits.append(pltpu.make_async_copy(blocks[mask], place, sems.at[mask]))
        waits[-1].start()
    for copy in waits:
        copy.wait()
    span, total = qkv_ref.shape
    width = total // 3
    last = width - HEAD_DIM
    block = min(256, span)

    def attend(live):
        lane = lax.broadcasted_iota(jnp.int32, (block, 128), 1)
        left = lane < HEAD_DIM

        def old(part, lo, hi):
            at = part * half_rows
            return jnp.concatenate(
                [old_scr[i * rows + at : i * rows + at + half_rows, lo:hi] for i in range(live)],
                axis=0,
            )

        for lo in range(0, width, 128):
            pair = lo < last
            hi = lo + 128 if pair else width
            k_at = width + HEAD_DIM + lo if pair else width
            k_old, v_old = old(0, lo, hi), old(1, lo, hi)
            for begin in range(0, span, block):
                stop = begin + block
                q = qkv_ref[begin:stop, lo:hi]
                k_new = qkv_ref[0:stop, k_at : k_at + hi - lo]
                v_new = qkv_ref[0:stop, 2 * width + lo : 2 * width + hi]
                row = begin + lax.broadcasted_iota(jnp.int32, (block, 1), 0)
                limit = jnp.minimum(row + 1, count)
                if pair:
                    zero = jnp.zeros_like(q)
                    even = attend_block(
                        jnp.where(left, q, zero), k_new, v_new, k_old, v_old, limit, length
                    )
                    odd = attend_block(
                        jnp.where(left, zero, q), k_new, v_new, k_old, v_old, limit, length
                    )
                    both = jnp.where(left, even, odd)
                else:
                    both = attend_block(q, k_new, v_new, k_old, v_old, limit, length)
                att_scr[begin:stop, lo:hi] = both.astype(jnp.bfloat16)

    @pl.when(length <= half_rows)
    def _():
        attend(1)

    @pl.when(length > half_rows)
    def _():
        attend(size)

    chunk = span // size
    for slot, ref in ((0, keep_ref), (1, send_ref), (2, keep_ref), (3, send_ref)):
        start = pl.multiple_of(jnp.bitwise_xor(me_row, slot) * chunk, chunk)
        at = slot // 2 * chunk
        ref[at : at + chunk, :] = att_scr[pl.ds(start, chunk), :]
    group = lax.div(count - 1, 16)
    rows16 = att_scr[pl.ds(pl.multiple_of(group * 16, 16), 16), :].astype(jnp.float32)
    at16 = lax.broadcasted_iota(jnp.int32, rows16.shape, 0) == count - 1 - group * 16
    row = jnp.sum(jnp.where(at16, rows16, 0.0), axis=0, keepdims=True)
    last_ref[...] = jnp.broadcast_to(row, last_ref.shape).astype(jnp.bfloat16)


NT = (((1,), (1,)), ((), ()))


def last_row_kernel(layout, block_rows, scalars, *refs):
    pieces = len(layout)
    weights = refs[:pieces]
    last_ref, out_ref, w_scr, sems = refs[pieces:]
    columns = w_scr.shape[1]
    weights = [ref.at[:, 0:columns] for ref in weights]
    copies = weight_copies(weights, layout, w_scr, sems, scalars[1], block_rows)
    for copy in copies:
        copy.start()
    for copy in copies:
        copy.wait()
    width = last_ref.shape[1]
    for tile in range(0, out_ref.shape[1], 256):
        out_ref[:, tile : tile + 256] = lax.dot_general(
            last_ref[...],
            w_scr[tile : tile + 256, 0:width],
            NT,
            preferred_element_type=jnp.float32,
        )


def project_kernel(layout, block_rows, scalars, *refs):
    pieces = len(layout)
    keep_ref, got_ref, in_ref, own_ref, mate_ref, w_scr, sems = refs[pieces:]
    copies = weight_copies(refs[:pieces], layout, w_scr, sems, scalars[1], block_rows)
    for copy in copies:
        copy.start()
    attended = jnp.concatenate([keep_ref[...], got_ref[...]], axis=1)
    for copy in copies:
        copy.wait()
    chunk = own_ref.shape[0]
    for tile in range(0, own_ref.shape[1], 256):
        to = tile + 256
        total = lax.dot_general(
            attended, w_scr[tile:to, :], NT, preferred_element_type=jnp.float32
        )
        own_ref[:, tile:to] = total[:chunk] + in_ref[:, tile:to].astype(jnp.float32)
        mate_ref[:, tile:to] = total[chunk:].astype(jnp.bfloat16)


def sum_line(value, size):
    total = value
    for mask in range(1, size):
        total = total + lax.ppermute(value, "row", xor_pairs(size, mask))
    return total


def butterfly(value, axis, size, combine):
    bit = 1
    while bit < size:
        value = combine(value, lax.ppermute(value, axis, xor_pairs(size, bit)))
        bit *= 2
    return value


def merge_stats(one, other):
    top = jnp.maximum(one[0], other[0])
    total = one[1] * jnp.exp(one[0] - top) + other[1] * jnp.exp(other[0] - top)
    return jnp.stack([top, total])


def on_device(
    n_req,
    n_row,
    hidden_in,
    cache_len,
    new_count,
    key_cache,
    value_cache,
    attn_gain,
    w_query,
    w_key,
    w_value,
    w_out,
    final_gain,
    head_weight,
):
    me_row = lax.axis_index("row")
    me_req = lax.axis_index("req")
    inputs = hidden_in[0]
    rows, model = inputs.shape
    span = rows * n_row
    block_rows, width = w_query.shape
    length, count = cache_len[0], new_count[0]
    scalars = jnp.stack([me_row, me_req, length, count]).astype(jnp.int32)

    def params(mib):
        return pltpu.CompilerParams(vmem_limit_bytes=mib * 1024 * 1024)


    normed = rms_scale(inputs.astype(jnp.float32), attn_gain).astype(jnp.bfloat16)
    last = width - HEAD_DIM
    joined = jnp.concatenate([w_query, w_key[:, last:], w_key[:, :last], w_value], axis=1)
    x_ups, x_downs = gather_line(normed, n_row)
    joined = after(joined, normed)
    pieces = gather_weights(joined, n_req)
    layout = tuple(piece[1:] for piece in pieces)

    out_own = w_out.T
    out_next = lax.ppermute(out_own, "row", xor_pairs(n_row, 1))
    out_both = jnp.concatenate([out_own, out_next], axis=1)
    out_both = after(out_both, *[piece[0] for piece in pieces[1:]], x_ups[-1], x_downs[-1])

    def cache_for(owner):
        return jnp.concatenate(
            [
                lax.dynamic_slice_in_dim(key_cache[0], owner * width, width, 1),
                lax.dynamic_slice_in_dim(value_cache[0], owner * width, width, 1),
            ],
            axis=0,
        )

    cached_rows = key_cache.shape[1]
    old_blocks = []
    for mask in range(1, n_row):
        block = after(cache_for(jnp.bitwise_xor(me_row, mask)), x_ups[-1], x_downs[-1])
        old_blocks.append(lax.ppermute(block, "row", xor_pairs(n_row, mask)))
    cosine, sine = rotary_tables(length + jnp.arange(span, dtype=jnp.int32))

    qkv = pl.pallas_call(
        functools.partial(qkv_kernel, n_row, layout, block_rows),
        out_shape=jax.ShapeDtypeStruct((span, 3 * width), jnp.bfloat16),
        in_specs=[SMEM] + [ANY] * (2 * n_row - 1 + len(pieces)) + [VMEM] * 2,
        out_specs=VMEM,
        scratch_shapes=[
            pltpu.VMEM((span, model), jnp.bfloat16),
            pltpu.VMEM((model, 3 * width), jnp.bfloat16),
            pltpu.SemaphoreType.DMA((n_row,)),
            pltpu.SemaphoreType.DMA((len(pieces),)),
        ],
        compiler_params=params(24),
        cost_estimate=pl.CostEstimate(
            flops=6 * span * model * width, bytes_accessed=14 * 2**20, transcendentals=0
        ),
        name="qkv",
    )(scalars, normed, *x_ups, *x_downs, *[piece[0] for piece in pieces], cosine, sine)

    out_pieces = gather_weights(out_both, n_req, qkv)

    chunk = span // n_row
    keep, send, last_attended = pl.pallas_call(
        functools.partial(attention_kernel, n_row),
        out_shape=(
            jax.ShapeDtypeStruct((2 * chunk, width), jnp.bfloat16),
            jax.ShapeDtypeStruct((2 * chunk, width), jnp.bfloat16),
            jax.ShapeDtypeStruct((16, width), jnp.bfloat16),
        ),
        in_specs=[SMEM] + [ANY] * n_row + [VMEM],
        out_specs=(VMEM, VMEM, VMEM),
        scratch_shapes=[
            pltpu.VMEM((2 * cached_rows * n_row, width), jnp.bfloat16),
            pltpu.VMEM((span, width), jnp.bfloat16),
            pltpu.SemaphoreType.DMA((n_row,)),
        ],
        compiler_params=params(24),
        cost_estimate=pl.CostEstimate(
            flops=6 * span * span * width, bytes_accessed=4 * 2**20, transcendentals=0
        ),
        name="attention",
    )(scalars, cache_for(me_row), *old_blocks, qkv)

    out_layout = tuple(piece[1:] for piece in out_pieces)
    out_weights = [piece[0] for piece in out_pieces]
    own_columns = -(-width // 128) * 128
    own_part = pl.pallas_call(
        functools.partial(last_row_kernel, out_layout, block_rows),
        out_shape=jax.ShapeDtypeStruct((16, model), jnp.float32),
        in_specs=[SMEM] + [ANY] * len(out_weights) + [VMEM],
        out_specs=VMEM,
        scratch_shapes=[
            pltpu.VMEM((model, own_columns), jnp.bfloat16),
            pltpu.SemaphoreType.DMA((len(out_weights),)),
        ],
        compiler_params=params(8),
        cost_estimate=pl.CostEstimate(
            flops=32 * model * width, bytes_accessed=4 * 2**20, transcendentals=0
        ),
        name="last_row",
    )(scalars, *out_weights, last_attended)[:1]

    local_index = count - 1 - me_row * rows
    is_owner = (local_index >= 0) & (local_index < rows)
    residual = lax.dynamic_slice_in_dim(inputs, jnp.clip(local_index, 0, rows - 1), 1, 0)
    own_part += jnp.where(is_owner, residual.astype(jnp.float32), 0.0)
    last_row = sum_line(own_part, n_row)

    got = lax.ppermute(send, "row", xor_pairs(n_row, 1))
    got = after(got, last_row)
    own_sum, mate_part = pl.pallas_call(
        functools.partial(project_kernel, out_layout, block_rows),
        out_shape=(
            jax.ShapeDtypeStruct((chunk, model), jnp.float32),
            jax.ShapeDtypeStruct((chunk, model), jnp.bfloat16),
        ),
        in_specs=[SMEM] + [ANY] * len(out_weights) + [VMEM] * 3,
        out_specs=(VMEM, VMEM),
        scratch_shapes=[
            pltpu.VMEM((model, 2 * width), jnp.bfloat16),
            pltpu.SemaphoreType.DMA((len(out_weights),)),
        ],
        compiler_params=params(16),
        cost_estimate=pl.CostEstimate(
            flops=2 * span * model * width, bytes_accessed=8 * 2**20, transcendentals=0
        ),
        name="project",
    )(scalars, *out_weights, keep, got, inputs)
    others = lax.ppermute(mate_part, "row", xor_pairs(n_row, 2))
    layer_rows = (own_sum + others.astype(jnp.float32)).astype(jnp.bfloat16)

    final_row = rms_scale(
        last_row.astype(jnp.bfloat16).astype(jnp.float32), final_gain
    ).astype(jnp.bfloat16)
    final_row = after(final_row, mate_part)
    table = jnp.where(jnp.arange(n_req)[:, None] == me_req, final_row, jnp.zeros_like(final_row))
    table = butterfly(table, "req", n_req, jnp.add)
    logits = jnp.dot(table, head_weight, preferred_element_type=jnp.float32)
    top = jnp.max(logits, axis=1)
    stats = jnp.stack([top, jnp.sum(jnp.exp(logits - top[:, None]), axis=1)])
    stats = after(stats, others)
    stats = butterfly(stats, "req", n_req, merge_stats)
    stats = butterfly(stats, "row", n_row, merge_stats)
    logprobs = logits - stats[0][:, None] - jnp.log(stats[1])[:, None]
    return (layer_rows[None], logprobs)


def solution(mesh):
    placed = (
        P("req", "row", None),
        P("req"),
        P("req"),
        P("req", "row", None),
        P("req", "row", None),
        P(),
        P("req", "row"),
        P("req", "row"),
        P("req", "row"),
        P("row", "req"),
        P(),
        P(None, ("req", "row")),
    )
    return jax.shard_map(
        functools.partial(on_device, mesh.shape["req"], mesh.shape["row"]),
        mesh=mesh,
        in_specs=placed,
        out_specs=(P("req", "row", None), P(None, ("req", "row"))),
        check_vma=False,
    )
```

time: 226 us -> 191 us (0.85)
  starting transfers between devices: 81.1 us -> 43.5 us
  other arithmetic: 13.7 us -> 8.32 us
  waiting for transfers between devices: 79 us -> 83.3 us
    ppermute x10 -> x8, starting transfers between devices: 27.8 us -> 7.66 us  [butterfly(): value = combine(value, lax.ppermute(value, axis, xor_pairs(size, bit)))]
    ppermute x16 -> x13, starting transfers between devices: 33.3 us -> 18.5 us  [the longest x3 4.45 us: sum_line(): total = total + lax.ppermute(value, 'row', xor_pairs(size, mask))]
    ppermute x3, waiting for transfers between devices: 0.01 us -> 10.7 us  [gather_line(): up = lax.ppermute(up, 'row', up_pairs(size, 1, step - 1))]
    ppermute x2, waiting for transfers between devices: 9.55 us -> 0.98 us  [gather_weights(): from_x = lax.ppermute(block, 'req', xor_pairs(size, 2))]
    unnamed x52 -> x48, local copies, waits for them, and re-layouts: 4.11 us -> 10.8 us
    ppermute x16 -> x13, waiting for transfers between devices: 29.1 us -> 35.2 us  [the longest x1 15.3 us: on_device(): others = lax.ppermute(mate_part, 'row', xor_pairs(n_row, 2))]
    convert_element_type x3 -> x1, other arithmetic: 4.08 us -> 0.02 us  [on_device(): final_row = rms_scale(last_row.astype(jnp.bfloat16).astype(jnp.float32),...]
    ppermute x10 -> x8, waiting for transfers between devices: 19.8 us -> 17.4 us  [butterfly(): value = combine(value, lax.ppermute(value, axis, xor_pairs(size, bit)))]
  transfers between devices with their start and end apart: 46 -> 41, of which waited for: 18 -> 20; matrix products, arithmetic and copies ran while one was open for 10% -> 11% of each run, Pallas kernels for 5% -> 11%
where the time goes in v2:
time: 191 us
  waiting for transfers between devices  83.3 us (44%)
  starting transfers between devices  43.5 us (23%)
  Pallas kernels  26.2 us (14%)
  local copies, waits for them, and re-layouts  17.6 us (9%)
  matrix products  8.54 us (4%)
  other arithmetic  8.32 us (4%)
  between operations  3.2 us (2%)
    ppermute x3, waiting for transfers between devices, gather_line(): down = lax.ppermute(down, 'row', down_pairs(size, 1, size - step))  18.4 us
    ppermute x8, waiting for transfers between devices, butterfly(): value = combine(value, lax.ppermute(value, axis, xor_pairs(size, bit)))  17.4 us
    ppermute x1, waiting for transfers between devices, on_device(): others = lax.ppermute(mate_part, 'row', xor_pairs(n_row, 2))  15.3 us
    ppermute x3, waiting for transfers between devices, on_device(): old_blocks.append(lax.ppermute(block, 'row', xor_pairs(n_row, mask)))  10.9 us
    unnamed x48, local copies, waits for them, and re-layouts  10.8 us
    ppermute x3, waiting for transfers between devices, gather_line(): up = lax.ppermute(up, 'row', up_pairs(size, 1, step - 1))  10.7 us
    pallas_call x1, Pallas kernels, on_device(): pl.pallas_call(functools.partial(attention_kernel, n_row), out_shape=(jax...  9.02 us
    pallas_call x1, Pallas kernels, on_device(): pl.pallas_call(functools.partial(qkv_kernel, n_row, layout, block_rows),...  8.98 us
  transfers between devices with their start and end apart: 41, of which 20 were waited for; matrix products, arithmetic and copies ran while one was open for 11% of the time, Pallas kernels for 11%

profile of v2, /device:TPU:0, one launch (start us, length us, event | category | flops | bytes accessed | tf_op | source)
XLA Modules:
  0.0 190.8 jit_solution(8739260010960897495)
XLA Ops:
  0.7 1.4 fusion
  2.8 3.0 %collective-permute-start.1 = (bf16[288,1728]{1,0:T(8,128)(2,1)S(1)}, bf16[288,1728]{1,0:T(8,128)(2,1)}, u32[]{:S(2)}, u32[]{:S(2)}) collective-permute-start(bf16[288,1728]{1,0:T(8,128)(2,1)S(1)} %concatenate.25.refs_7_), channel_id=1, source_target_pairs={{0,8},{4,12},{8,0},{12,4},{16,24},{20,28},{24,16},{28,20},{1,9},{5... | collective-permute-start | bytes 2985992 | tf_op jit(solution)/shard_map/ppermute | solution.py:69
  5.8 1.5 collective-permute-start.2
  7.3 3.5 %collective-permute-start.10 = (bf16[128,2304]{1,0:T(8,128)(2,1)S(1)}, bf16[128,2304]{1,0:T(8,128)(2,1)S(1)}, u32[]{:S(2)}, u32[]{:S(2)}) collective-permute-start(bf16[128,2304]{1,0:T(8,128)(2,1)S(1)} %fusion.2.refs_0_), channel_id=1, source_target_pairs={{0,1},{1,2},{2,3},{4,5},{5,6},{6,7},{8,9},{9,10},{10,11},{12,13},{... | collective-permute-start | bytes 1769480 | tf_op jit(solution)/shard_map/ppermute | solution.py:55
  10.8 1.3 collective-permute-start.11
  12.1 10.7 %collective-permute-done.10.refs_1_ = bf16[128,2304]{1,0:T(8,128)(2,1)S(1)} collective-permute-done((bf16[128,2304]{1,0:T(8,128)(2,1)S(1)}, bf16[128,2304]{1,0:T(8,128)(2,1)S(1)}, u32[]{:S(2)}, u32[]{:S(2)}) %collective-permute-start.10) | collective-permute-done | bytes 589856 | tf_op jit(solution)/shard_map/ppermute | solution.py:55
  22.8 4.3 %collective-permute-done.11.refs_4_ = bf16[128,2304]{1,0:T(8,128)(2,1)} collective-permute-done((bf16[128,2304]{1,0:T(8,128)(2,1)S(1)}, bf16[128,2304]{1,0:T(8,128)(2,1)}, u32[]{:S(2)}, u32[]{:S(2)}) %collective-permute-start.11) | collective-permute-done | bytes 589856 | tf_op jit(solution)/shard_map/ppermute | solution.py:56
  27.0 1.5 collective-permute-start.12
  28.5 1.3 collective-permute-start.13
  30.2 1.9 slice.65
  32.0 1.9 slice.66
  34.2 1.7 collective-permute-start.4
  35.9 3.7 %collective-permute-start = (bf16[288,576]{1,0:T(8,128)(2,1)S(1)}, bf16[288,576]{1,0:T(8,128)(2,1)}, u32[]{:S(2)}, u32[]{:S(2)}) collective-permute-start(bf16[288,576]{1,0:T(8,128)(2,1)S(1)} %bitcast.153), channel_id=1, source_target_pairs={{0,1},{1,0},{2,3},{3,2},{4,5},{5,4},{6,7},{7,6},{8,9},{9,8},{10,11... | collective-permute-start | bytes 995336 | tf_op jit(solution)/shard_map/ppermute | solution.py:358
  40.9 8.4 %collective-permute-done.13.refs_5_ = bf16[128,2304]{1,0:T(8,128)(2,1)} collective-permute-done((bf16[128,2304]{1,0:T(8,128)(2,1)}, bf16[128,2304]{1,0:T(8,128)(2,1)}, u32[]{:S(2)}, u32[]{:S(2)}) %collective-permute-start.13) | collective-permute-done | bytes 589856 | tf_op jit(solution)/shard_map/ppermute | solution.py:56
  50.0 1.3 collective-permute-start.15
  51.3 5.9 %collective-permute-done = bf16[288,576]{1,0:T(8,128)(2,1)} collective-permute-done((bf16[288,576]{1,0:T(8,128)(2,1)S(1)}, bf16[288,576]{1,0:T(8,128)(2,1)}, u32[]{:S(2)}, u32[]{:S(2)}) %collective-permute-start) | collective-permute-done | bytes 331808 | tf_op jit(solution)/shard_map/ppermute | solution.py:358
  57.8 2.7 %dynamic-slice_bitcast_fusion = (bf16[128,576]{1,0:T(8,128)(2,1)S(1)}, bf16[128,576]{1,0:T(8,128)(2,1)S(1)}, bf16[128,576]{1,0:T(8,128)(2,1)S(1)}, bf16[128,576]...) fusion(bf16[1,128,2304]{2,1,0:T(8,128)(2,1)} %param.16, ...), kind=kLoop, calls=%fused_computation.16 | loop fusion | bytes 2359312 | tf_op jit(solution)/shard_map/dynamic_slice | solution.py:366
  61.1 5.7 %collective-permute-done.15.refs_6_ = bf16[128,2304]{1,0:T(8,128)(2,1)S(1)} collective-permute-done((bf16[128,2304]{1,0:T(8,128)(2,1)}, bf16[128,2304]{1,0:T(8,128)(2,1)S(1)}, u32[]{:S(2)}, u32[]{:S(2)}) %collective-permute-start.15) | collective-permute-done | bytes 589856 | tf_op jit(solution)/shard_map/ppermute | solution.py:56
  67.8 1.2 pad_maximum_fusion.refs_0_
  70.8 1.1 collective-permute-start.26
  71.9 3.3 %collective-permute-start.25 = (bf16[256,576]{1,0:T(8,128)(2,1)S(1)}, bf16[256,576]{1,0:T(8,128)(2,1)S(1)}, u32[]{:S(2)}, u32[]{:S(2)}) collective-permute-start(bf16[256,576]{1,0:T(8,128)(2,1)S(1)} %pad_maximum_fusion.2), channel_id=1, source_target_pairs={{0,1},{1,0},{2,3},{3,2},{4,5},{5,4},{6,7},{7,6},{8,9},{9,8},{10,11... | collective-permute-start | bytes 884744 | tf_op jit(solution)/shard_map/ppermute | solution.py:375
  75.2 9.0 %qkv.1.refs_4_ = bf16[512,1728]{1,0:T(8,128)(2,1)S(1)} custom-call(s32[4]{0:T(128)S(1)} %pad_add_fusion.scalars, bf16[128,2304]{1,0:T(8,128)(2,1)S(1)} %fusion.2.refs_0_, bf16[128,2304]{1,0:T(8,128)(2,1)S(1)} %copy-done.8, bf16[128,2304]{1,0:T(8,128)(2,1)} %collective-permute-done.12.refs_2_, bf16[128,2304]{1,0:T(8,128)(2,1)S(1)} %collective-permute-done.14.refs_3_, ...), custom_call_target="tpu_custom_call" | custom-call | flops 4076863488 | bytes 14680064 | tf_op jit(solution)/shard_map/qkv/pallas_call | solution.py:378
  84.2 1.2 copy-done.16
  86.9 1.6 collective-permute-start.18
  89.7 10.9 %collective-permute-done.26.refs_2_ = bf16[256,576]{1,0:T(8,128)(2,1)S(1)} collective-permute-done((bf16[256,576]{1,0:T(8,128)(2,1)S(1)}, bf16[256,576]{1,0:T(8,128)(2,1)S(1)}, u32[]{:S(2)}, u32[]{:S(2)}) %collective-permute-start.26) | collective-permute-done | bytes 294944 | tf_op jit(solution)/shard_map/ppermute | solution.py:375
  106.9 1.5 copy-done.17
  108.4 9.0 %attention.1 = (bf16[256,576]{1,0:T(8,128)(2,1)S(1)}, bf16[256,576]{1,0:T(8,128)(2,1)}, bf16[16,576]{1,0:T(8,128)(2,1)S(1)}) custom-call(s32[4]{0:T(128)S(1)} %pad_add_fusion.scalars, bf16[256,576]{1,0:T(8,128)(2,1)S(1)} %pad_maximum_fusion.1.refs_0_, bf16[256,576]{1,0:T(8,128)(2,1)S(1)} %copy-done.15, bf16[256,576]{1,0:T(8,128)(2,1)S(1)} %copy-done.13, ...), custom_call_target="tpu_custom_call" | custom-call | flops 905969664 | bytes 4194304 | tf_op jit(solution)/shard_map/attention/pallas_call | solution.py:399
  118.4 3.0 %last_row.1 = f32[16,2304]{1,0:T(8,128)S(1)} custom-call(s32[4]{0:T(128)S(1)} %pad_add_fusion.scalars, bf16[288,1152]{1,0:T(8,128)(2,1)S(1)} %pad_maximum_fusion.refs_0_, bf16[288,1152]{1,0:T(8,128)(2,1)S(1)} %collective-permute-done.16.refs_1_, bf16[288,1152]{1,0:T(8,128)(2,1)S(1)} %collective-permute-done.17.refs_2_, ...), custom_call_target="tpu_custom_call" | custom-call | flops 42467328 | bytes 4194304 | tf_op jit(solution)/shard_map/last_row/pallas_call | solution.py:423
  121.5 1.3 collective-permute-start.29
  123.6 2.3 %collective-permute-start.31 = (f32[1,2304]{1,0:T(1,128)S(1)}, f32[1,2304]{1,0:T(1,128)S(1)}, u32[]{:S(2)}, u32[]{:S(2)}) collective-permute-start(f32[1,2304]{1,0:T(1,128)S(1)} %fusion.8), channel_id=1, source_target_pairs={{0,3},{1,2},{2,1},{3,0},{4,7},{5,6},{6,5},{7,4},{8,11},{9,10},{10,... | collective-permute-start | bytes 27656 | tf_op jit(solution)/shard_map/ppermute | solution.py:302
  125.9 1.9 %collective-permute-done.29 = f32[1,2304]{1,0:T(1,128)S(1)} collective-permute-done((f32[1,2304]{1,0:T(1,128)S(1)}, f32[1,2304]{1,0:T(1,128)S(1)}, u32[]{:S(2)}, u32[]{:S(2)}) %collective-permute-start.29) | collective-permute-done | bytes 9248 | tf_op jit(solution)/shard_map/ppermute | solution.py:302
  127.8 1.2 collective-permute-done.31
  131.4 5.2 %project.1 = (f32[128,2304]{1,0:T(8,128)S(1)}, bf16[128,2304]{1,0:T(8,128)(2,1)S(1)}) custom-call(s32[4]{0:T(128)S(1)} %pad_add_fusion.scalars, bf16[288,1152]{1,0:T(8,128)(2,1)S(1)} %pad_maximum_fusion.refs_0_, bf16[288,1152]{1,0:T(8,128)(2,1)S(1)} %collective-permute-done.16.refs_1_, bf16[288,1152]{1,0:T(8,128)(2,1)S(1)} %collective-permute-done.17.refs_2_, ...), custom_call_target="tpu_custom_call" | custom-call | flops 1358954496 | bytes 8388608 | tf_op jit(solution)/shard_map/project/pallas_call | solution.py:447
  136.6 1.0 copy-done.1
  138.6 1.2 collective-permute-done.33
  139.9 3.3 %collective-permute-start.34 = (bf16[8,2304]{1,0:T(8,128)(2,1)S(1)}, bf16[8,2304]{1,0:T(8,128)(2,1)S(1)}, u32[]{:S(2)}, u32[]{:S(2)}) collective-permute-start(bf16[8,2304]{1,0:T(8,128)(2,1)S(1)} %fusion.9), channel_id=1, source_target_pairs={{0,8},{4,12},{8,0},{12,4},{16,24},{20,28},{24,16},{28,20},{1,9},{5... | collective-permute-start | bytes 110600 | tf_op jit(solution)/shard_map/ppermute | solution.py:309
  143.2 1.9 %collective-permute-done.34 = bf16[8,2304]{1,0:T(8,128)(2,1)S(1)} collective-permute-done((bf16[8,2304]{1,0:T(8,128)(2,1)S(1)}, bf16[8,2304]{1,0:T(8,128)(2,1)S(1)}, u32[]{:S(2)}, u32[]{:S(2)}) %collective-permute-start.34) | collective-permute-done | bytes 36896 | tf_op jit(solution)/shard_map/ppermute | solution.py:309
  145.5 1.0 collective-permute-start.32
  146.5 2.7 %collective-permute-done.35 = bf16[8,2304]{1,0:T(8,128)(2,1)S(1)} collective-permute-done((bf16[8,2304]{1,0:T(8,128)(2,1)S(1)}, bf16[8,2304]{1,0:T(8,128)(2,1)S(1)}, u32[]{:S(2)}, u32[]{:S(2)}) %collective-permute-start.35) | collective-permute-done | bytes 36896 | tf_op jit(solution)/shard_map/ppermute | solution.py:309
  149.2 8.5 %fusion.26 = (f32[8]{0:T(128)S(1)}, f32[8,3840]{1,0:T(8,128)S(1)}) fusion(bf16[2304,3840]{1,0:T(8,128)(2,1)} %param.23, bf16[8,2304]{1,0:T(8,128)(2,1)S(1)} %fusion.28, bf16[8,2304]{1,0:T(8,128)(2,1)S(1)} %collective-permute-done.35), kind=kOutput, calls=%fused_computation.88 | convolution fusion | flops 141606912 | bytes 17891360 | tf_op jit(solution)/shard_map/dot_general | solution.py:474
  158.0 15.3 %collective-permute-done.32 = bf16[128,2304]{1,0:T(8,128)(2,1)S(1)} collective-permute-done((bf16[128,2304]{1,0:T(8,128)(2,1)}, bf16[128,2304]{1,0:T(8,128)(2,1)S(1)}, u32[]{:S(2)}, u32[]{:S(2)}) %collective-permute-start.32) | collective-permute-done | bytes 589856 | tf_op jit(solution)/shard_map/ppermute | solution.py:465
  173.3 1.1 collective-permute-done.36
  174.5 1.8 collective-permute-start.37
  176.3 1.8 collective-permute-done.37
  178.1 1.7 collective-permute-start.38
  179.9 1.9 collective-permute-done.38
  181.9 3.6 %collective-permute-done.39 = f32[2,8]{1,0:T(2,128)S(1)} collective-permute-done((f32[2,8]{1,0:T(2,128)S(1)}, f32[2,8]{1,0:T(2,128)S(1)}, u32[]{:S(2)}, u32[]{:S(2)}) %collective-permute-start.39) | collective-permute-done | bytes 96 | tf_op jit(solution)/shard_map/ppermute | solution.py:309
  186.8 3.2 %collective-permute-done.40 = f32[2,8]{1,0:T(2,128)S(1)} collective-permute-done((f32[2,8]{1,0:T(2,128)S(1)}, f32[2,8]{1,0:T(2,128)S(1)}, u32[]{:S(2)}, u32[]{:S(2)}) %collective-permute-start.40) | collective-permute-done | bytes 96 | tf_op jit(solution)/shard_map/ppermute | solution.py:309
  (131 shorter events, 22.2 us)
Async XLA Ops:
  2.8 57.7 %copy-start.3 = (bf16[288,1728]{1,0:T(8,128)(2,1)}, bf16[288,1728]{1,0:T(8,128)(2,1)S(1)}, u32[]{:S(2)}) copy-start(bf16[288,1728]{1,0:T(8,128)(2,1)S(1)} %concatenate.25.refs_7_) | copy-start | bytes 2985988
  2.8 33.2 %copy-start.20 = (bf16[576,288]{0,1:T(8,128)(2,1)S(1)}, bf16[576,288]{0,1:T(8,128)(2,1)}, u32[]{:S(2)}) copy-start(bf16[576,288]{0,1:T(8,128)(2,1)} %param.21) | copy-start | bytes 995332
  2.8 27.0 %collective-permute-start.1 = (bf16[288,1728]{1,0:T(8,128)(2,1)S(1)}, bf16[288,1728]{1,0:T(8,128)(2,1)}, u32[]{:S(2)}, u32[]{:S(2)}) collective-permute-start(bf16[288,1728]{1,0:T(8,128)(2,1)S(1)} %concatenate.25.refs_7_), channel_id=1, source_target_pairs={{0,8},{4,12},{8,0},{12,4},{16,24},{20,28},{24,16},{28,20},{1,9},{5... | collective-permute-start | bytes 2985992 | tf_op jit(solution)/shard_map/ppermute | solution.py:69
  5.8 24.4 %collective-permute-start.2 = (bf16[288,1728]{1,0:T(8,128)(2,1)S(1)}, bf16[288,1728]{1,0:T(8,128)(2,1)}, u32[]{:S(2)}, u32[]{:S(2)}) collective-permute-start(bf16[288,1728]{1,0:T(8,128)(2,1)S(1)} %concatenate.25.refs_7_), channel_id=1, source_target_pairs={{0,16},{4,20},{8,24},{12,28},{16,0},{20,4},{24,8},{28,12},{1,17},{... | collective-permute-start | bytes 2985992 | tf_op jit(solution)/shard_map/ppermute | solution.py:70
  7.3 15.5 %collective-permute-start.10 = (bf16[128,2304]{1,0:T(8,128)(2,1)S(1)}, bf16[128,2304]{1,0:T(8,128)(2,1)S(1)}, u32[]{:S(2)}, u32[]{:S(2)}) collective-permute-start(bf16[128,2304]{1,0:T(8,128)(2,1)S(1)} %fusion.2.refs_0_), channel_id=1, source_target_pairs={{0,1},{1,2},{2,3},{4,5},{5,6},{6,7},{8,9},{9,10},{10,11},{12,13},{... | collective-permute-start | bytes 1769480 | tf_op jit(solution)/shard_map/ppermute | solution.py:55
  10.8 16.2 %collective-permute-start.11 = (bf16[128,2304]{1,0:T(8,128)(2,1)S(1)}, bf16[128,2304]{1,0:T(8,128)(2,1)}, u32[]{:S(2)}, u32[]{:S(2)}) collective-permute-start(bf16[128,2304]{1,0:T(8,128)(2,1)S(1)} %fusion.2.refs_0_), channel_id=1, source_target_pairs={{1,0},{2,1},{3,2},{5,4},{6,5},{7,6},{9,8},{10,9},{11,10},{13,12},{... | collective-permute-start | bytes 1769480 | tf_op jit(solution)/shard_map/ppermute | solution.py:56
  22.8 37.7 %copy-start.7 = (bf16[128,2304]{1,0:T(8,128)(2,1)}, bf16[128,2304]{1,0:T(8,128)(2,1)S(1)}, u32[]{:S(2)}) copy-start(bf16[128,2304]{1,0:T(8,128)(2,1)S(1)} %collective-permute-done.10.refs_1_) | copy-start | bytes 1769476
  27.0 13.9 %collective-permute-start.12 = (bf16[128,2304]{1,0:T(8,128)(2,1)S(1)}, bf16[128,2304]{1,0:T(8,128)(2,1)}, u32[]{:S(2)}, u32[]{:S(2)}) collective-permute-start(bf16[128,2304]{1,0:T(8,128)(2,1)S(1)} %collective-permute-done.10.refs_1_), channel_id=1, source_target_pairs={{1,2},{2,3},{5,6},{6,7},{9,10},{10,11},{13,14},{14,15},{17,18},{18... | collective-permute-start | bytes 1769480 | tf_op jit(solution)/shard_map/ppermute | solution.py:55
  28.5 20.8 %collective-permute-start.13 = (bf16[128,2304]{1,0:T(8,128)(2,1)}, bf16[128,2304]{1,0:T(8,128)(2,1)}, u32[]{:S(2)}, u32[]{:S(2)}) collective-permute-start(bf16[128,2304]{1,0:T(8,128)(2,1)} %collective-permute-done.11.refs_4_), channel_id=1, source_target_pairs={{1,0},{2,1},{5,4},{6,5},{9,8},{10,9},{13,12},{14,13},{17,16},{18,1... | collective-permute-start | bytes 1769480 | tf_op jit(solution)/shard_map/ppermute | solution.py:56
  33.9 23.4 %collective-permute-start.3 = (bf16[144,1728]{1,0:T(8,128)(2,1)}, bf16[144,1728]{1,0:T(8,128)(2,1)}, u32[]{:S(2)}, u32[]{:S(2)}) collective-permute-start(bf16[144,1728]{1,0:T(8,128)(2,1)} %slice.66), channel_id=1, source_target_pairs={{0,8},{4,12},{8,0},{12,4},{16,24},{20,28},{24,16},{28,20},{1,9},{5... | collective-permute-start | bytes 1493000 | tf_op jit(solution)/shard_map/ppermute | solution.py:74
  34.2 23.5 %collective-permute-start.4 = (bf16[144,1728]{1,0:T(8,128)(2,1)}, bf16[144,1728]{1,0:T(8,128)(2,1)}, u32[]{:S(2)}, u32[]{:S(2)}) collective-permute-start(bf16[144,1728]{1,0:T(8,128)(2,1)} %slice.65), channel_id=1, source_target_pairs={{0,16},{4,20},{8,24},{12,28},{16,0},{20,4},{24,8},{28,12},{1,17},{... | collective-permute-start | bytes 1493000 | tf_op jit(solution)/shard_map/ppermute | solution.py:75
  35.9 21.3 %collective-permute-start = (bf16[288,576]{1,0:T(8,128)(2,1)S(1)}, bf16[288,576]{1,0:T(8,128)(2,1)}, u32[]{:S(2)}, u32[]{:S(2)}) collective-permute-start(bf16[288,576]{1,0:T(8,128)(2,1)S(1)} %bitcast.153), channel_id=1, source_target_pairs={{0,1},{1,0},{2,3},{3,2},{4,5},{5,4},{6,7},{7,6},{8,9},{9,8},{10,11... | collective-permute-start | bytes 995336 | tf_op jit(solution)/shard_map/ppermute | solution.py:358
  49.3 11.2 %collective-permute-start.14 = (bf16[128,2304]{1,0:T(8,128)(2,1)}, bf16[128,2304]{1,0:T(8,128)(2,1)S(1)}, u32[]{:S(2)}, u32[]{:S(2)}) collective-permute-start(bf16[128,2304]{1,0:T(8,128)(2,1)} %collective-permute-done.12.refs_2_), channel_id=1, source_target_pairs={{2,3},{6,7},{10,11},{14,15},{18,19},{22,23},{26,27},{30,31}} | collective-permute-start | bytes 1769480 | tf_op jit(solution)/shard_map/ppermute | solution.py:55
  50.0 16.8 %collective-permute-start.15 = (bf16[128,2304]{1,0:T(8,128)(2,1)}, bf16[128,2304]{1,0:T(8,128)(2,1)S(1)}, u32[]{:S(2)}, u32[]{:S(2)}) collective-permute-start(bf16[128,2304]{1,0:T(8,128)(2,1)} %collective-permute-done.13.refs_5_), channel_id=1, source_target_pairs={{1,0},{5,4},{9,8},{13,12},{17,16},{21,20},{25,24},{29,28}} | collective-permute-start | bytes 1769480 | tf_op jit(solution)/shard_map/ppermute | solution.py:56
  57.2 11.8 %collective-permute-start.6 = (bf16[288,1728]{1,0:T(8,128)(2,1)}, bf16[288,1728]{1,0:T(8,128)(2,1)S(1)}, u32[]{:S(2)}, u32[]{:S(2)}) collective-permute-start(bf16[288,1728]{1,0:T(8,128)(2,1)} %collective-permute-done.1.refs_8_), channel_id=1, source_target_pairs={{0,4},{4,0},{8,12},{12,8},{16,20},{20,16},{24,28},{28,24},{1,5},{5... | collective-permute-start | bytes 2985992 | tf_op jit(solution)/shard_map/ppermute | solution.py:85
  57.2 11.8 %collective-permute-start.7 = (bf16[288,1728]{1,0:T(8,128)(2,1)}, bf16[288,1728]{1,0:T(8,128)(2,1)S(1)}, u32[]{:S(2)}, u32[]{:S(2)}) collective-permute-start(bf16[288,1728]{1,0:T(8,128)(2,1)} %collective-permute-done.2.refs_9_), channel_id=1, source_target_pairs={{0,4},{4,0},{8,12},{12,8},{16,20},{20,16},{24,28},{28,24},{1,5},{5... | collective-permute-start | bytes 2985992 | tf_op jit(solution)/shard_map/ppermute | solution.py:85
  57.8 11.3 %collective-permute-start.5 = (bf16[288,1728]{1,0:T(8,128)(2,1)S(1)}, bf16[288,1728]{1,0:T(8,128)(2,1)S(1)}, u32[]{:S(2)}, u32[]{:S(2)}) collective-permute-start(bf16[288,1728]{1,0:T(8,128)(2,1)S(1)} %concatenate.25.refs_7_), channel_id=1, source_target_pairs={{0,4},{4,0},{8,12},{12,8},{16,20},{20,16},{24,28},{28,24},{1,5},{5... | collective-permute-start | bytes 2985992 | tf_op jit(solution)/shard_map/ppermute | solution.py:72
  60.5 7.3 %copy-start.21 = (bf16[576,288]{0,1:T(8,128)(2,1)S(1)}, bf16[576,288]{0,1:T(8,128)(2,1)}, u32[]{:S(2)}) copy-start(bf16[576,288]{0,1:T(8,128)(2,1)} %param.21) | copy-start | bytes 995332
  60.6 8.4 %collective-permute-start.8 = (bf16[144,1728]{1,0:T(8,128)(2,1)}, bf16[144,1728]{1,0:T(8,128)(2,1)S(1)}, u32[]{:S(2)}, u32[]{:S(2)}) collective-permute-start(bf16[144,1728]{1,0:T(8,128)(2,1)} %collective-permute-done.3.refs_10_), channel_id=1, source_target_pairs={{0,4},{4,0},{8,12},{12,8},{16,20},{20,16},{24,28},{28,24},{1,5},{5... | collective-permute-start | bytes 1493000 | tf_op jit(solution)/shard_map/ppermute | solution.py:85
  66.8 2.2 %collective-permute-start.9 = (bf16[144,1728]{1,0:T(8,128)(2,1)}, bf16[144,1728]{1,0:T(8,128)(2,1)S(1)}, u32[]{:S(2)}, u32[]{:S(2)}) collective-permute-start(bf16[144,1728]{1,0:T(8,128)(2,1)} %collective-permute-done.4.refs_11_), channel_id=1, source_target_pairs={{0,4},{4,0},{8,12},{12,8},{16,20},{20,16},{24,28},{28,24},{1,5},{5... | collective-permute-start | bytes 1493000 | tf_op jit(solution)/shard_map/ppermute | solution.py:85
  69.0 6.2 %copy-start.4 = (bf16[288,1728]{1,0:T(8,128)(2,1)S(1)}, bf16[288,1728]{1,0:T(8,128)(2,1)}, u32[]{:S(2)}) copy-start(bf16[288,1728]{1,0:T(8,128)(2,1)} %copy-done.3) | copy-start | bytes 2985988
  69.1 17.4 %collective-permute-start.16 = (bf16[288,1152]{1,0:T(8,128)(2,1)S(1)}, bf16[288,1152]{1,0:T(8,128)(2,1)S(1)}, u32[]{:S(2)}, u32[]{:S(2)}) collective-permute-start(bf16[288,1152]{1,0:T(8,128)(2,1)S(1)} %pad_maximum_fusion.refs_0_), channel_id=1, source_target_pairs={{0,8},{4,12},{8,0},{12,4},{16,24},{20,28},{24,16},{28,20},{1,9},{5... | collective-permute-start | bytes 1990664 | tf_op jit(solution)/shard_map/ppermute | solution.py:69
  69.7 17.0 %collective-permute-start.17 = (bf16[288,1152]{1,0:T(8,128)(2,1)S(1)}, bf16[288,1152]{1,0:T(8,128)(2,1)S(1)}, u32[]{:S(2)}, u32[]{:S(2)}) collective-permute-start(bf16[288,1152]{1,0:T(8,128)(2,1)S(1)} %pad_maximum_fusion.refs_0_), channel_id=1, source_target_pairs={{0,16},{4,20},{8,24},{12,28},{16,0},{20,4},{24,8},{28,12},{1,17},{... | collective-permute-start | bytes 1990664 | tf_op jit(solution)/shard_map/ppermute | solution.py:70
  70.8 17.6 %collective-permute-start.27 = (bf16[256,576]{1,0:T(8,128)(2,1)S(1)}, bf16[256,576]{1,0:T(8,128)(2,1)S(1)}, u32[]{:S(2)}, u32[]{:S(2)}) collective-permute-start(bf16[256,576]{1,0:T(8,128)(2,1)S(1)} %pad_maximum_fusion.4), channel_id=1, source_target_pairs={{0,3},{1,2},{2,1},{3,0},{4,7},{5,6},{6,5},{7,4},{8,11},{9,10},{10,... | collective-permute-start | bytes 884744 | tf_op jit(solution)/shard_map/ppermute | solution.py:375
  70.8 29.7 %collective-permute-start.26 = (bf16[256,576]{1,0:T(8,128)(2,1)S(1)}, bf16[256,576]{1,0:T(8,128)(2,1)S(1)}, u32[]{:S(2)}, u32[]{:S(2)}) collective-permute-start(bf16[256,576]{1,0:T(8,128)(2,1)S(1)} %pad_maximum_fusion.3), channel_id=1, source_target_pairs={{0,2},{1,3},{2,0},{3,1},{4,6},{5,7},{6,4},{7,5},{8,10},{9,11},{10,... | collective-permute-start | bytes 884744 | tf_op jit(solution)/shard_map/ppermute | solution.py:375
  71.9 29.4 %collective-permute-start.25 = (bf16[256,576]{1,0:T(8,128)(2,1)S(1)}, bf16[256,576]{1,0:T(8,128)(2,1)S(1)}, u32[]{:S(2)}, u32[]{:S(2)}) collective-permute-start(bf16[256,576]{1,0:T(8,128)(2,1)S(1)} %pad_maximum_fusion.2), channel_id=1, source_target_pairs={{0,1},{1,0},{2,3},{3,2},{4,5},{5,4},{6,7},{7,6},{8,9},{9,8},{10,11... | collective-permute-start | bytes 884744 | tf_op jit(solution)/shard_map/ppermute | solution.py:375
  86.7 31.6 %collective-permute-start.21 = (bf16[288,1152]{1,0:T(8,128)(2,1)S(1)}, bf16[288,1152]{1,0:T(8,128)(2,1)S(1)}, u32[]{:S(2)}, u32[]{:S(2)}) collective-permute-start(bf16[288,1152]{1,0:T(8,128)(2,1)S(1)} %collective-permute-done.16.refs_1_), channel_id=1, source_target_pairs={{0,4},{4,0},{8,12},{12,8},{16,20},{20,16},{24,28},{28,24},{1,5},{5... | collective-permute-start | bytes 1990664 | tf_op jit(solution)/shard_map/ppermute | solution.py:85
  86.9 15.7 %collective-permute-start.18 = (bf16[144,1152]{1,0:T(8,128)(2,1)S(1)}, bf16[144,1152]{1,0:T(8,128)(2,1)}, u32[]{:S(2)}, u32[]{:S(2)}) collective-permute-start(bf16[144,1152]{1,0:T(8,128)(2,1)S(1)} %slice.68), channel_id=1, source_target_pairs={{0,8},{4,12},{8,0},{12,4},{16,24},{20,28},{24,16},{28,20},{1,9},{5... | collective-permute-start | bytes 995336 | tf_op jit(solution)/shard_map/ppermute | solution.py:74
  89.2 13.4 %collective-permute-start.19 = (bf16[144,1152]{1,0:T(8,128)(2,1)S(1)}, bf16[144,1152]{1,0:T(8,128)(2,1)}, u32[]{:S(2)}, u32[]{:S(2)}) collective-permute-start(bf16[144,1152]{1,0:T(8,128)(2,1)S(1)} %slice.67), channel_id=1, source_target_pairs={{0,16},{4,20},{8,24},{12,28},{16,0},{20,4},{24,8},{28,12},{1,17},{... | collective-permute-start | bytes 995336 | tf_op jit(solution)/shard_map/ppermute | solution.py:75
  101.3 17.0 %collective-permute-start.20 = (bf16[288,1152]{1,0:T(8,128)(2,1)S(1)}, bf16[288,1152]{1,0:T(8,128)(2,1)}, u32[]{:S(2)}, u32[]{:S(2)}) collective-permute-start(bf16[288,1152]{1,0:T(8,128)(2,1)S(1)} %pad_maximum_fusion.refs_0_), channel_id=1, source_target_pairs={{0,4},{4,0},{8,12},{12,8},{16,20},{20,16},{24,28},{28,24},{1,5},{5... | collective-permute-start | bytes 1990664 | tf_op jit(solution)/shard_map/ppermute | solution.py:72
  102.0 16.3 %collective-permute-start.22 = (bf16[288,1152]{1,0:T(8,128)(2,1)S(1)}, bf16[288,1152]{1,0:T(8,128)(2,1)}, u32[]{:S(2)}, u32[]{:S(2)}) collective-permute-start(bf16[288,1152]{1,0:T(8,128)(2,1)S(1)} %collective-permute-done.17.refs_2_), channel_id=1, source_target_pairs={{0,4},{4,0},{8,12},{12,8},{16,20},{20,16},{24,28},{28,24},{1,5},{5... | collective-permute-start | bytes 1990664 | tf_op jit(solution)/shard_map/ppermute | solution.py:85
  102.5 14.9 %collective-permute-start.23 = (bf16[144,1152]{1,0:T(8,128)(2,1)}, bf16[144,1152]{1,0:T(8,128)(2,1)}, u32[]{:S(2)}, u32[]{:S(2)}) collective-permute-start(bf16[144,1152]{1,0:T(8,128)(2,1)} %collective-permute-done.18.refs_3_), channel_id=1, source_target_pairs={{0,4},{4,0},{8,12},{12,8},{16,20},{20,16},{24,28},{28,24},{1,5},{5... | collective-permute-start | bytes 995336 | tf_op jit(solution)/shard_map/ppermute | solution.py:85
  102.5 15.8 %collective-permute-start.24 = (bf16[144,1152]{1,0:T(8,128)(2,1)}, bf16[144,1152]{1,0:T(8,128)(2,1)}, u32[]{:S(2)}, u32[]{:S(2)}) collective-permute-start(bf16[144,1152]{1,0:T(8,128)(2,1)} %collective-permute-done.19.refs_4_), channel_id=1, source_target_pairs={{0,4},{4,0},{8,12},{12,8},{16,20},{20,16},{24,28},{28,24},{1,5},{5... | collective-permute-start | bytes 995336 | tf_op jit(solution)/shard_map/ppermute | solution.py:85
  117.5 12.9 %collective-permute-start.28 = (bf16[256,576]{1,0:T(8,128)(2,1)}, bf16[256,576]{1,0:T(8,128)(2,1)}, u32[]{:S(2)}, u32[]{:S(2)}) collective-permute-start(bf16[256,576]{1,0:T(8,128)(2,1)} %get-tuple-element.53), channel_id=1, source_target_pairs={{0,1},{1,0},{2,3},{3,2},{4,5},{5,4},{6,7},{7,6},{8,9},{9,8},{10,11... | collective-permute-start | bytes 884744 | tf_op jit(solution)/shard_map/ppermute | solution.py:445
  118.3 12.0 %copy-start.23 = (f32[2304]{0:T(1024)S(1)}, f32[2304]{0:T(1024)}, u32[]{:S(2)}) copy-start(f32[2304]{0:T(1024)} %param.22) | copy-start | bytes 27652
  121.5 6.4 %collective-permute-start.29 = (f32[1,2304]{1,0:T(1,128)S(1)}, f32[1,2304]{1,0:T(1,128)S(1)}, u32[]{:S(2)}, u32[]{:S(2)}) collective-permute-start(f32[1,2304]{1,0:T(1,128)S(1)} %fusion.8), channel_id=1, source_target_pairs={{0,1},{1,0},{2,3},{3,2},{4,5},{5,4},{6,7},{7,6},{8,9},{9,8},{10,11... | collective-permute-start | bytes 27656 | tf_op jit(solution)/shard_map/ppermute | solution.py:302
  122.7 5.1 %collective-permute-start.30 = (f32[1,2304]{1,0:T(1,128)S(1)}, f32[1,2304]{1,0:T(1,128)S(1)}, u32[]{:S(2)}, u32[]{:S(2)}) collective-permute-start(f32[1,2304]{1,0:T(1,128)S(1)} %fusion.8), channel_id=1, source_target_pairs={{0,2},{1,3},{2,0},{3,1},{4,6},{5,7},{6,4},{7,5},{8,10},{9,11},{10,... | collective-permute-start | bytes 27656 | tf_op jit(solution)/shard_map/ppermute | solution.py:302
  123.6 5.5 %collective-permute-start.31 = (f32[1,2304]{1,0:T(1,128)S(1)}, f32[1,2304]{1,0:T(1,128)S(1)}, u32[]{:S(2)}, u32[]{:S(2)}) collective-permute-start(f32[1,2304]{1,0:T(1,128)S(1)} %fusion.8), channel_id=1, source_target_pairs={{0,3},{1,2},{2,1},{3,0},{4,7},{5,6},{6,5},{7,4},{8,11},{9,10},{10,... | collective-permute-start | bytes 27656 | tf_op jit(solution)/shard_map/ppermute | solution.py:302
  138.6 1.2 collective-permute-start.33
  139.9 5.2 %collective-permute-start.34 = (bf16[8,2304]{1,0:T(8,128)(2,1)S(1)}, bf16[8,2304]{1,0:T(8,128)(2,1)S(1)}, u32[]{:S(2)}, u32[]{:S(2)}) collective-permute-start(bf16[8,2304]{1,0:T(8,128)(2,1)S(1)} %fusion.9), channel_id=1, source_target_pairs={{0,8},{4,12},{8,0},{12,4},{16,24},{20,28},{24,16},{28,20},{1,9},{5... | collective-permute-start | bytes 110600 | tf_op jit(solution)/shard_map/ppermute | solution.py:309
  145.2 40.7 %copy-start.2 = (f32[128,2304]{1,0:T(8,128)S(1)}, f32[128,2304]{1,0:T(8,128)}, u32[]{:S(2)}) copy-start(f32[128,2304]{1,0:T(8,128)} %copy-done.1) | copy-start | bytes 3538948
  145.2 4.0 %collective-permute-start.35 = (bf16[8,2304]{1,0:T(8,128)(2,1)S(1)}, bf16[8,2304]{1,0:T(8,128)(2,1)S(1)}, u32[]{:S(2)}, u32[]{:S(2)}) collective-permute-start(bf16[8,2304]{1,0:T(8,128)(2,1)S(1)} %fusion.28), channel_id=1, source_target_pairs={{0,16},{4,20},{8,24},{12,28},{16,0},{20,4},{24,8},{28,12},{1,17},{... | collective-permute-start | bytes 110600 | tf_op jit(solution)/shard_map/ppermute | solution.py:309
  145.5 27.8 %collective-permute-start.32 = (bf16[128,2304]{1,0:T(8,128)(2,1)}, bf16[128,2304]{1,0:T(8,128)(2,1)S(1)}, u32[]{:S(2)}, u32[]{:S(2)}) collective-permute-start(bf16[128,2304]{1,0:T(8,128)(2,1)} %copy-done.9), channel_id=1, source_target_pairs={{0,2},{1,3},{2,0},{3,1},{4,6},{5,7},{6,4},{7,5},{8,10},{9,11},{10,... | collective-permute-start | bytes 1769480 | tf_op jit(solution)/shard_map/ppermute | solution.py:465
  173.3 1.1 collective-permute-start.36
  174.5 3.6 %collective-permute-start.37 = (f32[2,8]{1,0:T(2,128)S(1)}, f32[2,8]{1,0:T(2,128)S(1)}, u32[]{:S(2)}, u32[]{:S(2)}) collective-permute-start(f32[2,8]{1,0:T(2,128)S(1)} %pad_maximum_fusion.8), channel_id=1, source_target_pairs={{0,8},{4,12},{8,0},{12,4},{16,24},{20,28},{24,16},{28,20},{1,9},{5... | collective-permute-start | bytes 200 | tf_op jit(solution)/shard_map/ppermute | solution.py:309
  178.1 3.6 %collective-permute-start.38 = (f32[2,8]{1,0:T(2,128)S(1)}, f32[2,8]{1,0:T(2,128)S(1)}, u32[]{:S(2)}, u32[]{:S(2)}) collective-permute-start(f32[2,8]{1,0:T(2,128)S(1)} %pad_maximum_fusion.9), channel_id=1, source_target_pairs={{0,16},{4,20},{8,24},{12,28},{16,0},{20,4},{24,8},{28,12},{1,17},{... | collective-permute-start | bytes 200 | tf_op jit(solution)/shard_map/ppermute | solution.py:309
  181.8 3.6 %collective-permute-start.39 = (f32[2,8]{1,0:T(2,128)S(1)}, f32[2,8]{1,0:T(2,128)S(1)}, u32[]{:S(2)}, u32[]{:S(2)}) collective-permute-start(f32[2,8]{1,0:T(2,128)S(1)} %pad_maximum_fusion.10), channel_id=1, source_target_pairs={{0,1},{1,0},{2,3},{3,2},{4,5},{5,4},{6,7},{7,6},{8,9},{9,8},{10,11... | collective-permute-start | bytes 200 | tf_op jit(solution)/shard_map/ppermute | solution.py:309
  185.5 4.5 %collective-permute-start.40 = (f32[2,8]{1,0:T(2,128)S(1)}, f32[2,8]{1,0:T(2,128)S(1)}, u32[]{:S(2)}, u32[]{:S(2)}) collective-permute-start(f32[2,8]{1,0:T(2,128)S(1)} %pad_maximum_fusion.11), channel_id=1, source_target_pairs={{0,2},{1,3},{2,0},{3,1},{4,6},{5,7},{6,4},{7,5},{8,10},{9,11},{10,... | collective-permute-start | bytes 200 | tf_op jit(solution)/shard_map/ppermute | solution.py:309
  (19 other events, 30.4 us)

commit v3 on v2

--- a/solution.py
+++ b/solution.py
@@ -9,7 +9,7 @@
 
 HEAD_DIM = 64
 EPSILON = 1e-05
-ANY = pl.BlockSpec(memory_space=pl.ANY)
+HBM = pl.BlockSpec(memory_space=pltpu.HBM)
 SMEM = pl.BlockSpec(memory_space=pltpu.SMEM)
 VMEM = pl.BlockSpec(memory_space=pltpu.VMEM)
 
@@ -48,42 +48,68 @@
     return lax.optimization_barrier((value, *earlier))[0]
 
 
-def gather_line(block, size):
+class Rows:
+    def __init__(self, block, size):
+        self.block, self.size, self.rows = block, size, block.shape[0]
+        self.half = self.rows // 2
+
+    def send(self, array, mask):
+        return lax.ppermute(array, "req", xor_pairs(self.size, mask))
+
+    def neighbours(self):
+        if self.size != 8:
+            return [lax.all_gather(self.block, "req", axis=0, tiled=True)]
+        return [self.send(self.block, 2), self.send(self.block, 4)]
+
+    def diagonal(self, got):
+        if self.size != 8:
+            return []
+        half_x, half_y = lax.optimization_barrier((got[0][self.half :], got[1][: self.half]))
+        return [self.send(half_y, 2), self.send(half_x, 4)]
+
+    def cores(self, arrays):
+        return [self.send(array, 1) for array in arrays] if self.size == 8 else []
+
+    def pieces(self, got, diagonal, others):
+        if self.size != 8:
+            return [(got[0], None, 0, self.rows * self.size)]
+        places = [
+            (0, 0, self.rows),
+            (2, 0, self.rows),
+            (4, 0, self.rows),
+            (6, 0, self.half),
+            (6, self.half, self.half),
+        ]
+        pieces = []
+        for here, there, (mask, at, count) in zip(
+            [self.block, *got, *diagonal], others, places, strict=True
+        ):
+            pieces += [(here, mask, at, count), (there, mask ^ 1, at, count)]
+        return pieces
+
+
+def gather_line(block, size, *ready):
     ups, downs = [], []
     up, down = block, block
     for step in range(1, size):
         up = lax.ppermute(up, "row", up_pairs(size, 1, step - 1))
         down = lax.ppermute(down, "row", down_pairs(size, 1, size - step))
-        up, down = lax.optimization_barrier((up, down))
+        if step == size - 2:
+            up, down, *ready = lax.optimization_barrier((up, down, *ready))
+        else:
+            up, down = lax.optimization_barrier((up, down))
         ups.append(up)
         downs.append(down)
-    return ups, downs
-
-
-def gather_weights(block, size, *earlier):
-    rows = block.shape[0]
-    if size != 8:
-        whole = lax.all_gather(block, "req", axis=0, tiled=True)
-        return [(whole, None, 0, rows * size)]
-    half = rows // 2
-    from_x = lax.ppermute(block, "req", xor_pairs(size, 2))
-    from_y = lax.ppermute(block, "req", xor_pairs(size, 4))
-    block, from_x, from_y, *_ = lax.optimization_barrier((block, from_x, from_y, *earlier))
-    from_c = lax.ppermute(block, "req", xor_pairs(size, 1))
-    half_x, half_y = lax.optimization_barrier((from_x[half:], from_y[:half]))
-    diag_a = lax.ppermute(half_y, "req", xor_pairs(size, 2))
-    diag_b = lax.ppermute(half_x, "req", xor_pairs(size, 4))
-    pieces = [
-        (block, 0, 0, rows),
-        (from_x, 2, 0, rows),
-        (from_y, 4, 0, rows),
-        (diag_a, 6, 0, half),
-        (diag_b, 6, half, half),
-        (from_c, 1, 0, rows),
-    ]
-    for array, mask, first, count in pieces[1:5]:
-        pieces.append((lax.ppermute(array, "req", xor_pairs(size, 1)), mask ^ 1, first, count))
-    return pieces
+    return ups, downs, *ready
+
+
+def together(*groups):
+    flat = lax.optimization_barrier(tuple(array for group in groups for array in group))
+    result, at = [], 0
+    for group in groups:
+        result.append(list(flat[at : at + len(group)]))
+        at += len(group)
+    return result
 
 
 def weight_copies(refs, layout, target, sems, me_req, block_rows):
@@ -127,6 +153,7 @@
     weights = refs[2 * size - 1 : 2 * size - 1 + pieces]
     cos_ref, sin_ref, out_ref, x_scr, w_scr, x_sems, w_sems = refs[2 * size - 1 + pieces :]
     rows = own.shape[0]
+    total = out_ref.shape[1]
     copies = weight_copies(weights, layout, w_scr, w_sems, scalars[1], block_rows)
     for copy in copies:
         copy.start()
@@ -134,16 +161,14 @@
     for copy in waits + copies:
         copy.wait()
     span = x_scr.shape[0]
-    total = out_ref.shape[1]
     width = total // 3
     half = HEAD_DIM // 2
     lane = lax.broadcasted_iota(jnp.int32, (span, 128), 1)
     first_half = lax.rem(lane, HEAD_DIM) < half
     cosine, sine = cos_ref[...], sin_ref[...]
-    x = x_scr[...]
     for tile in range(0, total, 256):
         end = min(tile + 256, total)
-        raw = jnp.dot(x, w_scr[:, tile:end], preferred_element_type=jnp.float32)
+        raw = jnp.dot(x_scr[...], w_scr[:, tile:end], preferred_element_type=jnp.float32)
         for at in range(tile, end, 128):
             stop = min(at + 128, end)
             part = raw[:, at - tile : stop - tile]
@@ -180,16 +205,20 @@
 
 def attention_kernel(size, scalars, *refs):
     blocks = refs[:size]
-    qkv_ref, keep_ref, send_ref, last_ref, old_scr, att_scr, sems = refs[size:]
-    rows = blocks[0].shape[0]
-    half_rows = rows // 2
+    qkv_ref, keep_ref, send_ref, last_ref, k_old, v_old, att_scr, sems = refs[size:]
+    rows = blocks[0].shape[0] // 2
     me_row, length, count = scalars[0], scalars[2], scalars[3]
     waits = []
     for mask in range(size):
         index = jnp.bitwise_xor(me_row, mask)
-        place = old_scr.at[pl.ds(pl.multiple_of(index * rows, rows), rows), :]
-        waits.append(pltpu.make_async_copy(blocks[mask], place, sems.at[mask]))
-        waits[-1].start()
+        for part, target in enumerate((k_old, v_old)):
+            copy = pltpu.make_async_copy(
+                blocks[mask].at[pl.ds(part * rows, rows), :],
+                target.at[pl.ds(pl.multiple_of(index * rows, rows), rows), :],
+                sems.at[part, mask],
+            )
+            copy.start()
+            waits.append(copy)
     for copy in waits:
         copy.wait()
     span, total = qkv_ref.shape
@@ -201,45 +230,44 @@
         lane = lax.broadcasted_iota(jnp.int32, (block, 128), 1)
         left = lane < HEAD_DIM
 
-        def old(part, lo, hi):
-            at = part * half_rows
-            return jnp.concatenate(
-                [old_scr[i * rows + at : i * rows + at + half_rows, lo:hi] for i in range(live)],
-                axis=0,
-            )
-
-        for lo in range(0, width, 128):
-            pair = lo < last
-            hi = lo + 128 if pair else width
-            k_at = width + HEAD_DIM + lo if pair else width
-            k_old, v_old = old(0, lo, hi), old(1, lo, hi)
+        def heads(q_at, k_at, v_at, lo, wide):
+            old_k, old_v = k_old[0:live, pl.ds(lo, wide)], v_old[0:live, pl.ds(lo, wide)]
             for begin in range(0, span, block):
                 stop = begin + block
-                q = qkv_ref[begin:stop, lo:hi]
-                k_new = qkv_ref[0:stop, k_at : k_at + hi - lo]
-                v_new = qkv_ref[0:stop, 2 * width + lo : 2 * width + hi]
+                q = qkv_ref[begin:stop, pl.ds(q_at, wide)]
+                k_new = qkv_ref[0:stop, pl.ds(k_at, wide)]
+                v_new = qkv_ref[0:stop, pl.ds(v_at, wide)]
                 row = begin + lax.broadcasted_iota(jnp.int32, (block, 1), 0)
                 limit = jnp.minimum(row + 1, count)
-                if pair:
+                if wide == 128:
                     zero = jnp.zeros_like(q)
-                    even = attend_block(
-                        jnp.where(left, q, zero), k_new, v_new, k_old, v_old, limit, length
+                    both = jnp.where(
+                        left,
+                        attend_block(
+                            jnp.where(left, q, zero), k_new, v_new, old_k, old_v, limit, length
+                        ),
+                        attend_block(
+                            jnp.where(left, zero, q), k_new, v_new, old_k, old_v, limit, length
+                        ),
                     )
-                    odd = attend_block(
-                        jnp.where(left, zero, q), k_new, v_new, k_old, v_old, limit, length
-                    )
-                    both = jnp.where(left, even, odd)
                 else:
-                    both = attend_block(q, k_new, v_new, k_old, v_old, limit, length)
-                att_scr[begin:stop, lo:hi] = both.astype(jnp.bfloat16)
-
-    @pl.when(length <= half_rows)
+                    both = attend_block(q, k_new, v_new, old_k, old_v, limit, length)
+                att_scr[begin:stop, pl.ds(lo, wide)] = both.astype(jnp.bfloat16)
+
+        @pl.loop(0, last // 128)
+        def _(pair):
+            lo = pl.multiple_of(pair * 128, 128)
+            heads(lo, lo + width + HEAD_DIM, lo + 2 * width, lo, 128)
+
+        heads(last, width, 2 * width + last, last, HEAD_DIM)
+
+    @pl.when(length <= rows)
     def _():
-        attend(1)
-
-    @pl.when(length > half_rows)
+        attend(rows)
+
+    @pl.when(length > rows)
     def _():
-        attend(size)
+        attend(size * rows)
 
     chunk = span // size
     for slot, ref in ((0, keep_ref), (1, send_ref), (2, keep_ref), (3, send_ref)):
@@ -296,6 +324,24 @@
         mate_ref[:, tile:to] = total[chunk:].astype(jnp.bfloat16)
 
 
+def head_kernel(table_ref, *refs):
+    weights, (logits_ref, stats_ref) = refs[:-2], refs[-2:]
+    step = pl.program_id(0)
+    wide = weights[0].shape[1]
+    for index, ref in enumerate(weights):
+        start = pl.multiple_of((step * len(weights) + index) * wide, 128)
+        logits_ref[:, pl.ds(start, wide)] = jnp.dot(
+            table_ref[...], ref[...], preferred_element_type=jnp.float32
+        )
+
+    @pl.when(step == pl.num_programs(0) - 1)
+    def _():
+        logits = logits_ref[...]
+        top = jnp.max(logits, axis=1, keepdims=True)
+        stats_ref[:, 0:1] = top
+        stats_ref[:, 1:2] = jnp.sum(jnp.exp(logits - top), axis=1, keepdims=True)
+
+
 def sum_line(value, size):
     total = value
     for mask in range(1, size):
@@ -303,18 +349,26 @@
     return total
 
 
-def butterfly(value, axis, size, combine):
+def combine_all(value, axis, size, combine, width=4):
     bit = 1
     while bit < size:
-        value = combine(value, lax.ppermute(value, axis, xor_pairs(size, bit)))
-        bit *= 2
+        count = min(width, size // bit)
+        others = [
+            lax.ppermute(value, axis, xor_pairs(size, bit * index)) for index in range(1, count)
+        ]
+        value = combine(value, *others)
+        bit *= count
     return value
 
 
-def merge_stats(one, other):
-    top = jnp.maximum(one[0], other[0])
-    total = one[1] * jnp.exp(one[0] - top) + other[1] * jnp.exp(other[0] - top)
-    return jnp.stack([top, total])
+def add_all(*tables):
+    return functools.reduce(jnp.add, tables)
+
+
+def merge_stats(*stats):
+    top = functools.reduce(jnp.maximum, [one[:, :1] for one in stats])
+    total = add_all(*[one[:, 1:] * jnp.exp(one[:, :1] - top) for one in stats])
+    return jnp.concatenate([top, total], axis=1)
 
 
 def on_device(
@@ -349,15 +403,6 @@
     normed = rms_scale(inputs.astype(jnp.float32), attn_gain).astype(jnp.bfloat16)
     last = width - HEAD_DIM
     joined = jnp.concatenate([w_query, w_key[:, last:], w_key[:, :last], w_value], axis=1)
-    x_ups, x_downs = gather_line(normed, n_row)
-    joined = after(joined, normed)
-    pieces = gather_weights(joined, n_req)
-    layout = tuple(piece[1:] for piece in pieces)
-
-    out_own = w_out.T
-    out_next = lax.ppermute(out_own, "row", xor_pairs(n_row, 1))
-    out_both = jnp.concatenate([out_own, out_next], axis=1)
-    out_both = after(out_both, *[piece[0] for piece in pieces[1:]], x_ups[-1], x_downs[-1])
 
     def cache_for(owner):
         return jnp.concatenate(
@@ -369,16 +414,37 @@
         )
 
     cached_rows = key_cache.shape[1]
-    old_blocks = []
-    for mask in range(1, n_row):
-        block = after(cache_for(jnp.bitwise_xor(me_row, mask)), x_ups[-1], x_downs[-1])
-        old_blocks.append(lax.ppermute(block, "row", xor_pairs(n_row, mask)))
+
+    joined = after(joined, normed)
+    out_own = w_out.T
+    weights = Rows(joined, n_req)
+    got = weights.neighbours()
     cosine, sine = rotary_tables(length + jnp.arange(span, dtype=jnp.int32))
+    x_ups, x_downs, scalars, cosine, sine = gather_line(normed, n_row, scalars, cosine, sine)
+    got, own = together(got, [joined])
+    diagonal = weights.diagonal(got)
+    others = weights.cores([*own, *got, *diagonal])
+    pieces = weights.pieces(got, diagonal, others)
+    layout = tuple(piece[1:] for piece in pieces)
+
+    out_next = lax.ppermute(out_own, "row", xor_pairs(n_row, 1))
+    old_blocks = [
+        lax.ppermute(
+            after(cache_for(jnp.bitwise_xor(me_row, mask)), x_ups[-1], x_downs[-1]),
+            "row",
+            xor_pairs(n_row, mask),
+        )
+        for mask in range(1, n_row)
+    ]
+    out_rows = Rows(
+        after(jnp.concatenate([out_own, out_next], axis=1), x_ups[-1], x_downs[-1], *others), n_req
+    )
+    out_got = out_rows.neighbours()
 
     qkv = pl.pallas_call(
         functools.partial(qkv_kernel, n_row, layout, block_rows),
         out_shape=jax.ShapeDtypeStruct((span, 3 * width), jnp.bfloat16),
-        in_specs=[SMEM] + [ANY] * (2 * n_row - 1 + len(pieces)) + [VMEM] * 2,
+        in_specs=[SMEM] + [HBM] * (2 * n_row - 1 + len(pieces)) + [VMEM] * 2,
         out_specs=VMEM,
         scratch_shapes=[
             pltpu.VMEM((span, model), jnp.bfloat16),
@@ -393,7 +459,9 @@
         name="qkv",
     )(scalars, normed, *x_ups, *x_downs, *[piece[0] for piece in pieces], cosine, sine)
 
-    out_pieces = gather_weights(out_both, n_req, qkv)
+    out_block, *out_got = lax.optimization_barrier((out_rows.block, *out_got, qkv))[:-1]
+    out_diagonal = out_rows.diagonal(out_got)
+    out_others = out_rows.cores([out_block, *out_got])
 
     chunk = span // n_row
     keep, send, last_attended = pl.pallas_call(
@@ -403,12 +471,13 @@
             jax.ShapeDtypeStruct((2 * chunk, width), jnp.bfloat16),
             jax.ShapeDtypeStruct((16, width), jnp.bfloat16),
         ),
-        in_specs=[SMEM] + [ANY] * n_row + [VMEM],
+        in_specs=[SMEM] + [HBM] * (1 + len(old_blocks)) + [VMEM],
         out_specs=(VMEM, VMEM, VMEM),
         scratch_shapes=[
-            pltpu.VMEM((2 * cached_rows * n_row, width), jnp.bfloat16),
+            pltpu.VMEM((cached_rows * n_row, width), jnp.bfloat16),
+            pltpu.VMEM((cached_rows * n_row, width), jnp.bfloat16),
             pltpu.VMEM((span, width), jnp.bfloat16),
-            pltpu.SemaphoreType.DMA((n_row,)),
+            pltpu.SemaphoreType.DMA((2, n_row)),
         ],
         compiler_params=params(24),
         cost_estimate=pl.CostEstimate(
@@ -417,13 +486,15 @@
         name="attention",
     )(scalars, cache_for(me_row), *old_blocks, qkv)
 
+    out_others += out_rows.cores(out_diagonal)
+    out_pieces = out_rows.pieces(out_got, out_diagonal, out_others)
     out_layout = tuple(piece[1:] for piece in out_pieces)
     out_weights = [piece[0] for piece in out_pieces]
     own_columns = -(-width // 128) * 128
     own_part = pl.pallas_call(
         functools.partial(last_row_kernel, out_layout, block_rows),
         out_shape=jax.ShapeDtypeStruct((16, model), jnp.float32),
-        in_specs=[SMEM] + [ANY] * len(out_weights) + [VMEM],
+        in_specs=[SMEM] + [HBM] * len(out_weights) + [VMEM],
         out_specs=VMEM,
         scratch_shapes=[
             pltpu.VMEM((model, own_columns), jnp.bfloat16),
@@ -442,15 +513,14 @@
     own_part += jnp.where(is_owner, residual.astype(jnp.float32), 0.0)
     last_row = sum_line(own_part, n_row)
 
-    got = lax.ppermute(send, "row", xor_pairs(n_row, 1))
-    got = after(got, last_row)
+    got = after(lax.ppermute(send, "row", xor_pairs(n_row, 1)), last_row)
     own_sum, mate_part = pl.pallas_call(
         functools.partial(project_kernel, out_layout, block_rows),
         out_shape=(
             jax.ShapeDtypeStruct((chunk, model), jnp.float32),
             jax.ShapeDtypeStruct((chunk, model), jnp.bfloat16),
         ),
-        in_specs=[SMEM] + [ANY] * len(out_weights) + [VMEM] * 3,
+        in_specs=[SMEM] + [HBM] * len(out_weights) + [VMEM] * 3,
         out_specs=(VMEM, VMEM),
         scratch_shapes=[
             pltpu.VMEM((model, 2 * width), jnp.bfloat16),
@@ -468,16 +538,38 @@
     final_row = rms_scale(
         last_row.astype(jnp.bfloat16).astype(jnp.float32), final_gain
     ).astype(jnp.bfloat16)
-    final_row = after(final_row, mate_part)
     table = jnp.where(jnp.arange(n_req)[:, None] == me_req, final_row, jnp.zeros_like(final_row))
-    table = butterfly(table, "req", n_req, jnp.add)
-    logits = jnp.dot(table, head_weight, preferred_element_type=jnp.float32)
-    top = jnp.max(logits, axis=1)
-    stats = jnp.stack([top, jnp.sum(jnp.exp(logits - top[:, None]), axis=1)])
+    table = combine_all(table, "req", n_req, add_all, 2)
+    table = after(table, mate_part)
+    vocab = head_weight.shape[1]
+    wide, streams = 256, 3
+
+    def columns(index):
+        return pl.BlockSpec((model, wide), lambda step: (0, step * streams + index))
+
+    logits, stats = pl.pallas_call(
+        head_kernel,
+        grid=(vocab // (wide * streams),),
+        out_shape=(
+            jax.ShapeDtypeStruct((n_req, vocab), jnp.float32),
+            jax.ShapeDtypeStruct((n_req, 2), jnp.float32),
+        ),
+        in_specs=[
+            pl.BlockSpec((n_req, model), lambda step: (0, 0)),
+            *[columns(index) for index in range(streams)],
+        ],
+        out_specs=(
+            pl.BlockSpec((n_req, vocab), lambda step: (0, 0)),
+            pl.BlockSpec((n_req, 2), lambda step: (0, 0)),
+        ),
+        compiler_params=params(48),
+        cost_estimate=pl.CostEstimate(flops=0, bytes_accessed=0, transcendentals=0),
+        name="head",
+    )(table, *[head_weight] * streams)
+    stats = combine_all(stats, "req", n_req, merge_stats, 8)
     stats = after(stats, others)
-    stats = butterfly(stats, "req", n_req, merge_stats)
-    stats = butterfly(stats, "row", n_row, merge_stats)
-    logprobs = logits - stats[0][:, None] - jnp.log(stats[1])[:, None]
+    stats = combine_all(stats, "row", n_row, merge_stats)
+    logprobs = logits - stats[:, :1] - jnp.log(stats[:, 1:])
     return (layer_rows[None], logprobs)
 
 

time: 191 us -> 181 us (0.948)
  waiting for transfers between devices: 83.3 us -> 58.6 us
  Pallas kernels: 26.2 us -> 37 us
  matrix products: 8.54 us -> 0 us
  starting transfers between devices: 43.5 us -> 50.8 us
  other arithmetic: 8.32 us -> 11.5 us
    ppermute x1, waiting for transfers between devices: 15.3 us -> 4.1 us  [on_device(): others = lax.ppermute(mate_part, 'row', xor_pairs(n_row, 2))]
    dot_general x1 -> x0, matrix products: 8.54 us -> none  [on_device(): logits = jnp.dot(table, head_weight, preferred_element_type=jnp.float32)]
    pallas_call x0 -> x1, Pallas kernels: none -> 8.38 us  [on_device(): pl.pallas_call(head_kernel, grid=(vocab // (wide * streams),), out_shape=...]
    ppermute x30 -> x35, waiting for transfers between devices: 29.9 us -> 22.1 us  [the longest x13 8.44 us: combine_all(): lax.ppermute(value, axis, xor_pairs(size, bit * index))]
    ppermute x1, waiting for transfers between devices: 5.89 us -> 0.01 us  [on_device(): out_next = lax.ppermute(out_own, 'row', xor_pairs(n_row, 1))]
    ppermute x30 -> x35, starting transfers between devices: 24.9 us -> 29.5 us  [the longest x13 13.6 us: combine_all(): lax.ppermute(value, axis, xor_pairs(size, bit * index))]
    ppermute x3, starting transfers between devices: 4.45 us -> 7.38 us  [sum_line(): total = total + lax.ppermute(value, 'row', xor_pairs(size, mask))]
    concatenate x1, other arithmetic: 0.47 us -> 2.89 us  [rotary_tables(): jnp.concatenate([cosine] * 4, axis=1)]
  transfers between devices with their start and end apart: 41 -> 46, of which waited for: 20 -> 18; matrix products, arithmetic and copies ran while one was open for 11% -> 9% of each run, Pallas kernels for 11% -> 19%
where the time goes in v3:
time: 181 us; the launch traced here: 180 us
  waiting for transfers between devices  58.6 us (32%)
  starting transfers between devices  50.8 us (28%)
  Pallas kernels  37 us (20%)
  local copies, waits for them, and re-layouts  18.7 us (10%)
  other arithmetic  11.5 us (6%)
  between operations  3.19 us (2%)
    ppermute x3, waiting for transfers between devices, gather_line(): down = lax.ppermute(down, 'row', down_pairs(size, 1, size - step))  20.2 us
    ppermute x13, starting transfers between devices, combine_all(): lax.ppermute(value, axis, xor_pairs(size, bit * index))  13.6 us
    unnamed x56, local copies, waits for them, and re-layouts  11.5 us
    pallas_call x1, Pallas kernels, on_device(): pl.pallas_call(functools.partial(attention_kernel, n_row), out_shape=(jax...  10.7 us
    ppermute x18, starting transfers between devices, send(): return lax.ppermute(array, 'req', xor_pairs(self.size, mask))  10.4 us
    ppermute x3, waiting for transfers between devices, gather_line(): up = lax.ppermute(up, 'row', up_pairs(size, 1, step - 1))  9.07 us
    pallas_call x1, Pallas kernels, on_device(): pl.pallas_call(functools.partial(qkv_kernel, n_row, layout, block_rows),...  8.98 us
    ppermute x13, waiting for transfers between devices, combine_all(): lax.ppermute(value, axis, xor_pairs(size, bit * index))  8.44 us
  transfers between devices with their start and end apart: 46, of which 18 were waited for; matrix products, arithmetic and copies ran while one was open for 9% of the time, Pallas kernels for 19%

profile of v3, /device:TPU:0, one launch (start us, length us, event | category | flops | bytes accessed | tf_op | source)
XLA Modules:
  0.0 179.8 jit_solution(9465629056942717578)
XLA Ops:
  0.7 1.4 fusion
  2.8 3.0 %collective-permute-start.7 = (bf16[288,1728]{1,0:T(8,128)(2,1)S(1)}, bf16[288,1728]{1,0:T(8,128)(2,1)}, u32[]{:S(2)}, u32[]{:S(2)}) collective-permute-start(bf16[288,1728]{1,0:T(8,128)(2,1)S(1)} %concatenate.30.refs_7_), channel_id=1, source_target_pairs={{0,8},{4,12},{8,0},{12,4},{16,24},{20,28},{24,16},{28,20},{1,9},{5... | collective-permute-start | bytes 2985992 | tf_op jit(solution)/shard_map/ppermute | solution.py:57
  5.8 1.5 collective-permute-start.8
  7.3 3.5 %collective-permute-start = (bf16[128,2304]{1,0:T(8,128)(2,1)S(1)}, bf16[128,2304]{1,0:T(8,128)(2,1)S(1)}, u32[]{:S(2)}, u32[]{:S(2)}) collective-permute-start(bf16[128,2304]{1,0:T(8,128)(2,1)S(1)} %fusion.2.refs_0_), channel_id=1, source_target_pairs={{0,1},{1,2},{2,3},{4,5},{5,6},{6,7},{8,9},{9,10},{10,11},{12,13},{... | collective-permute-start | bytes 1769480 | tf_op jit(solution)/shard_map/ppermute | solution.py:95
  10.8 1.3 collective-permute-start.1
  12.1 2.7 %collective-permute-start.4 = (bf16[288,576]{1,0:T(8,128)(2,1)}, bf16[288,576]{1,0:T(8,128)(2,1)}, u32[]{:S(2)}, u32[]{:S(2)}) collective-permute-start(bf16[288,576]{1,0:T(8,128)(2,1)} %bitcast.35), channel_id=1, source_target_pairs={{0,1},{1,0},{2,3},{3,2},{4,5},{5,4},{6,7},{7,6},{8,9},{9,8},{10,11... | collective-permute-start | bytes 995336 | tf_op jit(solution)/shard_map/ppermute | solution.py:430
  15.5 9.1 %collective-permute-done.refs_1_ = bf16[128,2304]{1,0:T(8,128)(2,1)S(1)} collective-permute-done((bf16[128,2304]{1,0:T(8,128)(2,1)S(1)}, bf16[128,2304]{1,0:T(8,128)(2,1)S(1)}, u32[]{:S(2)}, u32[]{:S(2)}) %collective-permute-start) | collective-permute-done | bytes 589856 | tf_op jit(solution)/shard_map/ppermute | solution.py:95
  24.5 4.5 %collective-permute-done.1.refs_4_ = bf16[128,2304]{1,0:T(8,128)(2,1)} collective-permute-done((bf16[128,2304]{1,0:T(8,128)(2,1)S(1)}, bf16[128,2304]{1,0:T(8,128)(2,1)}, u32[]{:S(2)}, u32[]{:S(2)}) %collective-permute-start.1) | collective-permute-done | bytes 589856 | tf_op jit(solution)/shard_map/ppermute | solution.py:96
  29.1 1.5 collective-permute-start.2
  30.6 1.3 collective-permute-start.3
  31.9 1.9 %slice.107 = bf16[144,1728]{1,0:T(8,128)(2,1)} slice(bf16[288,1728]{1,0:T(8,128)(2,1)} %collective-permute-done.7.refs_9_), slice={[144:288], [0:1728]} | slice | bytes 995328 | tf_op jit(solution)/shard_map/slice | solution.py:67
  33.8 1.9 %slice.108 = bf16[144,1728]{1,0:T(8,128)(2,1)} slice(bf16[288,1728]{1,0:T(8,128)(2,1)} %collective-permute-done.8.refs_11_), slice={[0:144], [0:1728]} | slice | bytes 995328 | tf_op jit(solution)/shard_map/slice | solution.py:67
  36.8 1.8 %fusion.4 = (f32[512,32]{1,0:T(8,128)S(1)}, f32[512,32]{1,0:T(8,128)}, f32[512,32]{1,0:T(8,128)}) fusion(f32[32]{0:T(128)S(1)} %multiply_power_fusion, f32[512]{0:T(512)S(1)} %add_convert_fusion.1), kind=kLoop, calls=%fused_computation.25 | loop fusion | flops 32768 | bytes 198784 | tf_op jit(solution)/shard_map/neg | solution.py:30
  39.3 2.9 %pad_maximum_fusion.5 = (f32[512,128]{1,0:T(8,128)S(1)}, f32[512,128]{1,0:T(8,128)}) fusion(f32[512,32]{1,0:T(8,128)} %get-tuple-element.86, f32[512,32]{1,0:T(8,128)} %get-tuple-element.85, f32[512,32]{1,0:T(8,128)S(1)} %get-tuple-element.84), kind=kLoop, calls=%fused_computation.14 | loop fusion | flops 393216 | bytes 720896 | tf_op jit(solution)/shard_map/concatenate | solution.py:29
  42.2 5.3 %collective-permute-done.3.refs_5_ = bf16[128,2304]{1,0:T(8,128)(2,1)} collective-permute-done((bf16[128,2304]{1,0:T(8,128)(2,1)}, bf16[128,2304]{1,0:T(8,128)(2,1)}, u32[]{:S(2)}, u32[]{:S(2)}) %collective-permute-start.3) | collective-permute-done | bytes 589856 | tf_op jit(solution)/shard_map/ppermute | solution.py:96
  48.3 1.3 collective-permute-start.6
  51.5 10.3 %collective-permute-done.6.refs_6_ = bf16[128,2304]{1,0:T(8,128)(2,1)S(1)} collective-permute-done((bf16[128,2304]{1,0:T(8,128)(2,1)}, bf16[128,2304]{1,0:T(8,128)(2,1)S(1)}, u32[]{:S(2)}, u32[]{:S(2)}) %collective-permute-start.6) | collective-permute-done | bytes 589856 | tf_op jit(solution)/shard_map/ppermute | solution.py:96
  62.7 2.8 %dynamic-slice_bitcast_fusion = (bf16[128,576]{1,0:T(8,128)(2,1)S(1)}, bf16[128,576]{1,0:T(8,128)(2,1)S(1)}, bf16[128,576]{1,0:T(8,128)(2,1)}, bf16[128,576]{1,0...) fusion(bf16[1,128,2304]{2,1,0:T(8,128)(2,1)} %param.16, ...), kind=kLoop, calls=%fused_computation.16 | loop fusion | bytes 2359312 | tf_op jit(solution)/shard_map/dynamic_slice | solution.py:411
  65.5 1.3 pad_maximum_fusion.refs_0_
  68.1 3.6 %collective-permute-start.26 = (bf16[256,576]{1,0:T(8,128)(2,1)S(1)}, bf16[256,576]{1,0:T(8,128)(2,1)S(1)}, u32[]{:S(2)}, u32[]{:S(2)}) collective-permute-start(bf16[256,576]{1,0:T(8,128)(2,1)S(1)} %pad_maximum_fusion.3), channel_id=1, source_target_pairs={{0,2},{1,3},{2,0},{3,1},{4,6},{5,7},{6,4},{7,5},{8,10},{9,11},{10,... | collective-permute-start | bytes 884744 | tf_op jit(solution)/shard_map/ppermute | solution.py:432
  72.5 9.0 %qkv.1.refs_4_ = bf16[512,1728]{1,0:T(8,128)(2,1)S(1)} custom-call(s32[4]{0:T(128)S(1)} %pad_add_fusion.scalars, bf16[128,2304]{1,0:T(8,128)(2,1)S(1)} %fusion.2.refs_0_, bf16[128,2304]{1,0:T(8,128)(2,1)S(1)} %copy-done.9, bf16[128,2304]{1,0:T(8,128)(2,1)} %collective-permute-done.2.refs_2_, bf16[128,2304]{1,0:T(8,128)(2,1)S(1)} %copy-done.11, ...), custom_call_target="tpu_custom_call" | custom-call | flops 4076863488 | bytes 14680064 | tf_op jit(solution)/shard_map/qkv/pallas_call | solution.py:444
  81.5 1.2 copy-done.20
  82.8 1.4 collective-permute-done.16.refs_2_
  84.6 1.6 collective-permute-start.21
  87.4 7.0 %collective-permute-done.26.refs_2_ = bf16[256,576]{1,0:T(8,128)(2,1)S(1)} collective-permute-done((bf16[256,576]{1,0:T(8,128)(2,1)S(1)}, bf16[256,576]{1,0:T(8,128)(2,1)S(1)}, u32[]{:S(2)}, u32[]{:S(2)}) %collective-permute-start.26) | collective-permute-done | bytes 294944 | tf_op jit(solution)/shard_map/ppermute | solution.py:432
  100.8 1.5 copy-done.21
  102.3 10.7 %attention.1 = (bf16[256,576]{1,0:T(8,128)(2,1)S(1)}, bf16[256,576]{1,0:T(8,128)(2,1)}, bf16[16,576]{1,0:T(8,128)(2,1)S(1)}) custom-call(s32[4]{0:T(128)S(1)} %pad_add_fusion.scalars, bf16[256,576]{1,0:T(8,128)(2,1)S(1)} %pad_maximum_fusion.1.refs_0_, bf16[256,576]{1,0:T(8,128)(2,1)S(1)} %copy-done.15, bf16[256,576]{1,0:T(8,128)(2,1)S(1)} %copy-done.17, ...), custom_call_target="tpu_custom_call" | custom-call | flops 905969664 | bytes 4194304 | tf_op jit(solution)/shard_map/attention/pallas_call | solution.py:467
  113.0 2.9 %last_row.1 = f32[16,2304]{1,0:T(8,128)S(1)} custom-call(s32[4]{0:T(128)S(1)} %pad_add_fusion.scalars, bf16[288,1152]{1,0:T(8,128)(2,1)S(1)} %pad_maximum_fusion.refs_0_, bf16[288,1152]{1,0:T(8,128)(2,1)} %collective-permute-done.18.refs_1_, bf16[288,1152]{1,0:T(8,128)(2,1)S(1)} %collective-permute-done.16.refs_2_, ...), custom_call_target="tpu_custom_call" | custom-call | flops 42467328 | bytes 4194304 | tf_op jit(solution)/shard_map/last_row/pallas_call | solution.py:494
  116.0 4.9 %collective-permute-start.29 = (f32[1,2304]{1,0:T(1,128)S(1)}, f32[1,2304]{1,0:T(1,128)S(1)}, u32[]{:S(2)}, u32[]{:S(2)}) collective-permute-start(f32[1,2304]{1,0:T(1,128)S(1)} %fusion.6), channel_id=1, source_target_pairs={{0,1},{1,0},{2,3},{3,2},{4,5},{5,4},{6,7},{7,6},{8,9},{9,8},{10,11... | collective-permute-start | bytes 27656 | tf_op jit(solution)/shard_map/ppermute | solution.py:348
  122.0 1.4 collective-permute-start.31
  124.4 1.1 collective-permute-done.30
  125.5 2.0 %collective-permute-done.31 = f32[1,2304]{1,0:T(1,128)S(1)} collective-permute-done((f32[1,2304]{1,0:T(1,128)S(1)}, f32[1,2304]{1,0:T(1,128)S(1)}, u32[]{:S(2)}, u32[]{:S(2)}) %collective-permute-start.31) | collective-permute-done | bytes 9248 | tf_op jit(solution)/shard_map/ppermute | solution.py:348
  129.0 4.4 %collective-permute-done.28.refs_11_ = bf16[256,576]{1,0:T(8,128)(2,1)} collective-permute-done((bf16[256,576]{1,0:T(8,128)(2,1)}, bf16[256,576]{1,0:T(8,128)(2,1)}, u32[]{:S(2)}, u32[]{:S(2)}) %collective-permute-start.28) | collective-permute-done | bytes 294944 | tf_op jit(solution)/shard_map/ppermute | solution.py:516
  133.5 1.5 collective-permute-start.34
  136.0 6.1 %project.1 = (f32[128,2304]{1,0:T(8,128)S(1)}, bf16[128,2304]{1,0:T(8,128)(2,1)}) custom-call(s32[4]{0:T(128)S(1)} %pad_add_fusion.scalars, bf16[288,1152]{1,0:T(8,128)(2,1)S(1)} %pad_maximum_fusion.refs_0_, bf16[288,1152]{1,0:T(8,128)(2,1)} %collective-permute-done.18.refs_1_, bf16[288,1152]{1,0:T(8,128)(2,1)S(1)} %collective-permute-done.16.refs_2_, ...), custom_call_target="tpu_custom_call" | custom-call | flops 1358954496 | bytes 8388608 | tf_op jit(solution)/shard_map/project/pallas_call | solution.py:517
  143.1 1.6 collective-permute-start.32
  144.8 1.5 collective-permute-start.35
  146.3 2.4 %collective-permute-done.35 = bf16[8,2304]{1,0:T(8,128)(2,1)S(1)} collective-permute-done((bf16[8,2304]{1,0:T(8,128)(2,1)S(1)}, bf16[8,2304]{1,0:T(8,128)(2,1)S(1)}, u32[]{:S(2)}, u32[]{:S(2)}) %collective-permute-start.35) | collective-permute-done | bytes 36896 | tf_op jit(solution)/shard_map/ppermute | solution.py:357
  148.8 8.4 %head.1 = (f32[8,3840]{1,0:T(8,128)S(1)}, f32[8,2]{1,0:T(8,128)S(1)}) custom-call(bf16[8,2304]{1,0:T(8,128)(2,1)S(1)} %add.114.table_ref, bf16[2304,3840]{1,0:T(8,128)(2,1)} %refs_2_.1, bf16[2304,3840]{1,0:T(8,128)(2,1)} %refs_2_.1, bf16[2304,3840]{1,0:T(8,128)(2,1)} %refs_2_.1), custom_call_target="tpu_custom_call" | custom-call | tf_op jit(solution)/shard_map/head/pallas_call | solution.py:550
  157.8 1.3 collective-permute-start.38
  159.1 1.5 collective-permute-start.39
  160.9 1.5 collective-permute-start.41
  162.4 1.1 collective-permute-start.42
  163.6 1.8 collective-permute-done.41
  166.6 4.1 %collective-permute-done.32 = bf16[128,2304]{1,0:T(8,128)(2,1)S(1)} collective-permute-done((bf16[128,2304]{1,0:T(8,128)(2,1)}, bf16[128,2304]{1,0:T(8,128)(2,1)S(1)}, u32[]{:S(2)}, u32[]{:S(2)}) %collective-permute-start.32) | collective-permute-done | bytes 589856 | tf_op jit(solution)/shard_map/ppermute | solution.py:535
  170.7 3.0 %collective-permute-start.44 = (f32[8,2]{0,1:T(2,128)S(1)}, f32[8,2]{0,1:T(2,128)S(1)}, u32[]{:S(2)}, u32[]{:S(2)}) collective-permute-start(f32[8,2]{0,1:T(2,128)S(1)} %pad_maximum_fusion.7), channel_id=1, source_target_pairs={{0,2},{1,3},{2,0},{3,1},{4,6},{5,7},{6,4},{7,5},{8,10},{9,11},{10,... | collective-permute-start | bytes 200 | tf_op jit(solution)/shard_map/ppermute | solution.py:357
  173.7 1.4 collective-permute-start.45
  176.0 3.0 %collective-permute-done.45 = f32[8,2]{0,1:T(2,128)S(1)} collective-permute-done((f32[8,2]{0,1:T(2,128)S(1)}, f32[8,2]{0,1:T(2,128)S(1)}, u32[]{:S(2)}, u32[]{:S(2)}) %collective-permute-start.45) | collective-permute-done | bytes 96 | tf_op jit(solution)/shard_map/ppermute | solution.py:357
  (143 shorter events, 24.2 us)
Async XLA Ops:
  2.8 47.4 %copy-start.3 = (bf16[288,1728]{1,0:T(8,128)(2,1)}, bf16[288,1728]{1,0:T(8,128)(2,1)S(1)}, u32[]{:S(2)}) copy-start(bf16[288,1728]{1,0:T(8,128)(2,1)S(1)} %concatenate.30.refs_7_) | copy-start | bytes 2985988
  2.8 29.2 %collective-permute-start.7 = (bf16[288,1728]{1,0:T(8,128)(2,1)S(1)}, bf16[288,1728]{1,0:T(8,128)(2,1)}, u32[]{:S(2)}, u32[]{:S(2)}) collective-permute-start(bf16[288,1728]{1,0:T(8,128)(2,1)S(1)} %concatenate.30.refs_7_), channel_id=1, source_target_pairs={{0,8},{4,12},{8,0},{12,4},{16,24},{20,28},{24,16},{28,20},{1,9},{5... | collective-permute-start | bytes 2985992 | tf_op jit(solution)/shard_map/ppermute | solution.py:57
  5.8 26.2 %collective-permute-start.8 = (bf16[288,1728]{1,0:T(8,128)(2,1)S(1)}, bf16[288,1728]{1,0:T(8,128)(2,1)}, u32[]{:S(2)}, u32[]{:S(2)}) collective-permute-start(bf16[288,1728]{1,0:T(8,128)(2,1)S(1)} %concatenate.30.refs_7_), channel_id=1, source_target_pairs={{0,16},{4,20},{8,24},{12,28},{16,0},{20,4},{24,8},{28,12},{1,17},{... | collective-permute-start | bytes 2985992 | tf_op jit(solution)/shard_map/ppermute | solution.py:57
  7.3 17.2 %collective-permute-start = (bf16[128,2304]{1,0:T(8,128)(2,1)S(1)}, bf16[128,2304]{1,0:T(8,128)(2,1)S(1)}, u32[]{:S(2)}, u32[]{:S(2)}) collective-permute-start(bf16[128,2304]{1,0:T(8,128)(2,1)S(1)} %fusion.2.refs_0_), channel_id=1, source_target_pairs={{0,1},{1,2},{2,3},{4,5},{5,6},{6,7},{8,9},{9,10},{10,11},{12,13},{... | collective-permute-start | bytes 1769480 | tf_op jit(solution)/shard_map/ppermute | solution.py:95
  10.8 18.3 %collective-permute-start.1 = (bf16[128,2304]{1,0:T(8,128)(2,1)S(1)}, bf16[128,2304]{1,0:T(8,128)(2,1)}, u32[]{:S(2)}, u32[]{:S(2)}) collective-permute-start(bf16[128,2304]{1,0:T(8,128)(2,1)S(1)} %fusion.2.refs_0_), channel_id=1, source_target_pairs={{1,0},{2,1},{3,2},{5,4},{6,5},{7,6},{9,8},{10,9},{11,10},{13,12},{... | collective-permute-start | bytes 1769480 | tf_op jit(solution)/shard_map/ppermute | solution.py:96
  12.1 37.5 %collective-permute-start.4 = (bf16[288,576]{1,0:T(8,128)(2,1)}, bf16[288,576]{1,0:T(8,128)(2,1)}, u32[]{:S(2)}, u32[]{:S(2)}) collective-permute-start(bf16[288,576]{1,0:T(8,128)(2,1)} %bitcast.35), channel_id=1, source_target_pairs={{0,1},{1,0},{2,3},{3,2},{4,5},{5,4},{6,7},{7,6},{8,9},{9,8},{10,11... | collective-permute-start | bytes 995336 | tf_op jit(solution)/shard_map/ppermute | solution.py:430
  29.1 13.2 %collective-permute-start.2 = (bf16[128,2304]{1,0:T(8,128)(2,1)S(1)}, bf16[128,2304]{1,0:T(8,128)(2,1)}, u32[]{:S(2)}, u32[]{:S(2)}) collective-permute-start(bf16[128,2304]{1,0:T(8,128)(2,1)S(1)} %collective-permute-done.refs_1_), channel_id=1, source_target_pairs={{1,2},{2,3},{5,6},{6,7},{9,10},{10,11},{13,14},{14,15},{17,18},{18... | collective-permute-start | bytes 1769480 | tf_op jit(solution)/shard_map/ppermute | solution.py:95
  30.6 17.0 %collective-permute-start.3 = (bf16[128,2304]{1,0:T(8,128)(2,1)}, bf16[128,2304]{1,0:T(8,128)(2,1)}, u32[]{:S(2)}, u32[]{:S(2)}) collective-permute-start(bf16[128,2304]{1,0:T(8,128)(2,1)} %collective-permute-done.1.refs_4_), channel_id=1, source_target_pairs={{1,0},{2,1},{5,4},{6,5},{9,8},{10,9},{13,12},{14,13},{17,16},{18,1... | collective-permute-start | bytes 1769480 | tf_op jit(solution)/shard_map/ppermute | solution.py:96
  35.7 13.9 %collective-permute-start.12 = (bf16[144,1728]{1,0:T(8,128)(2,1)}, bf16[144,1728]{1,0:T(8,128)(2,1)}, u32[]{:S(2)}, u32[]{:S(2)}) collective-permute-start(bf16[144,1728]{1,0:T(8,128)(2,1)} %slice.108), channel_id=1, source_target_pairs={{0,8},{4,12},{8,0},{12,4},{16,24},{20,28},{24,16},{28,20},{1,9},{5... | collective-permute-start | bytes 1493000 | tf_op jit(solution)/shard_map/ppermute | solution.py:57
  36.3 13.9 %collective-permute-start.14 = (bf16[144,1728]{1,0:T(8,128)(2,1)}, bf16[144,1728]{1,0:T(8,128)(2,1)}, u32[]{:S(2)}, u32[]{:S(2)}) collective-permute-start(bf16[144,1728]{1,0:T(8,128)(2,1)} %slice.107), channel_id=1, source_target_pairs={{0,16},{4,20},{8,24},{12,28},{16,0},{20,4},{24,8},{28,12},{1,17},{... | collective-permute-start | bytes 1493000 | tf_op jit(solution)/shard_map/ppermute | solution.py:57
  47.6 2.7 %collective-permute-start.5 = (bf16[128,2304]{1,0:T(8,128)(2,1)}, bf16[128,2304]{1,0:T(8,128)(2,1)S(1)}, u32[]{:S(2)}, u32[]{:S(2)}) collective-permute-start(bf16[128,2304]{1,0:T(8,128)(2,1)} %collective-permute-done.2.refs_2_), channel_id=1, source_target_pairs={{2,3},{6,7},{10,11},{14,15},{18,19},{22,23},{26,27},{30,31}} | collective-permute-start | bytes 1769480 | tf_op jit(solution)/shard_map/ppermute | solution.py:95
  48.3 13.6 %collective-permute-start.6 = (bf16[128,2304]{1,0:T(8,128)(2,1)}, bf16[128,2304]{1,0:T(8,128)(2,1)S(1)}, u32[]{:S(2)}, u32[]{:S(2)}) collective-permute-start(bf16[128,2304]{1,0:T(8,128)(2,1)} %collective-permute-done.3.refs_5_), channel_id=1, source_target_pairs={{1,0},{5,4},{9,8},{13,12},{17,16},{21,20},{25,24},{29,28}} | collective-permute-start | bytes 1769480 | tf_op jit(solution)/shard_map/ppermute | solution.py:96
  49.6 17.2 %collective-permute-start.10 = (bf16[288,1728]{1,0:T(8,128)(2,1)}, bf16[288,1728]{1,0:T(8,128)(2,1)}, u32[]{:S(2)}, u32[]{:S(2)}) collective-permute-start(bf16[288,1728]{1,0:T(8,128)(2,1)} %collective-permute-done.7.refs_9_), channel_id=1, source_target_pairs={{0,4},{4,0},{8,12},{12,8},{16,20},{20,16},{24,28},{28,24},{1,5},{5... | collective-permute-start | bytes 2985992 | tf_op jit(solution)/shard_map/ppermute | solution.py:57
  49.7 17.2 %collective-permute-start.11 = (bf16[288,1728]{1,0:T(8,128)(2,1)}, bf16[288,1728]{1,0:T(8,128)(2,1)}, u32[]{:S(2)}, u32[]{:S(2)}) collective-permute-start(bf16[288,1728]{1,0:T(8,128)(2,1)} %collective-permute-done.8.refs_11_), channel_id=1, source_target_pairs={{0,4},{4,0},{8,12},{12,8},{16,20},{20,16},{24,28},{28,24},{1,5},{5... | collective-permute-start | bytes 2985992 | tf_op jit(solution)/shard_map/ppermute | solution.py:57
  50.2 16.7 %collective-permute-start.9 = (bf16[288,1728]{1,0:T(8,128)(2,1)S(1)}, bf16[288,1728]{1,0:T(8,128)(2,1)}, u32[]{:S(2)}, u32[]{:S(2)}) collective-permute-start(bf16[288,1728]{1,0:T(8,128)(2,1)S(1)} %concatenate.30.refs_7_), channel_id=1, source_target_pairs={{0,4},{4,0},{8,12},{12,8},{16,20},{20,16},{24,28},{28,24},{1,5},{5... | collective-permute-start | bytes 2985992 | tf_op jit(solution)/shard_map/ppermute | solution.py:57
  51.1 15.7 %collective-permute-start.13 = (bf16[144,1728]{1,0:T(8,128)(2,1)}, bf16[144,1728]{1,0:T(8,128)(2,1)}, u32[]{:S(2)}, u32[]{:S(2)}) collective-permute-start(bf16[144,1728]{1,0:T(8,128)(2,1)} %collective-permute-done.12.refs_13_), channel_id=1, source_target_pairs={{0,4},{4,0},{8,12},{12,8},{16,20},{20,16},{24,28},{28,24},{1,5},{5... | collective-permute-start | bytes 1493000 | tf_op jit(solution)/shard_map/ppermute | solution.py:57
  62.7 4.1 %collective-permute-start.15 = (bf16[144,1728]{1,0:T(8,128)(2,1)}, bf16[144,1728]{1,0:T(8,128)(2,1)}, u32[]{:S(2)}, u32[]{:S(2)}) collective-permute-start(bf16[144,1728]{1,0:T(8,128)(2,1)} %collective-permute-done.14.refs_15_), channel_id=1, source_target_pairs={{0,4},{4,0},{8,12},{12,8},{16,20},{20,16},{24,28},{28,24},{1,5},{5... | collective-permute-start | bytes 1493000 | tf_op jit(solution)/shard_map/ppermute | solution.py:57
  66.8 17.4 %collective-permute-start.16 = (bf16[288,1152]{1,0:T(8,128)(2,1)S(1)}, bf16[288,1152]{1,0:T(8,128)(2,1)S(1)}, u32[]{:S(2)}, u32[]{:S(2)}) collective-permute-start(bf16[288,1152]{1,0:T(8,128)(2,1)S(1)} %pad_maximum_fusion.refs_0_), channel_id=1, source_target_pairs={{0,8},{4,12},{8,0},{12,4},{16,24},{20,28},{24,16},{28,20},{1,9},{5... | collective-permute-start | bytes 1990664 | tf_op jit(solution)/shard_map/ppermute | solution.py:57
  67.4 17.0 %collective-permute-start.17 = (bf16[288,1152]{1,0:T(8,128)(2,1)S(1)}, bf16[288,1152]{1,0:T(8,128)(2,1)S(1)}, u32[]{:S(2)}, u32[]{:S(2)}) collective-permute-start(bf16[288,1152]{1,0:T(8,128)(2,1)S(1)} %pad_maximum_fusion.refs_0_), channel_id=1, source_target_pairs={{0,16},{4,20},{8,24},{12,28},{16,0},{20,4},{24,8},{28,12},{1,17},{... | collective-permute-start | bytes 1990664 | tf_op jit(solution)/shard_map/ppermute | solution.py:57
  68.1 18.1 %collective-permute-start.25 = (bf16[256,576]{1,0:T(8,128)(2,1)S(1)}, bf16[256,576]{1,0:T(8,128)(2,1)S(1)}, u32[]{:S(2)}, u32[]{:S(2)}) collective-permute-start(bf16[256,576]{1,0:T(8,128)(2,1)S(1)} %pad_maximum_fusion.2), channel_id=1, source_target_pairs={{0,1},{1,0},{2,3},{3,2},{4,5},{5,4},{6,7},{7,6},{8,9},{9,8},{10,11... | collective-permute-start | bytes 884744 | tf_op jit(solution)/shard_map/ppermute | solution.py:432
  68.1 26.3 %collective-permute-start.26 = (bf16[256,576]{1,0:T(8,128)(2,1)S(1)}, bf16[256,576]{1,0:T(8,128)(2,1)S(1)}, u32[]{:S(2)}, u32[]{:S(2)}) collective-permute-start(bf16[256,576]{1,0:T(8,128)(2,1)S(1)} %pad_maximum_fusion.3), channel_id=1, source_target_pairs={{0,2},{1,3},{2,0},{3,1},{4,6},{5,7},{6,4},{7,5},{8,10},{9,11},{10,... | collective-permute-start | bytes 884744 | tf_op jit(solution)/shard_map/ppermute | solution.py:432
  71.8 23.4 %collective-permute-start.27 = (bf16[256,576]{1,0:T(8,128)(2,1)S(1)}, bf16[256,576]{1,0:T(8,128)(2,1)S(1)}, u32[]{:S(2)}, u32[]{:S(2)}) collective-permute-start(bf16[256,576]{1,0:T(8,128)(2,1)S(1)} %pad_maximum_fusion.4), channel_id=1, source_target_pairs={{0,3},{1,2},{2,1},{3,0},{4,7},{5,6},{6,5},{7,4},{8,11},{9,10},{10,... | collective-permute-start | bytes 884744 | tf_op jit(solution)/shard_map/ppermute | solution.py:432
  84.5 28.5 %collective-permute-start.19 = (bf16[288,1152]{1,0:T(8,128)(2,1)S(1)}, bf16[288,1152]{1,0:T(8,128)(2,1)S(1)}, u32[]{:S(2)}, u32[]{:S(2)}) collective-permute-start(bf16[288,1152]{1,0:T(8,128)(2,1)S(1)} %collective-permute-done.16.refs_2_), channel_id=1, source_target_pairs={{0,4},{4,0},{8,12},{12,8},{16,20},{20,16},{24,28},{28,24},{1,5},{5... | collective-permute-start | bytes 1990664 | tf_op jit(solution)/shard_map/ppermute | solution.py:57
  84.6 11.8 %collective-permute-start.21 = (bf16[144,1152]{1,0:T(8,128)(2,1)S(1)}, bf16[144,1152]{1,0:T(8,128)(2,1)}, u32[]{:S(2)}, u32[]{:S(2)}) collective-permute-start(bf16[144,1152]{1,0:T(8,128)(2,1)S(1)} %slice.110), channel_id=1, source_target_pairs={{0,8},{4,12},{8,0},{12,4},{16,24},{20,28},{24,16},{28,20},{1,9},{5... | collective-permute-start | bytes 995336 | tf_op jit(solution)/shard_map/ppermute | solution.py:57
  86.9 10.0 %collective-permute-start.23 = (bf16[144,1152]{1,0:T(8,128)(2,1)S(1)}, bf16[144,1152]{1,0:T(8,128)(2,1)}, u32[]{:S(2)}, u32[]{:S(2)}) collective-permute-start(bf16[144,1152]{1,0:T(8,128)(2,1)S(1)} %slice.109), channel_id=1, source_target_pairs={{0,16},{4,20},{8,24},{12,28},{16,0},{20,4},{24,8},{28,12},{1,17},{... | collective-permute-start | bytes 995336 | tf_op jit(solution)/shard_map/ppermute | solution.py:57
  95.2 17.8 %collective-permute-start.18 = (bf16[288,1152]{1,0:T(8,128)(2,1)S(1)}, bf16[288,1152]{1,0:T(8,128)(2,1)}, u32[]{:S(2)}, u32[]{:S(2)}) collective-permute-start(bf16[288,1152]{1,0:T(8,128)(2,1)S(1)} %pad_maximum_fusion.refs_0_), channel_id=1, source_target_pairs={{0,4},{4,0},{8,12},{12,8},{16,20},{20,16},{24,28},{28,24},{1,5},{5... | collective-permute-start | bytes 1990664 | tf_op jit(solution)/shard_map/ppermute | solution.py:57
  95.9 17.1 %collective-permute-start.20 = (bf16[288,1152]{1,0:T(8,128)(2,1)S(1)}, bf16[288,1152]{1,0:T(8,128)(2,1)}, u32[]{:S(2)}, u32[]{:S(2)}) collective-permute-start(bf16[288,1152]{1,0:T(8,128)(2,1)S(1)} %collective-permute-done.17.refs_4_), channel_id=1, source_target_pairs={{0,4},{4,0},{8,12},{12,8},{16,20},{20,16},{24,28},{28,24},{1,5},{5... | collective-permute-start | bytes 1990664 | tf_op jit(solution)/shard_map/ppermute | solution.py:57
  96.4 16.6 %collective-permute-start.22 = (bf16[144,1152]{1,0:T(8,128)(2,1)}, bf16[144,1152]{1,0:T(8,128)(2,1)}, u32[]{:S(2)}, u32[]{:S(2)}) collective-permute-start(bf16[144,1152]{1,0:T(8,128)(2,1)} %collective-permute-done.21.refs_6_), channel_id=1, source_target_pairs={{0,4},{4,0},{8,12},{12,8},{16,20},{20,16},{24,28},{28,24},{1,5},{5... | collective-permute-start | bytes 995336 | tf_op jit(solution)/shard_map/ppermute | solution.py:57
  96.9 16.1 %collective-permute-start.24 = (bf16[144,1152]{1,0:T(8,128)(2,1)}, bf16[144,1152]{1,0:T(8,128)(2,1)}, u32[]{:S(2)}, u32[]{:S(2)}) collective-permute-start(bf16[144,1152]{1,0:T(8,128)(2,1)} %collective-permute-done.23.refs_8_), channel_id=1, source_target_pairs={{0,4},{4,0},{8,12},{12,8},{16,20},{20,16},{24,28},{28,24},{1,5},{5... | collective-permute-start | bytes 995336 | tf_op jit(solution)/shard_map/ppermute | solution.py:57
  116.0 8.4 %collective-permute-start.29 = (f32[1,2304]{1,0:T(1,128)S(1)}, f32[1,2304]{1,0:T(1,128)S(1)}, u32[]{:S(2)}, u32[]{:S(2)}) collective-permute-start(f32[1,2304]{1,0:T(1,128)S(1)} %fusion.6), channel_id=1, source_target_pairs={{0,1},{1,0},{2,3},{3,2},{4,5},{5,4},{6,7},{7,6},{8,9},{9,8},{10,11... | collective-permute-start | bytes 27656 | tf_op jit(solution)/shard_map/ppermute | solution.py:348
  121.0 4.6 %collective-permute-start.30 = (f32[1,2304]{1,0:T(1,128)S(1)}, f32[1,2304]{1,0:T(1,128)S(1)}, u32[]{:S(2)}, u32[]{:S(2)}) collective-permute-start(f32[1,2304]{1,0:T(1,128)S(1)} %fusion.6), channel_id=1, source_target_pairs={{0,2},{1,3},{2,0},{3,1},{4,6},{5,7},{6,4},{7,5},{8,10},{9,11},{10,... | collective-permute-start | bytes 27656 | tf_op jit(solution)/shard_map/ppermute | solution.py:348
  122.0 5.6 %collective-permute-start.31 = (f32[1,2304]{1,0:T(1,128)S(1)}, f32[1,2304]{1,0:T(1,128)S(1)}, u32[]{:S(2)}, u32[]{:S(2)}) collective-permute-start(f32[1,2304]{1,0:T(1,128)S(1)} %fusion.6), channel_id=1, source_target_pairs={{0,3},{1,2},{2,1},{3,0},{4,7},{5,6},{6,5},{7,4},{8,11},{9,10},{10,... | collective-permute-start | bytes 27656 | tf_op jit(solution)/shard_map/ppermute | solution.py:348
  123.4 10.0 %collective-permute-start.28 = (bf16[256,576]{1,0:T(8,128)(2,1)}, bf16[256,576]{1,0:T(8,128)(2,1)}, u32[]{:S(2)}, u32[]{:S(2)}) collective-permute-start(bf16[256,576]{1,0:T(8,128)(2,1)} %get-tuple-element.61), channel_id=1, source_target_pairs={{0,1},{1,0},{2,3},{3,2},{4,5},{5,4},{6,7},{7,6},{8,9},{9,8},{10,11... | collective-permute-start | bytes 884744 | tf_op jit(solution)/shard_map/ppermute | solution.py:516
  129.0 4.4 %collective-permute-start.33 = (bf16[8,2304]{1,0:T(8,128)(2,1)S(1)}, bf16[8,2304]{1,0:T(8,128)(2,1)S(1)}, u32[]{:S(2)}, u32[]{:S(2)}) collective-permute-start(bf16[8,2304]{1,0:T(8,128)(2,1)S(1)} %broadcast_select_fusion), channel_id=1, source_target_pairs={{0,4},{4,0},{8,12},{12,8},{16,20},{20,16},{24,28},{28,24},{1,5},{5... | collective-permute-start | bytes 110600 | tf_op jit(solution)/shard_map/ppermute | solution.py:357
  133.5 11.2 %collective-permute-start.34 = (bf16[8,2304]{1,0:T(8,128)(2,1)S(1)}, bf16[8,2304]{1,0:T(8,128)(2,1)S(1)}, u32[]{:S(2)}, u32[]{:S(2)}) collective-permute-start(bf16[8,2304]{1,0:T(8,128)(2,1)S(1)} %fusion.7), channel_id=1, source_target_pairs={{0,8},{4,12},{8,0},{12,4},{16,24},{20,28},{24,16},{28,20},{1,9},{5... | collective-permute-start | bytes 110600 | tf_op jit(solution)/shard_map/ppermute | solution.py:357
  143.1 27.6 %collective-permute-start.32 = (bf16[128,2304]{1,0:T(8,128)(2,1)}, bf16[128,2304]{1,0:T(8,128)(2,1)S(1)}, u32[]{:S(2)}, u32[]{:S(2)}) collective-permute-start(bf16[128,2304]{1,0:T(8,128)(2,1)} %get-tuple-element.65), channel_id=1, source_target_pairs={{0,2},{1,3},{2,0},{3,1},{4,6},{5,7},{6,4},{7,5},{8,10},{9,11},{10,... | collective-permute-start | bytes 1769480 | tf_op jit(solution)/shard_map/ppermute | solution.py:535
  144.8 4.0 %collective-permute-start.35 = (bf16[8,2304]{1,0:T(8,128)(2,1)S(1)}, bf16[8,2304]{1,0:T(8,128)(2,1)S(1)}, u32[]{:S(2)}, u32[]{:S(2)}) collective-permute-start(bf16[8,2304]{1,0:T(8,128)(2,1)S(1)} %fusion.8), channel_id=1, source_target_pairs={{0,16},{4,20},{8,24},{12,28},{16,0},{20,4},{24,8},{28,12},{1,17},{... | collective-permute-start | bytes 110600 | tf_op jit(solution)/shard_map/ppermute | solution.py:357
  148.8 26.3 %copy-start.2 = (f32[128,2304]{1,0:T(8,128)S(1)}, f32[128,2304]{1,0:T(8,128)}, u32[]{:S(2)}) copy-start(f32[128,2304]{1,0:T(8,128)} %copy-done.1) | copy-start | bytes 3538948
  157.2 3.4 %collective-permute-start.36 = (f32[8,2]{1,0:T(8,128)S(1)}, f32[8,2]{1,0:T(8,128)S(1)}, u32[]{:S(2)}, u32[]{:S(2)}) collective-permute-start(f32[8,2]{1,0:T(8,128)S(1)} %get-tuple-element.68), channel_id=1, source_target_pairs={{0,4},{4,0},{8,12},{12,8},{16,20},{20,16},{24,28},{28,24},{1,5},{5... | collective-permute-start | bytes 200 | tf_op jit(solution)/shard_map/ppermute | solution.py:357
  157.2 3.7 %collective-permute-start.37 = (f32[8,2]{1,0:T(8,128)S(1)}, f32[8,2]{1,0:T(8,128)S(1)}, u32[]{:S(2)}, u32[]{:S(2)}) collective-permute-start(f32[8,2]{1,0:T(8,128)S(1)} %get-tuple-element.68), channel_id=1, source_target_pairs={{0,8},{4,12},{8,0},{12,4},{16,24},{20,28},{24,16},{28,20},{1,9},{5... | collective-permute-start | bytes 200 | tf_op jit(solution)/shard_map/ppermute | solution.py:357
  157.8 4.6 %collective-permute-start.38 = (f32[8,2]{1,0:T(8,128)S(1)}, f32[8,2]{1,0:T(8,128)S(1)}, u32[]{:S(2)}, u32[]{:S(2)}) collective-permute-start(f32[8,2]{1,0:T(8,128)S(1)} %get-tuple-element.68), channel_id=1, source_target_pairs={{0,12},{4,8},{8,4},{12,0},{16,28},{20,24},{24,20},{28,16},{1,13},{... | collective-permute-start | bytes 200 | tf_op jit(solution)/shard_map/ppermute | solution.py:357
  159.1 4.4 %collective-permute-start.39 = (f32[8,2]{1,0:T(8,128)S(1)}, f32[8,2]{1,0:T(8,128)S(1)}, u32[]{:S(2)}, u32[]{:S(2)}) collective-permute-start(f32[8,2]{1,0:T(8,128)S(1)} %get-tuple-element.68), channel_id=1, source_target_pairs={{0,16},{4,20},{8,24},{12,28},{16,0},{20,4},{24,8},{28,12},{1,17},{... | collective-permute-start | bytes 200 | tf_op jit(solution)/shard_map/ppermute | solution.py:357
  160.6 3.0 %collective-permute-start.40 = (f32[8,2]{1,0:T(8,128)S(1)}, f32[8,2]{1,0:T(8,128)S(1)}, u32[]{:S(2)}, u32[]{:S(2)}) collective-permute-start(f32[8,2]{1,0:T(8,128)S(1)} %get-tuple-element.68), channel_id=1, source_target_pairs={{0,20},{4,16},{8,28},{12,24},{16,4},{20,0},{24,12},{28,8},{1,21},{... | collective-permute-start | bytes 200 | tf_op jit(solution)/shard_map/ppermute | solution.py:357
  160.9 4.5 %collective-permute-start.41 = (f32[8,2]{1,0:T(8,128)S(1)}, f32[8,2]{1,0:T(8,128)S(1)}, u32[]{:S(2)}, u32[]{:S(2)}) collective-permute-start(f32[8,2]{1,0:T(8,128)S(1)} %get-tuple-element.68), channel_id=1, source_target_pairs={{0,24},{4,28},{8,16},{12,20},{16,8},{20,12},{24,0},{28,4},{1,25},{... | collective-permute-start | bytes 200 | tf_op jit(solution)/shard_map/ppermute | solution.py:357
  162.4 3.9 %collective-permute-start.42 = (f32[8,2]{1,0:T(8,128)S(1)}, f32[8,2]{1,0:T(8,128)S(1)}, u32[]{:S(2)}, u32[]{:S(2)}) collective-permute-start(f32[8,2]{1,0:T(8,128)S(1)} %get-tuple-element.68), channel_id=1, source_target_pairs={{0,28},{4,24},{8,20},{12,16},{16,12},{20,8},{24,4},{28,0},{1,29},{... | collective-permute-start | bytes 200 | tf_op jit(solution)/shard_map/ppermute | solution.py:357
  170.7 5.3 %collective-permute-start.43 = (f32[8,2]{0,1:T(2,128)S(1)}, f32[8,2]{0,1:T(2,128)S(1)}, u32[]{:S(2)}, u32[]{:S(2)}) collective-permute-start(f32[8,2]{0,1:T(2,128)S(1)} %pad_maximum_fusion.7), channel_id=1, source_target_pairs={{0,1},{1,0},{2,3},{3,2},{4,5},{5,4},{6,7},{7,6},{8,9},{9,8},{10,11... | collective-permute-start | bytes 200 | tf_op jit(solution)/shard_map/ppermute | solution.py:357
  170.7 5.3 %collective-permute-start.44 = (f32[8,2]{0,1:T(2,128)S(1)}, f32[8,2]{0,1:T(2,128)S(1)}, u32[]{:S(2)}, u32[]{:S(2)}) collective-permute-start(f32[8,2]{0,1:T(2,128)S(1)} %pad_maximum_fusion.7), channel_id=1, source_target_pairs={{0,2},{1,3},{2,0},{3,1},{4,6},{5,7},{6,4},{7,5},{8,10},{9,11},{10,... | collective-permute-start | bytes 200 | tf_op jit(solution)/shard_map/ppermute | solution.py:357
  173.7 5.4 %collective-permute-start.45 = (f32[8,2]{0,1:T(2,128)S(1)}, f32[8,2]{0,1:T(2,128)S(1)}, u32[]{:S(2)}, u32[]{:S(2)}) collective-permute-start(f32[8,2]{0,1:T(2,128)S(1)} %pad_maximum_fusion.7), channel_id=1, source_target_pairs={{0,3},{1,2},{2,1},{3,0},{4,7},{5,6},{6,5},{7,4},{8,11},{9,10},{10,... | collective-permute-start | bytes 200 | tf_op jit(solution)/shard_map/ppermute | solution.py:357
  (28 other events, 102.3 us)

commit v4 on v3

--- a/solution.py
+++ b/solution.py
@@ -12,6 +12,7 @@
 HBM = pl.BlockSpec(memory_space=pltpu.HBM)
 SMEM = pl.BlockSpec(memory_space=pltpu.SMEM)
 VMEM = pl.BlockSpec(memory_space=pltpu.VMEM)
+FREE = pl.CostEstimate(flops=0, bytes_accessed=0, transcendentals=0)
 
 
 def rms_scale(values, gain_vec):
@@ -86,6 +87,10 @@
         ):
             pieces += [(here, mask, at, count), (there, mask ^ 1, at, count)]
         return pieces
+
+
+def after_all(values, *earlier):
+    return list(lax.optimization_barrier((*values, *earlier)))[: len(values)]
 
 
 def gather_line(block, size, *ready):
@@ -287,22 +292,48 @@
 def last_row_kernel(layout, block_rows, scalars, *refs):
     pieces = len(layout)
     weights = refs[:pieces]
-    last_ref, out_ref, w_scr, sems = refs[pieces:]
+    last_ref, in_ref, out_ref, w_scr, sems = refs[pieces:]
     columns = w_scr.shape[1]
     weights = [ref.at[:, 0:columns] for ref in weights]
     copies = weight_copies(weights, layout, w_scr, sems, scalars[1], block_rows)
     for copy in copies:
         copy.start()
+    rows = in_ref.shape[0]
+    local = scalars[3] - 1 - scalars[0] * rows
+    group = jnp.clip(lax.div(local, 16), 0, rows // 16 - 1)
+    rows16 = in_ref[pl.ds(pl.multiple_of(group * 16, 16), 16), :].astype(jnp.float32)
+    at16 = lax.broadcasted_iota(jnp.int32, rows16.shape, 0) == local - group * 16
+    residual = jnp.sum(jnp.where(at16, rows16, 0.0), axis=0, keepdims=True)
     for copy in copies:
         copy.wait()
     width = last_ref.shape[1]
     for tile in range(0, out_ref.shape[1], 256):
-        out_ref[:, tile : tile + 256] = lax.dot_general(
+        share = lax.dot_general(
             last_ref[...],
             w_scr[tile : tile + 256, 0:width],
             NT,
             preferred_element_type=jnp.float32,
         )
+        out_ref[:, tile : tile + 256] = share[0:1] + residual[:, tile : tile + 256]
+
+
+def final_row_kernel(scalars, *refs):
+    shares, (gain_ref, table_ref) = refs[:-2], refs[-2:]
+    row = add_all(*[ref[...] for ref in shares]).astype(jnp.bfloat16).astype(jnp.float32)
+    row = rms_scale(row, gain_ref[...]).astype(jnp.bfloat16).astype(jnp.float32)
+    at = lax.broadcasted_iota(jnp.int32, table_ref.shape, 0) == scalars[1]
+    table_ref[...] = jnp.where(at, row, 0.0).astype(jnp.bfloat16)
+
+
+def merge_kernel(*refs):
+    stats, out_ref = refs[:-1], refs[-1]
+    out_ref[...] = merge_stats(*[ref[...] for ref in stats])
+
+
+def logprobs_kernel(logits_ref, *refs):
+    stats, out_ref = refs[:-1], refs[-1]
+    merged = merge_stats(*[ref[...] for ref in stats])
+    out_ref[...] = logits_ref[...] - merged[:, :1] - jnp.log(merged[:, 1:])
 
 
 def project_kernel(layout, block_rows, scalars, *refs):
@@ -342,13 +373,6 @@
         stats_ref[:, 1:2] = jnp.sum(jnp.exp(logits - top), axis=1, keepdims=True)
 
 
-def sum_line(value, size):
-    total = value
-    for mask in range(1, size):
-        total = total + lax.ppermute(value, "row", xor_pairs(size, mask))
-    return total
-
-
 def combine_all(value, axis, size, combine, width=4):
     bit = 1
     while bit < size:
@@ -369,6 +393,15 @@
     top = functools.reduce(jnp.maximum, [one[:, :1] for one in stats])
     total = add_all(*[one[:, 1:] * jnp.exp(one[:, :1] - top) for one in stats])
     return jnp.concatenate([top, total], axis=1)
+
+
+def merge(*stats):
+    return pl.pallas_call(
+        merge_kernel,
+        out_shape=jax.ShapeDtypeStruct(stats[0].shape, jnp.float32),
+        cost_estimate=FREE,
+        name="merge",
+    )(*stats)
 
 
 def on_device(
@@ -420,27 +453,29 @@
     weights = Rows(joined, n_req)
     got = weights.neighbours()
     cosine, sine = rotary_tables(length + jnp.arange(span, dtype=jnp.int32))
-    x_ups, x_downs, scalars, cosine, sine = gather_line(normed, n_row, scalars, cosine, sine)
+    out_next = lax.ppermute(out_own, "row", xor_pairs(n_row, 1))
+    out_both = jnp.concatenate([out_own, out_next], axis=1)
+    cached = [cache_for(jnp.bitwise_xor(me_row, mask)) for mask in range(n_row)]
+    x_ups, x_downs, scalars, cosine, sine, out_both, own_block, *cached = gather_line(
+        normed, n_row, scalars, cosine, sine, out_both, *cached
+    )
     got, own = together(got, [joined])
     diagonal = weights.diagonal(got)
     others = weights.cores([*own, *got, *diagonal])
     pieces = weights.pieces(got, diagonal, others)
     layout = tuple(piece[1:] for piece in pieces)
 
-    out_next = lax.ppermute(out_own, "row", xor_pairs(n_row, 1))
+    across = lax.ppermute(cached[1], "row", xor_pairs(n_row, 2))
+    beside, behind = after_all([cached[0], cached[2]], across, x_ups[-1], x_downs[-1])
     old_blocks = [
-        lax.ppermute(
-            after(cache_for(jnp.bitwise_xor(me_row, mask)), x_ups[-1], x_downs[-1]),
-            "row",
-            xor_pairs(n_row, mask),
-        )
-        for mask in range(1, n_row)
+        lax.ppermute(beside, "row", xor_pairs(n_row, 1)),
+        across,
+        lax.ppermute(behind, "row", xor_pairs(n_row, 3)),
     ]
-    out_rows = Rows(
-        after(jnp.concatenate([out_own, out_next], axis=1), x_ups[-1], x_downs[-1], *others), n_req
-    )
+    out_rows = Rows(after(out_both, *diagonal), n_req)
     out_got = out_rows.neighbours()
-
+    out_got, out_block = together(out_got, [out_rows.block])
+    out_diagonal = out_rows.diagonal(out_got)
     qkv = pl.pallas_call(
         functools.partial(qkv_kernel, n_row, layout, block_rows),
         out_shape=jax.ShapeDtypeStruct((span, 3 * width), jnp.bfloat16),
@@ -452,16 +487,16 @@
             pltpu.SemaphoreType.DMA((n_row,)),
             pltpu.SemaphoreType.DMA((len(pieces),)),
         ],
-        compiler_params=params(24),
+        compiler_params=params(17),
         cost_estimate=pl.CostEstimate(
             flops=6 * span * model * width, bytes_accessed=14 * 2**20, transcendentals=0
         ),
         name="qkv",
     )(scalars, normed, *x_ups, *x_downs, *[piece[0] for piece in pieces], cosine, sine)
 
-    out_block, *out_got = lax.optimization_barrier((out_rows.block, *out_got, qkv))[:-1]
-    out_diagonal = out_rows.diagonal(out_got)
-    out_others = out_rows.cores([out_block, *out_got])
+    out_here, _ = together([*out_block, *out_got, *out_diagonal], [qkv])
+    out_others = out_rows.cores(out_here)
+    out_pieces = out_rows.pieces(out_got, out_diagonal, out_others)
 
     chunk = span // n_row
     keep, send, last_attended = pl.pallas_call(
@@ -479,41 +514,35 @@
             pltpu.VMEM((span, width), jnp.bfloat16),
             pltpu.SemaphoreType.DMA((2, n_row)),
         ],
-        compiler_params=params(24),
+        compiler_params=params(11),
         cost_estimate=pl.CostEstimate(
             flops=6 * span * span * width, bytes_accessed=4 * 2**20, transcendentals=0
         ),
         name="attention",
-    )(scalars, cache_for(me_row), *old_blocks, qkv)
-
-    out_others += out_rows.cores(out_diagonal)
-    out_pieces = out_rows.pieces(out_got, out_diagonal, out_others)
+    )(scalars, own_block, *old_blocks, qkv)
+
     out_layout = tuple(piece[1:] for piece in out_pieces)
     out_weights = [piece[0] for piece in out_pieces]
     own_columns = -(-width // 128) * 128
-    own_part = pl.pallas_call(
+    share = pl.pallas_call(
         functools.partial(last_row_kernel, out_layout, block_rows),
-        out_shape=jax.ShapeDtypeStruct((16, model), jnp.float32),
-        in_specs=[SMEM] + [HBM] * len(out_weights) + [VMEM],
+        out_shape=jax.ShapeDtypeStruct((1, model), jnp.float32),
+        in_specs=[SMEM] + [HBM] * len(out_weights) + [VMEM] * 2,
         out_specs=VMEM,
         scratch_shapes=[
             pltpu.VMEM((model, own_columns), jnp.bfloat16),
             pltpu.SemaphoreType.DMA((len(out_weights),)),
         ],
-        compiler_params=params(8),
-        cost_estimate=pl.CostEstimate(
-            flops=32 * model * width, bytes_accessed=4 * 2**20, transcendentals=0
-        ),
+        compiler_params=params(7),
+        cost_estimate=FREE,
         name="last_row",
-    )(scalars, *out_weights, last_attended)[:1]
-
-    local_index = count - 1 - me_row * rows
-    is_owner = (local_index >= 0) & (local_index < rows)
-    residual = lax.dynamic_slice_in_dim(inputs, jnp.clip(local_index, 0, rows - 1), 1, 0)
-    own_part += jnp.where(is_owner, residual.astype(jnp.float32), 0.0)
-    last_row = sum_line(own_part, n_row)
-
-    got = after(lax.ppermute(send, "row", xor_pairs(n_row, 1)), last_row)
+    )(scalars, *out_weights, last_attended, inputs)
+
+    shares = [share] + [
+        lax.ppermute(share, "row", xor_pairs(n_row, mask)) for mask in range(1, n_row)
+    ]
+
+    got = after(lax.ppermute(send, "row", xor_pairs(n_row, 1)), share)
     own_sum, mate_part = pl.pallas_call(
         functools.partial(project_kernel, out_layout, block_rows),
         out_shape=(
@@ -526,23 +555,27 @@
             pltpu.VMEM((model, 2 * width), jnp.bfloat16),
             pltpu.SemaphoreType.DMA((len(out_weights),)),
         ],
-        compiler_params=params(16),
+        compiler_params=params(11),
         cost_estimate=pl.CostEstimate(
             flops=2 * span * model * width, bytes_accessed=8 * 2**20, transcendentals=0
         ),
         name="project",
     )(scalars, *out_weights, keep, got, inputs)
+    mate_part, *shares = lax.optimization_barrier((mate_part, *shares))
     others = lax.ppermute(mate_part, "row", xor_pairs(n_row, 2))
     layer_rows = (own_sum + others.astype(jnp.float32)).astype(jnp.bfloat16)
 
-    final_row = rms_scale(
-        last_row.astype(jnp.bfloat16).astype(jnp.float32), final_gain
-    ).astype(jnp.bfloat16)
-    table = jnp.where(jnp.arange(n_req)[:, None] == me_req, final_row, jnp.zeros_like(final_row))
+    table = pl.pallas_call(
+        final_row_kernel,
+        out_shape=jax.ShapeDtypeStruct((n_req, model), jnp.bfloat16),
+        in_specs=[SMEM] + [VMEM] * (n_row + 1),
+        out_specs=VMEM,
+        cost_estimate=FREE,
+        name="final_row",
+    )(scalars, *shares, final_gain[None])
     table = combine_all(table, "req", n_req, add_all, 2)
-    table = after(table, mate_part)
     vocab = head_weight.shape[1]
-    wide, streams = 256, 3
+    wide, streams = 256, 5
 
     def columns(index):
         return pl.BlockSpec((model, wide), lambda step: (0, step * streams + index))
@@ -563,13 +596,20 @@
             pl.BlockSpec((n_req, 2), lambda step: (0, 0)),
         ),
         compiler_params=params(48),
-        cost_estimate=pl.CostEstimate(flops=0, bytes_accessed=0, transcendentals=0),
+        cost_estimate=FREE,
         name="head",
     )(table, *[head_weight] * streams)
-    stats = combine_all(stats, "req", n_req, merge_stats, 8)
+    stats = combine_all(stats, "req", n_req, merge, 8)
     stats = after(stats, others)
-    stats = combine_all(stats, "row", n_row, merge_stats)
-    logprobs = logits - stats[:, :1] - jnp.log(stats[:, 1:])
+    stats = [stats] + [
+        lax.ppermute(stats, "row", xor_pairs(n_row, mask)) for mask in range(1, n_row)
+    ]
+    logprobs = pl.pallas_call(
+        logprobs_kernel,
+        out_shape=jax.ShapeDtypeStruct(logits.shape, jnp.float32),
+        cost_estimate=FREE,
+        name="logprobs",
+    )(logits, *stats)
     return (layer_rows[None], logprobs)
 
 

time: 181 us -> 159 us (0.88)
  waiting for transfers between devices: 58.6 us -> 45.3 us
  local copies, waits for them, and re-layouts: 18.7 us -> 8.73 us
  Pallas kernels: 37 us -> 40.4 us
  other arithmetic: 11.5 us -> 9.22 us
    unnamed x56 -> x48, local copies, waits for them, and re-layouts: 11.5 us -> 1.91 us
    ppermute x3, waiting for transfers between devices: 20.2 us -> 10.8 us  [gather_line(): down = lax.ppermute(down, 'row', down_pairs(size, 1, size - step))]
    ppermute x18, waiting for transfers between devices: 2.23 us -> 11.5 us  [send(): return lax.ppermute(array, 'req', xor_pairs(self.size, mask))]
    ppermute x3, waiting for transfers between devices: 9.07 us -> 0.01 us  [gather_line(): up = lax.ppermute(up, 'row', up_pairs(size, 1, step - 1))]
    pallas_call x0 -> x3, Pallas kernels: none -> 4.7 us  [the longest x1 1.73 us: on_device(): pl.pallas_call(logprobs_kernel, out_shape=jax.ShapeDtypeStruct(logits.sha...]
    ppermute x13 -> x10, starting transfers between devices: 13.6 us -> 9.31 us  [combine_all(): lax.ppermute(value, axis, xor_pairs(size, bit * index))]
    ppermute x1, waiting for transfers between devices: 4.1 us -> 0.01 us  [on_device(): others = lax.ppermute(mate_part, 'row', xor_pairs(n_row, 2))]
    ppermute x18, starting transfers between devices: 10.4 us -> 13.4 us  [send(): return lax.ppermute(array, 'req', xor_pairs(self.size, mask))]
  transfers between devices with their start and end apart: 46 -> 46, of which waited for: 18 -> 20; matrix products, arithmetic and copies ran while one was open for 9% -> 8% of each run, Pallas kernels for 19% -> 24%
where the time goes in v4:
time: 159 us
  starting transfers between devices  52.4 us (33%)
  waiting for transfers between devices  45.3 us (28%)
  Pallas kernels  40.4 us (25%)
  other arithmetic  9.22 us (6%)
  local copies, waits for them, and re-layouts  8.73 us (5%)
  between operations  2.52 us (2%)
    ppermute x18, starting transfers between devices, send(): return lax.ppermute(array, 'req', xor_pairs(self.size, mask))  13.4 us
    pallas_call x1, Pallas kernels, on_device(): pl.pallas_call(functools.partial(attention_kernel, n_row), out_shape=(jax...  11.8 us
    ppermute x18, waiting for transfers between devices, send(): return lax.ppermute(array, 'req', xor_pairs(self.size, mask))  11.5 us
    ppermute x3, waiting for transfers between devices, gather_line(): down = lax.ppermute(down, 'row', down_pairs(size, 1, size - step))  10.8 us
    ppermute x10, waiting for transfers between devices, combine_all(): lax.ppermute(value, axis, xor_pairs(size, bit * index))  10.1 us
    pallas_call x1, Pallas kernels, on_device(): pl.pallas_call(functools.partial(qkv_kernel, n_row, layout, block_rows),...  10 us
    ppermute x10, starting transfers between devices, combine_all(): lax.ppermute(value, axis, xor_pairs(size, bit * index))  9.31 us
    ppermute x1, waiting for transfers between devices, on_device(): across = lax.ppermute(cached[1], 'row', xor_pairs(n_row, 2))  8.97 us
  transfers between devices with their start and end apart: 46, of which 20 were waited for; matrix products, arithmetic and copies ran while one was open for 8% of the time, Pallas kernels for 24%

profile of v4, /device:TPU:0, one launch (start us, length us, event | category | flops | bytes accessed | tf_op | source)
XLA Modules:
  0.0 158.5 jit_solution(5815904400236149926)
XLA Ops:
  0.7 1.3 fusion
  3.3 5.0 %collective-permute-start = (bf16[128,2304]{1,0:T(8,128)(2,1)S(1)}, bf16[128,2304]{1,0:T(8,128)(2,1)S(1)}, u32[]{:S(2)}, u32[]{:S(2)}) collective-permute-start(bf16[128,2304]{1,0:T(8,128)(2,1)S(1)} %fusion.2.refs_0_), channel_id=1, source_target_pairs={{0,1},{1,2},{2,3},{4,5},{5,6},{6,7},{8,9},{9,10},{10,11},{12,13},{... | collective-permute-start | bytes 1769480 | tf_op jit(solution)/shard_map/ppermute | solution.py:100
  8.3 1.3 collective-permute-start.1
  9.6 2.0 %concatenate.31.refs_7_ = bf16[288,1728]{1,0:T(8,128)(2,1)S(1)} concatenate(bf16[288,576]{1,0:T(8,128)(2,1)S(1)} %copy-done.8, bf16[288,64]{1,0:T(8,128)(2,1)S(1)} %slice-done.1, bf16[288,512]{1,0:T(8,128)(2,1)S(1)} %slice-done, bf16[288,576]{1,0:T(8,128)(2,1)} %param.20), dimensions={1} | concatenate | bytes 1990656 | tf_op jit(solution)/shard_map/concatenate | solution.py:438
  11.6 1.6 collective-permute-start.5
  13.2 1.5 collective-permute-start.6
  14.7 2.6 %collective-permute-start.4 = (bf16[288,576]{1,0:T(8,128)(2,1)}, bf16[288,576]{1,0:T(8,128)(2,1)}, u32[]{:S(2)}, u32[]{:S(2)}) collective-permute-start(bf16[288,576]{1,0:T(8,128)(2,1)} %bitcast.28), channel_id=1, source_target_pairs={{0,1},{1,0},{2,3},{3,2},{4,5},{5,4},{6,7},{7,6},{8,9},{9,8},{10,11... | collective-permute-start | bytes 995336 | tf_op jit(solution)/shard_map/ppermute | solution.py:456
  18.0 3.0 %dynamic-slice_bitcast_fusion = (bf16[128,576]{1,0:T(8,128)(2,1)S(1)}, bf16[128,576]{1,0:T(8,128)(2,1)}, bf16[128,576]{1,0:T(8,128)(2,1)}, bf16[128,576]{1,0:T(8...) fusion(bf16[1,128,2304]{2,1,0:T(8,128)(2,1)} %param.16, ...), kind=kLoop, calls=%fused_computation.16 | loop fusion | bytes 2359312 | tf_op jit(solution)/shard_map/dynamic_slice | solution.py:444
  24.1 2.5 %collective-permute-done.1.refs_4_ = bf16[128,2304]{1,0:T(8,128)(2,1)} collective-permute-done((bf16[128,2304]{1,0:T(8,128)(2,1)S(1)}, bf16[128,2304]{1,0:T(8,128)(2,1)}, u32[]{:S(2)}, u32[]{:S(2)}) %collective-permute-start.1) | collective-permute-done | bytes 589856 | tf_op jit(solution)/shard_map/ppermute | solution.py:101
  27.2 1.3 collective-permute-start.3
  30.0 6.0 %collective-permute-done.5.refs_9_ = bf16[288,1728]{1,0:T(8,128)(2,1)S(1)} collective-permute-done((bf16[288,1728]{1,0:T(8,128)(2,1)S(1)}, bf16[288,1728]{1,0:T(8,128)(2,1)S(1)}, u32[]{:S(2)}, u32[]{:S(2)}) %collective-permute-start.5) | collective-permute-done | bytes 995360 | tf_op jit(solution)/shard_map/ppermute | solution.py:58
  36.0 1.3 collective-permute-done.6.refs_11_
  39.0 1.5 collective-permute-start.8
  41.7 3.8 %collective-permute-done.3.refs_5_ = bf16[128,2304]{1,0:T(8,128)(2,1)S(1)} collective-permute-done((bf16[128,2304]{1,0:T(8,128)(2,1)}, bf16[128,2304]{1,0:T(8,128)(2,1)S(1)}, u32[]{:S(2)}, u32[]{:S(2)}) %collective-permute-start.3) | collective-permute-done | bytes 589856 | tf_op jit(solution)/shard_map/ppermute | solution.py:101
  47.5 2.7 %collective-permute-start.25 = (bf16[256,576]{1,0:T(8,128)(2,1)S(1)}, bf16[256,576]{1,0:T(8,128)(2,1)S(1)}, u32[]{:S(2)}, u32[]{:S(2)}) collective-permute-start(bf16[256,576]{1,0:T(8,128)(2,1)S(1)} %pad_maximum_fusion.3), channel_id=1, source_target_pairs={{0,2},{1,3},{2,0},{3,1},{4,6},{5,7},{6,4},{7,5},{8,10},{9,11},{10,... | collective-permute-start | bytes 884744 | tf_op jit(solution)/shard_map/ppermute | solution.py:468
  50.9 1.5 collective-permute-start.10
  52.4 1.5 collective-permute-start.9
  53.9 9.0 %collective-permute-done.25.refs_2_ = bf16[256,576]{1,0:T(8,128)(2,1)S(1)} collective-permute-done((bf16[256,576]{1,0:T(8,128)(2,1)S(1)}, bf16[256,576]{1,0:T(8,128)(2,1)S(1)}, u32[]{:S(2)}, u32[]{:S(2)}) %collective-permute-start.25) | collective-permute-done | bytes 294944 | tf_op jit(solution)/shard_map/ppermute | solution.py:468
  63.4 4.6 %collective-permute-done.14.refs_6_ = bf16[128,2304]{1,0:T(8,128)(2,1)S(1)} collective-permute-done((bf16[128,2304]{1,0:T(8,128)(2,1)S(1)}, bf16[128,2304]{1,0:T(8,128)(2,1)S(1)}, u32[]{:S(2)}, u32[]{:S(2)}) %collective-permute-start.14) | collective-permute-done | bytes 589856 | tf_op jit(solution)/shard_map/ppermute | solution.py:101
  68.7 2.7 %collective-permute-done.18.refs_14_ = bf16[144,1728]{1,0:T(8,128)(2,1)S(1)} collective-permute-done((bf16[144,1728]{1,0:T(8,128)(2,1)S(1)}, bf16[144,1728]{1,0:T(8,128)(2,1)S(1)}, u32[]{:S(2)}, u32[]{:S(2)}) %collective-permute-start.18) | collective-permute-done | bytes 497696 | tf_op jit(solution)/shard_map/ppermute | solution.py:58
  72.1 2.4 %collective-permute-start.27 = (bf16[256,576]{1,0:T(8,128)(2,1)S(1)}, bf16[256,576]{1,0:T(8,128)(2,1)S(1)}, u32[]{:S(2)}, u32[]{:S(2)}) collective-permute-start(bf16[256,576]{1,0:T(8,128)(2,1)S(1)} %pad_maximum_fusion.4), channel_id=1, source_target_pairs={{0,3},{1,2},{2,1},{3,0},{4,7},{5,6},{6,5},{7,4},{8,11},{9,10},{10,... | collective-permute-start | bytes 884744 | tf_op jit(solution)/shard_map/ppermute | solution.py:473
  74.5 1.5 collective-permute-start.11
  76.0 1.5 collective-permute-start.12
  77.6 10.0 %qkv.1.refs_4_ = bf16[512,1728]{1,0:T(8,128)(2,1)S(1)} custom-call(s32[4]{0:T(128)S(1)} %pad_add_fusion.scalars, bf16[128,2304]{1,0:T(8,128)(2,1)S(1)} %fusion.2.refs_0_, bf16[128,2304]{1,0:T(8,128)(2,1)S(1)} %collective-permute-done.refs_1_, bf16[128,2304]{1,0:T(8,128)(2,1)S(1)} %collective-permute-done.2.refs_2_, ...), custom_call_target="tpu_custom_call" | custom-call | flops 4076863488 | bytes 14680064 | tf_op jit(solution)/shard_map/qkv/pallas_call | solution.py:479
  88.9 11.8 %attention.1 = (bf16[256,576]{1,0:T(8,128)(2,1)S(1)}, bf16[256,576]{1,0:T(8,128)(2,1)S(1)}, bf16[16,576]{1,0:T(8,128)(2,1)S(1)}) custom-call(s32[4]{0:T(128)S(1)} %pad_add_fusion.scalars, bf16[256,576]{1,0:T(8,128)(2,1)S(1)} %pad_maximum_fusion.1.refs_0_, bf16[256,576]{1,0:T(8,128)(2,1)S(1)} %collective-permute-done.26.refs_1_, ...), custom_call_target="tpu_custom_call" | custom-call | flops 905969664 | bytes 4194304 | tf_op jit(solution)/shard_map/attention/pallas_call | solution.py:502
  101.8 1.9 %last_row.1.refs_0_ = f32[1,2304]{1,0:T(1,128)S(1)} custom-call(s32[4]{0:T(128)S(1)} %pad_add_fusion.scalars, bf16[288,1152]{1,0:T(8,128)(2,1)S(1)} %pad_maximum_fusion.refs_0_, bf16[288,1152]{1,0:T(8,128)(2,1)S(1)} %collective-permute-done.20.refs_1_, bf16[288,1152]{1,0:T(8,128)(2,1)S(1)} %collective-permute-done.9.refs_2_, ...), custom_call_target="tpu_custom_call" | custom-call | tf_op jit(solution)/shard_map/last_row/pallas_call | solution.py:527
  104.8 1.9 %collective-permute-start.30 = (f32[1,2304]{1,0:T(1,128)S(1)}, f32[1,2304]{1,0:T(1,128)S(1)}, u32[]{:S(2)}, u32[]{:S(2)}) collective-permute-start(f32[1,2304]{1,0:T(1,128)S(1)} %last_row.1.refs_0_), channel_id=1, source_target_pairs={{0,2},{1,3},{2,0},{3,1},{4,6},{5,7},{6,4},{7,5},{8,10},{9,11},{10,... | collective-permute-start | bytes 27656 | tf_op jit(solution)/shard_map/ppermute | solution.py:542
  106.7 1.4 collective-permute-start.31
  108.1 1.4 collective-permute-done.28.refs_11_
  109.5 4.3 %project.1 = (f32[128,2304]{1,0:T(8,128)S(1)}, bf16[128,2304]{1,0:T(8,128)(2,1)S(1)}) custom-call(s32[4]{0:T(128)S(1)} %pad_add_fusion.scalars, bf16[288,1152]{1,0:T(8,128)(2,1)S(1)} %pad_maximum_fusion.refs_0_, bf16[288,1152]{1,0:T(8,128)(2,1)S(1)} %collective-permute-done.20.refs_1_, bf16[288,1152]{1,0:T(8,128)(2,1)S(1)} %collective-permute-done.9.refs_2_, ...), custom_call_target="tpu_custom_call" | custom-call | flops 1358954496 | bytes 8388608 | tf_op jit(solution)/shard_map/project/pallas_call | solution.py:546
  113.9 1.9 %collective-permute-start.32 = (bf16[128,2304]{1,0:T(8,128)(2,1)S(1)}, bf16[128,2304]{1,0:T(8,128)(2,1)S(1)}, u32[]{:S(2)}, u32[]{:S(2)}) collective-permute-start(bf16[128,2304]{1,0:T(8,128)(2,1)S(1)} %get-tuple-element.88), channel_id=1, source_target_pairs={{0,2},{1,3},{2,0},{3,1},{4,6},{5,7},{6,4},{7,5},{8,10},{9,11},{10,... | collective-permute-start | bytes 1769480 | tf_op jit(solution)/shard_map/ppermute | solution.py:565
  116.4 1.5 final_row.1
  118.0 1.4 collective-permute-done.33
  120.2 1.6 collective-permute-start.34
  121.7 2.5 %collective-permute-done.34 = bf16[8,2304]{1,0:T(8,128)(2,1)S(1)} collective-permute-done((bf16[8,2304]{1,0:T(8,128)(2,1)S(1)}, bf16[8,2304]{1,0:T(8,128)(2,1)S(1)}, u32[]{:S(2)}, u32[]{:S(2)}) %collective-permute-start.34) | collective-permute-done | bytes 36896 | tf_op jit(solution)/shard_map/ppermute | solution.py:381
  124.2 1.6 collective-permute-start.35
  125.8 2.4 %collective-permute-done.35 = bf16[8,2304]{1,0:T(8,128)(2,1)S(1)} collective-permute-done((bf16[8,2304]{1,0:T(8,128)(2,1)S(1)}, bf16[8,2304]{1,0:T(8,128)(2,1)S(1)}, u32[]{:S(2)}, u32[]{:S(2)}) %collective-permute-start.35) | collective-permute-done | bytes 36896 | tf_op jit(solution)/shard_map/ppermute | solution.py:381
  128.2 7.7 %head.1 = (f32[8,3840]{1,0:T(8,128)S(1)}, f32[8,2]{1,0:T(8,128)S(1)}) custom-call(bf16[8,2304]{1,0:T(8,128)(2,1)S(1)} %add.60.table_ref, bf16[2304,3840]{1,0:T(8,128)(2,1)} %refs_4_.1, bf16[2304,3840]{1,0:T(8,128)(2,1)} %refs_4_.1, bf16[2304,3840]{1,0:T(8,128)(2,1)} %refs_4_.1, bf16[2304,3840]{1,0:T(8,128)(2,1)} %refs_4_.1, bf16[2304,3840]{1,0:T(8,128)(2,1)} %refs_4_.1), custom_call_target="tpu_custom_call" | custom-call | tf_op jit(solution)/shard_map/head/pallas_call | solution.py:583
  136.6 1.5 collective-permute-start.37
  138.4 1.5 collective-permute-start.39
  140.2 2.5 %collective-permute-start.41 = (f32[8,2]{1,0:T(8,128)S(1)}, f32[8,2]{1,0:T(8,128)S(1)}, u32[]{:S(2)}, u32[]{:S(2)}) collective-permute-start(f32[8,2]{1,0:T(8,128)S(1)} %get-tuple-element.94.refs_0_), channel_id=1, source_target_pairs={{0,24},{4,28},{8,16},{12,20},{16,8},{20,12},{24,0},{28,4},{1,25},{... | collective-permute-start | bytes 200 | tf_op jit(solution)/shard_map/ppermute | solution.py:381
  143.0 1.7 %collective-permute-done.41.refs_6_ = f32[8,2]{1,0:T(8,128)S(1)} collective-permute-done((f32[8,2]{1,0:T(8,128)S(1)}, f32[8,2]{1,0:T(8,128)S(1)}, u32[]{:S(2)}, u32[]{:S(2)}) %collective-permute-start.41) | collective-permute-done | bytes 96 | tf_op jit(solution)/shard_map/ppermute | solution.py:381
  144.7 1.9 %collective-permute-done.42.refs_7_ = f32[8,2]{1,0:T(8,128)S(1)} collective-permute-done((f32[8,2]{1,0:T(8,128)S(1)}, f32[8,2]{1,0:T(8,128)S(1)}, u32[]{:S(2)}, u32[]{:S(2)}) %collective-permute-start.42) | collective-permute-done | bytes 96 | tf_op jit(solution)/shard_map/ppermute | solution.py:381
  147.2 1.4 merge.1.refs_0_
  148.9 1.7 %collective-permute-start.44 = (f32[8,2]{1,0:T(8,128)}, f32[8,2]{1,0:T(8,128)S(1)}, u32[]{:S(2)}, u32[]{:S(2)}) collective-permute-start(f32[8,2]{1,0:T(8,128)} %merge.1.refs_0_), channel_id=1, source_target_pairs={{0,2},{1,3},{2,0},{3,1},{4,6},{5,7},{6,4},{7,5},{8,10},{9,11},{10,... | collective-permute-start | bytes 200 | tf_op jit(solution)/shard_map/ppermute | solution.py:605
  150.6 2.4 %collective-permute-start.45 = (f32[8,2]{1,0:T(8,128)}, f32[8,2]{1,0:T(8,128)S(1)}, u32[]{:S(2)}, u32[]{:S(2)}) collective-permute-start(f32[8,2]{1,0:T(8,128)} %merge.1.refs_0_), channel_id=1, source_target_pairs={{0,3},{1,2},{2,1},{3,0},{4,7},{5,6},{6,5},{7,4},{8,11},{9,10},{10,... | collective-permute-start | bytes 200 | tf_op jit(solution)/shard_map/ppermute | solution.py:605
  154.0 2.2 %collective-permute-done.45.refs_3_ = f32[8,2]{1,0:T(8,128)S(1)} collective-permute-done((f32[8,2]{1,0:T(8,128)}, f32[8,2]{1,0:T(8,128)S(1)}, u32[]{:S(2)}, u32[]{:S(2)}) %collective-permute-start.45) | collective-permute-done | bytes 96 | tf_op jit(solution)/shard_map/ppermute | solution.py:605
  156.8 1.7 %logprobs.1 = f32[8,3840]{1,0:T(8,128)} custom-call(f32[8,3840]{1,0:T(8,128)} %copy-done.1, f32[8,2]{1,0:T(8,128)} %merge.1.refs_0_, f32[8,2]{1,0:T(8,128)} %copy-done.14, f32[8,2]{1,0:T(8,128)} %copy-done.15, f32[8,2]{1,0:T(8,128)} %copy-done.16), custom_call_target="tpu_custom_call" | custom-call | tf_op jit(solution)/shard_map/logprobs/pallas_call | solution.py:607
  (128 shorter events, 22.2 us)
Async XLA Ops:
  3.3 20.8 %collective-permute-start = (bf16[128,2304]{1,0:T(8,128)(2,1)S(1)}, bf16[128,2304]{1,0:T(8,128)(2,1)S(1)}, u32[]{:S(2)}, u32[]{:S(2)}) collective-permute-start(bf16[128,2304]{1,0:T(8,128)(2,1)S(1)} %fusion.2.refs_0_), channel_id=1, source_target_pairs={{0,1},{1,2},{2,3},{4,5},{5,6},{6,7},{8,9},{9,10},{10,11},{12,13},{... | collective-permute-start | bytes 1769480 | tf_op jit(solution)/shard_map/ppermute | solution.py:100
  8.3 18.3 %collective-permute-start.1 = (bf16[128,2304]{1,0:T(8,128)(2,1)S(1)}, bf16[128,2304]{1,0:T(8,128)(2,1)}, u32[]{:S(2)}, u32[]{:S(2)}) collective-permute-start(bf16[128,2304]{1,0:T(8,128)(2,1)S(1)} %fusion.2.refs_0_), channel_id=1, source_target_pairs={{1,0},{2,1},{3,2},{5,4},{6,5},{7,6},{9,8},{10,9},{11,10},{13,12},{... | collective-permute-start | bytes 1769480 | tf_op jit(solution)/shard_map/ppermute | solution.py:101
  11.6 24.3 %collective-permute-start.5 = (bf16[288,1728]{1,0:T(8,128)(2,1)S(1)}, bf16[288,1728]{1,0:T(8,128)(2,1)S(1)}, u32[]{:S(2)}, u32[]{:S(2)}) collective-permute-start(bf16[288,1728]{1,0:T(8,128)(2,1)S(1)} %concatenate.31.refs_7_), channel_id=1, source_target_pairs={{0,8},{4,12},{8,0},{12,4},{16,24},{20,28},{24,16},{28,20},{1,9},{5... | collective-permute-start | bytes 2985992 | tf_op jit(solution)/shard_map/ppermute | solution.py:58
  13.2 24.1 %collective-permute-start.6 = (bf16[288,1728]{1,0:T(8,128)(2,1)S(1)}, bf16[288,1728]{1,0:T(8,128)(2,1)}, u32[]{:S(2)}, u32[]{:S(2)}) collective-permute-start(bf16[288,1728]{1,0:T(8,128)(2,1)S(1)} %concatenate.31.refs_7_), channel_id=1, source_target_pairs={{0,16},{4,20},{8,24},{12,28},{16,0},{20,4},{24,8},{28,12},{1,17},{... | collective-permute-start | bytes 2985992 | tf_op jit(solution)/shard_map/ppermute | solution.py:58
  14.7 25.8 %collective-permute-start.4 = (bf16[288,576]{1,0:T(8,128)(2,1)}, bf16[288,576]{1,0:T(8,128)(2,1)}, u32[]{:S(2)}, u32[]{:S(2)}) collective-permute-start(bf16[288,576]{1,0:T(8,128)(2,1)} %bitcast.28), channel_id=1, source_target_pairs={{0,1},{1,0},{2,3},{3,2},{4,5},{5,4},{6,7},{7,6},{8,9},{9,8},{10,11... | collective-permute-start | bytes 995336 | tf_op jit(solution)/shard_map/ppermute | solution.py:456
  21.9 87.6 %copy-start.3 = (s32[4]{0:T(128)}, s32[4]{0:T(128)S(1)}, u32[]{:S(2)}) copy-start(s32[4]{0:T(128)S(1)} %pad_add_fusion.scalars) | copy-start | bytes 52
  26.5 15.2 %collective-permute-start.2 = (bf16[128,2304]{1,0:T(8,128)(2,1)S(1)}, bf16[128,2304]{1,0:T(8,128)(2,1)S(1)}, u32[]{:S(2)}, u32[]{:S(2)}) collective-permute-start(bf16[128,2304]{1,0:T(8,128)(2,1)S(1)} %collective-permute-done.refs_1_), channel_id=1, source_target_pairs={{1,2},{2,3},{5,6},{6,7},{9,10},{10,11},{13,14},{14,15},{17,18},{18... | collective-permute-start | bytes 1769480 | tf_op jit(solution)/shard_map/ppermute | solution.py:100
  27.2 18.3 %collective-permute-start.3 = (bf16[128,2304]{1,0:T(8,128)(2,1)}, bf16[128,2304]{1,0:T(8,128)(2,1)S(1)}, u32[]{:S(2)}, u32[]{:S(2)}) collective-permute-start(bf16[128,2304]{1,0:T(8,128)(2,1)} %collective-permute-done.1.refs_4_), channel_id=1, source_target_pairs={{1,0},{2,1},{5,4},{6,5},{9,8},{10,9},{13,12},{14,13},{17,16},{18,1... | collective-permute-start | bytes 1769480 | tf_op jit(solution)/shard_map/ppermute | solution.py:101
  38.4 12.1 %collective-permute-start.7 = (bf16[144,1728]{1,0:T(8,128)(2,1)S(1)}, bf16[144,1728]{1,0:T(8,128)(2,1)S(1)}, u32[]{:S(2)}, u32[]{:S(2)}) collective-permute-start(bf16[144,1728]{1,0:T(8,128)(2,1)S(1)} %slice.21), channel_id=1, source_target_pairs={{0,8},{4,12},{8,0},{12,4},{16,24},{20,28},{24,16},{28,20},{1,9},{5... | collective-permute-start | bytes 1493000 | tf_op jit(solution)/shard_map/ppermute | solution.py:58
  39.0 11.9 %collective-permute-start.8 = (bf16[144,1728]{1,0:T(8,128)(2,1)S(1)}, bf16[144,1728]{1,0:T(8,128)(2,1)S(1)}, u32[]{:S(2)}, u32[]{:S(2)}) collective-permute-start(bf16[144,1728]{1,0:T(8,128)(2,1)S(1)} %slice.20), channel_id=1, source_target_pairs={{0,16},{4,20},{8,24},{12,28},{16,0},{20,4},{24,8},{28,12},{1,17},{... | collective-permute-start | bytes 1493000 | tf_op jit(solution)/shard_map/ppermute | solution.py:58
  45.5 17.4 %collective-permute-start.13 = (bf16[128,2304]{1,0:T(8,128)(2,1)S(1)}, bf16[128,2304]{1,0:T(8,128)(2,1)S(1)}, u32[]{:S(2)}, u32[]{:S(2)}) collective-permute-start(bf16[128,2304]{1,0:T(8,128)(2,1)S(1)} %collective-permute-done.2.refs_2_), channel_id=1, source_target_pairs={{2,3},{6,7},{10,11},{14,15},{18,19},{22,23},{26,27},{30,31}} | collective-permute-start | bytes 1769480 | tf_op jit(solution)/shard_map/ppermute | solution.py:100
  46.2 21.8 %collective-permute-start.14 = (bf16[128,2304]{1,0:T(8,128)(2,1)S(1)}, bf16[128,2304]{1,0:T(8,128)(2,1)S(1)}, u32[]{:S(2)}, u32[]{:S(2)}) collective-permute-start(bf16[128,2304]{1,0:T(8,128)(2,1)S(1)} %collective-permute-done.3.refs_5_), channel_id=1, source_target_pairs={{1,0},{5,4},{9,8},{13,12},{17,16},{21,20},{25,24},{29,28}} | collective-permute-start | bytes 1769480 | tf_op jit(solution)/shard_map/ppermute | solution.py:101
  47.5 15.4 %collective-permute-start.25 = (bf16[256,576]{1,0:T(8,128)(2,1)S(1)}, bf16[256,576]{1,0:T(8,128)(2,1)S(1)}, u32[]{:S(2)}, u32[]{:S(2)}) collective-permute-start(bf16[256,576]{1,0:T(8,128)(2,1)S(1)} %pad_maximum_fusion.3), channel_id=1, source_target_pairs={{0,2},{1,3},{2,0},{3,1},{4,6},{5,7},{6,4},{7,5},{8,10},{9,11},{10,... | collective-permute-start | bytes 884744 | tf_op jit(solution)/shard_map/ppermute | solution.py:468
  50.9 17.1 %collective-permute-start.10 = (bf16[288,1152]{1,0:T(8,128)(2,1)S(1)}, bf16[288,1152]{1,0:T(8,128)(2,1)S(1)}, u32[]{:S(2)}, u32[]{:S(2)}) collective-permute-start(bf16[288,1152]{1,0:T(8,128)(2,1)S(1)} %pad_maximum_fusion.refs_0_), channel_id=1, source_target_pairs={{0,16},{4,20},{8,24},{12,28},{16,0},{20,4},{24,8},{28,12},{1,17},{... | collective-permute-start | bytes 1990664 | tf_op jit(solution)/shard_map/ppermute | solution.py:58
  52.4 16.1 %collective-permute-start.9 = (bf16[288,1152]{1,0:T(8,128)(2,1)S(1)}, bf16[288,1152]{1,0:T(8,128)(2,1)S(1)}, u32[]{:S(2)}, u32[]{:S(2)}) collective-permute-start(bf16[288,1152]{1,0:T(8,128)(2,1)S(1)} %pad_maximum_fusion.refs_0_), channel_id=1, source_target_pairs={{0,8},{4,12},{8,0},{12,4},{16,24},{20,28},{24,16},{28,20},{1,9},{5... | collective-permute-start | bytes 1990664 | tf_op jit(solution)/shard_map/ppermute | solution.py:58
  62.9 11.6 %collective-permute-start.16 = (bf16[288,1728]{1,0:T(8,128)(2,1)S(1)}, bf16[288,1728]{1,0:T(8,128)(2,1)S(1)}, u32[]{:S(2)}, u32[]{:S(2)}) collective-permute-start(bf16[288,1728]{1,0:T(8,128)(2,1)S(1)} %collective-permute-done.5.refs_9_), channel_id=1, source_target_pairs={{0,4},{4,0},{8,12},{12,8},{16,20},{20,16},{24,28},{28,24},{1,5},{5... | collective-permute-start | bytes 2985992 | tf_op jit(solution)/shard_map/ppermute | solution.py:58
  62.9 13.1 %collective-permute-start.17 = (bf16[288,1728]{1,0:T(8,128)(2,1)}, bf16[288,1728]{1,0:T(8,128)(2,1)S(1)}, u32[]{:S(2)}, u32[]{:S(2)}) collective-permute-start(bf16[288,1728]{1,0:T(8,128)(2,1)} %collective-permute-done.6.refs_11_), channel_id=1, source_target_pairs={{0,4},{4,0},{8,12},{12,8},{16,20},{20,16},{24,28},{28,24},{1,5},{5... | collective-permute-start | bytes 2985992 | tf_op jit(solution)/shard_map/ppermute | solution.py:58
  68.0 9.6 %collective-permute-start.15 = (bf16[288,1728]{1,0:T(8,128)(2,1)S(1)}, bf16[288,1728]{1,0:T(8,128)(2,1)S(1)}, u32[]{:S(2)}, u32[]{:S(2)}) collective-permute-start(bf16[288,1728]{1,0:T(8,128)(2,1)S(1)} %concatenate.31.refs_7_), channel_id=1, source_target_pairs={{0,4},{4,0},{8,12},{12,8},{16,20},{20,16},{24,28},{28,24},{1,5},{5... | collective-permute-start | bytes 2985992 | tf_op jit(solution)/shard_map/ppermute | solution.py:58
  68.0 3.4 %collective-permute-start.18 = (bf16[144,1728]{1,0:T(8,128)(2,1)S(1)}, bf16[144,1728]{1,0:T(8,128)(2,1)S(1)}, u32[]{:S(2)}, u32[]{:S(2)}) collective-permute-start(bf16[144,1728]{1,0:T(8,128)(2,1)S(1)} %collective-permute-done.7.refs_13_), channel_id=1, source_target_pairs={{0,4},{4,0},{8,12},{12,8},{16,20},{20,16},{24,28},{28,24},{1,5},{5... | collective-permute-start | bytes 1493000 | tf_op jit(solution)/shard_map/ppermute | solution.py:58
  68.5 3.6 %collective-permute-start.19 = (bf16[144,1728]{1,0:T(8,128)(2,1)S(1)}, bf16[144,1728]{1,0:T(8,128)(2,1)S(1)}, u32[]{:S(2)}, u32[]{:S(2)}) collective-permute-start(bf16[144,1728]{1,0:T(8,128)(2,1)S(1)} %collective-permute-done.8.refs_15_), channel_id=1, source_target_pairs={{0,4},{4,0},{8,12},{12,8},{16,20},{20,16},{24,28},{28,24},{1,5},{5... | collective-permute-start | bytes 1493000 | tf_op jit(solution)/shard_map/ppermute | solution.py:58
  71.4 16.9 %collective-permute-start.26 = (bf16[256,576]{1,0:T(8,128)(2,1)S(1)}, bf16[256,576]{1,0:T(8,128)(2,1)S(1)}, u32[]{:S(2)}, u32[]{:S(2)}) collective-permute-start(bf16[256,576]{1,0:T(8,128)(2,1)S(1)} %pad_maximum_fusion.2), channel_id=1, source_target_pairs={{0,1},{1,0},{2,3},{3,2},{4,5},{5,4},{6,7},{7,6},{8,9},{9,8},{10,11... | collective-permute-start | bytes 884744 | tf_op jit(solution)/shard_map/ppermute | solution.py:471
  72.1 16.8 %collective-permute-start.27 = (bf16[256,576]{1,0:T(8,128)(2,1)S(1)}, bf16[256,576]{1,0:T(8,128)(2,1)S(1)}, u32[]{:S(2)}, u32[]{:S(2)}) collective-permute-start(bf16[256,576]{1,0:T(8,128)(2,1)S(1)} %pad_maximum_fusion.4), channel_id=1, source_target_pairs={{0,3},{1,2},{2,1},{3,0},{4,7},{5,6},{6,5},{7,4},{8,11},{9,10},{10,... | collective-permute-start | bytes 884744 | tf_op jit(solution)/shard_map/ppermute | solution.py:473
  74.5 13.1 %collective-permute-start.11 = (bf16[144,1152]{1,0:T(8,128)(2,1)S(1)}, bf16[144,1152]{1,0:T(8,128)(2,1)S(1)}, u32[]{:S(2)}, u32[]{:S(2)}) collective-permute-start(bf16[144,1152]{1,0:T(8,128)(2,1)S(1)} %slice.23), channel_id=1, source_target_pairs={{0,8},{4,12},{8,0},{12,4},{16,24},{20,28},{24,16},{28,20},{1,9},{5... | collective-permute-start | bytes 995336 | tf_op jit(solution)/shard_map/ppermute | solution.py:58
  76.0 11.6 %collective-permute-start.12 = (bf16[144,1152]{1,0:T(8,128)(2,1)S(1)}, bf16[144,1152]{1,0:T(8,128)(2,1)S(1)}, u32[]{:S(2)}, u32[]{:S(2)}) collective-permute-start(bf16[144,1152]{1,0:T(8,128)(2,1)S(1)} %slice.22), channel_id=1, source_target_pairs={{0,16},{4,20},{8,24},{12,28},{16,0},{20,4},{24,8},{28,12},{1,17},{... | collective-permute-start | bytes 995336 | tf_op jit(solution)/shard_map/ppermute | solution.py:58
  87.6 14.2 %copy-start = (bf16[1,128,2304]{2,1,0:T(8,128)(2,1)S(1)}, bf16[1,128,2304]{2,1,0:T(8,128)(2,1)}, u32[]{:S(2)}) copy-start(bf16[1,128,2304]{2,1,0:T(8,128)(2,1)} %param.12) | copy-start | bytes 1769476
  87.6 14.1 %collective-permute-start.20 = (bf16[288,1152]{1,0:T(8,128)(2,1)S(1)}, bf16[288,1152]{1,0:T(8,128)(2,1)S(1)}, u32[]{:S(2)}, u32[]{:S(2)}) collective-permute-start(bf16[288,1152]{1,0:T(8,128)(2,1)S(1)} %pad_maximum_fusion.refs_0_), channel_id=1, source_target_pairs={{0,4},{4,0},{8,12},{12,8},{16,20},{20,16},{24,28},{28,24},{1,5},{5... | collective-permute-start | bytes 1990664 | tf_op jit(solution)/shard_map/ppermute | solution.py:58
  87.7 14.1 %collective-permute-start.21 = (bf16[288,1152]{1,0:T(8,128)(2,1)S(1)}, bf16[288,1152]{1,0:T(8,128)(2,1)S(1)}, u32[]{:S(2)}, u32[]{:S(2)}) collective-permute-start(bf16[288,1152]{1,0:T(8,128)(2,1)S(1)} %collective-permute-done.9.refs_2_), channel_id=1, source_target_pairs={{0,4},{4,0},{8,12},{12,8},{16,20},{20,16},{24,28},{28,24},{1,5},{5... | collective-permute-start | bytes 1990664 | tf_op jit(solution)/shard_map/ppermute | solution.py:58
  88.2 13.6 %collective-permute-start.22 = (bf16[288,1152]{1,0:T(8,128)(2,1)S(1)}, bf16[288,1152]{1,0:T(8,128)(2,1)S(1)}, u32[]{:S(2)}, u32[]{:S(2)}) collective-permute-start(bf16[288,1152]{1,0:T(8,128)(2,1)S(1)} %collective-permute-done.10.refs_4_), channel_id=1, source_target_pairs={{0,4},{4,0},{8,12},{12,8},{16,20},{20,16},{24,28},{28,24},{1,5},{5... | collective-permute-start | bytes 1990664 | tf_op jit(solution)/shard_map/ppermute | solution.py:58
  88.3 12.4 %collective-permute-start.23 = (bf16[144,1152]{1,0:T(8,128)(2,1)S(1)}, bf16[144,1152]{1,0:T(8,128)(2,1)S(1)}, u32[]{:S(2)}, u32[]{:S(2)}) collective-permute-start(bf16[144,1152]{1,0:T(8,128)(2,1)S(1)} %collective-permute-done.11.refs_6_), channel_id=1, source_target_pairs={{0,4},{4,0},{8,12},{12,8},{16,20},{20,16},{24,28},{28,24},{1,5},{5... | collective-permute-start | bytes 995336 | tf_op jit(solution)/shard_map/ppermute | solution.py:58
  88.9 12.8 %collective-permute-start.24 = (bf16[144,1152]{1,0:T(8,128)(2,1)S(1)}, bf16[144,1152]{1,0:T(8,128)(2,1)S(1)}, u32[]{:S(2)}, u32[]{:S(2)}) collective-permute-start(bf16[144,1152]{1,0:T(8,128)(2,1)S(1)} %collective-permute-done.12.refs_8_), channel_id=1, source_target_pairs={{0,4},{4,0},{8,12},{12,8},{16,20},{20,16},{24,28},{28,24},{1,5},{5... | collective-permute-start | bytes 995336 | tf_op jit(solution)/shard_map/ppermute | solution.py:58
  100.7 8.8 %collective-permute-start.28 = (bf16[256,576]{1,0:T(8,128)(2,1)S(1)}, bf16[256,576]{1,0:T(8,128)(2,1)S(1)}, u32[]{:S(2)}, u32[]{:S(2)}) collective-permute-start(bf16[256,576]{1,0:T(8,128)(2,1)S(1)} %get-tuple-element.83), channel_id=1, source_target_pairs={{0,1},{1,0},{2,3},{3,2},{4,5},{5,4},{6,7},{7,6},{8,9},{9,8},{10,11... | collective-permute-start | bytes 884744 | tf_op jit(solution)/shard_map/ppermute | solution.py:545
  103.7 10.2 %collective-permute-start.29 = (f32[1,2304]{1,0:T(1,128)S(1)}, f32[1,2304]{1,0:T(1,128)S(1)}, u32[]{:S(2)}, u32[]{:S(2)}) collective-permute-start(f32[1,2304]{1,0:T(1,128)S(1)} %last_row.1.refs_0_), channel_id=1, source_target_pairs={{0,1},{1,0},{2,3},{3,2},{4,5},{5,4},{6,7},{7,6},{8,9},{9,8},{10,11... | collective-permute-start | bytes 27656 | tf_op jit(solution)/shard_map/ppermute | solution.py:542
  104.8 9.0 %collective-permute-start.30 = (f32[1,2304]{1,0:T(1,128)S(1)}, f32[1,2304]{1,0:T(1,128)S(1)}, u32[]{:S(2)}, u32[]{:S(2)}) collective-permute-start(f32[1,2304]{1,0:T(1,128)S(1)} %last_row.1.refs_0_), channel_id=1, source_target_pairs={{0,2},{1,3},{2,0},{3,1},{4,6},{5,7},{6,4},{7,5},{8,10},{9,11},{10,... | collective-permute-start | bytes 27656 | tf_op jit(solution)/shard_map/ppermute | solution.py:542
  106.7 7.1 %collective-permute-start.31 = (f32[1,2304]{1,0:T(1,128)S(1)}, f32[1,2304]{1,0:T(1,128)S(1)}, u32[]{:S(2)}, u32[]{:S(2)}) collective-permute-start(f32[1,2304]{1,0:T(1,128)S(1)} %last_row.1.refs_0_), channel_id=1, source_target_pairs={{0,3},{1,2},{2,1},{3,0},{4,7},{5,6},{6,5},{7,4},{8,11},{9,10},{10,... | collective-permute-start | bytes 27656 | tf_op jit(solution)/shard_map/ppermute | solution.py:542
  113.9 34.7 %collective-permute-start.32 = (bf16[128,2304]{1,0:T(8,128)(2,1)S(1)}, bf16[128,2304]{1,0:T(8,128)(2,1)S(1)}, u32[]{:S(2)}, u32[]{:S(2)}) collective-permute-start(bf16[128,2304]{1,0:T(8,128)(2,1)S(1)} %get-tuple-element.88), channel_id=1, source_target_pairs={{0,2},{1,3},{2,0},{3,1},{4,6},{5,7},{6,4},{7,5},{8,10},{9,11},{10,... | collective-permute-start | bytes 1769480 | tf_op jit(solution)/shard_map/ppermute | solution.py:565
  117.9 1.4 collective-permute-start.33
  120.2 4.0 %collective-permute-start.34 = (bf16[8,2304]{1,0:T(8,128)(2,1)S(1)}, bf16[8,2304]{1,0:T(8,128)(2,1)S(1)}, u32[]{:S(2)}, u32[]{:S(2)}) collective-permute-start(bf16[8,2304]{1,0:T(8,128)(2,1)S(1)} %add.58), channel_id=1, source_target_pairs={{0,8},{4,12},{8,0},{12,4},{16,24},{20,28},{24,16},{28,20},{1,9},{5... | collective-permute-start | bytes 110600 | tf_op jit(solution)/shard_map/ppermute | solution.py:381
  124.2 4.0 %collective-permute-start.35 = (bf16[8,2304]{1,0:T(8,128)(2,1)S(1)}, bf16[8,2304]{1,0:T(8,128)(2,1)S(1)}, u32[]{:S(2)}, u32[]{:S(2)}) collective-permute-start(bf16[8,2304]{1,0:T(8,128)(2,1)S(1)} %add.59), channel_id=1, source_target_pairs={{0,16},{4,20},{8,24},{12,28},{16,0},{20,4},{24,8},{28,12},{1,17},{... | collective-permute-start | bytes 110600 | tf_op jit(solution)/shard_map/ppermute | solution.py:381
  136.6 3.4 %collective-permute-start.36 = (f32[8,2]{1,0:T(8,128)S(1)}, f32[8,2]{1,0:T(8,128)S(1)}, u32[]{:S(2)}, u32[]{:S(2)}) collective-permute-start(f32[8,2]{1,0:T(8,128)S(1)} %get-tuple-element.94.refs_0_), channel_id=1, source_target_pairs={{0,4},{4,0},{8,12},{12,8},{16,20},{20,16},{24,28},{28,24},{1,5},{5... | collective-permute-start | bytes 200 | tf_op jit(solution)/shard_map/ppermute | solution.py:381
  136.6 3.6 %collective-permute-start.37 = (f32[8,2]{1,0:T(8,128)S(1)}, f32[8,2]{1,0:T(8,128)S(1)}, u32[]{:S(2)}, u32[]{:S(2)}) collective-permute-start(f32[8,2]{1,0:T(8,128)S(1)} %get-tuple-element.94.refs_0_), channel_id=1, source_target_pairs={{0,8},{4,12},{8,0},{12,4},{16,24},{20,28},{24,16},{28,20},{1,9},{5... | collective-permute-start | bytes 200 | tf_op jit(solution)/shard_map/ppermute | solution.py:381
  138.1 4.6 %collective-permute-start.38 = (f32[8,2]{1,0:T(8,128)S(1)}, f32[8,2]{1,0:T(8,128)S(1)}, u32[]{:S(2)}, u32[]{:S(2)}) collective-permute-start(f32[8,2]{1,0:T(8,128)S(1)} %get-tuple-element.94.refs_0_), channel_id=1, source_target_pairs={{0,12},{4,8},{8,4},{12,0},{16,28},{20,24},{24,20},{28,16},{1,13},{... | collective-permute-start | bytes 200 | tf_op jit(solution)/shard_map/ppermute | solution.py:381
  138.4 4.4 %collective-permute-start.39 = (f32[8,2]{1,0:T(8,128)S(1)}, f32[8,2]{1,0:T(8,128)S(1)}, u32[]{:S(2)}, u32[]{:S(2)}) collective-permute-start(f32[8,2]{1,0:T(8,128)S(1)} %get-tuple-element.94.refs_0_), channel_id=1, source_target_pairs={{0,16},{4,20},{8,24},{12,28},{16,0},{20,4},{24,8},{28,12},{1,17},{... | collective-permute-start | bytes 200 | tf_op jit(solution)/shard_map/ppermute | solution.py:381
  140.0 3.0 %collective-permute-start.40 = (f32[8,2]{1,0:T(8,128)S(1)}, f32[8,2]{1,0:T(8,128)S(1)}, u32[]{:S(2)}, u32[]{:S(2)}) collective-permute-start(f32[8,2]{1,0:T(8,128)S(1)} %get-tuple-element.94.refs_0_), channel_id=1, source_target_pairs={{0,20},{4,16},{8,28},{12,24},{16,4},{20,0},{24,12},{28,8},{1,21},{... | collective-permute-start | bytes 200 | tf_op jit(solution)/shard_map/ppermute | solution.py:381
  140.2 4.5 %collective-permute-start.41 = (f32[8,2]{1,0:T(8,128)S(1)}, f32[8,2]{1,0:T(8,128)S(1)}, u32[]{:S(2)}, u32[]{:S(2)}) collective-permute-start(f32[8,2]{1,0:T(8,128)S(1)} %get-tuple-element.94.refs_0_), channel_id=1, source_target_pairs={{0,24},{4,28},{8,16},{12,20},{16,8},{20,12},{24,0},{28,4},{1,25},{... | collective-permute-start | bytes 200 | tf_op jit(solution)/shard_map/ppermute | solution.py:381
  142.6 3.9 %collective-permute-start.42 = (f32[8,2]{1,0:T(8,128)S(1)}, f32[8,2]{1,0:T(8,128)S(1)}, u32[]{:S(2)}, u32[]{:S(2)}) collective-permute-start(f32[8,2]{1,0:T(8,128)S(1)} %get-tuple-element.94.refs_0_), channel_id=1, source_target_pairs={{0,28},{4,24},{8,20},{12,16},{16,12},{20,8},{24,4},{28,0},{1,29},{... | collective-permute-start | bytes 200 | tf_op jit(solution)/shard_map/ppermute | solution.py:381
  148.6 5.3 %collective-permute-start.43 = (f32[8,2]{1,0:T(8,128)}, f32[8,2]{1,0:T(8,128)S(1)}, u32[]{:S(2)}, u32[]{:S(2)}) collective-permute-start(f32[8,2]{1,0:T(8,128)} %merge.1.refs_0_), channel_id=1, source_target_pairs={{0,1},{1,0},{2,3},{3,2},{4,5},{5,4},{6,7},{7,6},{8,9},{9,8},{10,11... | collective-permute-start | bytes 200 | tf_op jit(solution)/shard_map/ppermute | solution.py:605
  148.9 5.0 %collective-permute-start.44 = (f32[8,2]{1,0:T(8,128)}, f32[8,2]{1,0:T(8,128)S(1)}, u32[]{:S(2)}, u32[]{:S(2)}) collective-permute-start(f32[8,2]{1,0:T(8,128)} %merge.1.refs_0_), channel_id=1, source_target_pairs={{0,2},{1,3},{2,0},{3,1},{4,6},{5,7},{6,4},{7,5},{8,10},{9,11},{10,... | collective-permute-start | bytes 200 | tf_op jit(solution)/shard_map/ppermute | solution.py:605
  150.6 5.6 %collective-permute-start.45 = (f32[8,2]{1,0:T(8,128)}, f32[8,2]{1,0:T(8,128)S(1)}, u32[]{:S(2)}, u32[]{:S(2)}) collective-permute-start(f32[8,2]{1,0:T(8,128)} %merge.1.refs_0_), channel_id=1, source_target_pairs={{0,3},{1,2},{2,1},{3,0},{4,7},{5,6},{6,5},{7,4},{8,11},{9,10},{10,... | collective-permute-start | bytes 200 | tf_op jit(solution)/shard_map/ppermute | solution.py:605
  (24 other events, 112.6 us)

commit v5 on v4

--- a/solution.py
+++ b/solution.py
@@ -12,6 +12,12 @@
 HBM = pl.BlockSpec(memory_space=pltpu.HBM)
 SMEM = pl.BlockSpec(memory_space=pltpu.SMEM)
 VMEM = pl.BlockSpec(memory_space=pltpu.VMEM)
+
+
+def params(mib):
+    return pltpu.CompilerParams(vmem_limit_bytes=mib * 1024 * 1024)
+
+
 FREE = pl.CostEstimate(flops=0, bytes_accessed=0, transcendentals=0)
 
 
@@ -307,6 +313,7 @@
     for copy in copies:
         copy.wait()
     width = last_ref.shape[1]
+    here = lax.broadcasted_iota(jnp.int32, (out_ref.shape[0], 256), 0) == scalars[1]
     for tile in range(0, out_ref.shape[1], 256):
         share = lax.dot_general(
             last_ref[...],
@@ -314,15 +321,14 @@
             NT,
             preferred_element_type=jnp.float32,
         )
-        out_ref[:, tile : tile + 256] = share[0:1] + residual[:, tile : tile + 256]
-
-
-def final_row_kernel(scalars, *refs):
+        row = share[0:1] + residual[:, tile : tile + 256]
+        out_ref[:, tile : tile + 256] = jnp.where(here, row, 0.0)
+
+
+def final_rows_kernel(*refs):
     shares, (gain_ref, table_ref) = refs[:-2], refs[-2:]
-    row = add_all(*[ref[...] for ref in shares]).astype(jnp.bfloat16).astype(jnp.float32)
-    row = rms_scale(row, gain_ref[...]).astype(jnp.bfloat16).astype(jnp.float32)
-    at = lax.broadcasted_iota(jnp.int32, table_ref.shape, 0) == scalars[1]
-    table_ref[...] = jnp.where(at, row, 0.0).astype(jnp.bfloat16)
+    rows = add_all(*[ref[...] for ref in shares]).astype(jnp.bfloat16).astype(jnp.float32)
+    table_ref[...] = rms_scale(rows, gain_ref[...][None]).astype(jnp.bfloat16)
 
 
 def merge_kernel(*refs):
@@ -355,14 +361,16 @@
         mate_ref[:, tile:to] = total[chunk:].astype(jnp.bfloat16)
 
 
-def head_kernel(table_ref, *refs):
+def head_kernel(streams, *refs):
+    tables, refs = refs[: -streams - 2], refs[-streams - 2 :]
     weights, (logits_ref, stats_ref) = refs[:-2], refs[-2:]
+    table = add_all(*[ref[...] for ref in tables])
     step = pl.program_id(0)
     wide = weights[0].shape[1]
     for index, ref in enumerate(weights):
         start = pl.multiple_of((step * len(weights) + index) * wide, 128)
         logits_ref[:, pl.ds(start, wide)] = jnp.dot(
-            table_ref[...], ref[...], preferred_element_type=jnp.float32
+            table, ref[...], preferred_element_type=jnp.float32
         )
 
     @pl.when(step == pl.num_programs(0) - 1)
@@ -373,16 +381,17 @@
         stats_ref[:, 1:2] = jnp.sum(jnp.exp(logits - top), axis=1, keepdims=True)
 
 
-def combine_all(value, axis, size, combine, width=4):
-    bit = 1
+def exchange_all(value, axis, size, bit, combine=None):
+    values = [value]
     while bit < size:
-        count = min(width, size // bit)
-        others = [
+        count = min(4, size // bit)
+        if len(values) > 1:
+            value = combine(*values)
+        values = [value] + [
             lax.ppermute(value, axis, xor_pairs(size, bit * index)) for index in range(1, count)
         ]
-        value = combine(value, *others)
         bit *= count
-    return value
+    return values
 
 
 def add_all(*tables):
@@ -399,6 +408,7 @@
     return pl.pallas_call(
         merge_kernel,
         out_shape=jax.ShapeDtypeStruct(stats[0].shape, jnp.float32),
+        compiler_params=params(4),
         cost_estimate=FREE,
         name="merge",
     )(*stats)
@@ -428,10 +438,6 @@
     block_rows, width = w_query.shape
     length, count = cache_len[0], new_count[0]
     scalars = jnp.stack([me_row, me_req, length, count]).astype(jnp.int32)
-
-    def params(mib):
-        return pltpu.CompilerParams(vmem_limit_bytes=mib * 1024 * 1024)
-
 
     normed = rms_scale(inputs.astype(jnp.float32), attn_gain).astype(jnp.bfloat16)
     last = width - HEAD_DIM
@@ -494,7 +500,7 @@
         name="qkv",
     )(scalars, normed, *x_ups, *x_downs, *[piece[0] for piece in pieces], cosine, sine)
 
-    out_here, _ = together([*out_block, *out_got, *out_diagonal], [qkv])
+    out_here, old_blocks, _ = together([*out_block, *out_got, *out_diagonal], old_blocks, [qkv])
     out_others = out_rows.cores(out_here)
     out_pieces = out_rows.pieces(out_got, out_diagonal, out_others)
 
@@ -526,7 +532,7 @@
     own_columns = -(-width // 128) * 128
     share = pl.pallas_call(
         functools.partial(last_row_kernel, out_layout, block_rows),
-        out_shape=jax.ShapeDtypeStruct((1, model), jnp.float32),
+        out_shape=jax.ShapeDtypeStruct((n_req, model), jnp.float32),
         in_specs=[SMEM] + [HBM] * len(out_weights) + [VMEM] * 2,
         out_specs=VMEM,
         scratch_shapes=[
@@ -538,6 +544,8 @@
         name="last_row",
     )(scalars, *out_weights, last_attended, inputs)
 
+    pair = lax.ppermute(share, "req", xor_pairs(n_req, 1))
+    share = share + pair
     shares = [share] + [
         lax.ppermute(share, "row", xor_pairs(n_row, mask)) for mask in range(1, n_row)
     ]
@@ -566,14 +574,13 @@
     layer_rows = (own_sum + others.astype(jnp.float32)).astype(jnp.bfloat16)
 
     table = pl.pallas_call(
-        final_row_kernel,
+        final_rows_kernel,
         out_shape=jax.ShapeDtypeStruct((n_req, model), jnp.bfloat16),
-        in_specs=[SMEM] + [VMEM] * (n_row + 1),
-        out_specs=VMEM,
+        compiler_params=params(4),
         cost_estimate=FREE,
-        name="final_row",
-    )(scalars, *shares, final_gain[None])
-    table = combine_all(table, "req", n_req, add_all, 2)
+        name="final_rows",
+    )(*shares, final_gain)
+    tables = exchange_all(table, "req", n_req, 2, add_all)
     vocab = head_weight.shape[1]
     wide, streams = 256, 5
 
@@ -581,14 +588,14 @@
         return pl.BlockSpec((model, wide), lambda step: (0, step * streams + index))
 
     logits, stats = pl.pallas_call(
-        head_kernel,
+        functools.partial(head_kernel, streams),
         grid=(vocab // (wide * streams),),
         out_shape=(
             jax.ShapeDtypeStruct((n_req, vocab), jnp.float32),
             jax.ShapeDtypeStruct((n_req, 2), jnp.float32),
         ),
         in_specs=[
-            pl.BlockSpec((n_req, model), lambda step: (0, 0)),
+            *[pl.BlockSpec((n_req, model), lambda step: (0, 0))] * len(tables),
             *[columns(index) for index in range(streams)],
         ],
         out_specs=(
@@ -598,15 +605,14 @@
         compiler_params=params(48),
         cost_estimate=FREE,
         name="head",
-    )(table, *[head_weight] * streams)
-    stats = combine_all(stats, "req", n_req, merge, 8)
-    stats = after(stats, others)
-    stats = [stats] + [
-        lax.ppermute(stats, "row", xor_pairs(n_row, mask)) for mask in range(1, n_row)
-    ]
+    )(*tables, *[head_weight] * streams)
+    stats = merge(*exchange_all(stats, "req", n_req, 2, merge))
+    stats = merge(stats, lax.ppermute(stats, "req", xor_pairs(n_req, 1)))
+    stats = exchange_all(after(stats, others), "row", n_row, 1, merge)
     logprobs = pl.pallas_call(
         logprobs_kernel,
         out_shape=jax.ShapeDtypeStruct(logits.shape, jnp.float32),
+        compiler_params=params(4),
         cost_estimate=FREE,
         name="logprobs",
     )(logits, *stats)

time: 159 us -> 153 us (0.962)
  Pallas kernels: 40.4 us -> 34 us
  waiting for transfers between devices: 45.3 us -> 48.8 us
  local copies, waits for them, and re-layouts: 8.73 us -> 6.25 us
    ppermute x3, waiting for transfers between devices: 10.8 us -> 1.47 us  [gather_line(): down = lax.ppermute(down, 'row', down_pairs(size, 1, size - step))]
    ppermute x18, waiting for transfers between devices: 11.5 us -> 18.2 us  [send(): return lax.ppermute(array, 'req', xor_pairs(self.size, mask))]
    ppermute x1, waiting for transfers between devices: 0.01 us -> 3.6 us  [on_device(): others = lax.ppermute(mate_part, 'row', xor_pairs(n_row, 2))]
    ppermute x1, starting transfers between devices: 2.69 us -> 6 us  [on_device(): across = lax.ppermute(cached[1], 'row', xor_pairs(n_row, 2))]
    ppermute x1, waiting for transfers between devices: 1.36 us -> 4.62 us  [on_device(): got = after(lax.ppermute(send, 'row', xor_pairs(n_row, 1)), share)]
    ppermute x13 -> x11, waiting for transfers between devices: 12.4 us -> 9.15 us  [the longest x9 6.9 us: exchange_all(): lax.ppermute(value, axis, xor_pairs(size, bit * index))]
    ppermute x1, starting transfers between devices: 2.43 us -> 5.59 us  [on_device(): lax.ppermute(behind, 'row', xor_pairs(n_row, 3))]
    ppermute x18, starting transfers between devices: 13.4 us -> 11.3 us  [send(): return lax.ppermute(array, 'req', xor_pairs(self.size, mask))]
  transfers between devices with their start and end apart: 46 -> 44, of which waited for: 20 -> 23; matrix products, arithmetic and copies ran while one was open for 8% -> 8% of each run, Pallas kernels for 24% -> 22%
where the time goes in v5:
time: 153 us; the launch traced here: 152 us
  starting transfers between devices  52.4 us (34%)
  waiting for transfers between devices  48.8 us (32%)
  Pallas kernels  34 us (22%)
  other arithmetic  8.42 us (6%)
  local copies, waits for them, and re-layouts  6.25 us (4%)
  between operations  2.41 us (2%)
    ppermute x18, waiting for transfers between devices, send(): return lax.ppermute(array, 'req', xor_pairs(self.size, mask))  18.2 us
    ppermute x9, starting transfers between devices, exchange_all(): lax.ppermute(value, axis, xor_pairs(size, bit * index))  11.5 us
    ppermute x18, starting transfers between devices, send(): return lax.ppermute(array, 'req', xor_pairs(self.size, mask))  11.3 us
    pallas_call x1, Pallas kernels, on_device(): pl.pallas_call(functools.partial(attention_kernel, n_row), out_shape=(jax...  9.95 us
    ppermute x1, waiting for transfers between devices, on_device(): across = lax.ppermute(cached[1], 'row', xor_pairs(n_row, 2))  9.42 us
    pallas_call x1, Pallas kernels, on_device(): pl.pallas_call(functools.partial(qkv_kernel, n_row, layout, block_rows),...  9.09 us
    ppermute x3, starting transfers between devices, gather_line(): up = lax.ppermute(up, 'row', up_pairs(size, 1, step - 1))  7.78 us
    pallas_call x1, Pallas kernels, on_device(): pl.pallas_call(functools.partial(head_kernel, streams), grid=(vocab // (w...  7.67 us
  transfers between devices with their start and end apart: 44, of which 23 were waited for; matrix products, arithmetic and copies ran while one was open for 8% of the time, Pallas kernels for 22%

profile of v5, /device:TPU:0, one launch (start us, length us, event | category | flops | bytes accessed | tf_op | source)
XLA Modules:
  0.0 152.3 jit_solution(3443078227106805231)
XLA Ops:
  0.7 1.3 fusion
  2.0 1.3 fusion.2.refs_0_
  3.3 1.3 collective-permute-start.1
  4.6 6.4 %collective-permute-start = (bf16[128,2304]{1,0:T(8,128)(2,1)S(1)}, bf16[128,2304]{1,0:T(8,128)(2,1)}, u32[]{:S(2)}, u32[]{:S(2)}) collective-permute-start(bf16[128,2304]{1,0:T(8,128)(2,1)S(1)} %fusion.2.refs_0_), channel_id=1, source_target_pairs={{0,1},{1,2},{2,3},{4,5},{5,6},{6,7},{8,9},{9,10},{10,11},{12,13},{... | collective-permute-start | bytes 1769480 | tf_op jit(solution)/shard_map/ppermute | solution.py:106
  11.0 2.0 %concatenate.31.refs_7_ = bf16[288,1728]{1,0:T(8,128)(2,1)S(1)} concatenate(bf16[288,576]{1,0:T(8,128)(2,1)S(1)} %copy-done.5, bf16[288,64]{1,0:T(8,128)(2,1)S(1)} %slice-done, bf16[288,512]{1,0:T(8,128)(2,1)S(1)} %slice-done.1, bf16[288,576]{1,0:T(8,128)(2,1)} %param.20), dimensions={1} | concatenate | bytes 1990656 | tf_op jit(solution)/shard_map/concatenate | solution.py:444
  13.0 2.0 %collective-permute-start.6 = (bf16[288,1728]{1,0:T(8,128)(2,1)S(1)}, bf16[288,1728]{1,0:T(8,128)(2,1)S(1)}, u32[]{:S(2)}, u32[]{:S(2)}) collective-permute-start(bf16[288,1728]{1,0:T(8,128)(2,1)S(1)} %concatenate.31.refs_7_), channel_id=1, source_target_pairs={{0,16},{4,20},{8,24},{12,28},{16,0},{20,4},{24,8},{28,12},{1,17},{... | collective-permute-start | bytes 2985992 | tf_op jit(solution)/shard_map/ppermute | solution.py:64
  15.0 1.5 collective-permute-start.5
  18.0 3.0 %dynamic-slice_bitcast_fusion = (bf16[128,576]{1,0:T(8,128)(2,1)}, bf16[128,576]{1,0:T(8,128)(2,1)}, bf16[128,576]{1,0:T(8,128)(2,1)}, bf16[128,576]{1,0:T(8,128...) fusion(bf16[1,128,2304]{2,1,0:T(8,128)(2,1)} %param.16, ...), kind=kLoop, calls=%fused_computation.16 | loop fusion | bytes 2359312 | tf_op jit(solution)/shard_map/dynamic_slice | solution.py:450
  21.8 1.0 pad_maximum_fusion.4
  22.9 1.0 pad_maximum_fusion.2
  24.7 1.3 collective-permute-start.3
  26.0 1.0 fusion.4
  27.5 9.8 %collective-permute-done.6.refs_11_ = bf16[288,1728]{1,0:T(8,128)(2,1)S(1)} collective-permute-done((bf16[288,1728]{1,0:T(8,128)(2,1)S(1)}, bf16[288,1728]{1,0:T(8,128)(2,1)S(1)}, u32[]{:S(2)}, u32[]{:S(2)}) %collective-permute-start.6) | collective-permute-done | bytes 995360 | tf_op jit(solution)/shard_map/ppermute | solution.py:64
  37.4 1.5 collective-permute-done.5.refs_9_
  38.9 1.1 slice.20
  40.0 1.6 %collective-permute-start.7 = (bf16[144,1728]{1,0:T(8,128)(2,1)S(1)}, bf16[144,1728]{1,0:T(8,128)(2,1)S(1)}, u32[]{:S(2)}, u32[]{:S(2)}) collective-permute-start(bf16[144,1728]{1,0:T(8,128)(2,1)S(1)} %slice.21), channel_id=1, source_target_pairs={{0,8},{4,12},{8,0},{12,4},{16,24},{20,28},{24,16},{28,20},{1,9},{5... | collective-permute-start | bytes 1493000 | tf_op jit(solution)/shard_map/ppermute | solution.py:64
  42.0 1.2 pad_maximum_fusion.refs_0_
  43.9 1.3 collective-permute-start.15
  45.2 6.0 %collective-permute-start.13 = (bf16[256,576]{1,0:T(8,128)(2,1)S(1)}, bf16[256,576]{1,0:T(8,128)(2,1)S(1)}, u32[]{:S(2)}, u32[]{:S(2)}) collective-permute-start(bf16[256,576]{1,0:T(8,128)(2,1)S(1)} %pad_maximum_fusion.3), channel_id=1, source_target_pairs={{0,2},{1,3},{2,0},{3,1},{4,6},{5,7},{6,4},{7,5},{8,10},{9,11},{10,... | collective-permute-start | bytes 884744 | tf_op jit(solution)/shard_map/ppermute | solution.py:474
  51.8 1.7 %collective-permute-done.8.refs_15_ = bf16[144,1728]{1,0:T(8,128)(2,1)S(1)} collective-permute-done((bf16[144,1728]{1,0:T(8,128)(2,1)S(1)}, bf16[144,1728]{1,0:T(8,128)(2,1)S(1)}, u32[]{:S(2)}, u32[]{:S(2)}) %collective-permute-start.8) | collective-permute-done | bytes 497696 | tf_op jit(solution)/shard_map/ppermute | solution.py:64
  54.3 9.4 %collective-permute-done.13.refs_2_ = bf16[256,576]{1,0:T(8,128)(2,1)S(1)} collective-permute-done((bf16[256,576]{1,0:T(8,128)(2,1)S(1)}, bf16[256,576]{1,0:T(8,128)(2,1)S(1)}, u32[]{:S(2)}, u32[]{:S(2)}) %collective-permute-start.13) | collective-permute-done | bytes 294944 | tf_op jit(solution)/shard_map/ppermute | solution.py:474
  64.2 1.5 collective-permute-done.15.refs_6_
  65.7 1.5 %collective-permute-done.10.refs_4_ = bf16[288,1152]{1,0:T(8,128)(2,1)S(1)} collective-permute-done((bf16[288,1152]{1,0:T(8,128)(2,1)S(1)}, bf16[288,1152]{1,0:T(8,128)(2,1)S(1)}, u32[]{:S(2)}, u32[]{:S(2)}) %collective-permute-start.10) | collective-permute-done | bytes 663584 | tf_op jit(solution)/shard_map/ppermute | solution.py:64
  67.8 2.2 %collective-permute-done.21.refs_14_ = bf16[144,1728]{1,0:T(8,128)(2,1)S(1)} collective-permute-done((bf16[144,1728]{1,0:T(8,128)(2,1)S(1)}, bf16[144,1728]{1,0:T(8,128)(2,1)S(1)}, u32[]{:S(2)}, u32[]{:S(2)}) %collective-permute-start.21) | collective-permute-done | bytes 497696 | tf_op jit(solution)/shard_map/ppermute | solution.py:64
  70.8 5.6 %collective-permute-start.17 = (bf16[256,576]{1,0:T(8,128)(2,1)S(1)}, bf16[256,576]{1,0:T(8,128)(2,1)S(1)}, u32[]{:S(2)}, u32[]{:S(2)}) collective-permute-start(bf16[256,576]{1,0:T(8,128)(2,1)S(1)} %pad_maximum_fusion.4), channel_id=1, source_target_pairs={{0,3},{1,2},{2,1},{3,0},{4,7},{5,6},{6,5},{7,4},{8,11},{9,10},{10,... | collective-permute-start | bytes 884744 | tf_op jit(solution)/shard_map/ppermute | solution.py:479
  76.3 1.5 collective-permute-start.11
  77.8 1.5 collective-permute-start.12
  79.4 9.1 %qkv.1.refs_4_ = bf16[512,1728]{1,0:T(8,128)(2,1)S(1)} custom-call(s32[4]{0:T(128)S(1)} %pad_add_fusion.scalars, bf16[128,2304]{1,0:T(8,128)(2,1)S(1)} %fusion.2.refs_0_, bf16[128,2304]{1,0:T(8,128)(2,1)} %collective-permute-done.refs_1_, bf16[128,2304]{1,0:T(8,128)(2,1)S(1)} %collective-permute-done.2.refs_2_, ...), custom_call_target="tpu_custom_call" | custom-call | flops 4076863488 | bytes 14680064 | tf_op jit(solution)/shard_map/qkv/pallas_call | solution.py:485
  88.5 2.3 %collective-permute-done.17.refs_3_ = bf16[256,576]{1,0:T(8,128)(2,1)S(1)} collective-permute-done((bf16[256,576]{1,0:T(8,128)(2,1)S(1)}, bf16[256,576]{1,0:T(8,128)(2,1)S(1)}, u32[]{:S(2)}, u32[]{:S(2)}) %collective-permute-start.17) | collective-permute-done | bytes 294944 | tf_op jit(solution)/shard_map/ppermute | solution.py:479
  91.8 9.9 %attention.1 = (bf16[256,576]{1,0:T(8,128)(2,1)S(1)}, bf16[256,576]{1,0:T(8,128)(2,1)S(1)}, bf16[16,576]{1,0:T(8,128)(2,1)S(1)}) custom-call(s32[4]{0:T(128)S(1)} %pad_add_fusion.scalars, bf16[256,576]{1,0:T(8,128)(2,1)S(1)} %pad_maximum_fusion.1.refs_0_, bf16[256,576]{1,0:T(8,128)(2,1)S(1)} %collective-permute-done.16.refs_1_, ...), custom_call_target="tpu_custom_call" | custom-call | flops 905969664 | bytes 4194304 | tf_op jit(solution)/shard_map/attention/pallas_call | solution.py:508
  102.7 1.9 %last_row.1 = f32[8,2304]{1,0:T(8,128)S(1)} custom-call(s32[4]{0:T(128)S(1)} %pad_add_fusion.scalars, bf16[288,1152]{1,0:T(8,128)(2,1)S(1)} %pad_maximum_fusion.refs_0_, bf16[288,1152]{1,0:T(8,128)(2,1)S(1)} %collective-permute-done.23.refs_1_, bf16[288,1152]{1,0:T(8,128)(2,1)S(1)} %collective-permute-done.9.refs_2_, ...), custom_call_target="tpu_custom_call" | custom-call | tf_op jit(solution)/shard_map/last_row/pallas_call | solution.py:533
  104.8 1.1 collective-permute-done.29
  105.9 2.7 %collective-permute-start.32 = (f32[8,2304]{1,0:T(8,128)S(1)}, f32[8,2304]{1,0:T(8,128)S(1)}, u32[]{:S(2)}, u32[]{:S(2)}) collective-permute-start(f32[8,2304]{1,0:T(8,128)S(1)} %add.51.refs_0_), channel_id=1, source_target_pairs={{0,3},{1,2},{2,1},{3,0},{4,7},{5,6},{6,5},{7,4},{8,11},{9,10},{10,... | collective-permute-start | bytes 221192 | tf_op jit(solution)/shard_map/ppermute | solution.py:550
  108.7 1.7 %collective-permute-start.30 = (f32[8,2304]{1,0:T(8,128)S(1)}, f32[8,2304]{1,0:T(8,128)S(1)}, u32[]{:S(2)}, u32[]{:S(2)}) collective-permute-start(f32[8,2304]{1,0:T(8,128)S(1)} %add.51.refs_0_), channel_id=1, source_target_pairs={{0,1},{1,0},{2,3},{3,2},{4,5},{5,4},{6,7},{7,6},{8,9},{9,8},{10,11... | collective-permute-start | bytes 221192 | tf_op jit(solution)/shard_map/ppermute | solution.py:550
  110.4 4.6 %collective-permute-done.28.refs_11_ = bf16[256,576]{1,0:T(8,128)(2,1)S(1)} collective-permute-done((bf16[256,576]{1,0:T(8,128)(2,1)S(1)}, bf16[256,576]{1,0:T(8,128)(2,1)S(1)}, u32[]{:S(2)}, u32[]{:S(2)}) %collective-permute-start.28) | collective-permute-done | bytes 294944 | tf_op jit(solution)/shard_map/ppermute | solution.py:553
  115.0 4.3 %project.1 = (f32[128,2304]{1,0:T(8,128)S(1)}, bf16[128,2304]{1,0:T(8,128)(2,1)S(1)}) custom-call(s32[4]{0:T(128)S(1)} %pad_add_fusion.scalars, bf16[288,1152]{1,0:T(8,128)(2,1)S(1)} %pad_maximum_fusion.refs_0_, bf16[288,1152]{1,0:T(8,128)(2,1)S(1)} %collective-permute-done.23.refs_1_, bf16[288,1152]{1,0:T(8,128)(2,1)S(1)} %collective-permute-done.9.refs_2_, ...), custom_call_target="tpu_custom_call" | custom-call | flops 1358954496 | bytes 8388608 | tf_op jit(solution)/shard_map/project/pallas_call | solution.py:554
  119.6 2.5 %collective-permute-start.36 = (bf16[8,2304]{1,0:T(8,128)(2,1)S(1)}, bf16[8,2304]{1,0:T(8,128)(2,1)S(1)}, u32[]{:S(2)}, u32[]{:S(2)}) collective-permute-start(bf16[8,2304]{1,0:T(8,128)(2,1)S(1)} %final_rows.1.refs_0_), channel_id=1, source_target_pairs={{0,24},{4,28},{8,16},{12,20},{16,8},{20,12},{24,0},{28,4},{1,25},{... | collective-permute-start | bytes 110600 | tf_op jit(solution)/shard_map/ppermute | solution.py:391
  123.1 1.7 %collective-permute-done.36.refs_3_ = bf16[8,2304]{1,0:T(8,128)(2,1)S(1)} collective-permute-done((bf16[8,2304]{1,0:T(8,128)(2,1)S(1)}, bf16[8,2304]{1,0:T(8,128)(2,1)S(1)}, u32[]{:S(2)}, u32[]{:S(2)}) %collective-permute-start.36) | collective-permute-done | bytes 36896 | tf_op jit(solution)/shard_map/ppermute | solution.py:391
  124.8 1.3 collective-permute-done.35.refs_2_
  126.3 7.7 %head.1 = (f32[8,3840]{1,0:T(8,128)S(1)}, f32[8,2]{1,0:T(8,128)S(1)}) custom-call(bf16[8,2304]{1,0:T(8,128)(2,1)S(1)} %final_rows.1.refs_0_, bf16[8,2304]{1,0:T(8,128)(2,1)S(1)} %collective-permute-done.34.refs_1_, bf16[8,2304]{1,0:T(8,128)(2,1)S(1)} %collective-permute-done.35.refs_2_, bf16[8,2304]{1,0:T(8,128)(2,1)S(1)} %collective-permute-done.36.refs_3_, ...), custom_call_target="tpu_custom_call" | custom-call | tf_op jit(solution)/shard_map/head/pallas_call | solution.py:590
  134.0 1.8 %collective-permute-start.39 = (f32[8,2]{1,0:T(8,128)S(1)}, f32[8,2]{1,0:T(8,128)S(1)}, u32[]{:S(2)}, u32[]{:S(2)}) collective-permute-start(f32[8,2]{1,0:T(8,128)S(1)} %get-tuple-element.100.refs_0_), channel_id=1, source_target_pairs={{0,24},{4,28},{8,16},{12,20},{16,8},{20,12},{24,0},{28,4},{1,25},{... | collective-permute-start | bytes 200 | tf_op jit(solution)/shard_map/ppermute | solution.py:391
  136.2 1.3 collective-permute-start.37
  137.5 1.0 collective-permute-done.39.refs_3_
  140.0 1.2 collective-permute-done.40.refs_1_
  141.2 3.6 %collective-permute-done.33 = bf16[128,2304]{1,0:T(8,128)(2,1)S(1)} collective-permute-done((bf16[128,2304]{1,0:T(8,128)(2,1)S(1)}, bf16[128,2304]{1,0:T(8,128)(2,1)S(1)}, u32[]{:S(2)}, u32[]{:S(2)}) %collective-permute-start.33) | collective-permute-done | bytes 589856 | tf_op jit(solution)/shard_map/ppermute | solution.py:573
  144.8 2.2 %collective-permute-start.43 = (f32[8,2]{1,0:T(8,128)S(1)}, f32[8,2]{1,0:T(8,128)S(1)}, u32[]{:S(2)}, u32[]{:S(2)}) collective-permute-start(f32[8,2]{1,0:T(8,128)S(1)} %merge.3.refs_0_), channel_id=1, source_target_pairs={{0,3},{1,2},{2,1},{3,0},{4,7},{5,6},{6,5},{7,4},{8,11},{9,10},{10,... | collective-permute-start | bytes 200 | tf_op jit(solution)/shard_map/ppermute | solution.py:391
  147.0 2.2 %collective-permute-start.41 = (f32[8,2]{1,0:T(8,128)S(1)}, f32[8,2]{1,0:T(8,128)S(1)}, u32[]{:S(2)}, u32[]{:S(2)}) collective-permute-start(f32[8,2]{1,0:T(8,128)S(1)} %merge.3.refs_0_), channel_id=1, source_target_pairs={{0,1},{1,0},{2,3},{3,2},{4,5},{5,4},{6,7},{7,6},{8,9},{9,8},{10,11... | collective-permute-start | bytes 200 | tf_op jit(solution)/shard_map/ppermute | solution.py:391
  150.2 1.3 collective-permute-done.42.refs_2_
  (88 shorter events, 14.2 us)
Async XLA Ops:
  0.6 10.4 %slice-start = ((bf16[288,576]{1,0:T(8,128)(2,1)}), bf16[288,64]{1,0:T(8,128)(2,1)S(1)}, s32[]{:S(2)}) async-start(bf16[288,576]{1,0:T(8,128)(2,1)} %param.19), calls=%async_computation | async-start | bytes 147456 | tf_op jit(solution)/shard_map/slice | solution.py:444
  0.6 10.3 %slice-start.1 = ((bf16[288,576]{1,0:T(8,128)(2,1)}), bf16[288,512]{1,0:T(8,128)(2,1)S(1)}, s32[]{:S(2)}) async-start(bf16[288,576]{1,0:T(8,128)(2,1)} %param.19), calls=%async_computation.1 | async-start | bytes 589824 | tf_op jit(solution)/shard_map/slice | solution.py:444
  3.3 20.7 %collective-permute-start.1 = (bf16[128,2304]{1,0:T(8,128)(2,1)S(1)}, bf16[128,2304]{1,0:T(8,128)(2,1)S(1)}, u32[]{:S(2)}, u32[]{:S(2)}) collective-permute-start(bf16[128,2304]{1,0:T(8,128)(2,1)S(1)} %fusion.2.refs_0_), channel_id=1, source_target_pairs={{1,0},{2,1},{3,2},{5,4},{6,5},{7,6},{9,8},{10,9},{11,10},{13,12},{... | collective-permute-start | bytes 1769480 | tf_op jit(solution)/shard_map/ppermute | solution.py:107
  4.6 19.4 %collective-permute-start = (bf16[128,2304]{1,0:T(8,128)(2,1)S(1)}, bf16[128,2304]{1,0:T(8,128)(2,1)}, u32[]{:S(2)}, u32[]{:S(2)}) collective-permute-start(bf16[128,2304]{1,0:T(8,128)(2,1)S(1)} %fusion.2.refs_0_), channel_id=1, source_target_pairs={{0,1},{1,2},{2,3},{4,5},{5,6},{6,7},{8,9},{9,10},{10,11},{12,13},{... | collective-permute-start | bytes 1769480 | tf_op jit(solution)/shard_map/ppermute | solution.py:106
  13.0 24.3 %collective-permute-start.6 = (bf16[288,1728]{1,0:T(8,128)(2,1)S(1)}, bf16[288,1728]{1,0:T(8,128)(2,1)S(1)}, u32[]{:S(2)}, u32[]{:S(2)}) collective-permute-start(bf16[288,1728]{1,0:T(8,128)(2,1)S(1)} %concatenate.31.refs_7_), channel_id=1, source_target_pairs={{0,16},{4,20},{8,24},{12,28},{16,0},{20,4},{24,8},{28,12},{1,17},{... | collective-permute-start | bytes 2985992 | tf_op jit(solution)/shard_map/ppermute | solution.py:64
  15.0 23.8 %collective-permute-start.5 = (bf16[288,1728]{1,0:T(8,128)(2,1)S(1)}, bf16[288,1728]{1,0:T(8,128)(2,1)}, u32[]{:S(2)}, u32[]{:S(2)}) collective-permute-start(bf16[288,1728]{1,0:T(8,128)(2,1)S(1)} %concatenate.31.refs_7_), channel_id=1, source_target_pairs={{0,8},{4,12},{8,0},{12,4},{16,24},{20,28},{24,16},{28,20},{1,9},{5... | collective-permute-start | bytes 2985992 | tf_op jit(solution)/shard_map/ppermute | solution.py:64
  16.5 25.5 %collective-permute-start.4 = (bf16[288,576]{1,0:T(8,128)(2,1)}, bf16[288,576]{1,0:T(8,128)(2,1)}, u32[]{:S(2)}, u32[]{:S(2)}) collective-permute-start(bf16[288,576]{1,0:T(8,128)(2,1)} %bitcast.28), channel_id=1, source_target_pairs={{0,1},{1,0},{2,3},{3,2},{4,5},{5,4},{6,7},{7,6},{8,9},{9,8},{10,11... | collective-permute-start | bytes 995336 | tf_op jit(solution)/shard_map/ppermute | solution.py:462
  24.0 19.2 %collective-permute-start.2 = (bf16[128,2304]{1,0:T(8,128)(2,1)}, bf16[128,2304]{1,0:T(8,128)(2,1)S(1)}, u32[]{:S(2)}, u32[]{:S(2)}) collective-permute-start(bf16[128,2304]{1,0:T(8,128)(2,1)} %collective-permute-done.refs_1_), channel_id=1, source_target_pairs={{1,2},{2,3},{5,6},{6,7},{9,10},{10,11},{13,14},{14,15},{17,18},{18... | collective-permute-start | bytes 1769480 | tf_op jit(solution)/shard_map/ppermute | solution.py:106
  24.7 18.5 %collective-permute-start.3 = (bf16[128,2304]{1,0:T(8,128)(2,1)S(1)}, bf16[128,2304]{1,0:T(8,128)(2,1)S(1)}, u32[]{:S(2)}, u32[]{:S(2)}) collective-permute-start(bf16[128,2304]{1,0:T(8,128)(2,1)S(1)} %collective-permute-done.1.refs_4_), channel_id=1, source_target_pairs={{1,0},{2,1},{5,4},{6,5},{9,8},{10,9},{13,12},{14,13},{17,16},{18,1... | collective-permute-start | bytes 1769480 | tf_op jit(solution)/shard_map/ppermute | solution.py:107
  27.5 14.5 %copy-start.6 = (bf16[576,288]{0,1:T(8,128)(2,1)S(1)}, bf16[576,288]{0,1:T(8,128)(2,1)}, u32[]{:S(2)}) copy-start(bf16[576,288]{0,1:T(8,128)(2,1)} %param.21) | copy-start | bytes 995332
  40.0 11.8 %collective-permute-start.7 = (bf16[144,1728]{1,0:T(8,128)(2,1)S(1)}, bf16[144,1728]{1,0:T(8,128)(2,1)S(1)}, u32[]{:S(2)}, u32[]{:S(2)}) collective-permute-start(bf16[144,1728]{1,0:T(8,128)(2,1)S(1)} %slice.21), channel_id=1, source_target_pairs={{0,8},{4,12},{8,0},{12,4},{16,24},{20,28},{24,16},{28,20},{1,9},{5... | collective-permute-start | bytes 1493000 | tf_op jit(solution)/shard_map/ppermute | solution.py:64
  41.5 11.9 %collective-permute-start.8 = (bf16[144,1728]{1,0:T(8,128)(2,1)S(1)}, bf16[144,1728]{1,0:T(8,128)(2,1)S(1)}, u32[]{:S(2)}, u32[]{:S(2)}) collective-permute-start(bf16[144,1728]{1,0:T(8,128)(2,1)S(1)} %slice.20), channel_id=1, source_target_pairs={{0,16},{4,20},{8,24},{12,28},{16,0},{20,4},{24,8},{28,12},{1,17},{... | collective-permute-start | bytes 1493000 | tf_op jit(solution)/shard_map/ppermute | solution.py:64
  43.2 20.4 %collective-permute-start.14 = (bf16[128,2304]{1,0:T(8,128)(2,1)S(1)}, bf16[128,2304]{1,0:T(8,128)(2,1)S(1)}, u32[]{:S(2)}, u32[]{:S(2)}) collective-permute-start(bf16[128,2304]{1,0:T(8,128)(2,1)S(1)} %collective-permute-done.2.refs_2_), channel_id=1, source_target_pairs={{2,3},{6,7},{10,11},{14,15},{18,19},{22,23},{26,27},{30,31}} | collective-permute-start | bytes 1769480 | tf_op jit(solution)/shard_map/ppermute | solution.py:106
  43.9 21.7 %collective-permute-start.15 = (bf16[128,2304]{1,0:T(8,128)(2,1)S(1)}, bf16[128,2304]{1,0:T(8,128)(2,1)S(1)}, u32[]{:S(2)}, u32[]{:S(2)}) collective-permute-start(bf16[128,2304]{1,0:T(8,128)(2,1)S(1)} %collective-permute-done.3.refs_5_), channel_id=1, source_target_pairs={{1,0},{5,4},{9,8},{13,12},{17,16},{21,20},{25,24},{29,28}} | collective-permute-start | bytes 1769480 | tf_op jit(solution)/shard_map/ppermute | solution.py:107
  45.2 18.4 %collective-permute-start.13 = (bf16[256,576]{1,0:T(8,128)(2,1)S(1)}, bf16[256,576]{1,0:T(8,128)(2,1)S(1)}, u32[]{:S(2)}, u32[]{:S(2)}) collective-permute-start(bf16[256,576]{1,0:T(8,128)(2,1)S(1)} %pad_maximum_fusion.3), channel_id=1, source_target_pairs={{0,2},{1,3},{2,0},{3,1},{4,6},{5,7},{6,4},{7,5},{8,10},{9,11},{10,... | collective-permute-start | bytes 884744 | tf_op jit(solution)/shard_map/ppermute | solution.py:474
  53.5 13.7 %collective-permute-start.10 = (bf16[288,1152]{1,0:T(8,128)(2,1)S(1)}, bf16[288,1152]{1,0:T(8,128)(2,1)S(1)}, u32[]{:S(2)}, u32[]{:S(2)}) collective-permute-start(bf16[288,1152]{1,0:T(8,128)(2,1)S(1)} %pad_maximum_fusion.refs_0_), channel_id=1, source_target_pairs={{0,16},{4,20},{8,24},{12,28},{16,0},{20,4},{24,8},{28,12},{1,17},{... | collective-permute-start | bytes 1990664 | tf_op jit(solution)/shard_map/ppermute | solution.py:64
  53.6 13.8 %collective-permute-start.9 = (bf16[288,1152]{1,0:T(8,128)(2,1)S(1)}, bf16[288,1152]{1,0:T(8,128)(2,1)S(1)}, u32[]{:S(2)}, u32[]{:S(2)}) collective-permute-start(bf16[288,1152]{1,0:T(8,128)(2,1)S(1)} %pad_maximum_fusion.refs_0_), channel_id=1, source_target_pairs={{0,8},{4,12},{8,0},{12,4},{16,24},{20,28},{24,16},{28,20},{1,9},{5... | collective-permute-start | bytes 1990664 | tf_op jit(solution)/shard_map/ppermute | solution.py:64
  63.7 12.7 %collective-permute-start.18 = (bf16[288,1728]{1,0:T(8,128)(2,1)S(1)}, bf16[288,1728]{1,0:T(8,128)(2,1)S(1)}, u32[]{:S(2)}, u32[]{:S(2)}) collective-permute-start(bf16[288,1728]{1,0:T(8,128)(2,1)S(1)} %concatenate.31.refs_7_), channel_id=1, source_target_pairs={{0,4},{4,0},{8,12},{12,8},{16,20},{20,16},{24,28},{28,24},{1,5},{5... | collective-permute-start | bytes 2985992 | tf_op jit(solution)/shard_map/ppermute | solution.py:64
  63.7 14.2 %collective-permute-start.19 = (bf16[288,1728]{1,0:T(8,128)(2,1)}, bf16[288,1728]{1,0:T(8,128)(2,1)S(1)}, u32[]{:S(2)}, u32[]{:S(2)}) collective-permute-start(bf16[288,1728]{1,0:T(8,128)(2,1)} %collective-permute-done.5.refs_9_), channel_id=1, source_target_pairs={{0,4},{4,0},{8,12},{12,8},{16,20},{20,16},{24,28},{28,24},{1,5},{5... | collective-permute-start | bytes 2985992 | tf_op jit(solution)/shard_map/ppermute | solution.py:64
  65.7 13.7 %collective-permute-start.20 = (bf16[288,1728]{1,0:T(8,128)(2,1)S(1)}, bf16[288,1728]{1,0:T(8,128)(2,1)S(1)}, u32[]{:S(2)}, u32[]{:S(2)}) collective-permute-start(bf16[288,1728]{1,0:T(8,128)(2,1)S(1)} %collective-permute-done.6.refs_11_), channel_id=1, source_target_pairs={{0,4},{4,0},{8,12},{12,8},{16,20},{20,16},{24,28},{28,24},{1,5},{5... | collective-permute-start | bytes 2985992 | tf_op jit(solution)/shard_map/ppermute | solution.py:64
  67.2 2.8 %collective-permute-start.21 = (bf16[144,1728]{1,0:T(8,128)(2,1)S(1)}, bf16[144,1728]{1,0:T(8,128)(2,1)S(1)}, u32[]{:S(2)}, u32[]{:S(2)}) collective-permute-start(bf16[144,1728]{1,0:T(8,128)(2,1)S(1)} %collective-permute-done.7.refs_13_), channel_id=1, source_target_pairs={{0,4},{4,0},{8,12},{12,8},{16,20},{20,16},{24,28},{28,24},{1,5},{5... | collective-permute-start | bytes 1493000 | tf_op jit(solution)/shard_map/ppermute | solution.py:64
  67.4 3.4 %collective-permute-start.22 = (bf16[144,1728]{1,0:T(8,128)(2,1)S(1)}, bf16[144,1728]{1,0:T(8,128)(2,1)S(1)}, u32[]{:S(2)}, u32[]{:S(2)}) collective-permute-start(bf16[144,1728]{1,0:T(8,128)(2,1)S(1)} %collective-permute-done.8.refs_15_), channel_id=1, source_target_pairs={{0,4},{4,0},{8,12},{12,8},{16,20},{20,16},{24,28},{28,24},{1,5},{5... | collective-permute-start | bytes 1493000 | tf_op jit(solution)/shard_map/ppermute | solution.py:64
  70.0 18.5 %collective-permute-start.16 = (bf16[256,576]{1,0:T(8,128)(2,1)S(1)}, bf16[256,576]{1,0:T(8,128)(2,1)S(1)}, u32[]{:S(2)}, u32[]{:S(2)}) collective-permute-start(bf16[256,576]{1,0:T(8,128)(2,1)S(1)} %pad_maximum_fusion.2), channel_id=1, source_target_pairs={{0,1},{1,0},{2,3},{3,2},{4,5},{5,4},{6,7},{7,6},{8,9},{9,8},{10,11... | collective-permute-start | bytes 884744 | tf_op jit(solution)/shard_map/ppermute | solution.py:477
  70.8 20.0 %collective-permute-start.17 = (bf16[256,576]{1,0:T(8,128)(2,1)S(1)}, bf16[256,576]{1,0:T(8,128)(2,1)S(1)}, u32[]{:S(2)}, u32[]{:S(2)}) collective-permute-start(bf16[256,576]{1,0:T(8,128)(2,1)S(1)} %pad_maximum_fusion.4), channel_id=1, source_target_pairs={{0,3},{1,2},{2,1},{3,0},{4,7},{5,6},{6,5},{7,4},{8,11},{9,10},{10,... | collective-permute-start | bytes 884744 | tf_op jit(solution)/shard_map/ppermute | solution.py:479
  76.3 14.4 %collective-permute-start.11 = (bf16[144,1152]{1,0:T(8,128)(2,1)S(1)}, bf16[144,1152]{1,0:T(8,128)(2,1)S(1)}, u32[]{:S(2)}, u32[]{:S(2)}) collective-permute-start(bf16[144,1152]{1,0:T(8,128)(2,1)S(1)} %slice.23), channel_id=1, source_target_pairs={{0,8},{4,12},{8,0},{12,4},{16,24},{20,28},{24,16},{28,20},{1,9},{5... | collective-permute-start | bytes 995336 | tf_op jit(solution)/shard_map/ppermute | solution.py:64
  77.8 12.9 %collective-permute-start.12 = (bf16[144,1152]{1,0:T(8,128)(2,1)S(1)}, bf16[144,1152]{1,0:T(8,128)(2,1)S(1)}, u32[]{:S(2)}, u32[]{:S(2)}) collective-permute-start(bf16[144,1152]{1,0:T(8,128)(2,1)S(1)} %slice.22), channel_id=1, source_target_pairs={{0,16},{4,20},{8,24},{12,28},{16,0},{20,4},{24,8},{28,12},{1,17},{... | collective-permute-start | bytes 995336 | tf_op jit(solution)/shard_map/ppermute | solution.py:64
  88.5 14.2 %copy-start = (bf16[1,128,2304]{2,1,0:T(8,128)(2,1)S(1)}, bf16[1,128,2304]{2,1,0:T(8,128)(2,1)}, u32[]{:S(2)}) copy-start(bf16[1,128,2304]{2,1,0:T(8,128)(2,1)} %param.12) | copy-start | bytes 1769476
  90.8 11.9 %collective-permute-start.23 = (bf16[288,1152]{1,0:T(8,128)(2,1)S(1)}, bf16[288,1152]{1,0:T(8,128)(2,1)S(1)}, u32[]{:S(2)}, u32[]{:S(2)}) collective-permute-start(bf16[288,1152]{1,0:T(8,128)(2,1)S(1)} %pad_maximum_fusion.refs_0_), channel_id=1, source_target_pairs={{0,4},{4,0},{8,12},{12,8},{16,20},{20,16},{24,28},{28,24},{1,5},{5... | collective-permute-start | bytes 1990664 | tf_op jit(solution)/shard_map/ppermute | solution.py:64
  90.8 11.9 %collective-permute-start.24 = (bf16[288,1152]{1,0:T(8,128)(2,1)S(1)}, bf16[288,1152]{1,0:T(8,128)(2,1)S(1)}, u32[]{:S(2)}, u32[]{:S(2)}) collective-permute-start(bf16[288,1152]{1,0:T(8,128)(2,1)S(1)} %collective-permute-done.9.refs_2_), channel_id=1, source_target_pairs={{0,4},{4,0},{8,12},{12,8},{16,20},{20,16},{24,28},{28,24},{1,5},{5... | collective-permute-start | bytes 1990664 | tf_op jit(solution)/shard_map/ppermute | solution.py:64
  91.3 11.4 %collective-permute-start.25 = (bf16[288,1152]{1,0:T(8,128)(2,1)S(1)}, bf16[288,1152]{1,0:T(8,128)(2,1)S(1)}, u32[]{:S(2)}, u32[]{:S(2)}) collective-permute-start(bf16[288,1152]{1,0:T(8,128)(2,1)S(1)} %collective-permute-done.10.refs_4_), channel_id=1, source_target_pairs={{0,4},{4,0},{8,12},{12,8},{16,20},{20,16},{24,28},{28,24},{1,5},{5... | collective-permute-start | bytes 1990664 | tf_op jit(solution)/shard_map/ppermute | solution.py:64
  91.3 10.5 %collective-permute-start.26 = (bf16[144,1152]{1,0:T(8,128)(2,1)S(1)}, bf16[144,1152]{1,0:T(8,128)(2,1)S(1)}, u32[]{:S(2)}, u32[]{:S(2)}) collective-permute-start(bf16[144,1152]{1,0:T(8,128)(2,1)S(1)} %collective-permute-done.11.refs_6_), channel_id=1, source_target_pairs={{0,4},{4,0},{8,12},{12,8},{16,20},{20,16},{24,28},{28,24},{1,5},{5... | collective-permute-start | bytes 995336 | tf_op jit(solution)/shard_map/ppermute | solution.py:64
  91.8 10.9 %collective-permute-start.27 = (bf16[144,1152]{1,0:T(8,128)(2,1)S(1)}, bf16[144,1152]{1,0:T(8,128)(2,1)S(1)}, u32[]{:S(2)}, u32[]{:S(2)}) collective-permute-start(bf16[144,1152]{1,0:T(8,128)(2,1)S(1)} %collective-permute-done.12.refs_8_), channel_id=1, source_target_pairs={{0,4},{4,0},{8,12},{12,8},{16,20},{20,16},{24,28},{28,24},{1,5},{5... | collective-permute-start | bytes 995336 | tf_op jit(solution)/shard_map/ppermute | solution.py:64
  101.8 13.2 %collective-permute-start.28 = (bf16[256,576]{1,0:T(8,128)(2,1)S(1)}, bf16[256,576]{1,0:T(8,128)(2,1)S(1)}, u32[]{:S(2)}, u32[]{:S(2)}) collective-permute-start(bf16[256,576]{1,0:T(8,128)(2,1)S(1)} %get-tuple-element.89), channel_id=1, source_target_pairs={{0,1},{1,0},{2,3},{3,2},{4,5},{5,4},{6,7},{7,6},{8,9},{9,8},{10,11... | collective-permute-start | bytes 884744 | tf_op jit(solution)/shard_map/ppermute | solution.py:553
  104.6 1.3 collective-permute-start.29
  105.9 13.4 %collective-permute-start.32 = (f32[8,2304]{1,0:T(8,128)S(1)}, f32[8,2304]{1,0:T(8,128)S(1)}, u32[]{:S(2)}, u32[]{:S(2)}) collective-permute-start(f32[8,2304]{1,0:T(8,128)S(1)} %add.51.refs_0_), channel_id=1, source_target_pairs={{0,3},{1,2},{2,1},{3,0},{4,7},{5,6},{6,5},{7,4},{8,11},{9,10},{10,... | collective-permute-start | bytes 221192 | tf_op jit(solution)/shard_map/ppermute | solution.py:550
  108.6 10.7 %collective-permute-start.31 = (f32[8,2304]{1,0:T(8,128)S(1)}, f32[8,2304]{1,0:T(8,128)S(1)}, u32[]{:S(2)}, u32[]{:S(2)}) collective-permute-start(f32[8,2304]{1,0:T(8,128)S(1)} %add.51.refs_0_), channel_id=1, source_target_pairs={{0,2},{1,3},{2,0},{3,1},{4,6},{5,7},{6,4},{7,5},{8,10},{9,11},{10,... | collective-permute-start | bytes 221192 | tf_op jit(solution)/shard_map/ppermute | solution.py:550
  108.7 10.6 %collective-permute-start.30 = (f32[8,2304]{1,0:T(8,128)S(1)}, f32[8,2304]{1,0:T(8,128)S(1)}, u32[]{:S(2)}, u32[]{:S(2)}) collective-permute-start(f32[8,2304]{1,0:T(8,128)S(1)} %add.51.refs_0_), channel_id=1, source_target_pairs={{0,1},{1,0},{2,3},{3,2},{4,5},{5,4},{6,7},{7,6},{8,9},{9,8},{10,11... | collective-permute-start | bytes 221192 | tf_op jit(solution)/shard_map/ppermute | solution.py:550
  119.3 25.4 %collective-permute-start.33 = (bf16[128,2304]{1,0:T(8,128)(2,1)S(1)}, bf16[128,2304]{1,0:T(8,128)(2,1)S(1)}, u32[]{:S(2)}, u32[]{:S(2)}) collective-permute-start(bf16[128,2304]{1,0:T(8,128)(2,1)S(1)} %get-tuple-element.94), channel_id=1, source_target_pairs={{0,2},{1,3},{2,0},{3,1},{4,6},{5,7},{6,4},{7,5},{8,10},{9,11},{10,... | collective-permute-start | bytes 1769480 | tf_op jit(solution)/shard_map/ppermute | solution.py:573
  119.6 5.2 %collective-permute-start.36 = (bf16[8,2304]{1,0:T(8,128)(2,1)S(1)}, bf16[8,2304]{1,0:T(8,128)(2,1)S(1)}, u32[]{:S(2)}, u32[]{:S(2)}) collective-permute-start(bf16[8,2304]{1,0:T(8,128)(2,1)S(1)} %final_rows.1.refs_0_), channel_id=1, source_target_pairs={{0,24},{4,28},{8,16},{12,20},{16,8},{20,12},{24,0},{28,4},{1,25},{... | collective-permute-start | bytes 110600 | tf_op jit(solution)/shard_map/ppermute | solution.py:391
  122.1 4.0 %collective-permute-start.35 = (bf16[8,2304]{1,0:T(8,128)(2,1)S(1)}, bf16[8,2304]{1,0:T(8,128)(2,1)S(1)}, u32[]{:S(2)}, u32[]{:S(2)}) collective-permute-start(bf16[8,2304]{1,0:T(8,128)(2,1)S(1)} %final_rows.1.refs_0_), channel_id=1, source_target_pairs={{0,16},{4,20},{8,24},{12,28},{16,0},{20,4},{24,8},{28,12},{1,17},{... | collective-permute-start | bytes 110600 | tf_op jit(solution)/shard_map/ppermute | solution.py:391
  122.3 4.0 %collective-permute-start.34 = (bf16[8,2304]{1,0:T(8,128)(2,1)S(1)}, bf16[8,2304]{1,0:T(8,128)(2,1)S(1)}, u32[]{:S(2)}, u32[]{:S(2)}) collective-permute-start(bf16[8,2304]{1,0:T(8,128)(2,1)S(1)} %final_rows.1.refs_0_), channel_id=1, source_target_pairs={{0,8},{4,12},{8,0},{12,4},{16,24},{20,28},{24,16},{28,20},{1,9},{5... | collective-permute-start | bytes 110600 | tf_op jit(solution)/shard_map/ppermute | solution.py:391
  134.0 4.6 %collective-permute-start.39 = (f32[8,2]{1,0:T(8,128)S(1)}, f32[8,2]{1,0:T(8,128)S(1)}, u32[]{:S(2)}, u32[]{:S(2)}) collective-permute-start(f32[8,2]{1,0:T(8,128)S(1)} %get-tuple-element.100.refs_0_), channel_id=1, source_target_pairs={{0,24},{4,28},{8,16},{12,20},{16,8},{20,12},{24,0},{28,4},{1,25},{... | collective-permute-start | bytes 200 | tf_op jit(solution)/shard_map/ppermute | solution.py:391
  135.7 3.6 %collective-permute-start.38 = (f32[8,2]{1,0:T(8,128)S(1)}, f32[8,2]{1,0:T(8,128)S(1)}, u32[]{:S(2)}, u32[]{:S(2)}) collective-permute-start(f32[8,2]{1,0:T(8,128)S(1)} %get-tuple-element.100.refs_0_), channel_id=1, source_target_pairs={{0,16},{4,20},{8,24},{12,28},{16,0},{20,4},{24,8},{28,12},{1,17},{... | collective-permute-start | bytes 200 | tf_op jit(solution)/shard_map/ppermute | solution.py:391
  136.2 3.6 %collective-permute-start.37 = (f32[8,2]{1,0:T(8,128)S(1)}, f32[8,2]{1,0:T(8,128)S(1)}, u32[]{:S(2)}, u32[]{:S(2)}) collective-permute-start(f32[8,2]{1,0:T(8,128)S(1)} %get-tuple-element.100.refs_0_), channel_id=1, source_target_pairs={{0,8},{4,12},{8,0},{12,4},{16,24},{20,28},{24,16},{28,20},{1,9},{5... | collective-permute-start | bytes 200 | tf_op jit(solution)/shard_map/ppermute | solution.py:391
  139.9 1.2 collective-permute-start.40
  144.8 5.4 %collective-permute-start.43 = (f32[8,2]{1,0:T(8,128)S(1)}, f32[8,2]{1,0:T(8,128)S(1)}, u32[]{:S(2)}, u32[]{:S(2)}) collective-permute-start(f32[8,2]{1,0:T(8,128)S(1)} %merge.3.refs_0_), channel_id=1, source_target_pairs={{0,3},{1,2},{2,1},{3,0},{4,7},{5,6},{6,5},{7,4},{8,11},{9,10},{10,... | collective-permute-start | bytes 200 | tf_op jit(solution)/shard_map/ppermute | solution.py:391
  147.0 4.5 %collective-permute-start.42 = (f32[8,2]{1,0:T(8,128)S(1)}, f32[8,2]{1,0:T(8,128)S(1)}, u32[]{:S(2)}, u32[]{:S(2)}) collective-permute-start(f32[8,2]{1,0:T(8,128)S(1)} %merge.3.refs_0_), channel_id=1, source_target_pairs={{0,2},{1,3},{2,0},{3,1},{4,6},{5,7},{6,4},{7,5},{8,10},{9,11},{10,... | collective-permute-start | bytes 200 | tf_op jit(solution)/shard_map/ppermute | solution.py:391
  147.0 4.5 %collective-permute-start.41 = (f32[8,2]{1,0:T(8,128)S(1)}, f32[8,2]{1,0:T(8,128)S(1)}, u32[]{:S(2)}, u32[]{:S(2)}) collective-permute-start(f32[8,2]{1,0:T(8,128)S(1)} %merge.3.refs_0_), channel_id=1, source_target_pairs={{0,1},{1,0},{2,3},{3,2},{4,5},{5,4},{6,7},{7,6},{8,9},{9,8},{10,11... | collective-permute-start | bytes 200 | tf_op jit(solution)/shard_map/ppermute | solution.py:391
  (5 other events, 23.4 us)

commit v6 on v5

--- a/solution.py
+++ b/solution.py
@@ -252,22 +252,17 @@
                 limit = jnp.minimum(row + 1, count)
                 if wide == 128:
                     zero = jnp.zeros_like(q)
-                    both = jnp.where(
-                        left,
-                        attend_block(
-                            jnp.where(left, q, zero), k_new, v_new, old_k, old_v, limit, length
-                        ),
-                        attend_block(
-                            jnp.where(left, zero, q), k_new, v_new, old_k, old_v, limit, length
-                        ),
+                    stacked = jnp.concatenate(
+                        [jnp.where(left, q, zero), jnp.where(left, zero, q)], axis=0
                     )
+                    limits = jnp.concatenate([limit, limit], axis=0)
+                    got = attend_block(stacked, k_new, v_new, old_k, old_v, limits, length)
+                    both = jnp.where(left, got[:block], got[block:])
                 else:
                     both = attend_block(q, k_new, v_new, old_k, old_v, limit, length)
                 att_scr[begin:stop, pl.ds(lo, wide)] = both.astype(jnp.bfloat16)
 
-        @pl.loop(0, last // 128)
-        def _(pair):
-            lo = pl.multiple_of(pair * 128, 128)
+        for lo in range(0, last, 128):
             heads(lo, lo + width + HEAD_DIM, lo + 2 * width, lo, 128)
 
         heads(last, width, 2 * width + last, last, HEAD_DIM)
@@ -520,7 +515,7 @@
             pltpu.VMEM((span, width), jnp.bfloat16),
             pltpu.SemaphoreType.DMA((2, n_row)),
         ],
-        compiler_params=params(11),
+        compiler_params=params(18),
         cost_estimate=pl.CostEstimate(
             flops=6 * span * span * width, bytes_accessed=4 * 2**20, transcendentals=0
         ),

time: 153 us -> 151 us (0.987)
  Pallas kernels: 34 us -> 31.9 us
    pallas_call x1, Pallas kernels: 9.95 us -> 7.79 us  [on_device(): pl.pallas_call(functools.partial(attention_kernel, n_row), out_shape=(jax...]
  transfers between devices with their start and end apart: 44 -> 44, of which waited for: 23 -> 23; matrix products, arithmetic and copies ran while one was open for 8% -> 8% of each run, Pallas kernels for 22% -> 21%
where the time goes in v6:
time: 151 us; the launch traced here: 150 us
  starting transfers between devices  52.4 us (35%)
  waiting for transfers between devices  48.8 us (32%)
  Pallas kernels  31.9 us (21%)
  other arithmetic  8.42 us (6%)
  local copies, waits for them, and re-layouts  6.25 us (4%)
  between operations  2.41 us (2%)
    ppermute x18, waiting for transfers between devices, send(): return lax.ppermute(array, 'req', xor_pairs(self.size, mask))  18.2 us
    ppermute x9, starting transfers between devices, exchange_all(): lax.ppermute(value, axis, xor_pairs(size, bit * index))  11.5 us
    ppermute x18, starting transfers between devices, send(): return lax.ppermute(array, 'req', xor_pairs(self.size, mask))  11.3 us
    ppermute x1, waiting for transfers between devices, on_device(): across = lax.ppermute(cached[1], 'row', xor_pairs(n_row, 2))  9.42 us
    pallas_call x1, Pallas kernels, on_device(): pl.pallas_call(functools.partial(qkv_kernel, n_row, layout, block_rows),...  9.09 us
    pallas_call x1, Pallas kernels, on_device(): pl.pallas_call(functools.partial(attention_kernel, n_row), out_shape=(jax...  7.79 us
    ppermute x3, starting transfers between devices, gather_line(): up = lax.ppermute(up, 'row', up_pairs(size, 1, step - 1))  7.78 us
    pallas_call x1, Pallas kernels, on_device(): pl.pallas_call(functools.partial(head_kernel, streams), grid=(vocab // (w...  7.67 us
  transfers between devices with their start and end apart: 44, of which 23 were waited for; matrix products, arithmetic and copies ran while one was open for 8% of the time, Pallas kernels for 21%

profile of v6, /device:TPU:0, one launch (start us, length us, event | category | flops | bytes accessed | tf_op | source)
XLA Modules:
  0.0 150.1 jit_solution(4111279130118769803)
XLA Ops:
  0.7 1.3 fusion
  2.0 1.3 fusion.2.refs_0_
  3.3 1.3 collective-permute-start.1
  4.6 6.4 %collective-permute-start = (bf16[128,2304]{1,0:T(8,128)(2,1)S(1)}, bf16[128,2304]{1,0:T(8,128)(2,1)}, u32[]{:S(2)}, u32[]{:S(2)}) collective-permute-start(bf16[128,2304]{1,0:T(8,128)(2,1)S(1)} %fusion.2.refs_0_), channel_id=1, source_target_pairs={{0,1},{1,2},{2,3},{4,5},{5,6},{6,7},{8,9},{9,10},{10,11},{12,13},{... | collective-permute-start | bytes 1769480 | tf_op jit(solution)/shard_map/ppermute | solution.py:106
  11.0 2.0 %concatenate.31.refs_7_ = bf16[288,1728]{1,0:T(8,128)(2,1)S(1)} concatenate(bf16[288,576]{1,0:T(8,128)(2,1)S(1)} %copy-done.5, bf16[288,64]{1,0:T(8,128)(2,1)S(1)} %slice-done, bf16[288,512]{1,0:T(8,128)(2,1)S(1)} %slice-done.1, bf16[288,576]{1,0:T(8,128)(2,1)} %param.20), dimensions={1} | concatenate | bytes 1990656 | tf_op jit(solution)/shard_map/concatenate | solution.py:439
  13.0 2.0 %collective-permute-start.6 = (bf16[288,1728]{1,0:T(8,128)(2,1)S(1)}, bf16[288,1728]{1,0:T(8,128)(2,1)S(1)}, u32[]{:S(2)}, u32[]{:S(2)}) collective-permute-start(bf16[288,1728]{1,0:T(8,128)(2,1)S(1)} %concatenate.31.refs_7_), channel_id=1, source_target_pairs={{0,16},{4,20},{8,24},{12,28},{16,0},{20,4},{24,8},{28,12},{1,17},{... | collective-permute-start | bytes 2985992 | tf_op jit(solution)/shard_map/ppermute | solution.py:64
  15.0 1.5 collective-permute-start.5
  18.0 3.0 %dynamic-slice_bitcast_fusion = (bf16[128,576]{1,0:T(8,128)(2,1)}, bf16[128,576]{1,0:T(8,128)(2,1)}, bf16[128,576]{1,0:T(8,128)(2,1)}, bf16[128,576]{1,0:T(8,128...) fusion(bf16[1,128,2304]{2,1,0:T(8,128)(2,1)} %param.16, ...), kind=kLoop, calls=%fused_computation.16 | loop fusion | bytes 2359312 | tf_op jit(solution)/shard_map/dynamic_slice | solution.py:445
  21.8 1.0 pad_maximum_fusion.4
  22.9 1.0 pad_maximum_fusion.2
  24.7 1.3 collective-permute-start.3
  26.0 1.0 fusion.4
  27.5 9.8 %collective-permute-done.6.refs_11_ = bf16[288,1728]{1,0:T(8,128)(2,1)S(1)} collective-permute-done((bf16[288,1728]{1,0:T(8,128)(2,1)S(1)}, bf16[288,1728]{1,0:T(8,128)(2,1)S(1)}, u32[]{:S(2)}, u32[]{:S(2)}) %collective-permute-start.6) | collective-permute-done | bytes 995360 | tf_op jit(solution)/shard_map/ppermute | solution.py:64
  37.4 1.5 %collective-permute-done.5.refs_9_ = bf16[288,1728]{1,0:T(8,128)(2,1)} collective-permute-done((bf16[288,1728]{1,0:T(8,128)(2,1)S(1)}, bf16[288,1728]{1,0:T(8,128)(2,1)}, u32[]{:S(2)}, u32[]{:S(2)}) %collective-permute-start.5) | collective-permute-done | bytes 995360 | tf_op jit(solution)/shard_map/ppermute | solution.py:64
  38.9 1.1 slice.20
  40.0 1.6 %collective-permute-start.7 = (bf16[144,1728]{1,0:T(8,128)(2,1)S(1)}, bf16[144,1728]{1,0:T(8,128)(2,1)S(1)}, u32[]{:S(2)}, u32[]{:S(2)}) collective-permute-start(bf16[144,1728]{1,0:T(8,128)(2,1)S(1)} %slice.21), channel_id=1, source_target_pairs={{0,8},{4,12},{8,0},{12,4},{16,24},{20,28},{24,16},{28,20},{1,9},{5... | collective-permute-start | bytes 1493000 | tf_op jit(solution)/shard_map/ppermute | solution.py:64
  42.0 1.2 pad_maximum_fusion.refs_0_
  43.9 1.3 collective-permute-start.15
  45.2 6.0 %collective-permute-start.13 = (bf16[256,576]{1,0:T(8,128)(2,1)S(1)}, bf16[256,576]{1,0:T(8,128)(2,1)S(1)}, u32[]{:S(2)}, u32[]{:S(2)}) collective-permute-start(bf16[256,576]{1,0:T(8,128)(2,1)S(1)} %pad_maximum_fusion.3), channel_id=1, source_target_pairs={{0,2},{1,3},{2,0},{3,1},{4,6},{5,7},{6,4},{7,5},{8,10},{9,11},{10,... | collective-permute-start | bytes 884744 | tf_op jit(solution)/shard_map/ppermute | solution.py:469
  51.8 1.7 %collective-permute-done.8.refs_15_ = bf16[144,1728]{1,0:T(8,128)(2,1)S(1)} collective-permute-done((bf16[144,1728]{1,0:T(8,128)(2,1)S(1)}, bf16[144,1728]{1,0:T(8,128)(2,1)S(1)}, u32[]{:S(2)}, u32[]{:S(2)}) %collective-permute-start.8) | collective-permute-done | bytes 497696 | tf_op jit(solution)/shard_map/ppermute | solution.py:64
  54.3 9.4 %collective-permute-done.13.refs_2_ = bf16[256,576]{1,0:T(8,128)(2,1)S(1)} collective-permute-done((bf16[256,576]{1,0:T(8,128)(2,1)S(1)}, bf16[256,576]{1,0:T(8,128)(2,1)S(1)}, u32[]{:S(2)}, u32[]{:S(2)}) %collective-permute-start.13) | collective-permute-done | bytes 294944 | tf_op jit(solution)/shard_map/ppermute | solution.py:469
  64.2 1.5 collective-permute-done.15.refs_6_
  65.7 1.5 %collective-permute-done.10.refs_4_ = bf16[288,1152]{1,0:T(8,128)(2,1)S(1)} collective-permute-done((bf16[288,1152]{1,0:T(8,128)(2,1)S(1)}, bf16[288,1152]{1,0:T(8,128)(2,1)S(1)}, u32[]{:S(2)}, u32[]{:S(2)}) %collective-permute-start.10) | collective-permute-done | bytes 663584 | tf_op jit(solution)/shard_map/ppermute | solution.py:64
  67.8 2.2 %collective-permute-done.21.refs_14_ = bf16[144,1728]{1,0:T(8,128)(2,1)S(1)} collective-permute-done((bf16[144,1728]{1,0:T(8,128)(2,1)S(1)}, bf16[144,1728]{1,0:T(8,128)(2,1)S(1)}, u32[]{:S(2)}, u32[]{:S(2)}) %collective-permute-start.21) | collective-permute-done | bytes 497696 | tf_op jit(solution)/shard_map/ppermute | solution.py:64
  70.8 5.6 %collective-permute-start.17 = (bf16[256,576]{1,0:T(8,128)(2,1)S(1)}, bf16[256,576]{1,0:T(8,128)(2,1)S(1)}, u32[]{:S(2)}, u32[]{:S(2)}) collective-permute-start(bf16[256,576]{1,0:T(8,128)(2,1)S(1)} %pad_maximum_fusion.4), channel_id=1, source_target_pairs={{0,3},{1,2},{2,1},{3,0},{4,7},{5,6},{6,5},{7,4},{8,11},{9,10},{10,... | collective-permute-start | bytes 884744 | tf_op jit(solution)/shard_map/ppermute | solution.py:474
  76.3 1.5 collective-permute-start.11
  77.8 1.5 %collective-permute-start.12 = (bf16[144,1152]{1,0:T(8,128)(2,1)S(1)}, bf16[144,1152]{1,0:T(8,128)(2,1)S(1)}, u32[]{:S(2)}, u32[]{:S(2)}) collective-permute-start(bf16[144,1152]{1,0:T(8,128)(2,1)S(1)} %slice.22), channel_id=1, source_target_pairs={{0,16},{4,20},{8,24},{12,28},{16,0},{20,4},{24,8},{28,12},{1,17},{... | collective-permute-start | bytes 995336 | tf_op jit(solution)/shard_map/ppermute | solution.py:64
  79.4 9.1 %qkv.1.refs_4_ = bf16[512,1728]{1,0:T(8,128)(2,1)S(1)} custom-call(s32[4]{0:T(128)S(1)} %pad_add_fusion.scalars, bf16[128,2304]{1,0:T(8,128)(2,1)S(1)} %fusion.2.refs_0_, bf16[128,2304]{1,0:T(8,128)(2,1)} %collective-permute-done.refs_1_, bf16[128,2304]{1,0:T(8,128)(2,1)S(1)} %collective-permute-done.2.refs_2_, ...), custom_call_target="tpu_custom_call" | custom-call | flops 4076863488 | bytes 14680064 | tf_op jit(solution)/shard_map/qkv/pallas_call | solution.py:480
  88.5 2.3 %collective-permute-done.17.refs_3_ = bf16[256,576]{1,0:T(8,128)(2,1)S(1)} collective-permute-done((bf16[256,576]{1,0:T(8,128)(2,1)S(1)}, bf16[256,576]{1,0:T(8,128)(2,1)S(1)}, u32[]{:S(2)}, u32[]{:S(2)}) %collective-permute-start.17) | collective-permute-done | bytes 294944 | tf_op jit(solution)/shard_map/ppermute | solution.py:474
  91.8 7.8 %attention.1 = (bf16[256,576]{1,0:T(8,128)(2,1)S(1)}, bf16[256,576]{1,0:T(8,128)(2,1)S(1)}, bf16[16,576]{1,0:T(8,128)(2,1)S(1)}) custom-call(s32[4]{0:T(128)S(1)} %pad_add_fusion.scalars, bf16[256,576]{1,0:T(8,128)(2,1)S(1)} %pad_maximum_fusion.1.refs_0_, bf16[256,576]{1,0:T(8,128)(2,1)S(1)} %collective-permute-done.16.refs_1_, ...), custom_call_target="tpu_custom_call" | custom-call | flops 905969664 | bytes 4194304 | tf_op jit(solution)/shard_map/attention/pallas_call | solution.py:503
  100.5 1.9 %last_row.1 = f32[8,2304]{1,0:T(8,128)S(1)} custom-call(s32[4]{0:T(128)S(1)} %pad_add_fusion.scalars, bf16[288,1152]{1,0:T(8,128)(2,1)S(1)} %pad_maximum_fusion.refs_0_, bf16[288,1152]{1,0:T(8,128)(2,1)S(1)} %collective-permute-done.23.refs_1_, bf16[288,1152]{1,0:T(8,128)(2,1)S(1)} %collective-permute-done.9.refs_2_, ...), custom_call_target="tpu_custom_call" | custom-call | tf_op jit(solution)/shard_map/last_row/pallas_call | solution.py:528
  102.6 1.1 collective-permute-done.29
  103.7 2.7 %collective-permute-start.32 = (f32[8,2304]{1,0:T(8,128)S(1)}, f32[8,2304]{1,0:T(8,128)S(1)}, u32[]{:S(2)}, u32[]{:S(2)}) collective-permute-start(f32[8,2304]{1,0:T(8,128)S(1)} %add.51.refs_0_), channel_id=1, source_target_pairs={{0,3},{1,2},{2,1},{3,0},{4,7},{5,6},{6,5},{7,4},{8,11},{9,10},{10,... | collective-permute-start | bytes 221192 | tf_op jit(solution)/shard_map/ppermute | solution.py:545
  106.6 1.6 %collective-permute-start.30 = (f32[8,2304]{1,0:T(8,128)S(1)}, f32[8,2304]{1,0:T(8,128)S(1)}, u32[]{:S(2)}, u32[]{:S(2)}) collective-permute-start(f32[8,2304]{1,0:T(8,128)S(1)} %add.51.refs_0_), channel_id=1, source_target_pairs={{0,1},{1,0},{2,3},{3,2},{4,5},{5,4},{6,7},{7,6},{8,9},{9,8},{10,11... | collective-permute-start | bytes 221192 | tf_op jit(solution)/shard_map/ppermute | solution.py:545
  108.2 4.6 %collective-permute-done.28.refs_11_ = bf16[256,576]{1,0:T(8,128)(2,1)S(1)} collective-permute-done((bf16[256,576]{1,0:T(8,128)(2,1)S(1)}, bf16[256,576]{1,0:T(8,128)(2,1)S(1)}, u32[]{:S(2)}, u32[]{:S(2)}) %collective-permute-start.28) | collective-permute-done | bytes 294944 | tf_op jit(solution)/shard_map/ppermute | solution.py:548
  112.8 4.3 %project.1 = (f32[128,2304]{1,0:T(8,128)S(1)}, bf16[128,2304]{1,0:T(8,128)(2,1)S(1)}) custom-call(s32[4]{0:T(128)S(1)} %pad_add_fusion.scalars, bf16[288,1152]{1,0:T(8,128)(2,1)S(1)} %pad_maximum_fusion.refs_0_, bf16[288,1152]{1,0:T(8,128)(2,1)S(1)} %collective-permute-done.23.refs_1_, bf16[288,1152]{1,0:T(8,128)(2,1)S(1)} %collective-permute-done.9.refs_2_, ...), custom_call_target="tpu_custom_call" | custom-call | flops 1358954496 | bytes 8388608 | tf_op jit(solution)/shard_map/project/pallas_call | solution.py:549
  117.4 2.6 %collective-permute-start.36 = (bf16[8,2304]{1,0:T(8,128)(2,1)S(1)}, bf16[8,2304]{1,0:T(8,128)(2,1)S(1)}, u32[]{:S(2)}, u32[]{:S(2)}) collective-permute-start(bf16[8,2304]{1,0:T(8,128)(2,1)S(1)} %final_rows.1.refs_0_), channel_id=1, source_target_pairs={{0,24},{4,28},{8,16},{12,20},{16,8},{20,12},{24,0},{28,4},{1,25},{... | collective-permute-start | bytes 110600 | tf_op jit(solution)/shard_map/ppermute | solution.py:386
  121.0 1.4 collective-permute-done.36.refs_3_
  122.3 1.6 %collective-permute-done.35.refs_2_ = bf16[8,2304]{1,0:T(8,128)(2,1)S(1)} collective-permute-done((bf16[8,2304]{1,0:T(8,128)(2,1)S(1)}, bf16[8,2304]{1,0:T(8,128)(2,1)S(1)}, u32[]{:S(2)}, u32[]{:S(2)}) %collective-permute-start.35) | collective-permute-done | bytes 36896 | tf_op jit(solution)/shard_map/ppermute | solution.py:386
  124.4 7.7 %head.1 = (f32[8,3840]{1,0:T(8,128)S(1)}, f32[8,2]{1,0:T(8,128)S(1)}) custom-call(bf16[8,2304]{1,0:T(8,128)(2,1)S(1)} %final_rows.1.refs_0_, bf16[8,2304]{1,0:T(8,128)(2,1)S(1)} %collective-permute-done.34.refs_1_, bf16[8,2304]{1,0:T(8,128)(2,1)S(1)} %collective-permute-done.35.refs_2_, bf16[8,2304]{1,0:T(8,128)(2,1)S(1)} %collective-permute-done.36.refs_3_, ...), custom_call_target="tpu_custom_call" | custom-call | tf_op jit(solution)/shard_map/head/pallas_call | solution.py:585
  132.0 1.6 %collective-permute-start.39 = (f32[8,2]{1,0:T(8,128)S(1)}, f32[8,2]{1,0:T(8,128)S(1)}, u32[]{:S(2)}, u32[]{:S(2)}) collective-permute-start(f32[8,2]{1,0:T(8,128)S(1)} %get-tuple-element.100.refs_0_), channel_id=1, source_target_pairs={{0,24},{4,28},{8,16},{12,20},{16,8},{20,12},{24,0},{28,4},{1,25},{... | collective-permute-start | bytes 200 | tf_op jit(solution)/shard_map/ppermute | solution.py:386
  134.1 1.5 collective-permute-start.37
  135.6 1.0 collective-permute-done.39.refs_3_
  137.8 1.2 collective-permute-done.40.refs_1_
  139.0 3.6 %collective-permute-done.33 = bf16[128,2304]{1,0:T(8,128)(2,1)S(1)} collective-permute-done((bf16[128,2304]{1,0:T(8,128)(2,1)S(1)}, bf16[128,2304]{1,0:T(8,128)(2,1)S(1)}, u32[]{:S(2)}, u32[]{:S(2)}) %collective-permute-start.33) | collective-permute-done | bytes 589856 | tf_op jit(solution)/shard_map/ppermute | solution.py:568
  142.6 2.2 %collective-permute-start.43 = (f32[8,2]{1,0:T(8,128)S(1)}, f32[8,2]{1,0:T(8,128)S(1)}, u32[]{:S(2)}, u32[]{:S(2)}) collective-permute-start(f32[8,2]{1,0:T(8,128)S(1)} %merge.3.refs_0_), channel_id=1, source_target_pairs={{0,3},{1,2},{2,1},{3,0},{4,7},{5,6},{6,5},{7,4},{8,11},{9,10},{10,... | collective-permute-start | bytes 200 | tf_op jit(solution)/shard_map/ppermute | solution.py:386
  144.8 2.2 %collective-permute-start.41 = (f32[8,2]{1,0:T(8,128)S(1)}, f32[8,2]{1,0:T(8,128)S(1)}, u32[]{:S(2)}, u32[]{:S(2)}) collective-permute-start(f32[8,2]{1,0:T(8,128)S(1)} %merge.3.refs_0_), channel_id=1, source_target_pairs={{0,1},{1,0},{2,3},{3,2},{4,5},{5,4},{6,7},{7,6},{8,9},{9,8},{10,11... | collective-permute-start | bytes 200 | tf_op jit(solution)/shard_map/ppermute | solution.py:386
  148.0 1.3 collective-permute-done.42.refs_2_
  (88 shorter events, 14.1 us)
Async XLA Ops:
  0.6 10.4 %slice-start = ((bf16[288,576]{1,0:T(8,128)(2,1)}), bf16[288,64]{1,0:T(8,128)(2,1)S(1)}, s32[]{:S(2)}) async-start(bf16[288,576]{1,0:T(8,128)(2,1)} %param.19), calls=%async_computation | async-start | bytes 147456 | tf_op jit(solution)/shard_map/slice | solution.py:439
  0.6 10.3 %slice-start.1 = ((bf16[288,576]{1,0:T(8,128)(2,1)}), bf16[288,512]{1,0:T(8,128)(2,1)S(1)}, s32[]{:S(2)}) async-start(bf16[288,576]{1,0:T(8,128)(2,1)} %param.19), calls=%async_computation.1 | async-start | bytes 589824 | tf_op jit(solution)/shard_map/slice | solution.py:439
  3.3 20.7 %collective-permute-start.1 = (bf16[128,2304]{1,0:T(8,128)(2,1)S(1)}, bf16[128,2304]{1,0:T(8,128)(2,1)S(1)}, u32[]{:S(2)}, u32[]{:S(2)}) collective-permute-start(bf16[128,2304]{1,0:T(8,128)(2,1)S(1)} %fusion.2.refs_0_), channel_id=1, source_target_pairs={{1,0},{2,1},{3,2},{5,4},{6,5},{7,6},{9,8},{10,9},{11,10},{13,12},{... | collective-permute-start | bytes 1769480 | tf_op jit(solution)/shard_map/ppermute | solution.py:107
  4.6 19.4 %collective-permute-start = (bf16[128,2304]{1,0:T(8,128)(2,1)S(1)}, bf16[128,2304]{1,0:T(8,128)(2,1)}, u32[]{:S(2)}, u32[]{:S(2)}) collective-permute-start(bf16[128,2304]{1,0:T(8,128)(2,1)S(1)} %fusion.2.refs_0_), channel_id=1, source_target_pairs={{0,1},{1,2},{2,3},{4,5},{5,6},{6,7},{8,9},{9,10},{10,11},{12,13},{... | collective-permute-start | bytes 1769480 | tf_op jit(solution)/shard_map/ppermute | solution.py:106
  13.0 24.3 %collective-permute-start.6 = (bf16[288,1728]{1,0:T(8,128)(2,1)S(1)}, bf16[288,1728]{1,0:T(8,128)(2,1)S(1)}, u32[]{:S(2)}, u32[]{:S(2)}) collective-permute-start(bf16[288,1728]{1,0:T(8,128)(2,1)S(1)} %concatenate.31.refs_7_), channel_id=1, source_target_pairs={{0,16},{4,20},{8,24},{12,28},{16,0},{20,4},{24,8},{28,12},{1,17},{... | collective-permute-start | bytes 2985992 | tf_op jit(solution)/shard_map/ppermute | solution.py:64
  15.0 23.8 %collective-permute-start.5 = (bf16[288,1728]{1,0:T(8,128)(2,1)S(1)}, bf16[288,1728]{1,0:T(8,128)(2,1)}, u32[]{:S(2)}, u32[]{:S(2)}) collective-permute-start(bf16[288,1728]{1,0:T(8,128)(2,1)S(1)} %concatenate.31.refs_7_), channel_id=1, source_target_pairs={{0,8},{4,12},{8,0},{12,4},{16,24},{20,28},{24,16},{28,20},{1,9},{5... | collective-permute-start | bytes 2985992 | tf_op jit(solution)/shard_map/ppermute | solution.py:64
  16.5 25.5 %collective-permute-start.4 = (bf16[288,576]{1,0:T(8,128)(2,1)}, bf16[288,576]{1,0:T(8,128)(2,1)}, u32[]{:S(2)}, u32[]{:S(2)}) collective-permute-start(bf16[288,576]{1,0:T(8,128)(2,1)} %bitcast.28), channel_id=1, source_target_pairs={{0,1},{1,0},{2,3},{3,2},{4,5},{5,4},{6,7},{7,6},{8,9},{9,8},{10,11... | collective-permute-start | bytes 995336 | tf_op jit(solution)/shard_map/ppermute | solution.py:457
  24.0 19.2 %collective-permute-start.2 = (bf16[128,2304]{1,0:T(8,128)(2,1)}, bf16[128,2304]{1,0:T(8,128)(2,1)S(1)}, u32[]{:S(2)}, u32[]{:S(2)}) collective-permute-start(bf16[128,2304]{1,0:T(8,128)(2,1)} %collective-permute-done.refs_1_), channel_id=1, source_target_pairs={{1,2},{2,3},{5,6},{6,7},{9,10},{10,11},{13,14},{14,15},{17,18},{18... | collective-permute-start | bytes 1769480 | tf_op jit(solution)/shard_map/ppermute | solution.py:106
  24.7 18.5 %collective-permute-start.3 = (bf16[128,2304]{1,0:T(8,128)(2,1)S(1)}, bf16[128,2304]{1,0:T(8,128)(2,1)S(1)}, u32[]{:S(2)}, u32[]{:S(2)}) collective-permute-start(bf16[128,2304]{1,0:T(8,128)(2,1)S(1)} %collective-permute-done.1.refs_4_), channel_id=1, source_target_pairs={{1,0},{2,1},{5,4},{6,5},{9,8},{10,9},{13,12},{14,13},{17,16},{18,1... | collective-permute-start | bytes 1769480 | tf_op jit(solution)/shard_map/ppermute | solution.py:107
  27.5 14.5 %copy-start.6 = (bf16[576,288]{0,1:T(8,128)(2,1)S(1)}, bf16[576,288]{0,1:T(8,128)(2,1)}, u32[]{:S(2)}) copy-start(bf16[576,288]{0,1:T(8,128)(2,1)} %param.21) | copy-start | bytes 995332
  40.0 11.8 %collective-permute-start.7 = (bf16[144,1728]{1,0:T(8,128)(2,1)S(1)}, bf16[144,1728]{1,0:T(8,128)(2,1)S(1)}, u32[]{:S(2)}, u32[]{:S(2)}) collective-permute-start(bf16[144,1728]{1,0:T(8,128)(2,1)S(1)} %slice.21), channel_id=1, source_target_pairs={{0,8},{4,12},{8,0},{12,4},{16,24},{20,28},{24,16},{28,20},{1,9},{5... | collective-permute-start | bytes 1493000 | tf_op jit(solution)/shard_map/ppermute | solution.py:64
  41.5 11.9 %collective-permute-start.8 = (bf16[144,1728]{1,0:T(8,128)(2,1)S(1)}, bf16[144,1728]{1,0:T(8,128)(2,1)S(1)}, u32[]{:S(2)}, u32[]{:S(2)}) collective-permute-start(bf16[144,1728]{1,0:T(8,128)(2,1)S(1)} %slice.20), channel_id=1, source_target_pairs={{0,16},{4,20},{8,24},{12,28},{16,0},{20,4},{24,8},{28,12},{1,17},{... | collective-permute-start | bytes 1493000 | tf_op jit(solution)/shard_map/ppermute | solution.py:64
  43.2 20.4 %collective-permute-start.14 = (bf16[128,2304]{1,0:T(8,128)(2,1)S(1)}, bf16[128,2304]{1,0:T(8,128)(2,1)S(1)}, u32[]{:S(2)}, u32[]{:S(2)}) collective-permute-start(bf16[128,2304]{1,0:T(8,128)(2,1)S(1)} %collective-permute-done.2.refs_2_), channel_id=1, source_target_pairs={{2,3},{6,7},{10,11},{14,15},{18,19},{22,23},{26,27},{30,31}} | collective-permute-start | bytes 1769480 | tf_op jit(solution)/shard_map/ppermute | solution.py:106
  43.9 21.7 %collective-permute-start.15 = (bf16[128,2304]{1,0:T(8,128)(2,1)S(1)}, bf16[128,2304]{1,0:T(8,128)(2,1)S(1)}, u32[]{:S(2)}, u32[]{:S(2)}) collective-permute-start(bf16[128,2304]{1,0:T(8,128)(2,1)S(1)} %collective-permute-done.3.refs_5_), channel_id=1, source_target_pairs={{1,0},{5,4},{9,8},{13,12},{17,16},{21,20},{25,24},{29,28}} | collective-permute-start | bytes 1769480 | tf_op jit(solution)/shard_map/ppermute | solution.py:107
  45.2 18.4 %collective-permute-start.13 = (bf16[256,576]{1,0:T(8,128)(2,1)S(1)}, bf16[256,576]{1,0:T(8,128)(2,1)S(1)}, u32[]{:S(2)}, u32[]{:S(2)}) collective-permute-start(bf16[256,576]{1,0:T(8,128)(2,1)S(1)} %pad_maximum_fusion.3), channel_id=1, source_target_pairs={{0,2},{1,3},{2,0},{3,1},{4,6},{5,7},{6,4},{7,5},{8,10},{9,11},{10,... | collective-permute-start | bytes 884744 | tf_op jit(solution)/shard_map/ppermute | solution.py:469
  53.5 13.7 %collective-permute-start.10 = (bf16[288,1152]{1,0:T(8,128)(2,1)S(1)}, bf16[288,1152]{1,0:T(8,128)(2,1)S(1)}, u32[]{:S(2)}, u32[]{:S(2)}) collective-permute-start(bf16[288,1152]{1,0:T(8,128)(2,1)S(1)} %pad_maximum_fusion.refs_0_), channel_id=1, source_target_pairs={{0,16},{4,20},{8,24},{12,28},{16,0},{20,4},{24,8},{28,12},{1,17},{... | collective-permute-start | bytes 1990664 | tf_op jit(solution)/shard_map/ppermute | solution.py:64
  53.6 13.8 %collective-permute-start.9 = (bf16[288,1152]{1,0:T(8,128)(2,1)S(1)}, bf16[288,1152]{1,0:T(8,128)(2,1)S(1)}, u32[]{:S(2)}, u32[]{:S(2)}) collective-permute-start(bf16[288,1152]{1,0:T(8,128)(2,1)S(1)} %pad_maximum_fusion.refs_0_), channel_id=1, source_target_pairs={{0,8},{4,12},{8,0},{12,4},{16,24},{20,28},{24,16},{28,20},{1,9},{5... | collective-permute-start | bytes 1990664 | tf_op jit(solution)/shard_map/ppermute | solution.py:64
  63.7 12.7 %collective-permute-start.18 = (bf16[288,1728]{1,0:T(8,128)(2,1)S(1)}, bf16[288,1728]{1,0:T(8,128)(2,1)S(1)}, u32[]{:S(2)}, u32[]{:S(2)}) collective-permute-start(bf16[288,1728]{1,0:T(8,128)(2,1)S(1)} %concatenate.31.refs_7_), channel_id=1, source_target_pairs={{0,4},{4,0},{8,12},{12,8},{16,20},{20,16},{24,28},{28,24},{1,5},{5... | collective-permute-start | bytes 2985992 | tf_op jit(solution)/shard_map/ppermute | solution.py:64
  63.7 14.2 %collective-permute-start.19 = (bf16[288,1728]{1,0:T(8,128)(2,1)}, bf16[288,1728]{1,0:T(8,128)(2,1)S(1)}, u32[]{:S(2)}, u32[]{:S(2)}) collective-permute-start(bf16[288,1728]{1,0:T(8,128)(2,1)} %collective-permute-done.5.refs_9_), channel_id=1, source_target_pairs={{0,4},{4,0},{8,12},{12,8},{16,20},{20,16},{24,28},{28,24},{1,5},{5... | collective-permute-start | bytes 2985992 | tf_op jit(solution)/shard_map/ppermute | solution.py:64
  65.7 13.7 %collective-permute-start.20 = (bf16[288,1728]{1,0:T(8,128)(2,1)S(1)}, bf16[288,1728]{1,0:T(8,128)(2,1)S(1)}, u32[]{:S(2)}, u32[]{:S(2)}) collective-permute-start(bf16[288,1728]{1,0:T(8,128)(2,1)S(1)} %collective-permute-done.6.refs_11_), channel_id=1, source_target_pairs={{0,4},{4,0},{8,12},{12,8},{16,20},{20,16},{24,28},{28,24},{1,5},{5... | collective-permute-start | bytes 2985992 | tf_op jit(solution)/shard_map/ppermute | solution.py:64
  67.2 2.8 %collective-permute-start.21 = (bf16[144,1728]{1,0:T(8,128)(2,1)S(1)}, bf16[144,1728]{1,0:T(8,128)(2,1)S(1)}, u32[]{:S(2)}, u32[]{:S(2)}) collective-permute-start(bf16[144,1728]{1,0:T(8,128)(2,1)S(1)} %collective-permute-done.7.refs_13_), channel_id=1, source_target_pairs={{0,4},{4,0},{8,12},{12,8},{16,20},{20,16},{24,28},{28,24},{1,5},{5... | collective-permute-start | bytes 1493000 | tf_op jit(solution)/shard_map/ppermute | solution.py:64
  67.4 3.4 %collective-permute-start.22 = (bf16[144,1728]{1,0:T(8,128)(2,1)S(1)}, bf16[144,1728]{1,0:T(8,128)(2,1)S(1)}, u32[]{:S(2)}, u32[]{:S(2)}) collective-permute-start(bf16[144,1728]{1,0:T(8,128)(2,1)S(1)} %collective-permute-done.8.refs_15_), channel_id=1, source_target_pairs={{0,4},{4,0},{8,12},{12,8},{16,20},{20,16},{24,28},{28,24},{1,5},{5... | collective-permute-start | bytes 1493000 | tf_op jit(solution)/shard_map/ppermute | solution.py:64
  70.0 18.5 %collective-permute-start.16 = (bf16[256,576]{1,0:T(8,128)(2,1)S(1)}, bf16[256,576]{1,0:T(8,128)(2,1)S(1)}, u32[]{:S(2)}, u32[]{:S(2)}) collective-permute-start(bf16[256,576]{1,0:T(8,128)(2,1)S(1)} %pad_maximum_fusion.2), channel_id=1, source_target_pairs={{0,1},{1,0},{2,3},{3,2},{4,5},{5,4},{6,7},{7,6},{8,9},{9,8},{10,11... | collective-permute-start | bytes 884744 | tf_op jit(solution)/shard_map/ppermute | solution.py:472
  70.8 20.0 %collective-permute-start.17 = (bf16[256,576]{1,0:T(8,128)(2,1)S(1)}, bf16[256,576]{1,0:T(8,128)(2,1)S(1)}, u32[]{:S(2)}, u32[]{:S(2)}) collective-permute-start(bf16[256,576]{1,0:T(8,128)(2,1)S(1)} %pad_maximum_fusion.4), channel_id=1, source_target_pairs={{0,3},{1,2},{2,1},{3,0},{4,7},{5,6},{6,5},{7,4},{8,11},{9,10},{10,... | collective-permute-start | bytes 884744 | tf_op jit(solution)/shard_map/ppermute | solution.py:474
  76.3 14.4 %collective-permute-start.11 = (bf16[144,1152]{1,0:T(8,128)(2,1)S(1)}, bf16[144,1152]{1,0:T(8,128)(2,1)S(1)}, u32[]{:S(2)}, u32[]{:S(2)}) collective-permute-start(bf16[144,1152]{1,0:T(8,128)(2,1)S(1)} %slice.23), channel_id=1, source_target_pairs={{0,8},{4,12},{8,0},{12,4},{16,24},{20,28},{24,16},{28,20},{1,9},{5... | collective-permute-start | bytes 995336 | tf_op jit(solution)/shard_map/ppermute | solution.py:64
  77.8 12.9 %collective-permute-start.12 = (bf16[144,1152]{1,0:T(8,128)(2,1)S(1)}, bf16[144,1152]{1,0:T(8,128)(2,1)S(1)}, u32[]{:S(2)}, u32[]{:S(2)}) collective-permute-start(bf16[144,1152]{1,0:T(8,128)(2,1)S(1)} %slice.22), channel_id=1, source_target_pairs={{0,16},{4,20},{8,24},{12,28},{16,0},{20,4},{24,8},{28,12},{1,17},{... | collective-permute-start | bytes 995336 | tf_op jit(solution)/shard_map/ppermute | solution.py:64
  88.5 12.0 %copy-start = (bf16[1,128,2304]{2,1,0:T(8,128)(2,1)S(1)}, bf16[1,128,2304]{2,1,0:T(8,128)(2,1)}, u32[]{:S(2)}) copy-start(bf16[1,128,2304]{2,1,0:T(8,128)(2,1)} %param.12) | copy-start | bytes 1769476
  90.8 9.7 %collective-permute-start.23 = (bf16[288,1152]{1,0:T(8,128)(2,1)S(1)}, bf16[288,1152]{1,0:T(8,128)(2,1)S(1)}, u32[]{:S(2)}, u32[]{:S(2)}) collective-permute-start(bf16[288,1152]{1,0:T(8,128)(2,1)S(1)} %pad_maximum_fusion.refs_0_), channel_id=1, source_target_pairs={{0,4},{4,0},{8,12},{12,8},{16,20},{20,16},{24,28},{28,24},{1,5},{5... | collective-permute-start | bytes 1990664 | tf_op jit(solution)/shard_map/ppermute | solution.py:64
  90.8 9.7 %collective-permute-start.24 = (bf16[288,1152]{1,0:T(8,128)(2,1)S(1)}, bf16[288,1152]{1,0:T(8,128)(2,1)S(1)}, u32[]{:S(2)}, u32[]{:S(2)}) collective-permute-start(bf16[288,1152]{1,0:T(8,128)(2,1)S(1)} %collective-permute-done.9.refs_2_), channel_id=1, source_target_pairs={{0,4},{4,0},{8,12},{12,8},{16,20},{20,16},{24,28},{28,24},{1,5},{5... | collective-permute-start | bytes 1990664 | tf_op jit(solution)/shard_map/ppermute | solution.py:64
  91.3 9.2 %collective-permute-start.25 = (bf16[288,1152]{1,0:T(8,128)(2,1)S(1)}, bf16[288,1152]{1,0:T(8,128)(2,1)S(1)}, u32[]{:S(2)}, u32[]{:S(2)}) collective-permute-start(bf16[288,1152]{1,0:T(8,128)(2,1)S(1)} %collective-permute-done.10.refs_4_), channel_id=1, source_target_pairs={{0,4},{4,0},{8,12},{12,8},{16,20},{20,16},{24,28},{28,24},{1,5},{5... | collective-permute-start | bytes 1990664 | tf_op jit(solution)/shard_map/ppermute | solution.py:64
  91.3 8.3 %collective-permute-start.26 = (bf16[144,1152]{1,0:T(8,128)(2,1)S(1)}, bf16[144,1152]{1,0:T(8,128)(2,1)S(1)}, u32[]{:S(2)}, u32[]{:S(2)}) collective-permute-start(bf16[144,1152]{1,0:T(8,128)(2,1)S(1)} %collective-permute-done.11.refs_6_), channel_id=1, source_target_pairs={{0,4},{4,0},{8,12},{12,8},{16,20},{20,16},{24,28},{28,24},{1,5},{5... | collective-permute-start | bytes 995336 | tf_op jit(solution)/shard_map/ppermute | solution.py:64
  91.8 8.7 %collective-permute-start.27 = (bf16[144,1152]{1,0:T(8,128)(2,1)S(1)}, bf16[144,1152]{1,0:T(8,128)(2,1)S(1)}, u32[]{:S(2)}, u32[]{:S(2)}) collective-permute-start(bf16[144,1152]{1,0:T(8,128)(2,1)S(1)} %collective-permute-done.12.refs_8_), channel_id=1, source_target_pairs={{0,4},{4,0},{8,12},{12,8},{16,20},{20,16},{24,28},{28,24},{1,5},{5... | collective-permute-start | bytes 995336 | tf_op jit(solution)/shard_map/ppermute | solution.py:64
  99.7 13.2 %collective-permute-start.28 = (bf16[256,576]{1,0:T(8,128)(2,1)S(1)}, bf16[256,576]{1,0:T(8,128)(2,1)S(1)}, u32[]{:S(2)}, u32[]{:S(2)}) collective-permute-start(bf16[256,576]{1,0:T(8,128)(2,1)S(1)} %get-tuple-element.89), channel_id=1, source_target_pairs={{0,1},{1,0},{2,3},{3,2},{4,5},{5,4},{6,7},{7,6},{8,9},{9,8},{10,11... | collective-permute-start | bytes 884744 | tf_op jit(solution)/shard_map/ppermute | solution.py:548
  102.4 1.3 collective-permute-start.29
  103.7 13.4 %collective-permute-start.32 = (f32[8,2304]{1,0:T(8,128)S(1)}, f32[8,2304]{1,0:T(8,128)S(1)}, u32[]{:S(2)}, u32[]{:S(2)}) collective-permute-start(f32[8,2304]{1,0:T(8,128)S(1)} %add.51.refs_0_), channel_id=1, source_target_pairs={{0,3},{1,2},{2,1},{3,0},{4,7},{5,6},{6,5},{7,4},{8,11},{9,10},{10,... | collective-permute-start | bytes 221192 | tf_op jit(solution)/shard_map/ppermute | solution.py:545
  106.4 10.7 %collective-permute-start.31 = (f32[8,2304]{1,0:T(8,128)S(1)}, f32[8,2304]{1,0:T(8,128)S(1)}, u32[]{:S(2)}, u32[]{:S(2)}) collective-permute-start(f32[8,2304]{1,0:T(8,128)S(1)} %add.51.refs_0_), channel_id=1, source_target_pairs={{0,2},{1,3},{2,0},{3,1},{4,6},{5,7},{6,4},{7,5},{8,10},{9,11},{10,... | collective-permute-start | bytes 221192 | tf_op jit(solution)/shard_map/ppermute | solution.py:545
  106.6 10.6 %collective-permute-start.30 = (f32[8,2304]{1,0:T(8,128)S(1)}, f32[8,2304]{1,0:T(8,128)S(1)}, u32[]{:S(2)}, u32[]{:S(2)}) collective-permute-start(f32[8,2304]{1,0:T(8,128)S(1)} %add.51.refs_0_), channel_id=1, source_target_pairs={{0,1},{1,0},{2,3},{3,2},{4,5},{5,4},{6,7},{7,6},{8,9},{9,8},{10,11... | collective-permute-start | bytes 221192 | tf_op jit(solution)/shard_map/ppermute | solution.py:545
  117.2 25.4 %collective-permute-start.33 = (bf16[128,2304]{1,0:T(8,128)(2,1)S(1)}, bf16[128,2304]{1,0:T(8,128)(2,1)S(1)}, u32[]{:S(2)}, u32[]{:S(2)}) collective-permute-start(bf16[128,2304]{1,0:T(8,128)(2,1)S(1)} %get-tuple-element.94), channel_id=1, source_target_pairs={{0,2},{1,3},{2,0},{3,1},{4,6},{5,7},{6,4},{7,5},{8,10},{9,11},{10,... | collective-permute-start | bytes 1769480 | tf_op jit(solution)/shard_map/ppermute | solution.py:568
  117.4 4.9 %collective-permute-start.36 = (bf16[8,2304]{1,0:T(8,128)(2,1)S(1)}, bf16[8,2304]{1,0:T(8,128)(2,1)S(1)}, u32[]{:S(2)}, u32[]{:S(2)}) collective-permute-start(bf16[8,2304]{1,0:T(8,128)(2,1)S(1)} %final_rows.1.refs_0_), channel_id=1, source_target_pairs={{0,24},{4,28},{8,16},{12,20},{16,8},{20,12},{24,0},{28,4},{1,25},{... | collective-permute-start | bytes 110600 | tf_op jit(solution)/shard_map/ppermute | solution.py:386
  120.0 4.0 %collective-permute-start.35 = (bf16[8,2304]{1,0:T(8,128)(2,1)S(1)}, bf16[8,2304]{1,0:T(8,128)(2,1)S(1)}, u32[]{:S(2)}, u32[]{:S(2)}) collective-permute-start(bf16[8,2304]{1,0:T(8,128)(2,1)S(1)} %final_rows.1.refs_0_), channel_id=1, source_target_pairs={{0,16},{4,20},{8,24},{12,28},{16,0},{20,4},{24,8},{28,12},{1,17},{... | collective-permute-start | bytes 110600 | tf_op jit(solution)/shard_map/ppermute | solution.py:386
  120.4 4.0 %collective-permute-start.34 = (bf16[8,2304]{1,0:T(8,128)(2,1)S(1)}, bf16[8,2304]{1,0:T(8,128)(2,1)S(1)}, u32[]{:S(2)}, u32[]{:S(2)}) collective-permute-start(bf16[8,2304]{1,0:T(8,128)(2,1)S(1)} %final_rows.1.refs_0_), channel_id=1, source_target_pairs={{0,8},{4,12},{8,0},{12,4},{16,24},{20,28},{24,16},{28,20},{1,9},{5... | collective-permute-start | bytes 110600 | tf_op jit(solution)/shard_map/ppermute | solution.py:386
  132.0 4.6 %collective-permute-start.39 = (f32[8,2]{1,0:T(8,128)S(1)}, f32[8,2]{1,0:T(8,128)S(1)}, u32[]{:S(2)}, u32[]{:S(2)}) collective-permute-start(f32[8,2]{1,0:T(8,128)S(1)} %get-tuple-element.100.refs_0_), channel_id=1, source_target_pairs={{0,24},{4,28},{8,16},{12,20},{16,8},{20,12},{24,0},{28,4},{1,25},{... | collective-permute-start | bytes 200 | tf_op jit(solution)/shard_map/ppermute | solution.py:386
  133.6 3.6 %collective-permute-start.38 = (f32[8,2]{1,0:T(8,128)S(1)}, f32[8,2]{1,0:T(8,128)S(1)}, u32[]{:S(2)}, u32[]{:S(2)}) collective-permute-start(f32[8,2]{1,0:T(8,128)S(1)} %get-tuple-element.100.refs_0_), channel_id=1, source_target_pairs={{0,16},{4,20},{8,24},{12,28},{16,0},{20,4},{24,8},{28,12},{1,17},{... | collective-permute-start | bytes 200 | tf_op jit(solution)/shard_map/ppermute | solution.py:386
  134.1 3.6 %collective-permute-start.37 = (f32[8,2]{1,0:T(8,128)S(1)}, f32[8,2]{1,0:T(8,128)S(1)}, u32[]{:S(2)}, u32[]{:S(2)}) collective-permute-start(f32[8,2]{1,0:T(8,128)S(1)} %get-tuple-element.100.refs_0_), channel_id=1, source_target_pairs={{0,8},{4,12},{8,0},{12,4},{16,24},{20,28},{24,16},{28,20},{1,9},{5... | collective-permute-start | bytes 200 | tf_op jit(solution)/shard_map/ppermute | solution.py:386
  137.8 1.2 collective-permute-start.40
  142.6 5.4 %collective-permute-start.43 = (f32[8,2]{1,0:T(8,128)S(1)}, f32[8,2]{1,0:T(8,128)S(1)}, u32[]{:S(2)}, u32[]{:S(2)}) collective-permute-start(f32[8,2]{1,0:T(8,128)S(1)} %merge.3.refs_0_), channel_id=1, source_target_pairs={{0,3},{1,2},{2,1},{3,0},{4,7},{5,6},{6,5},{7,4},{8,11},{9,10},{10,... | collective-permute-start | bytes 200 | tf_op jit(solution)/shard_map/ppermute | solution.py:386
  144.8 4.5 %collective-permute-start.42 = (f32[8,2]{1,0:T(8,128)S(1)}, f32[8,2]{1,0:T(8,128)S(1)}, u32[]{:S(2)}, u32[]{:S(2)}) collective-permute-start(f32[8,2]{1,0:T(8,128)S(1)} %merge.3.refs_0_), channel_id=1, source_target_pairs={{0,2},{1,3},{2,0},{3,1},{4,6},{5,7},{6,4},{7,5},{8,10},{9,11},{10,... | collective-permute-start | bytes 200 | tf_op jit(solution)/shard_map/ppermute | solution.py:386
  144.8 4.5 %collective-permute-start.41 = (f32[8,2]{1,0:T(8,128)S(1)}, f32[8,2]{1,0:T(8,128)S(1)}, u32[]{:S(2)}, u32[]{:S(2)}) collective-permute-start(f32[8,2]{1,0:T(8,128)S(1)} %merge.3.refs_0_), channel_id=1, source_target_pairs={{0,1},{1,0},{2,3},{3,2},{4,5},{5,4},{6,7},{7,6},{8,9},{9,8},{10,11... | collective-permute-start | bytes 200 | tf_op jit(solution)/shard_map/ppermute | solution.py:386
  (5 other events, 23.4 us)

commit v7 on v6

--- a/solution.py
+++ b/solution.py
@@ -156,6 +156,11 @@
 
         waits.append(below)
     return waits
+
+
+def norm_kernel(in_ref, gain_ref, out_ref):
+    rows = rms_scale(in_ref[...].astype(jnp.float32), gain_ref[...][None])
+    out_ref[...] = rows.astype(jnp.bfloat16)
 
 
 def qkv_kernel(size, layout, block_rows, scalars, *refs):
@@ -308,7 +313,7 @@
     for copy in copies:
         copy.wait()
     width = last_ref.shape[1]
-    here = lax.broadcasted_iota(jnp.int32, (out_ref.shape[0], 256), 0) == scalars[1]
+    here = lax.broadcasted_iota(jnp.int32, (out_ref.shape[0], 256), 0) == lax.rem(scalars[1], 2)
     for tile in range(0, out_ref.shape[1], 256):
         share = lax.dot_general(
             last_ref[...],
@@ -320,10 +325,13 @@
         out_ref[:, tile : tile + 256] = jnp.where(here, row, 0.0)
 
 
-def final_rows_kernel(*refs):
+def final_rows_kernel(scalars, *refs):
     shares, (gain_ref, table_ref) = refs[:-2], refs[-2:]
     rows = add_all(*[ref[...] for ref in shares]).astype(jnp.bfloat16).astype(jnp.float32)
-    table_ref[...] = rms_scale(rows, gain_ref[...][None]).astype(jnp.bfloat16)
+    rows = rms_scale(rows, gain_ref[...][None]).astype(jnp.bfloat16).astype(jnp.float32)
+    at = lax.broadcasted_iota(jnp.int32, table_ref.shape, 0) - lax.div(scalars[1], 2) * 2
+    table = jnp.where(at == 0, rows[0:1], jnp.where(at == 1, rows[1:2], 0.0))
+    table_ref[...] = table.astype(jnp.bfloat16)
 
 
 def merge_kernel(*refs):
@@ -434,7 +442,13 @@
     length, count = cache_len[0], new_count[0]
     scalars = jnp.stack([me_row, me_req, length, count]).astype(jnp.int32)
 
-    normed = rms_scale(inputs.astype(jnp.float32), attn_gain).astype(jnp.bfloat16)
+    normed = pl.pallas_call(
+        norm_kernel,
+        out_shape=jax.ShapeDtypeStruct(inputs.shape, jnp.bfloat16),
+        compiler_params=params(6),
+        cost_estimate=FREE,
+        name="norm",
+    )(inputs, attn_gain)
     last = width - HEAD_DIM
     joined = jnp.concatenate([w_query, w_key[:, last:], w_key[:, :last], w_value], axis=1)
 
@@ -527,7 +541,7 @@
     own_columns = -(-width // 128) * 128
     share = pl.pallas_call(
         functools.partial(last_row_kernel, out_layout, block_rows),
-        out_shape=jax.ShapeDtypeStruct((n_req, model), jnp.float32),
+        out_shape=jax.ShapeDtypeStruct((2, model), jnp.float32),
         in_specs=[SMEM] + [HBM] * len(out_weights) + [VMEM] * 2,
         out_specs=VMEM,
         scratch_shapes=[
@@ -571,10 +585,12 @@
     table = pl.pallas_call(
         final_rows_kernel,
         out_shape=jax.ShapeDtypeStruct((n_req, model), jnp.bfloat16),
+        in_specs=[SMEM] + [VMEM] * (n_row + 1),
+        out_specs=VMEM,
         compiler_params=params(4),
         cost_estimate=FREE,
         name="final_rows",
-    )(*shares, final_gain)
+    )(scalars, *shares, final_gain)
     tables = exchange_all(table, "req", n_req, 2, add_all)
     vocab = head_weight.shape[1]
     wide, streams = 256, 5

time: 151 us -> 150 us (level)
  waiting for transfers between devices: 48.8 us -> 44.3 us
  other arithmetic: 8.42 us -> 5.79 us
  Pallas kernels: 31.9 us -> 34.2 us
  starting transfers between devices: 52.4 us -> 54.6 us
  local copies, waits for them, and re-layouts: 6.25 us -> 8 us
    ppermute x1, waiting for transfers between devices: 4.64 us -> 0.15 us  [on_device(): got = after(lax.ppermute(send, 'row', xor_pairs(n_row, 1)), share)]
    ppermute x1, starting transfers between devices: 0.07 us -> 2.37 us  [on_device(): others = lax.ppermute(mate_part, 'row', xor_pairs(n_row, 2))]
    unnamed x14 -> x18, local copies, waits for them, and re-layouts: 0.03 us -> 1.8 us
    pallas_call x1, Pallas kernels: 7.79 us -> 9.31 us  [on_device(): pl.pallas_call(functools.partial(attention_kernel, n_row), out_shape=(jax...]
  transfers between devices with their start and end apart: 44 -> 44, of which waited for: 23 -> 23; matrix products, arithmetic and copies ran while one was open for 8% -> 8% of each run, Pallas kernels for 21% -> 22%
where the time goes in v7:
time: 150 us; the launch traced here: 149 us
  starting transfers between devices  54.6 us (36%)
  waiting for transfers between devices  44.3 us (30%)
  Pallas kernels  34.2 us (23%)
  local copies, waits for them, and re-layouts  8 us (5%)
  other arithmetic  5.79 us (4%)
  between operations  2.4 us (2%)
    ppermute x18, waiting for transfers between devices, send(): return lax.ppermute(array, 'req', xor_pairs(self.size, mask))  18.3 us
    ppermute x9, starting transfers between devices, exchange_all(): lax.ppermute(value, axis, xor_pairs(size, bit * index))  11.5 us
    ppermute x18, starting transfers between devices, send(): return lax.ppermute(array, 'req', xor_pairs(self.size, mask))  11.3 us
    ppermute x1, waiting for transfers between devices, on_device(): across = lax.ppermute(cached[1], 'row', xor_pairs(n_row, 2))  9.42 us
    pallas_call x1, Pallas kernels, on_device(): pl.pallas_call(functools.partial(attention_kernel, n_row), out_shape=(jax...  9.31 us
    pallas_call x1, Pallas kernels, on_device(): pl.pallas_call(functools.partial(qkv_kernel, n_row, layout, block_rows),...  9.09 us
    ppermute x3, starting transfers between devices, gather_line(): up = lax.ppermute(up, 'row', up_pairs(size, 1, step - 1))  7.78 us
    pallas_call x1, Pallas kernels, on_device(): pl.pallas_call(functools.partial(head_kernel, streams), grid=(vocab // (w...  7.67 us
  transfers between devices with their start and end apart: 44, of which 23 were waited for; matrix products, arithmetic and copies ran while one was open for 8% of the time, Pallas kernels for 22%

profile of v7, /device:TPU:0, one launch (start us, length us, event | category | flops | bytes accessed | tf_op | source)
XLA Modules:
  0.0 149.2 jit_solution(725353170551164648)
XLA Ops:
  0.6 1.1 copy-done
  2.6 1.3 collective-permute-start.1
  4.0 6.4 %collective-permute-start = (bf16[128,2304]{1,0:T(8,128)(2,1)S(1)}, bf16[128,2304]{1,0:T(8,128)(2,1)}, u32[]{:S(2)}, u32[]{:S(2)}) collective-permute-start(bf16[128,2304]{1,0:T(8,128)(2,1)S(1)} %norm.1.refs_0_), channel_id=1, source_target_pairs={{0,1},{1,2},{2,3},{4,5},{5,6},{6,7},{8,9},{9,10},{10,11},{12,13},{... | collective-permute-start | bytes 1769480 | tf_op jit(solution)/shard_map/ppermute | solution.py:106
  10.3 2.0 %concatenate.31.refs_7_ = bf16[288,1728]{1,0:T(8,128)(2,1)S(1)} concatenate(bf16[288,576]{1,0:T(8,128)(2,1)S(1)} %copy-done.7, bf16[288,64]{1,0:T(8,128)(2,1)S(1)} %slice-done, bf16[288,512]{1,0:T(8,128)(2,1)S(1)} %slice-done.1, bf16[288,576]{1,0:T(8,128)(2,1)} %param.20), dimensions={1} | concatenate | bytes 1990656 | tf_op jit(solution)/shard_map/concatenate | solution.py:453
  12.4 2.0 %collective-permute-start.6 = (bf16[288,1728]{1,0:T(8,128)(2,1)S(1)}, bf16[288,1728]{1,0:T(8,128)(2,1)S(1)}, u32[]{:S(2)}, u32[]{:S(2)}) collective-permute-start(bf16[288,1728]{1,0:T(8,128)(2,1)S(1)} %concatenate.31.refs_7_), channel_id=1, source_target_pairs={{0,16},{4,20},{8,24},{12,28},{16,0},{20,4},{24,8},{28,12},{1,17},{... | collective-permute-start | bytes 2985992 | tf_op jit(solution)/shard_map/ppermute | solution.py:64
  14.4 1.5 collective-permute-start.5
  17.4 3.0 %dynamic-slice_bitcast_fusion = (bf16[128,576]{1,0:T(8,128)(2,1)}, bf16[128,576]{1,0:T(8,128)(2,1)}, bf16[128,576]{1,0:T(8,128)(2,1)}, bf16[128,576]{1,0:T(8,128...) fusion(bf16[1,128,2304]{2,1,0:T(8,128)(2,1)} %param.16, ...), kind=kLoop, calls=%fused_computation.11 | loop fusion | bytes 2359312 | tf_op jit(solution)/shard_map/dynamic_slice | solution.py:459
  21.2 1.0 pad_maximum_fusion.4
  22.2 1.0 pad_maximum_fusion.2
  24.1 1.3 collective-permute-start.3
  25.4 1.0 fusion.1
  26.9 9.8 %collective-permute-done.6.refs_11_ = bf16[288,1728]{1,0:T(8,128)(2,1)S(1)} collective-permute-done((bf16[288,1728]{1,0:T(8,128)(2,1)S(1)}, bf16[288,1728]{1,0:T(8,128)(2,1)S(1)}, u32[]{:S(2)}, u32[]{:S(2)}) %collective-permute-start.6) | collective-permute-done | bytes 995360 | tf_op jit(solution)/shard_map/ppermute | solution.py:64
  36.7 1.5 %collective-permute-done.5.refs_9_ = bf16[288,1728]{1,0:T(8,128)(2,1)} collective-permute-done((bf16[288,1728]{1,0:T(8,128)(2,1)S(1)}, bf16[288,1728]{1,0:T(8,128)(2,1)}, u32[]{:S(2)}, u32[]{:S(2)}) %collective-permute-start.5) | collective-permute-done | bytes 995360 | tf_op jit(solution)/shard_map/ppermute | solution.py:64
  38.2 1.1 slice.20
  39.3 1.6 %collective-permute-start.7 = (bf16[144,1728]{1,0:T(8,128)(2,1)S(1)}, bf16[144,1728]{1,0:T(8,128)(2,1)S(1)}, u32[]{:S(2)}, u32[]{:S(2)}) collective-permute-start(bf16[144,1728]{1,0:T(8,128)(2,1)S(1)} %slice.21), channel_id=1, source_target_pairs={{0,8},{4,12},{8,0},{12,4},{16,24},{20,28},{24,16},{28,20},{1,9},{5... | collective-permute-start | bytes 1493000 | tf_op jit(solution)/shard_map/ppermute | solution.py:64
  41.4 1.2 pad_maximum_fusion.refs_0_
  43.3 1.3 collective-permute-start.15
  44.6 6.0 %collective-permute-start.13 = (bf16[256,576]{1,0:T(8,128)(2,1)S(1)}, bf16[256,576]{1,0:T(8,128)(2,1)S(1)}, u32[]{:S(2)}, u32[]{:S(2)}) collective-permute-start(bf16[256,576]{1,0:T(8,128)(2,1)S(1)} %pad_maximum_fusion.3), channel_id=1, source_target_pairs={{0,2},{1,3},{2,0},{3,1},{4,6},{5,7},{6,4},{7,5},{8,10},{9,11},{10,... | collective-permute-start | bytes 884744 | tf_op jit(solution)/shard_map/ppermute | solution.py:483
  51.1 1.7 %collective-permute-done.8.refs_15_ = bf16[144,1728]{1,0:T(8,128)(2,1)S(1)} collective-permute-done((bf16[144,1728]{1,0:T(8,128)(2,1)S(1)}, bf16[144,1728]{1,0:T(8,128)(2,1)S(1)}, u32[]{:S(2)}, u32[]{:S(2)}) %collective-permute-start.8) | collective-permute-done | bytes 497696 | tf_op jit(solution)/shard_map/ppermute | solution.py:64
  53.6 9.4 %collective-permute-done.13.refs_2_ = bf16[256,576]{1,0:T(8,128)(2,1)S(1)} collective-permute-done((bf16[256,576]{1,0:T(8,128)(2,1)S(1)}, bf16[256,576]{1,0:T(8,128)(2,1)S(1)}, u32[]{:S(2)}, u32[]{:S(2)}) %collective-permute-start.13) | collective-permute-done | bytes 294944 | tf_op jit(solution)/shard_map/ppermute | solution.py:483
  63.5 1.5 collective-permute-done.15.refs_6_
  65.0 1.5 %collective-permute-done.10.refs_4_ = bf16[288,1152]{1,0:T(8,128)(2,1)S(1)} collective-permute-done((bf16[288,1152]{1,0:T(8,128)(2,1)S(1)}, bf16[288,1152]{1,0:T(8,128)(2,1)S(1)}, u32[]{:S(2)}, u32[]{:S(2)}) %collective-permute-start.10) | collective-permute-done | bytes 663584 | tf_op jit(solution)/shard_map/ppermute | solution.py:64
  67.1 2.2 %collective-permute-done.21.refs_14_ = bf16[144,1728]{1,0:T(8,128)(2,1)S(1)} collective-permute-done((bf16[144,1728]{1,0:T(8,128)(2,1)S(1)}, bf16[144,1728]{1,0:T(8,128)(2,1)S(1)}, u32[]{:S(2)}, u32[]{:S(2)}) %collective-permute-start.21) | collective-permute-done | bytes 497696 | tf_op jit(solution)/shard_map/ppermute | solution.py:64
  70.1 5.6 %collective-permute-start.17 = (bf16[256,576]{1,0:T(8,128)(2,1)S(1)}, bf16[256,576]{1,0:T(8,128)(2,1)S(1)}, u32[]{:S(2)}, u32[]{:S(2)}) collective-permute-start(bf16[256,576]{1,0:T(8,128)(2,1)S(1)} %pad_maximum_fusion.4), channel_id=1, source_target_pairs={{0,3},{1,2},{2,1},{3,0},{4,7},{5,6},{6,5},{7,4},{8,11},{9,10},{10,... | collective-permute-start | bytes 884744 | tf_op jit(solution)/shard_map/ppermute | solution.py:488
  75.7 1.5 collective-permute-start.11
  77.2 1.5 %collective-permute-start.12 = (bf16[144,1152]{1,0:T(8,128)(2,1)S(1)}, bf16[144,1152]{1,0:T(8,128)(2,1)S(1)}, u32[]{:S(2)}, u32[]{:S(2)}) collective-permute-start(bf16[144,1152]{1,0:T(8,128)(2,1)S(1)} %slice.22), channel_id=1, source_target_pairs={{0,16},{4,20},{8,24},{12,28},{16,0},{20,4},{24,8},{28,12},{1,17},{... | collective-permute-start | bytes 995336 | tf_op jit(solution)/shard_map/ppermute | solution.py:64
  78.7 9.1 %qkv.1.refs_4_ = bf16[512,1728]{1,0:T(8,128)(2,1)S(1)} custom-call(s32[4]{0:T(128)S(1)} %pad_add_fusion.scalars, bf16[128,2304]{1,0:T(8,128)(2,1)S(1)} %norm.1.refs_0_, bf16[128,2304]{1,0:T(8,128)(2,1)} %collective-permute-done.refs_1_, bf16[128,2304]{1,0:T(8,128)(2,1)S(1)} %collective-permute-done.2.refs_2_, ...), custom_call_target="tpu_custom_call" | custom-call | flops 4076863488 | bytes 14680064 | tf_op jit(solution)/shard_map/qkv/pallas_call | solution.py:494
  87.8 2.3 %collective-permute-done.17.refs_3_ = bf16[256,576]{1,0:T(8,128)(2,1)S(1)} collective-permute-done((bf16[256,576]{1,0:T(8,128)(2,1)S(1)}, bf16[256,576]{1,0:T(8,128)(2,1)S(1)}, u32[]{:S(2)}, u32[]{:S(2)}) %collective-permute-start.17) | collective-permute-done | bytes 294944 | tf_op jit(solution)/shard_map/ppermute | solution.py:488
  91.2 9.3 %attention.1 = (bf16[256,576]{1,0:T(8,128)(2,1)S(1)}, bf16[256,576]{1,0:T(8,128)(2,1)S(1)}, bf16[16,576]{1,0:T(8,128)(2,1)S(1)}) custom-call(s32[4]{0:T(128)S(1)} %pad_add_fusion.scalars, bf16[256,576]{1,0:T(8,128)(2,1)S(1)} %pad_maximum_fusion.1.refs_0_, bf16[256,576]{1,0:T(8,128)(2,1)S(1)} %collective-permute-done.16.refs_1_, ...), custom_call_target="tpu_custom_call" | custom-call | flops 905969664 | bytes 4194304 | tf_op jit(solution)/shard_map/attention/pallas_call | solution.py:517
  101.4 1.9 %last_row.1 = f32[2,2304]{1,0:T(2,128)S(1)} custom-call(s32[4]{0:T(128)S(1)} %pad_add_fusion.scalars, bf16[288,1152]{1,0:T(8,128)(2,1)S(1)} %pad_maximum_fusion.refs_0_, bf16[288,1152]{1,0:T(8,128)(2,1)S(1)} %collective-permute-done.23.refs_1_, bf16[288,1152]{1,0:T(8,128)(2,1)S(1)} %collective-permute-done.9.refs_2_, ...), custom_call_target="tpu_custom_call" | custom-call | tf_op jit(solution)/shard_map/last_row/pallas_call | solution.py:542
  103.3 1.2 collective-permute-done.29
  104.5 2.7 %collective-permute-start.32 = (f32[2,2304]{1,0:T(2,128)S(1)}, f32[2,2304]{1,0:T(2,128)S(1)}, u32[]{:S(2)}, u32[]{:S(2)}) collective-permute-start(f32[2,2304]{1,0:T(2,128)S(1)} %add.38.refs_0_), channel_id=1, source_target_pairs={{0,3},{1,2},{2,1},{3,0},{4,7},{5,6},{6,5},{7,4},{8,11},{9,10},{10,... | collective-permute-start | bytes 55304 | tf_op jit(solution)/shard_map/ppermute | solution.py:559
  107.3 1.6 %collective-permute-start.30 = (f32[2,2304]{1,0:T(2,128)S(1)}, f32[2,2304]{1,0:T(2,128)S(1)}, u32[]{:S(2)}, u32[]{:S(2)}) collective-permute-start(f32[2,2304]{1,0:T(2,128)S(1)} %add.38.refs_0_), channel_id=1, source_target_pairs={{0,1},{1,0},{2,3},{3,2},{4,5},{5,4},{6,7},{7,6},{8,9},{9,8},{10,11... | collective-permute-start | bytes 55304 | tf_op jit(solution)/shard_map/ppermute | solution.py:559
  109.1 4.3 %project.1 = (f32[128,2304]{1,0:T(8,128)S(1)}, bf16[128,2304]{1,0:T(8,128)(2,1)S(1)}) custom-call(s32[4]{0:T(128)S(1)} %pad_add_fusion.scalars, bf16[288,1152]{1,0:T(8,128)(2,1)S(1)} %pad_maximum_fusion.refs_0_, bf16[288,1152]{1,0:T(8,128)(2,1)S(1)} %collective-permute-done.23.refs_1_, bf16[288,1152]{1,0:T(8,128)(2,1)S(1)} %collective-permute-done.9.refs_2_, ...), custom_call_target="tpu_custom_call" | custom-call | flops 1358954496 | bytes 8388608 | tf_op jit(solution)/shard_map/project/pallas_call | solution.py:563
  113.5 2.4 %collective-permute-start.33 = (bf16[128,2304]{1,0:T(8,128)(2,1)S(1)}, bf16[128,2304]{1,0:T(8,128)(2,1)S(1)}, u32[]{:S(2)}, u32[]{:S(2)}) collective-permute-start(bf16[128,2304]{1,0:T(8,128)(2,1)S(1)} %get-tuple-element.94), channel_id=1, source_target_pairs={{0,2},{1,3},{2,0},{3,1},{4,6},{5,7},{6,4},{7,5},{8,10},{9,11},{10,... | collective-permute-start | bytes 1769480 | tf_op jit(solution)/shard_map/ppermute | solution.py:582
  116.6 2.6 %collective-permute-start.36 = (bf16[8,2304]{1,0:T(8,128)(2,1)S(1)}, bf16[8,2304]{1,0:T(8,128)(2,1)S(1)}, u32[]{:S(2)}, u32[]{:S(2)}) collective-permute-start(bf16[8,2304]{1,0:T(8,128)(2,1)S(1)} %final_rows.1.refs_0_), channel_id=1, source_target_pairs={{0,24},{4,28},{8,16},{12,20},{16,8},{20,12},{24,0},{28,4},{1,25},{... | collective-permute-start | bytes 110600 | tf_op jit(solution)/shard_map/ppermute | solution.py:394
  120.1 1.4 collective-permute-done.36.refs_3_
  121.5 1.6 %collective-permute-done.35.refs_2_ = bf16[8,2304]{1,0:T(8,128)(2,1)S(1)} collective-permute-done((bf16[8,2304]{1,0:T(8,128)(2,1)S(1)}, bf16[8,2304]{1,0:T(8,128)(2,1)S(1)}, u32[]{:S(2)}, u32[]{:S(2)}) %collective-permute-start.35) | collective-permute-done | bytes 36896 | tf_op jit(solution)/shard_map/ppermute | solution.py:394
  123.6 7.7 %head.1 = (f32[8,3840]{1,0:T(8,128)S(1)}, f32[8,2]{1,0:T(8,128)S(1)}) custom-call(bf16[8,2304]{1,0:T(8,128)(2,1)S(1)} %final_rows.1.refs_0_, bf16[8,2304]{1,0:T(8,128)(2,1)S(1)} %collective-permute-done.34.refs_1_, bf16[8,2304]{1,0:T(8,128)(2,1)S(1)} %collective-permute-done.35.refs_2_, bf16[8,2304]{1,0:T(8,128)(2,1)S(1)} %collective-permute-done.36.refs_3_, ...), custom_call_target="tpu_custom_call" | custom-call | tf_op jit(solution)/shard_map/head/pallas_call | solution.py:601
  131.3 1.5 %collective-permute-start.39 = (f32[8,2]{1,0:T(8,128)S(1)}, f32[8,2]{1,0:T(8,128)S(1)}, u32[]{:S(2)}, u32[]{:S(2)}) collective-permute-start(f32[8,2]{1,0:T(8,128)S(1)} %get-tuple-element.100.refs_0_), channel_id=1, source_target_pairs={{0,24},{4,28},{8,16},{12,20},{16,8},{20,12},{24,0},{28,4},{1,25},{... | collective-permute-start | bytes 200 | tf_op jit(solution)/shard_map/ppermute | solution.py:394
  133.2 1.6 %collective-permute-start.37 = (f32[8,2]{1,0:T(8,128)S(1)}, f32[8,2]{1,0:T(8,128)S(1)}, u32[]{:S(2)}, u32[]{:S(2)}) collective-permute-start(f32[8,2]{1,0:T(8,128)S(1)} %get-tuple-element.100.refs_0_), channel_id=1, source_target_pairs={{0,8},{4,12},{8,0},{12,4},{16,24},{20,28},{24,16},{28,20},{1,9},{5... | collective-permute-start | bytes 200 | tf_op jit(solution)/shard_map/ppermute | solution.py:394
  134.8 1.0 collective-permute-done.39.refs_3_
  137.0 1.2 collective-permute-done.40.refs_1_
  138.2 3.3 %collective-permute-done.33 = bf16[128,2304]{1,0:T(8,128)(2,1)S(1)} collective-permute-done((bf16[128,2304]{1,0:T(8,128)(2,1)S(1)}, bf16[128,2304]{1,0:T(8,128)(2,1)S(1)}, u32[]{:S(2)}, u32[]{:S(2)}) %collective-permute-start.33) | collective-permute-done | bytes 589856 | tf_op jit(solution)/shard_map/ppermute | solution.py:582
  141.5 2.4 %collective-permute-start.43 = (f32[8,2]{1,0:T(8,128)S(1)}, f32[8,2]{1,0:T(8,128)S(1)}, u32[]{:S(2)}, u32[]{:S(2)}) collective-permute-start(f32[8,2]{1,0:T(8,128)S(1)} %merge.3.refs_0_), channel_id=1, source_target_pairs={{0,3},{1,2},{2,1},{3,0},{4,7},{5,6},{6,5},{7,4},{8,11},{9,10},{10,... | collective-permute-start | bytes 200 | tf_op jit(solution)/shard_map/ppermute | solution.py:394
  143.9 2.0 %collective-permute-start.41 = (f32[8,2]{1,0:T(8,128)S(1)}, f32[8,2]{1,0:T(8,128)S(1)}, u32[]{:S(2)}, u32[]{:S(2)}) collective-permute-start(f32[8,2]{1,0:T(8,128)S(1)} %merge.3.refs_0_), channel_id=1, source_target_pairs={{0,1},{1,0},{2,3},{3,2},{4,5},{5,4},{6,7},{7,6},{8,9},{9,8},{10,11... | collective-permute-start | bytes 200 | tf_op jit(solution)/shard_map/ppermute | solution.py:394
  145.9 0.9 fusion
  146.9 1.5 collective-permute-done.42.refs_2_
  (90 shorter events, 14.5 us)
Async XLA Ops:
  2.4 7.9 %slice-start.1 = ((bf16[288,576]{1,0:T(8,128)(2,1)}), bf16[288,512]{1,0:T(8,128)(2,1)S(1)}, s32[]{:S(2)}) async-start(bf16[288,576]{1,0:T(8,128)(2,1)} %param.19), calls=%async_computation.1 | async-start | bytes 589824 | tf_op jit(solution)/shard_map/slice | solution.py:453
  2.4 7.9 %copy-start.7 = (bf16[288,576]{1,0:T(8,128)(2,1)S(1)}, bf16[288,576]{1,0:T(8,128)(2,1)}, u32[]{:S(2)}) copy-start(bf16[288,576]{1,0:T(8,128)(2,1)} %param.18) | copy-start | bytes 995332
  2.6 20.7 %collective-permute-start.1 = (bf16[128,2304]{1,0:T(8,128)(2,1)S(1)}, bf16[128,2304]{1,0:T(8,128)(2,1)S(1)}, u32[]{:S(2)}, u32[]{:S(2)}) collective-permute-start(bf16[128,2304]{1,0:T(8,128)(2,1)S(1)} %norm.1.refs_0_), channel_id=1, source_target_pairs={{1,0},{2,1},{3,2},{5,4},{6,5},{7,6},{9,8},{10,9},{11,10},{13,12},{... | collective-permute-start | bytes 1769480 | tf_op jit(solution)/shard_map/ppermute | solution.py:107
  4.0 19.4 %collective-permute-start = (bf16[128,2304]{1,0:T(8,128)(2,1)S(1)}, bf16[128,2304]{1,0:T(8,128)(2,1)}, u32[]{:S(2)}, u32[]{:S(2)}) collective-permute-start(bf16[128,2304]{1,0:T(8,128)(2,1)S(1)} %norm.1.refs_0_), channel_id=1, source_target_pairs={{0,1},{1,2},{2,3},{4,5},{5,6},{6,7},{8,9},{9,10},{10,11},{12,13},{... | collective-permute-start | bytes 1769480 | tf_op jit(solution)/shard_map/ppermute | solution.py:106
  12.4 24.3 %collective-permute-start.6 = (bf16[288,1728]{1,0:T(8,128)(2,1)S(1)}, bf16[288,1728]{1,0:T(8,128)(2,1)S(1)}, u32[]{:S(2)}, u32[]{:S(2)}) collective-permute-start(bf16[288,1728]{1,0:T(8,128)(2,1)S(1)} %concatenate.31.refs_7_), channel_id=1, source_target_pairs={{0,16},{4,20},{8,24},{12,28},{16,0},{20,4},{24,8},{28,12},{1,17},{... | collective-permute-start | bytes 2985992 | tf_op jit(solution)/shard_map/ppermute | solution.py:64
  14.4 23.8 %collective-permute-start.5 = (bf16[288,1728]{1,0:T(8,128)(2,1)S(1)}, bf16[288,1728]{1,0:T(8,128)(2,1)}, u32[]{:S(2)}, u32[]{:S(2)}) collective-permute-start(bf16[288,1728]{1,0:T(8,128)(2,1)S(1)} %concatenate.31.refs_7_), channel_id=1, source_target_pairs={{0,8},{4,12},{8,0},{12,4},{16,24},{20,28},{24,16},{28,20},{1,9},{5... | collective-permute-start | bytes 2985992 | tf_op jit(solution)/shard_map/ppermute | solution.py:64
  15.9 25.5 %collective-permute-start.4 = (bf16[288,576]{1,0:T(8,128)(2,1)}, bf16[288,576]{1,0:T(8,128)(2,1)}, u32[]{:S(2)}, u32[]{:S(2)}) collective-permute-start(bf16[288,576]{1,0:T(8,128)(2,1)} %bitcast.27), channel_id=1, source_target_pairs={{0,1},{1,0},{2,3},{3,2},{4,5},{5,4},{6,7},{7,6},{8,9},{9,8},{10,11... | collective-permute-start | bytes 995336 | tf_op jit(solution)/shard_map/ppermute | solution.py:471
  23.4 19.2 %collective-permute-start.2 = (bf16[128,2304]{1,0:T(8,128)(2,1)}, bf16[128,2304]{1,0:T(8,128)(2,1)S(1)}, u32[]{:S(2)}, u32[]{:S(2)}) collective-permute-start(bf16[128,2304]{1,0:T(8,128)(2,1)} %collective-permute-done.refs_1_), channel_id=1, source_target_pairs={{1,2},{2,3},{5,6},{6,7},{9,10},{10,11},{13,14},{14,15},{17,18},{18... | collective-permute-start | bytes 1769480 | tf_op jit(solution)/shard_map/ppermute | solution.py:106
  24.1 18.5 %collective-permute-start.3 = (bf16[128,2304]{1,0:T(8,128)(2,1)S(1)}, bf16[128,2304]{1,0:T(8,128)(2,1)S(1)}, u32[]{:S(2)}, u32[]{:S(2)}) collective-permute-start(bf16[128,2304]{1,0:T(8,128)(2,1)S(1)} %collective-permute-done.1.refs_4_), channel_id=1, source_target_pairs={{1,0},{2,1},{5,4},{6,5},{9,8},{10,9},{13,12},{14,13},{17,16},{18,1... | collective-permute-start | bytes 1769480 | tf_op jit(solution)/shard_map/ppermute | solution.py:107
  26.9 14.5 %copy-start.8 = (bf16[576,288]{0,1:T(8,128)(2,1)S(1)}, bf16[576,288]{0,1:T(8,128)(2,1)}, u32[]{:S(2)}) copy-start(bf16[576,288]{0,1:T(8,128)(2,1)} %param.21) | copy-start | bytes 995332
  39.3 11.8 %collective-permute-start.7 = (bf16[144,1728]{1,0:T(8,128)(2,1)S(1)}, bf16[144,1728]{1,0:T(8,128)(2,1)S(1)}, u32[]{:S(2)}, u32[]{:S(2)}) collective-permute-start(bf16[144,1728]{1,0:T(8,128)(2,1)S(1)} %slice.21), channel_id=1, source_target_pairs={{0,8},{4,12},{8,0},{12,4},{16,24},{20,28},{24,16},{28,20},{1,9},{5... | collective-permute-start | bytes 1493000 | tf_op jit(solution)/shard_map/ppermute | solution.py:64
  40.9 11.9 %collective-permute-start.8 = (bf16[144,1728]{1,0:T(8,128)(2,1)S(1)}, bf16[144,1728]{1,0:T(8,128)(2,1)S(1)}, u32[]{:S(2)}, u32[]{:S(2)}) collective-permute-start(bf16[144,1728]{1,0:T(8,128)(2,1)S(1)} %slice.20), channel_id=1, source_target_pairs={{0,16},{4,20},{8,24},{12,28},{16,0},{20,4},{24,8},{28,12},{1,17},{... | collective-permute-start | bytes 1493000 | tf_op jit(solution)/shard_map/ppermute | solution.py:64
  42.6 20.4 %collective-permute-start.14 = (bf16[128,2304]{1,0:T(8,128)(2,1)S(1)}, bf16[128,2304]{1,0:T(8,128)(2,1)S(1)}, u32[]{:S(2)}, u32[]{:S(2)}) collective-permute-start(bf16[128,2304]{1,0:T(8,128)(2,1)S(1)} %collective-permute-done.2.refs_2_), channel_id=1, source_target_pairs={{2,3},{6,7},{10,11},{14,15},{18,19},{22,23},{26,27},{30,31}} | collective-permute-start | bytes 1769480 | tf_op jit(solution)/shard_map/ppermute | solution.py:106
  43.3 21.7 %collective-permute-start.15 = (bf16[128,2304]{1,0:T(8,128)(2,1)S(1)}, bf16[128,2304]{1,0:T(8,128)(2,1)S(1)}, u32[]{:S(2)}, u32[]{:S(2)}) collective-permute-start(bf16[128,2304]{1,0:T(8,128)(2,1)S(1)} %collective-permute-done.3.refs_5_), channel_id=1, source_target_pairs={{1,0},{5,4},{9,8},{13,12},{17,16},{21,20},{25,24},{29,28}} | collective-permute-start | bytes 1769480 | tf_op jit(solution)/shard_map/ppermute | solution.py:107
  44.6 18.4 %collective-permute-start.13 = (bf16[256,576]{1,0:T(8,128)(2,1)S(1)}, bf16[256,576]{1,0:T(8,128)(2,1)S(1)}, u32[]{:S(2)}, u32[]{:S(2)}) collective-permute-start(bf16[256,576]{1,0:T(8,128)(2,1)S(1)} %pad_maximum_fusion.3), channel_id=1, source_target_pairs={{0,2},{1,3},{2,0},{3,1},{4,6},{5,7},{6,4},{7,5},{8,10},{9,11},{10,... | collective-permute-start | bytes 884744 | tf_op jit(solution)/shard_map/ppermute | solution.py:483
  52.8 13.7 %collective-permute-start.10 = (bf16[288,1152]{1,0:T(8,128)(2,1)S(1)}, bf16[288,1152]{1,0:T(8,128)(2,1)S(1)}, u32[]{:S(2)}, u32[]{:S(2)}) collective-permute-start(bf16[288,1152]{1,0:T(8,128)(2,1)S(1)} %pad_maximum_fusion.refs_0_), channel_id=1, source_target_pairs={{0,16},{4,20},{8,24},{12,28},{16,0},{20,4},{24,8},{28,12},{1,17},{... | collective-permute-start | bytes 1990664 | tf_op jit(solution)/shard_map/ppermute | solution.py:64
  52.9 13.8 %collective-permute-start.9 = (bf16[288,1152]{1,0:T(8,128)(2,1)S(1)}, bf16[288,1152]{1,0:T(8,128)(2,1)S(1)}, u32[]{:S(2)}, u32[]{:S(2)}) collective-permute-start(bf16[288,1152]{1,0:T(8,128)(2,1)S(1)} %pad_maximum_fusion.refs_0_), channel_id=1, source_target_pairs={{0,8},{4,12},{8,0},{12,4},{16,24},{20,28},{24,16},{28,20},{1,9},{5... | collective-permute-start | bytes 1990664 | tf_op jit(solution)/shard_map/ppermute | solution.py:64
  63.0 12.7 %collective-permute-start.18 = (bf16[288,1728]{1,0:T(8,128)(2,1)S(1)}, bf16[288,1728]{1,0:T(8,128)(2,1)S(1)}, u32[]{:S(2)}, u32[]{:S(2)}) collective-permute-start(bf16[288,1728]{1,0:T(8,128)(2,1)S(1)} %concatenate.31.refs_7_), channel_id=1, source_target_pairs={{0,4},{4,0},{8,12},{12,8},{16,20},{20,16},{24,28},{28,24},{1,5},{5... | collective-permute-start | bytes 2985992 | tf_op jit(solution)/shard_map/ppermute | solution.py:64
  63.0 14.2 %collective-permute-start.19 = (bf16[288,1728]{1,0:T(8,128)(2,1)}, bf16[288,1728]{1,0:T(8,128)(2,1)S(1)}, u32[]{:S(2)}, u32[]{:S(2)}) collective-permute-start(bf16[288,1728]{1,0:T(8,128)(2,1)} %collective-permute-done.5.refs_9_), channel_id=1, source_target_pairs={{0,4},{4,0},{8,12},{12,8},{16,20},{20,16},{24,28},{28,24},{1,5},{5... | collective-permute-start | bytes 2985992 | tf_op jit(solution)/shard_map/ppermute | solution.py:64
  65.0 13.7 %collective-permute-start.20 = (bf16[288,1728]{1,0:T(8,128)(2,1)S(1)}, bf16[288,1728]{1,0:T(8,128)(2,1)S(1)}, u32[]{:S(2)}, u32[]{:S(2)}) collective-permute-start(bf16[288,1728]{1,0:T(8,128)(2,1)S(1)} %collective-permute-done.6.refs_11_), channel_id=1, source_target_pairs={{0,4},{4,0},{8,12},{12,8},{16,20},{20,16},{24,28},{28,24},{1,5},{5... | collective-permute-start | bytes 2985992 | tf_op jit(solution)/shard_map/ppermute | solution.py:64
  66.5 2.8 %collective-permute-start.21 = (bf16[144,1728]{1,0:T(8,128)(2,1)S(1)}, bf16[144,1728]{1,0:T(8,128)(2,1)S(1)}, u32[]{:S(2)}, u32[]{:S(2)}) collective-permute-start(bf16[144,1728]{1,0:T(8,128)(2,1)S(1)} %collective-permute-done.7.refs_13_), channel_id=1, source_target_pairs={{0,4},{4,0},{8,12},{12,8},{16,20},{20,16},{24,28},{28,24},{1,5},{5... | collective-permute-start | bytes 1493000 | tf_op jit(solution)/shard_map/ppermute | solution.py:64
  66.7 3.4 %collective-permute-start.22 = (bf16[144,1728]{1,0:T(8,128)(2,1)S(1)}, bf16[144,1728]{1,0:T(8,128)(2,1)S(1)}, u32[]{:S(2)}, u32[]{:S(2)}) collective-permute-start(bf16[144,1728]{1,0:T(8,128)(2,1)S(1)} %collective-permute-done.8.refs_15_), channel_id=1, source_target_pairs={{0,4},{4,0},{8,12},{12,8},{16,20},{20,16},{24,28},{28,24},{1,5},{5... | collective-permute-start | bytes 1493000 | tf_op jit(solution)/shard_map/ppermute | solution.py:64
  69.4 18.5 %collective-permute-start.16 = (bf16[256,576]{1,0:T(8,128)(2,1)S(1)}, bf16[256,576]{1,0:T(8,128)(2,1)S(1)}, u32[]{:S(2)}, u32[]{:S(2)}) collective-permute-start(bf16[256,576]{1,0:T(8,128)(2,1)S(1)} %pad_maximum_fusion.2), channel_id=1, source_target_pairs={{0,1},{1,0},{2,3},{3,2},{4,5},{5,4},{6,7},{7,6},{8,9},{9,8},{10,11... | collective-permute-start | bytes 884744 | tf_op jit(solution)/shard_map/ppermute | solution.py:486
  70.1 20.0 %collective-permute-start.17 = (bf16[256,576]{1,0:T(8,128)(2,1)S(1)}, bf16[256,576]{1,0:T(8,128)(2,1)S(1)}, u32[]{:S(2)}, u32[]{:S(2)}) collective-permute-start(bf16[256,576]{1,0:T(8,128)(2,1)S(1)} %pad_maximum_fusion.4), channel_id=1, source_target_pairs={{0,3},{1,2},{2,1},{3,0},{4,7},{5,6},{6,5},{7,4},{8,11},{9,10},{10,... | collective-permute-start | bytes 884744 | tf_op jit(solution)/shard_map/ppermute | solution.py:488
  75.7 14.4 %collective-permute-start.11 = (bf16[144,1152]{1,0:T(8,128)(2,1)S(1)}, bf16[144,1152]{1,0:T(8,128)(2,1)S(1)}, u32[]{:S(2)}, u32[]{:S(2)}) collective-permute-start(bf16[144,1152]{1,0:T(8,128)(2,1)S(1)} %slice.23), channel_id=1, source_target_pairs={{0,8},{4,12},{8,0},{12,4},{16,24},{20,28},{24,16},{28,20},{1,9},{5... | collective-permute-start | bytes 995336 | tf_op jit(solution)/shard_map/ppermute | solution.py:64
  77.2 12.9 %collective-permute-start.12 = (bf16[144,1152]{1,0:T(8,128)(2,1)S(1)}, bf16[144,1152]{1,0:T(8,128)(2,1)S(1)}, u32[]{:S(2)}, u32[]{:S(2)}) collective-permute-start(bf16[144,1152]{1,0:T(8,128)(2,1)S(1)} %slice.22), channel_id=1, source_target_pairs={{0,16},{4,20},{8,24},{12,28},{16,0},{20,4},{24,8},{28,12},{1,17},{... | collective-permute-start | bytes 995336 | tf_op jit(solution)/shard_map/ppermute | solution.py:64
  87.8 13.5 %copy-start.1 = (bf16[1,128,2304]{2,1,0:T(8,128)(2,1)S(1)}, bf16[1,128,2304]{2,1,0:T(8,128)(2,1)}, u32[]{:S(2)}) copy-start(bf16[1,128,2304]{2,1,0:T(8,128)(2,1)} %param.12) | copy-start | bytes 1769476
  90.1 11.2 %collective-permute-start.23 = (bf16[288,1152]{1,0:T(8,128)(2,1)S(1)}, bf16[288,1152]{1,0:T(8,128)(2,1)S(1)}, u32[]{:S(2)}, u32[]{:S(2)}) collective-permute-start(bf16[288,1152]{1,0:T(8,128)(2,1)S(1)} %pad_maximum_fusion.refs_0_), channel_id=1, source_target_pairs={{0,4},{4,0},{8,12},{12,8},{16,20},{20,16},{24,28},{28,24},{1,5},{5... | collective-permute-start | bytes 1990664 | tf_op jit(solution)/shard_map/ppermute | solution.py:64
  90.1 11.2 %collective-permute-start.24 = (bf16[288,1152]{1,0:T(8,128)(2,1)S(1)}, bf16[288,1152]{1,0:T(8,128)(2,1)S(1)}, u32[]{:S(2)}, u32[]{:S(2)}) collective-permute-start(bf16[288,1152]{1,0:T(8,128)(2,1)S(1)} %collective-permute-done.9.refs_2_), channel_id=1, source_target_pairs={{0,4},{4,0},{8,12},{12,8},{16,20},{20,16},{24,28},{28,24},{1,5},{5... | collective-permute-start | bytes 1990664 | tf_op jit(solution)/shard_map/ppermute | solution.py:64
  90.6 10.7 %collective-permute-start.25 = (bf16[288,1152]{1,0:T(8,128)(2,1)S(1)}, bf16[288,1152]{1,0:T(8,128)(2,1)S(1)}, u32[]{:S(2)}, u32[]{:S(2)}) collective-permute-start(bf16[288,1152]{1,0:T(8,128)(2,1)S(1)} %collective-permute-done.10.refs_4_), channel_id=1, source_target_pairs={{0,4},{4,0},{8,12},{12,8},{16,20},{20,16},{24,28},{28,24},{1,5},{5... | collective-permute-start | bytes 1990664 | tf_op jit(solution)/shard_map/ppermute | solution.py:64
  90.7 9.8 %collective-permute-start.26 = (bf16[144,1152]{1,0:T(8,128)(2,1)S(1)}, bf16[144,1152]{1,0:T(8,128)(2,1)S(1)}, u32[]{:S(2)}, u32[]{:S(2)}) collective-permute-start(bf16[144,1152]{1,0:T(8,128)(2,1)S(1)} %collective-permute-done.11.refs_6_), channel_id=1, source_target_pairs={{0,4},{4,0},{8,12},{12,8},{16,20},{20,16},{24,28},{28,24},{1,5},{5... | collective-permute-start | bytes 995336 | tf_op jit(solution)/shard_map/ppermute | solution.py:64
  91.1 10.2 %collective-permute-start.27 = (bf16[144,1152]{1,0:T(8,128)(2,1)S(1)}, bf16[144,1152]{1,0:T(8,128)(2,1)S(1)}, u32[]{:S(2)}, u32[]{:S(2)}) collective-permute-start(bf16[144,1152]{1,0:T(8,128)(2,1)S(1)} %collective-permute-done.12.refs_8_), channel_id=1, source_target_pairs={{0,4},{4,0},{8,12},{12,8},{16,20},{20,16},{24,28},{28,24},{1,5},{5... | collective-permute-start | bytes 995336 | tf_op jit(solution)/shard_map/ppermute | solution.py:64
  100.5 8.6 %collective-permute-start.28 = (bf16[256,576]{1,0:T(8,128)(2,1)S(1)}, bf16[256,576]{1,0:T(8,128)(2,1)S(1)}, u32[]{:S(2)}, u32[]{:S(2)}) collective-permute-start(bf16[256,576]{1,0:T(8,128)(2,1)S(1)} %get-tuple-element.89), channel_id=1, source_target_pairs={{0,1},{1,0},{2,3},{3,2},{4,5},{5,4},{6,7},{7,6},{8,9},{9,8},{10,11... | collective-permute-start | bytes 884744 | tf_op jit(solution)/shard_map/ppermute | solution.py:562
  103.3 1.3 collective-permute-start.29
  104.5 8.9 %collective-permute-start.32 = (f32[2,2304]{1,0:T(2,128)S(1)}, f32[2,2304]{1,0:T(2,128)S(1)}, u32[]{:S(2)}, u32[]{:S(2)}) collective-permute-start(f32[2,2304]{1,0:T(2,128)S(1)} %add.38.refs_0_), channel_id=1, source_target_pairs={{0,3},{1,2},{2,1},{3,0},{4,7},{5,6},{6,5},{7,4},{8,11},{9,10},{10,... | collective-permute-start | bytes 55304 | tf_op jit(solution)/shard_map/ppermute | solution.py:559
  107.2 6.2 %collective-permute-start.31 = (f32[2,2304]{1,0:T(2,128)S(1)}, f32[2,2304]{1,0:T(2,128)S(1)}, u32[]{:S(2)}, u32[]{:S(2)}) collective-permute-start(f32[2,2304]{1,0:T(2,128)S(1)} %add.38.refs_0_), channel_id=1, source_target_pairs={{0,2},{1,3},{2,0},{3,1},{4,6},{5,7},{6,4},{7,5},{8,10},{9,11},{10,... | collective-permute-start | bytes 55304 | tf_op jit(solution)/shard_map/ppermute | solution.py:559
  107.3 6.2 %collective-permute-start.30 = (f32[2,2304]{1,0:T(2,128)S(1)}, f32[2,2304]{1,0:T(2,128)S(1)}, u32[]{:S(2)}, u32[]{:S(2)}) collective-permute-start(f32[2,2304]{1,0:T(2,128)S(1)} %add.38.refs_0_), channel_id=1, source_target_pairs={{0,1},{1,0},{2,3},{3,2},{4,5},{5,4},{6,7},{7,6},{8,9},{9,8},{10,11... | collective-permute-start | bytes 55304 | tf_op jit(solution)/shard_map/ppermute | solution.py:559
  113.5 28.0 %collective-permute-start.33 = (bf16[128,2304]{1,0:T(8,128)(2,1)S(1)}, bf16[128,2304]{1,0:T(8,128)(2,1)S(1)}, u32[]{:S(2)}, u32[]{:S(2)}) collective-permute-start(bf16[128,2304]{1,0:T(8,128)(2,1)S(1)} %get-tuple-element.94), channel_id=1, source_target_pairs={{0,2},{1,3},{2,0},{3,1},{4,6},{5,7},{6,4},{7,5},{8,10},{9,11},{10,... | collective-permute-start | bytes 1769480 | tf_op jit(solution)/shard_map/ppermute | solution.py:582
  116.6 4.9 %collective-permute-start.36 = (bf16[8,2304]{1,0:T(8,128)(2,1)S(1)}, bf16[8,2304]{1,0:T(8,128)(2,1)S(1)}, u32[]{:S(2)}, u32[]{:S(2)}) collective-permute-start(bf16[8,2304]{1,0:T(8,128)(2,1)S(1)} %final_rows.1.refs_0_), channel_id=1, source_target_pairs={{0,24},{4,28},{8,16},{12,20},{16,8},{20,12},{24,0},{28,4},{1,25},{... | collective-permute-start | bytes 110600 | tf_op jit(solution)/shard_map/ppermute | solution.py:394
  119.1 4.0 %collective-permute-start.35 = (bf16[8,2304]{1,0:T(8,128)(2,1)S(1)}, bf16[8,2304]{1,0:T(8,128)(2,1)S(1)}, u32[]{:S(2)}, u32[]{:S(2)}) collective-permute-start(bf16[8,2304]{1,0:T(8,128)(2,1)S(1)} %final_rows.1.refs_0_), channel_id=1, source_target_pairs={{0,16},{4,20},{8,24},{12,28},{16,0},{20,4},{24,8},{28,12},{1,17},{... | collective-permute-start | bytes 110600 | tf_op jit(solution)/shard_map/ppermute | solution.py:394
  119.6 4.0 %collective-permute-start.34 = (bf16[8,2304]{1,0:T(8,128)(2,1)S(1)}, bf16[8,2304]{1,0:T(8,128)(2,1)S(1)}, u32[]{:S(2)}, u32[]{:S(2)}) collective-permute-start(bf16[8,2304]{1,0:T(8,128)(2,1)S(1)} %final_rows.1.refs_0_), channel_id=1, source_target_pairs={{0,8},{4,12},{8,0},{12,4},{16,24},{20,28},{24,16},{28,20},{1,9},{5... | collective-permute-start | bytes 110600 | tf_op jit(solution)/shard_map/ppermute | solution.py:394
  131.3 4.6 %collective-permute-start.39 = (f32[8,2]{1,0:T(8,128)S(1)}, f32[8,2]{1,0:T(8,128)S(1)}, u32[]{:S(2)}, u32[]{:S(2)}) collective-permute-start(f32[8,2]{1,0:T(8,128)S(1)} %get-tuple-element.100.refs_0_), channel_id=1, source_target_pairs={{0,24},{4,28},{8,16},{12,20},{16,8},{20,12},{24,0},{28,4},{1,25},{... | collective-permute-start | bytes 200 | tf_op jit(solution)/shard_map/ppermute | solution.py:394
  132.8 3.6 %collective-permute-start.38 = (f32[8,2]{1,0:T(8,128)S(1)}, f32[8,2]{1,0:T(8,128)S(1)}, u32[]{:S(2)}, u32[]{:S(2)}) collective-permute-start(f32[8,2]{1,0:T(8,128)S(1)} %get-tuple-element.100.refs_0_), channel_id=1, source_target_pairs={{0,16},{4,20},{8,24},{12,28},{16,0},{20,4},{24,8},{28,12},{1,17},{... | collective-permute-start | bytes 200 | tf_op jit(solution)/shard_map/ppermute | solution.py:394
  133.2 3.6 %collective-permute-start.37 = (f32[8,2]{1,0:T(8,128)S(1)}, f32[8,2]{1,0:T(8,128)S(1)}, u32[]{:S(2)}, u32[]{:S(2)}) collective-permute-start(f32[8,2]{1,0:T(8,128)S(1)} %get-tuple-element.100.refs_0_), channel_id=1, source_target_pairs={{0,8},{4,12},{8,0},{12,4},{16,24},{20,28},{24,16},{28,20},{1,9},{5... | collective-permute-start | bytes 200 | tf_op jit(solution)/shard_map/ppermute | solution.py:394
  136.9 1.2 collective-permute-start.40
  141.5 5.4 %collective-permute-start.43 = (f32[8,2]{1,0:T(8,128)S(1)}, f32[8,2]{1,0:T(8,128)S(1)}, u32[]{:S(2)}, u32[]{:S(2)}) collective-permute-start(f32[8,2]{1,0:T(8,128)S(1)} %merge.3.refs_0_), channel_id=1, source_target_pairs={{0,3},{1,2},{2,1},{3,0},{4,7},{5,6},{6,5},{7,4},{8,11},{9,10},{10,... | collective-permute-start | bytes 200 | tf_op jit(solution)/shard_map/ppermute | solution.py:394
  143.9 4.5 %collective-permute-start.42 = (f32[8,2]{1,0:T(8,128)S(1)}, f32[8,2]{1,0:T(8,128)S(1)}, u32[]{:S(2)}, u32[]{:S(2)}) collective-permute-start(f32[8,2]{1,0:T(8,128)S(1)} %merge.3.refs_0_), channel_id=1, source_target_pairs={{0,2},{1,3},{2,0},{3,1},{4,6},{5,7},{6,4},{7,5},{8,10},{9,11},{10,... | collective-permute-start | bytes 200 | tf_op jit(solution)/shard_map/ppermute | solution.py:394
  143.9 4.5 %collective-permute-start.41 = (f32[8,2]{1,0:T(8,128)S(1)}, f32[8,2]{1,0:T(8,128)S(1)}, u32[]{:S(2)}, u32[]{:S(2)}) collective-permute-start(f32[8,2]{1,0:T(8,128)S(1)} %merge.3.refs_0_), channel_id=1, source_target_pairs={{0,1},{1,0},{2,3},{3,2},{4,5},{5,4},{6,7},{7,6},{8,9},{9,8},{10,11... | collective-permute-start | bytes 200 | tf_op jit(solution)/shard_map/ppermute | solution.py:394
  (7 other events, 25.1 us)

commit v8 on v7

--- a/solution.py
+++ b/solution.py
@@ -371,10 +371,12 @@
     step = pl.program_id(0)
     wide = weights[0].shape[1]
     for index, ref in enumerate(weights):
-        start = pl.multiple_of((step * len(weights) + index) * wide, 128)
-        logits_ref[:, pl.ds(start, wide)] = jnp.dot(
-            table, ref[...], preferred_element_type=jnp.float32
-        )
+        part = jnp.dot(table, ref[...], preferred_element_type=jnp.float32)
+        if wide == logits_ref.shape[1]:
+            logits_ref[...] = part
+        else:
+            start = pl.multiple_of((step * len(weights) + index) * wide, 128)
+            logits_ref[:, pl.ds(start, wide)] = part
 
     @pl.when(step == pl.num_programs(0) - 1)
     def _():
@@ -594,6 +596,8 @@
     tables = exchange_all(table, "req", n_req, 2, add_all)
     vocab = head_weight.shape[1]
     wide, streams = 256, 5
+    if vocab % (wide * streams):
+        wide, streams = vocab, 1
 
     def columns(index):
         return pl.BlockSpec((model, wide), lambda step: (0, step * streams + index))

time: 150 us -> 150 us (level)
  waiting for transfers between devices: 44.3 us -> 46 us
  Pallas kernels: 34.2 us -> 32.6 us
    ppermute x1, waiting for transfers between devices: 0.15 us -> 2.06 us  [on_device(): got = after(lax.ppermute(send, 'row', xor_pairs(n_row, 1)), share)]
    pallas_call x1, Pallas kernels: 9.31 us -> 7.8 us  [on_device(): pl.pallas_call(functools.partial(attention_kernel, n_row), out_shape=(jax...]
  transfers between devices with their start and end apart: 44 -> 44, of which waited for: 23 -> 23; matrix products, arithmetic and copies ran while one was open for 8% -> 8% of each run, Pallas kernels for 22% -> 21%
where the time goes in v8:
time: 150 us; the launch traced here: 149 us
  starting transfers between devices  54.4 us (36%)
  waiting for transfers between devices  46 us (31%)
  Pallas kernels  32.6 us (22%)
  local copies, waits for them, and re-layouts  8 us (5%)
  other arithmetic  5.79 us (4%)
  between operations  2.39 us (2%)
    ppermute x18, waiting for transfers between devices, send(): return lax.ppermute(array, 'req', xor_pairs(self.size, mask))  18.3 us
    ppermute x9, starting transfers between devices, exchange_all(): lax.ppermute(value, axis, xor_pairs(size, bit * index))  11.5 us
    ppermute x18, starting transfers between devices, send(): return lax.ppermute(array, 'req', xor_pairs(self.size, mask))  11.3 us
    ppermute x1, waiting for transfers between devices, on_device(): across = lax.ppermute(cached[1], 'row', xor_pairs(n_row, 2))  9.42 us
    pallas_call x1, Pallas kernels, on_device(): pl.pallas_call(functools.partial(qkv_kernel, n_row, layout, block_rows),...  9.09 us
    pallas_call x1, Pallas kernels, on_device(): pl.pallas_call(functools.partial(attention_kernel, n_row), out_shape=(jax...  7.8 us
    ppermute x3, starting transfers between devices, gather_line(): up = lax.ppermute(up, 'row', up_pairs(size, 1, step - 1))  7.78 us
    pallas_call x1, Pallas kernels, on_device(): pl.pallas_call(functools.partial(head_kernel, streams), grid=(vocab // (w...  7.67 us
  transfers between devices with their start and end apart: 44, of which 23 were waited for; matrix products, arithmetic and copies ran while one was open for 8% of the time, Pallas kernels for 21%

profile of v8, /device:TPU:0, one launch (start us, length us, event | category | flops | bytes accessed | tf_op | source)
XLA Modules:
  0.0 149.2 jit_solution(725353170551164648)
XLA Ops:
  0.6 1.1 copy-done
  2.6 1.3 collective-permute-start.1
  4.0 6.4 %collective-permute-start = (bf16[128,2304]{1,0:T(8,128)(2,1)S(1)}, bf16[128,2304]{1,0:T(8,128)(2,1)}, u32[]{:S(2)}, u32[]{:S(2)}) collective-permute-start(bf16[128,2304]{1,0:T(8,128)(2,1)S(1)} %norm.1.refs_0_), channel_id=1, source_target_pairs={{0,1},{1,2},{2,3},{4,5},{5,6},{6,7},{8,9},{9,10},{10,11},{12,13},{... | collective-permute-start | bytes 1769480 | tf_op jit(solution)/shard_map/ppermute | solution.py:106
  10.3 2.0 %concatenate.31.refs_7_ = bf16[288,1728]{1,0:T(8,128)(2,1)S(1)} concatenate(bf16[288,576]{1,0:T(8,128)(2,1)S(1)} %copy-done.7, bf16[288,64]{1,0:T(8,128)(2,1)S(1)} %slice-done, bf16[288,512]{1,0:T(8,128)(2,1)S(1)} %slice-done.1, bf16[288,576]{1,0:T(8,128)(2,1)} %param.20), dimensions={1} | concatenate | bytes 1990656 | tf_op jit(solution)/shard_map/concatenate | solution.py:455
  12.4 2.0 %collective-permute-start.6 = (bf16[288,1728]{1,0:T(8,128)(2,1)S(1)}, bf16[288,1728]{1,0:T(8,128)(2,1)S(1)}, u32[]{:S(2)}, u32[]{:S(2)}) collective-permute-start(bf16[288,1728]{1,0:T(8,128)(2,1)S(1)} %concatenate.31.refs_7_), channel_id=1, source_target_pairs={{0,16},{4,20},{8,24},{12,28},{16,0},{20,4},{24,8},{28,12},{1,17},{... | collective-permute-start | bytes 2985992 | tf_op jit(solution)/shard_map/ppermute | solution.py:64
  14.4 1.5 collective-permute-start.5
  17.4 3.0 %dynamic-slice_bitcast_fusion = (bf16[128,576]{1,0:T(8,128)(2,1)}, bf16[128,576]{1,0:T(8,128)(2,1)}, bf16[128,576]{1,0:T(8,128)(2,1)}, bf16[128,576]{1,0:T(8,128...) fusion(bf16[1,128,2304]{2,1,0:T(8,128)(2,1)} %param.16, ...), kind=kLoop, calls=%fused_computation.11 | loop fusion | bytes 2359312 | tf_op jit(solution)/shard_map/dynamic_slice | solution.py:461
  21.2 1.0 pad_maximum_fusion.4
  22.2 1.0 pad_maximum_fusion.2
  24.1 1.3 collective-permute-start.3
  26.9 9.8 %collective-permute-done.6.refs_11_ = bf16[288,1728]{1,0:T(8,128)(2,1)S(1)} collective-permute-done((bf16[288,1728]{1,0:T(8,128)(2,1)S(1)}, bf16[288,1728]{1,0:T(8,128)(2,1)S(1)}, u32[]{:S(2)}, u32[]{:S(2)}) %collective-permute-start.6) | collective-permute-done | bytes 995360 | tf_op jit(solution)/shard_map/ppermute | solution.py:64
  36.7 1.5 %collective-permute-done.5.refs_9_ = bf16[288,1728]{1,0:T(8,128)(2,1)} collective-permute-done((bf16[288,1728]{1,0:T(8,128)(2,1)S(1)}, bf16[288,1728]{1,0:T(8,128)(2,1)}, u32[]{:S(2)}, u32[]{:S(2)}) %collective-permute-start.5) | collective-permute-done | bytes 995360 | tf_op jit(solution)/shard_map/ppermute | solution.py:64
  38.2 1.1 slice.20
  39.3 1.6 %collective-permute-start.7 = (bf16[144,1728]{1,0:T(8,128)(2,1)S(1)}, bf16[144,1728]{1,0:T(8,128)(2,1)S(1)}, u32[]{:S(2)}, u32[]{:S(2)}) collective-permute-start(bf16[144,1728]{1,0:T(8,128)(2,1)S(1)} %slice.21), channel_id=1, source_target_pairs={{0,8},{4,12},{8,0},{12,4},{16,24},{20,28},{24,16},{28,20},{1,9},{5... | collective-permute-start | bytes 1493000 | tf_op jit(solution)/shard_map/ppermute | solution.py:64
  41.4 1.2 pad_maximum_fusion.refs_0_
  43.3 1.3 collective-permute-start.15
  44.6 6.0 %collective-permute-start.13 = (bf16[256,576]{1,0:T(8,128)(2,1)S(1)}, bf16[256,576]{1,0:T(8,128)(2,1)S(1)}, u32[]{:S(2)}, u32[]{:S(2)}) collective-permute-start(bf16[256,576]{1,0:T(8,128)(2,1)S(1)} %pad_maximum_fusion.3), channel_id=1, source_target_pairs={{0,2},{1,3},{2,0},{3,1},{4,6},{5,7},{6,4},{7,5},{8,10},{9,11},{10,... | collective-permute-start | bytes 884744 | tf_op jit(solution)/shard_map/ppermute | solution.py:485
  51.1 1.7 %collective-permute-done.8.refs_15_ = bf16[144,1728]{1,0:T(8,128)(2,1)S(1)} collective-permute-done((bf16[144,1728]{1,0:T(8,128)(2,1)S(1)}, bf16[144,1728]{1,0:T(8,128)(2,1)S(1)}, u32[]{:S(2)}, u32[]{:S(2)}) %collective-permute-start.8) | collective-permute-done | bytes 497696 | tf_op jit(solution)/shard_map/ppermute | solution.py:64
  53.6 9.4 %collective-permute-done.13.refs_2_ = bf16[256,576]{1,0:T(8,128)(2,1)S(1)} collective-permute-done((bf16[256,576]{1,0:T(8,128)(2,1)S(1)}, bf16[256,576]{1,0:T(8,128)(2,1)S(1)}, u32[]{:S(2)}, u32[]{:S(2)}) %collective-permute-start.13) | collective-permute-done | bytes 294944 | tf_op jit(solution)/shard_map/ppermute | solution.py:485
  63.5 1.5 collective-permute-done.15.refs_6_
  65.0 1.5 %collective-permute-done.10.refs_4_ = bf16[288,1152]{1,0:T(8,128)(2,1)S(1)} collective-permute-done((bf16[288,1152]{1,0:T(8,128)(2,1)S(1)}, bf16[288,1152]{1,0:T(8,128)(2,1)S(1)}, u32[]{:S(2)}, u32[]{:S(2)}) %collective-permute-start.10) | collective-permute-done | bytes 663584 | tf_op jit(solution)/shard_map/ppermute | solution.py:64
  67.1 2.2 %collective-permute-done.21.refs_14_ = bf16[144,1728]{1,0:T(8,128)(2,1)S(1)} collective-permute-done((bf16[144,1728]{1,0:T(8,128)(2,1)S(1)}, bf16[144,1728]{1,0:T(8,128)(2,1)S(1)}, u32[]{:S(2)}, u32[]{:S(2)}) %collective-permute-start.21) | collective-permute-done | bytes 497696 | tf_op jit(solution)/shard_map/ppermute | solution.py:64
  70.1 5.6 %collective-permute-start.17 = (bf16[256,576]{1,0:T(8,128)(2,1)S(1)}, bf16[256,576]{1,0:T(8,128)(2,1)S(1)}, u32[]{:S(2)}, u32[]{:S(2)}) collective-permute-start(bf16[256,576]{1,0:T(8,128)(2,1)S(1)} %pad_maximum_fusion.4), channel_id=1, source_target_pairs={{0,3},{1,2},{2,1},{3,0},{4,7},{5,6},{6,5},{7,4},{8,11},{9,10},{10,... | collective-permute-start | bytes 884744 | tf_op jit(solution)/shard_map/ppermute | solution.py:490
  75.7 1.5 collective-permute-start.11
  77.2 1.5 %collective-permute-start.12 = (bf16[144,1152]{1,0:T(8,128)(2,1)S(1)}, bf16[144,1152]{1,0:T(8,128)(2,1)S(1)}, u32[]{:S(2)}, u32[]{:S(2)}) collective-permute-start(bf16[144,1152]{1,0:T(8,128)(2,1)S(1)} %slice.22), channel_id=1, source_target_pairs={{0,16},{4,20},{8,24},{12,28},{16,0},{20,4},{24,8},{28,12},{1,17},{... | collective-permute-start | bytes 995336 | tf_op jit(solution)/shard_map/ppermute | solution.py:64
  78.7 9.1 %qkv.1.refs_4_ = bf16[512,1728]{1,0:T(8,128)(2,1)S(1)} custom-call(s32[4]{0:T(128)S(1)} %pad_add_fusion.scalars, bf16[128,2304]{1,0:T(8,128)(2,1)S(1)} %norm.1.refs_0_, bf16[128,2304]{1,0:T(8,128)(2,1)} %collective-permute-done.refs_1_, bf16[128,2304]{1,0:T(8,128)(2,1)S(1)} %collective-permute-done.2.refs_2_, ...), custom_call_target="tpu_custom_call" | custom-call | flops 4076863488 | bytes 14680064 | tf_op jit(solution)/shard_map/qkv/pallas_call | solution.py:496
  87.8 2.3 %collective-permute-done.17.refs_3_ = bf16[256,576]{1,0:T(8,128)(2,1)S(1)} collective-permute-done((bf16[256,576]{1,0:T(8,128)(2,1)S(1)}, bf16[256,576]{1,0:T(8,128)(2,1)S(1)}, u32[]{:S(2)}, u32[]{:S(2)}) %collective-permute-start.17) | collective-permute-done | bytes 294944 | tf_op jit(solution)/shard_map/ppermute | solution.py:490
  91.2 7.8 %attention.1 = (bf16[256,576]{1,0:T(8,128)(2,1)S(1)}, bf16[256,576]{1,0:T(8,128)(2,1)S(1)}, bf16[16,576]{1,0:T(8,128)(2,1)S(1)}) custom-call(s32[4]{0:T(128)S(1)} %pad_add_fusion.scalars, bf16[256,576]{1,0:T(8,128)(2,1)S(1)} %pad_maximum_fusion.1.refs_0_, bf16[256,576]{1,0:T(8,128)(2,1)S(1)} %collective-permute-done.16.refs_1_, ...), custom_call_target="tpu_custom_call" | custom-call | flops 905969664 | bytes 4194304 | tf_op jit(solution)/shard_map/attention/pallas_call | solution.py:519
  99.9 1.9 %last_row.1 = f32[2,2304]{1,0:T(2,128)S(1)} custom-call(s32[4]{0:T(128)S(1)} %pad_add_fusion.scalars, bf16[288,1152]{1,0:T(8,128)(2,1)S(1)} %pad_maximum_fusion.refs_0_, bf16[288,1152]{1,0:T(8,128)(2,1)S(1)} %collective-permute-done.23.refs_1_, bf16[288,1152]{1,0:T(8,128)(2,1)S(1)} %collective-permute-done.9.refs_2_, ...), custom_call_target="tpu_custom_call" | custom-call | tf_op jit(solution)/shard_map/last_row/pallas_call | solution.py:544
  102.0 1.0 collective-permute-done.29
  103.0 2.7 %collective-permute-start.32 = (f32[2,2304]{1,0:T(2,128)S(1)}, f32[2,2304]{1,0:T(2,128)S(1)}, u32[]{:S(2)}, u32[]{:S(2)}) collective-permute-start(f32[2,2304]{1,0:T(2,128)S(1)} %add.38.refs_0_), channel_id=1, source_target_pairs={{0,3},{1,2},{2,1},{3,0},{4,7},{5,6},{6,5},{7,4},{8,11},{9,10},{10,... | collective-permute-start | bytes 55304 | tf_op jit(solution)/shard_map/ppermute | solution.py:561
  105.8 1.6 %collective-permute-start.30 = (f32[2,2304]{1,0:T(2,128)S(1)}, f32[2,2304]{1,0:T(2,128)S(1)}, u32[]{:S(2)}, u32[]{:S(2)}) collective-permute-start(f32[2,2304]{1,0:T(2,128)S(1)} %add.38.refs_0_), channel_id=1, source_target_pairs={{0,1},{1,0},{2,3},{3,2},{4,5},{5,4},{6,7},{7,6},{8,9},{9,8},{10,11... | collective-permute-start | bytes 55304 | tf_op jit(solution)/shard_map/ppermute | solution.py:561
  107.5 2.1 %collective-permute-done.28.refs_11_ = bf16[256,576]{1,0:T(8,128)(2,1)S(1)} collective-permute-done((bf16[256,576]{1,0:T(8,128)(2,1)S(1)}, bf16[256,576]{1,0:T(8,128)(2,1)S(1)}, u32[]{:S(2)}, u32[]{:S(2)}) %collective-permute-start.28) | collective-permute-done | bytes 294944 | tf_op jit(solution)/shard_map/ppermute | solution.py:564
  109.5 4.3 %project.1 = (f32[128,2304]{1,0:T(8,128)S(1)}, bf16[128,2304]{1,0:T(8,128)(2,1)S(1)}) custom-call(s32[4]{0:T(128)S(1)} %pad_add_fusion.scalars, bf16[288,1152]{1,0:T(8,128)(2,1)S(1)} %pad_maximum_fusion.refs_0_, bf16[288,1152]{1,0:T(8,128)(2,1)S(1)} %collective-permute-done.23.refs_1_, bf16[288,1152]{1,0:T(8,128)(2,1)S(1)} %collective-permute-done.9.refs_2_, ...), custom_call_target="tpu_custom_call" | custom-call | flops 1358954496 | bytes 8388608 | tf_op jit(solution)/shard_map/project/pallas_call | solution.py:565
  113.9 2.0 %collective-permute-start.33 = (bf16[128,2304]{1,0:T(8,128)(2,1)S(1)}, bf16[128,2304]{1,0:T(8,128)(2,1)S(1)}, u32[]{:S(2)}, u32[]{:S(2)}) collective-permute-start(bf16[128,2304]{1,0:T(8,128)(2,1)S(1)} %get-tuple-element.94), channel_id=1, source_target_pairs={{0,2},{1,3},{2,0},{3,1},{4,6},{5,7},{6,4},{7,5},{8,10},{9,11},{10,... | collective-permute-start | bytes 1769480 | tf_op jit(solution)/shard_map/ppermute | solution.py:584
  116.6 2.5 %collective-permute-start.36 = (bf16[8,2304]{1,0:T(8,128)(2,1)S(1)}, bf16[8,2304]{1,0:T(8,128)(2,1)S(1)}, u32[]{:S(2)}, u32[]{:S(2)}) collective-permute-start(bf16[8,2304]{1,0:T(8,128)(2,1)S(1)} %final_rows.1.refs_0_), channel_id=1, source_target_pairs={{0,24},{4,28},{8,16},{12,20},{16,8},{20,12},{24,0},{28,4},{1,25},{... | collective-permute-start | bytes 110600 | tf_op jit(solution)/shard_map/ppermute | solution.py:396
  120.2 1.4 collective-permute-done.36.refs_3_
  121.5 1.6 %collective-permute-done.35.refs_2_ = bf16[8,2304]{1,0:T(8,128)(2,1)S(1)} collective-permute-done((bf16[8,2304]{1,0:T(8,128)(2,1)S(1)}, bf16[8,2304]{1,0:T(8,128)(2,1)S(1)}, u32[]{:S(2)}, u32[]{:S(2)}) %collective-permute-start.35) | collective-permute-done | bytes 36896 | tf_op jit(solution)/shard_map/ppermute | solution.py:396
  123.6 7.7 %head.1 = (f32[8,3840]{1,0:T(8,128)S(1)}, f32[8,2]{1,0:T(8,128)S(1)}) custom-call(bf16[8,2304]{1,0:T(8,128)(2,1)S(1)} %final_rows.1.refs_0_, bf16[8,2304]{1,0:T(8,128)(2,1)S(1)} %collective-permute-done.34.refs_1_, bf16[8,2304]{1,0:T(8,128)(2,1)S(1)} %collective-permute-done.35.refs_2_, bf16[8,2304]{1,0:T(8,128)(2,1)S(1)} %collective-permute-done.36.refs_3_, ...), custom_call_target="tpu_custom_call" | custom-call | tf_op jit(solution)/shard_map/head/pallas_call | solution.py:605
  131.3 1.0 collective-permute-start.39
  132.3 1.0 collective-permute-start.38
  133.3 1.5 %collective-permute-start.37 = (f32[8,2]{1,0:T(8,128)S(1)}, f32[8,2]{1,0:T(8,128)S(1)}, u32[]{:S(2)}, u32[]{:S(2)}) collective-permute-start(f32[8,2]{1,0:T(8,128)S(1)} %get-tuple-element.100.refs_0_), channel_id=1, source_target_pairs={{0,8},{4,12},{8,0},{12,4},{16,24},{20,28},{24,16},{28,20},{1,9},{5... | collective-permute-start | bytes 200 | tf_op jit(solution)/shard_map/ppermute | solution.py:396
  134.8 1.0 collective-permute-done.39.refs_3_
  135.9 1.0 collective-permute-done.37.refs_1_
  137.0 1.2 collective-permute-done.40.refs_1_
  138.2 3.7 %collective-permute-done.33 = bf16[128,2304]{1,0:T(8,128)(2,1)S(1)} collective-permute-done((bf16[128,2304]{1,0:T(8,128)(2,1)S(1)}, bf16[128,2304]{1,0:T(8,128)(2,1)S(1)}, u32[]{:S(2)}, u32[]{:S(2)}) %collective-permute-start.33) | collective-permute-done | bytes 589856 | tf_op jit(solution)/shard_map/ppermute | solution.py:584
  142.0 1.9 %collective-permute-start.43 = (f32[8,2]{1,0:T(8,128)S(1)}, f32[8,2]{1,0:T(8,128)S(1)}, u32[]{:S(2)}, u32[]{:S(2)}) collective-permute-start(f32[8,2]{1,0:T(8,128)S(1)} %merge.3.refs_0_), channel_id=1, source_target_pairs={{0,3},{1,2},{2,1},{3,0},{4,7},{5,6},{6,5},{7,4},{8,11},{9,10},{10,... | collective-permute-start | bytes 200 | tf_op jit(solution)/shard_map/ppermute | solution.py:396
  143.9 2.5 %collective-permute-start.41 = (f32[8,2]{1,0:T(8,128)S(1)}, f32[8,2]{1,0:T(8,128)S(1)}, u32[]{:S(2)}, u32[]{:S(2)}) collective-permute-start(f32[8,2]{1,0:T(8,128)S(1)} %merge.3.refs_0_), channel_id=1, source_target_pairs={{0,1},{1,0},{2,3},{3,2},{4,5},{5,4},{6,7},{7,6},{8,9},{9,8},{10,11... | collective-permute-start | bytes 200 | tf_op jit(solution)/shard_map/ppermute | solution.py:396
  (90 shorter events, 16.1 us)
Async XLA Ops:
  2.4 7.9 %slice-start.1 = ((bf16[288,576]{1,0:T(8,128)(2,1)}), bf16[288,512]{1,0:T(8,128)(2,1)S(1)}, s32[]{:S(2)}) async-start(bf16[288,576]{1,0:T(8,128)(2,1)} %param.19), calls=%async_computation.1 | async-start | bytes 589824 | tf_op jit(solution)/shard_map/slice | solution.py:455
  2.4 7.9 %copy-start.7 = (bf16[288,576]{1,0:T(8,128)(2,1)S(1)}, bf16[288,576]{1,0:T(8,128)(2,1)}, u32[]{:S(2)}) copy-start(bf16[288,576]{1,0:T(8,128)(2,1)} %param.18) | copy-start | bytes 995332
  2.6 20.7 %collective-permute-start.1 = (bf16[128,2304]{1,0:T(8,128)(2,1)S(1)}, bf16[128,2304]{1,0:T(8,128)(2,1)S(1)}, u32[]{:S(2)}, u32[]{:S(2)}) collective-permute-start(bf16[128,2304]{1,0:T(8,128)(2,1)S(1)} %norm.1.refs_0_), channel_id=1, source_target_pairs={{1,0},{2,1},{3,2},{5,4},{6,5},{7,6},{9,8},{10,9},{11,10},{13,12},{... | collective-permute-start | bytes 1769480 | tf_op jit(solution)/shard_map/ppermute | solution.py:107
  4.0 19.4 %collective-permute-start = (bf16[128,2304]{1,0:T(8,128)(2,1)S(1)}, bf16[128,2304]{1,0:T(8,128)(2,1)}, u32[]{:S(2)}, u32[]{:S(2)}) collective-permute-start(bf16[128,2304]{1,0:T(8,128)(2,1)S(1)} %norm.1.refs_0_), channel_id=1, source_target_pairs={{0,1},{1,2},{2,3},{4,5},{5,6},{6,7},{8,9},{9,10},{10,11},{12,13},{... | collective-permute-start | bytes 1769480 | tf_op jit(solution)/shard_map/ppermute | solution.py:106
  12.4 24.3 %collective-permute-start.6 = (bf16[288,1728]{1,0:T(8,128)(2,1)S(1)}, bf16[288,1728]{1,0:T(8,128)(2,1)S(1)}, u32[]{:S(2)}, u32[]{:S(2)}) collective-permute-start(bf16[288,1728]{1,0:T(8,128)(2,1)S(1)} %concatenate.31.refs_7_), channel_id=1, source_target_pairs={{0,16},{4,20},{8,24},{12,28},{16,0},{20,4},{24,8},{28,12},{1,17},{... | collective-permute-start | bytes 2985992 | tf_op jit(solution)/shard_map/ppermute | solution.py:64
  14.4 23.8 %collective-permute-start.5 = (bf16[288,1728]{1,0:T(8,128)(2,1)S(1)}, bf16[288,1728]{1,0:T(8,128)(2,1)}, u32[]{:S(2)}, u32[]{:S(2)}) collective-permute-start(bf16[288,1728]{1,0:T(8,128)(2,1)S(1)} %concatenate.31.refs_7_), channel_id=1, source_target_pairs={{0,8},{4,12},{8,0},{12,4},{16,24},{20,28},{24,16},{28,20},{1,9},{5... | collective-permute-start | bytes 2985992 | tf_op jit(solution)/shard_map/ppermute | solution.py:64
  15.9 25.5 %collective-permute-start.4 = (bf16[288,576]{1,0:T(8,128)(2,1)}, bf16[288,576]{1,0:T(8,128)(2,1)}, u32[]{:S(2)}, u32[]{:S(2)}) collective-permute-start(bf16[288,576]{1,0:T(8,128)(2,1)} %bitcast.27), channel_id=1, source_target_pairs={{0,1},{1,0},{2,3},{3,2},{4,5},{5,4},{6,7},{7,6},{8,9},{9,8},{10,11... | collective-permute-start | bytes 995336 | tf_op jit(solution)/shard_map/ppermute | solution.py:473
  23.4 19.2 %collective-permute-start.2 = (bf16[128,2304]{1,0:T(8,128)(2,1)}, bf16[128,2304]{1,0:T(8,128)(2,1)S(1)}, u32[]{:S(2)}, u32[]{:S(2)}) collective-permute-start(bf16[128,2304]{1,0:T(8,128)(2,1)} %collective-permute-done.refs_1_), channel_id=1, source_target_pairs={{1,2},{2,3},{5,6},{6,7},{9,10},{10,11},{13,14},{14,15},{17,18},{18... | collective-permute-start | bytes 1769480 | tf_op jit(solution)/shard_map/ppermute | solution.py:106
  24.1 18.5 %collective-permute-start.3 = (bf16[128,2304]{1,0:T(8,128)(2,1)S(1)}, bf16[128,2304]{1,0:T(8,128)(2,1)S(1)}, u32[]{:S(2)}, u32[]{:S(2)}) collective-permute-start(bf16[128,2304]{1,0:T(8,128)(2,1)S(1)} %collective-permute-done.1.refs_4_), channel_id=1, source_target_pairs={{1,0},{2,1},{5,4},{6,5},{9,8},{10,9},{13,12},{14,13},{17,16},{18,1... | collective-permute-start | bytes 1769480 | tf_op jit(solution)/shard_map/ppermute | solution.py:107
  26.9 14.5 %copy-start.8 = (bf16[576,288]{0,1:T(8,128)(2,1)S(1)}, bf16[576,288]{0,1:T(8,128)(2,1)}, u32[]{:S(2)}) copy-start(bf16[576,288]{0,1:T(8,128)(2,1)} %param.21) | copy-start | bytes 995332
  39.3 11.8 %collective-permute-start.7 = (bf16[144,1728]{1,0:T(8,128)(2,1)S(1)}, bf16[144,1728]{1,0:T(8,128)(2,1)S(1)}, u32[]{:S(2)}, u32[]{:S(2)}) collective-permute-start(bf16[144,1728]{1,0:T(8,128)(2,1)S(1)} %slice.21), channel_id=1, source_target_pairs={{0,8},{4,12},{8,0},{12,4},{16,24},{20,28},{24,16},{28,20},{1,9},{5... | collective-permute-start | bytes 1493000 | tf_op jit(solution)/shard_map/ppermute | solution.py:64
  40.9 11.9 %collective-permute-start.8 = (bf16[144,1728]{1,0:T(8,128)(2,1)S(1)}, bf16[144,1728]{1,0:T(8,128)(2,1)S(1)}, u32[]{:S(2)}, u32[]{:S(2)}) collective-permute-start(bf16[144,1728]{1,0:T(8,128)(2,1)S(1)} %slice.20), channel_id=1, source_target_pairs={{0,16},{4,20},{8,24},{12,28},{16,0},{20,4},{24,8},{28,12},{1,17},{... | collective-permute-start | bytes 1493000 | tf_op jit(solution)/shard_map/ppermute | solution.py:64
  42.6 20.4 %collective-permute-start.14 = (bf16[128,2304]{1,0:T(8,128)(2,1)S(1)}, bf16[128,2304]{1,0:T(8,128)(2,1)S(1)}, u32[]{:S(2)}, u32[]{:S(2)}) collective-permute-start(bf16[128,2304]{1,0:T(8,128)(2,1)S(1)} %collective-permute-done.2.refs_2_), channel_id=1, source_target_pairs={{2,3},{6,7},{10,11},{14,15},{18,19},{22,23},{26,27},{30,31}} | collective-permute-start | bytes 1769480 | tf_op jit(solution)/shard_map/ppermute | solution.py:106
  43.3 21.7 %collective-permute-start.15 = (bf16[128,2304]{1,0:T(8,128)(2,1)S(1)}, bf16[128,2304]{1,0:T(8,128)(2,1)S(1)}, u32[]{:S(2)}, u32[]{:S(2)}) collective-permute-start(bf16[128,2304]{1,0:T(8,128)(2,1)S(1)} %collective-permute-done.3.refs_5_), channel_id=1, source_target_pairs={{1,0},{5,4},{9,8},{13,12},{17,16},{21,20},{25,24},{29,28}} | collective-permute-start | bytes 1769480 | tf_op jit(solution)/shard_map/ppermute | solution.py:107
  44.6 18.4 %collective-permute-start.13 = (bf16[256,576]{1,0:T(8,128)(2,1)S(1)}, bf16[256,576]{1,0:T(8,128)(2,1)S(1)}, u32[]{:S(2)}, u32[]{:S(2)}) collective-permute-start(bf16[256,576]{1,0:T(8,128)(2,1)S(1)} %pad_maximum_fusion.3), channel_id=1, source_target_pairs={{0,2},{1,3},{2,0},{3,1},{4,6},{5,7},{6,4},{7,5},{8,10},{9,11},{10,... | collective-permute-start | bytes 884744 | tf_op jit(solution)/shard_map/ppermute | solution.py:485
  52.8 13.7 %collective-permute-start.10 = (bf16[288,1152]{1,0:T(8,128)(2,1)S(1)}, bf16[288,1152]{1,0:T(8,128)(2,1)S(1)}, u32[]{:S(2)}, u32[]{:S(2)}) collective-permute-start(bf16[288,1152]{1,0:T(8,128)(2,1)S(1)} %pad_maximum_fusion.refs_0_), channel_id=1, source_target_pairs={{0,16},{4,20},{8,24},{12,28},{16,0},{20,4},{24,8},{28,12},{1,17},{... | collective-permute-start | bytes 1990664 | tf_op jit(solution)/shard_map/ppermute | solution.py:64
  52.9 13.8 %collective-permute-start.9 = (bf16[288,1152]{1,0:T(8,128)(2,1)S(1)}, bf16[288,1152]{1,0:T(8,128)(2,1)S(1)}, u32[]{:S(2)}, u32[]{:S(2)}) collective-permute-start(bf16[288,1152]{1,0:T(8,128)(2,1)S(1)} %pad_maximum_fusion.refs_0_), channel_id=1, source_target_pairs={{0,8},{4,12},{8,0},{12,4},{16,24},{20,28},{24,16},{28,20},{1,9},{5... | collective-permute-start | bytes 1990664 | tf_op jit(solution)/shard_map/ppermute | solution.py:64
  63.0 12.7 %collective-permute-start.18 = (bf16[288,1728]{1,0:T(8,128)(2,1)S(1)}, bf16[288,1728]{1,0:T(8,128)(2,1)S(1)}, u32[]{:S(2)}, u32[]{:S(2)}) collective-permute-start(bf16[288,1728]{1,0:T(8,128)(2,1)S(1)} %concatenate.31.refs_7_), channel_id=1, source_target_pairs={{0,4},{4,0},{8,12},{12,8},{16,20},{20,16},{24,28},{28,24},{1,5},{5... | collective-permute-start | bytes 2985992 | tf_op jit(solution)/shard_map/ppermute | solution.py:64
  63.0 14.2 %collective-permute-start.19 = (bf16[288,1728]{1,0:T(8,128)(2,1)}, bf16[288,1728]{1,0:T(8,128)(2,1)S(1)}, u32[]{:S(2)}, u32[]{:S(2)}) collective-permute-start(bf16[288,1728]{1,0:T(8,128)(2,1)} %collective-permute-done.5.refs_9_), channel_id=1, source_target_pairs={{0,4},{4,0},{8,12},{12,8},{16,20},{20,16},{24,28},{28,24},{1,5},{5... | collective-permute-start | bytes 2985992 | tf_op jit(solution)/shard_map/ppermute | solution.py:64
  65.0 13.7 %collective-permute-start.20 = (bf16[288,1728]{1,0:T(8,128)(2,1)S(1)}, bf16[288,1728]{1,0:T(8,128)(2,1)S(1)}, u32[]{:S(2)}, u32[]{:S(2)}) collective-permute-start(bf16[288,1728]{1,0:T(8,128)(2,1)S(1)} %collective-permute-done.6.refs_11_), channel_id=1, source_target_pairs={{0,4},{4,0},{8,12},{12,8},{16,20},{20,16},{24,28},{28,24},{1,5},{5... | collective-permute-start | bytes 2985992 | tf_op jit(solution)/shard_map/ppermute | solution.py:64
  66.5 2.8 %collective-permute-start.21 = (bf16[144,1728]{1,0:T(8,128)(2,1)S(1)}, bf16[144,1728]{1,0:T(8,128)(2,1)S(1)}, u32[]{:S(2)}, u32[]{:S(2)}) collective-permute-start(bf16[144,1728]{1,0:T(8,128)(2,1)S(1)} %collective-permute-done.7.refs_13_), channel_id=1, source_target_pairs={{0,4},{4,0},{8,12},{12,8},{16,20},{20,16},{24,28},{28,24},{1,5},{5... | collective-permute-start | bytes 1493000 | tf_op jit(solution)/shard_map/ppermute | solution.py:64
  66.7 3.4 %collective-permute-start.22 = (bf16[144,1728]{1,0:T(8,128)(2,1)S(1)}, bf16[144,1728]{1,0:T(8,128)(2,1)S(1)}, u32[]{:S(2)}, u32[]{:S(2)}) collective-permute-start(bf16[144,1728]{1,0:T(8,128)(2,1)S(1)} %collective-permute-done.8.refs_15_), channel_id=1, source_target_pairs={{0,4},{4,0},{8,12},{12,8},{16,20},{20,16},{24,28},{28,24},{1,5},{5... | collective-permute-start | bytes 1493000 | tf_op jit(solution)/shard_map/ppermute | solution.py:64
  69.4 18.5 %collective-permute-start.16 = (bf16[256,576]{1,0:T(8,128)(2,1)S(1)}, bf16[256,576]{1,0:T(8,128)(2,1)S(1)}, u32[]{:S(2)}, u32[]{:S(2)}) collective-permute-start(bf16[256,576]{1,0:T(8,128)(2,1)S(1)} %pad_maximum_fusion.2), channel_id=1, source_target_pairs={{0,1},{1,0},{2,3},{3,2},{4,5},{5,4},{6,7},{7,6},{8,9},{9,8},{10,11... | collective-permute-start | bytes 884744 | tf_op jit(solution)/shard_map/ppermute | solution.py:488
  70.1 20.0 %collective-permute-start.17 = (bf16[256,576]{1,0:T(8,128)(2,1)S(1)}, bf16[256,576]{1,0:T(8,128)(2,1)S(1)}, u32[]{:S(2)}, u32[]{:S(2)}) collective-permute-start(bf16[256,576]{1,0:T(8,128)(2,1)S(1)} %pad_maximum_fusion.4), channel_id=1, source_target_pairs={{0,3},{1,2},{2,1},{3,0},{4,7},{5,6},{6,5},{7,4},{8,11},{9,10},{10,... | collective-permute-start | bytes 884744 | tf_op jit(solution)/shard_map/ppermute | solution.py:490
  75.7 14.4 %collective-permute-start.11 = (bf16[144,1152]{1,0:T(8,128)(2,1)S(1)}, bf16[144,1152]{1,0:T(8,128)(2,1)S(1)}, u32[]{:S(2)}, u32[]{:S(2)}) collective-permute-start(bf16[144,1152]{1,0:T(8,128)(2,1)S(1)} %slice.23), channel_id=1, source_target_pairs={{0,8},{4,12},{8,0},{12,4},{16,24},{20,28},{24,16},{28,20},{1,9},{5... | collective-permute-start | bytes 995336 | tf_op jit(solution)/shard_map/ppermute | solution.py:64
  77.2 12.9 %collective-permute-start.12 = (bf16[144,1152]{1,0:T(8,128)(2,1)S(1)}, bf16[144,1152]{1,0:T(8,128)(2,1)S(1)}, u32[]{:S(2)}, u32[]{:S(2)}) collective-permute-start(bf16[144,1152]{1,0:T(8,128)(2,1)S(1)} %slice.22), channel_id=1, source_target_pairs={{0,16},{4,20},{8,24},{12,28},{16,0},{20,4},{24,8},{28,12},{1,17},{... | collective-permute-start | bytes 995336 | tf_op jit(solution)/shard_map/ppermute | solution.py:64
  87.8 12.0 %copy-start.1 = (bf16[1,128,2304]{2,1,0:T(8,128)(2,1)S(1)}, bf16[1,128,2304]{2,1,0:T(8,128)(2,1)}, u32[]{:S(2)}) copy-start(bf16[1,128,2304]{2,1,0:T(8,128)(2,1)} %param.12) | copy-start | bytes 1769476
  90.1 9.7 %collective-permute-start.23 = (bf16[288,1152]{1,0:T(8,128)(2,1)S(1)}, bf16[288,1152]{1,0:T(8,128)(2,1)S(1)}, u32[]{:S(2)}, u32[]{:S(2)}) collective-permute-start(bf16[288,1152]{1,0:T(8,128)(2,1)S(1)} %pad_maximum_fusion.refs_0_), channel_id=1, source_target_pairs={{0,4},{4,0},{8,12},{12,8},{16,20},{20,16},{24,28},{28,24},{1,5},{5... | collective-permute-start | bytes 1990664 | tf_op jit(solution)/shard_map/ppermute | solution.py:64
  90.1 9.7 %collective-permute-start.24 = (bf16[288,1152]{1,0:T(8,128)(2,1)S(1)}, bf16[288,1152]{1,0:T(8,128)(2,1)S(1)}, u32[]{:S(2)}, u32[]{:S(2)}) collective-permute-start(bf16[288,1152]{1,0:T(8,128)(2,1)S(1)} %collective-permute-done.9.refs_2_), channel_id=1, source_target_pairs={{0,4},{4,0},{8,12},{12,8},{16,20},{20,16},{24,28},{28,24},{1,5},{5... | collective-permute-start | bytes 1990664 | tf_op jit(solution)/shard_map/ppermute | solution.py:64
  90.6 9.2 %collective-permute-start.25 = (bf16[288,1152]{1,0:T(8,128)(2,1)S(1)}, bf16[288,1152]{1,0:T(8,128)(2,1)S(1)}, u32[]{:S(2)}, u32[]{:S(2)}) collective-permute-start(bf16[288,1152]{1,0:T(8,128)(2,1)S(1)} %collective-permute-done.10.refs_4_), channel_id=1, source_target_pairs={{0,4},{4,0},{8,12},{12,8},{16,20},{20,16},{24,28},{28,24},{1,5},{5... | collective-permute-start | bytes 1990664 | tf_op jit(solution)/shard_map/ppermute | solution.py:64
  90.7 8.3 %collective-permute-start.26 = (bf16[144,1152]{1,0:T(8,128)(2,1)S(1)}, bf16[144,1152]{1,0:T(8,128)(2,1)S(1)}, u32[]{:S(2)}, u32[]{:S(2)}) collective-permute-start(bf16[144,1152]{1,0:T(8,128)(2,1)S(1)} %collective-permute-done.11.refs_6_), channel_id=1, source_target_pairs={{0,4},{4,0},{8,12},{12,8},{16,20},{20,16},{24,28},{28,24},{1,5},{5... | collective-permute-start | bytes 995336 | tf_op jit(solution)/shard_map/ppermute | solution.py:64
  91.1 8.7 %collective-permute-start.27 = (bf16[144,1152]{1,0:T(8,128)(2,1)S(1)}, bf16[144,1152]{1,0:T(8,128)(2,1)S(1)}, u32[]{:S(2)}, u32[]{:S(2)}) collective-permute-start(bf16[144,1152]{1,0:T(8,128)(2,1)S(1)} %collective-permute-done.12.refs_8_), channel_id=1, source_target_pairs={{0,4},{4,0},{8,12},{12,8},{16,20},{20,16},{24,28},{28,24},{1,5},{5... | collective-permute-start | bytes 995336 | tf_op jit(solution)/shard_map/ppermute | solution.py:64
  99.0 10.5 %collective-permute-start.28 = (bf16[256,576]{1,0:T(8,128)(2,1)S(1)}, bf16[256,576]{1,0:T(8,128)(2,1)S(1)}, u32[]{:S(2)}, u32[]{:S(2)}) collective-permute-start(bf16[256,576]{1,0:T(8,128)(2,1)S(1)} %get-tuple-element.89), channel_id=1, source_target_pairs={{0,1},{1,0},{2,3},{3,2},{4,5},{5,4},{6,7},{7,6},{8,9},{9,8},{10,11... | collective-permute-start | bytes 884744 | tf_op jit(solution)/shard_map/ppermute | solution.py:564
  101.8 1.3 collective-permute-start.29
  103.0 10.8 %collective-permute-start.32 = (f32[2,2304]{1,0:T(2,128)S(1)}, f32[2,2304]{1,0:T(2,128)S(1)}, u32[]{:S(2)}, u32[]{:S(2)}) collective-permute-start(f32[2,2304]{1,0:T(2,128)S(1)} %add.38.refs_0_), channel_id=1, source_target_pairs={{0,3},{1,2},{2,1},{3,0},{4,7},{5,6},{6,5},{7,4},{8,11},{9,10},{10,... | collective-permute-start | bytes 55304 | tf_op jit(solution)/shard_map/ppermute | solution.py:561
  105.7 8.2 %collective-permute-start.31 = (f32[2,2304]{1,0:T(2,128)S(1)}, f32[2,2304]{1,0:T(2,128)S(1)}, u32[]{:S(2)}, u32[]{:S(2)}) collective-permute-start(f32[2,2304]{1,0:T(2,128)S(1)} %add.38.refs_0_), channel_id=1, source_target_pairs={{0,2},{1,3},{2,0},{3,1},{4,6},{5,7},{6,4},{7,5},{8,10},{9,11},{10,... | collective-permute-start | bytes 55304 | tf_op jit(solution)/shard_map/ppermute | solution.py:561
  105.8 8.1 %collective-permute-start.30 = (f32[2,2304]{1,0:T(2,128)S(1)}, f32[2,2304]{1,0:T(2,128)S(1)}, u32[]{:S(2)}, u32[]{:S(2)}) collective-permute-start(f32[2,2304]{1,0:T(2,128)S(1)} %add.38.refs_0_), channel_id=1, source_target_pairs={{0,1},{1,0},{2,3},{3,2},{4,5},{5,4},{6,7},{7,6},{8,9},{9,8},{10,11... | collective-permute-start | bytes 55304 | tf_op jit(solution)/shard_map/ppermute | solution.py:561
  113.9 28.1 %collective-permute-start.33 = (bf16[128,2304]{1,0:T(8,128)(2,1)S(1)}, bf16[128,2304]{1,0:T(8,128)(2,1)S(1)}, u32[]{:S(2)}, u32[]{:S(2)}) collective-permute-start(bf16[128,2304]{1,0:T(8,128)(2,1)S(1)} %get-tuple-element.94), channel_id=1, source_target_pairs={{0,2},{1,3},{2,0},{3,1},{4,6},{5,7},{6,4},{7,5},{8,10},{9,11},{10,... | collective-permute-start | bytes 1769480 | tf_op jit(solution)/shard_map/ppermute | solution.py:584
  116.6 4.9 %collective-permute-start.36 = (bf16[8,2304]{1,0:T(8,128)(2,1)S(1)}, bf16[8,2304]{1,0:T(8,128)(2,1)S(1)}, u32[]{:S(2)}, u32[]{:S(2)}) collective-permute-start(bf16[8,2304]{1,0:T(8,128)(2,1)S(1)} %final_rows.1.refs_0_), channel_id=1, source_target_pairs={{0,24},{4,28},{8,16},{12,20},{16,8},{20,12},{24,0},{28,4},{1,25},{... | collective-permute-start | bytes 110600 | tf_op jit(solution)/shard_map/ppermute | solution.py:396
  119.1 4.0 %collective-permute-start.35 = (bf16[8,2304]{1,0:T(8,128)(2,1)S(1)}, bf16[8,2304]{1,0:T(8,128)(2,1)S(1)}, u32[]{:S(2)}, u32[]{:S(2)}) collective-permute-start(bf16[8,2304]{1,0:T(8,128)(2,1)S(1)} %final_rows.1.refs_0_), channel_id=1, source_target_pairs={{0,16},{4,20},{8,24},{12,28},{16,0},{20,4},{24,8},{28,12},{1,17},{... | collective-permute-start | bytes 110600 | tf_op jit(solution)/shard_map/ppermute | solution.py:396
  119.6 4.0 %collective-permute-start.34 = (bf16[8,2304]{1,0:T(8,128)(2,1)S(1)}, bf16[8,2304]{1,0:T(8,128)(2,1)S(1)}, u32[]{:S(2)}, u32[]{:S(2)}) collective-permute-start(bf16[8,2304]{1,0:T(8,128)(2,1)S(1)} %final_rows.1.refs_0_), channel_id=1, source_target_pairs={{0,8},{4,12},{8,0},{12,4},{16,24},{20,28},{24,16},{28,20},{1,9},{5... | collective-permute-start | bytes 110600 | tf_op jit(solution)/shard_map/ppermute | solution.py:396
  131.3 4.6 %collective-permute-start.39 = (f32[8,2]{1,0:T(8,128)S(1)}, f32[8,2]{1,0:T(8,128)S(1)}, u32[]{:S(2)}, u32[]{:S(2)}) collective-permute-start(f32[8,2]{1,0:T(8,128)S(1)} %get-tuple-element.100.refs_0_), channel_id=1, source_target_pairs={{0,24},{4,28},{8,16},{12,20},{16,8},{20,12},{24,0},{28,4},{1,25},{... | collective-permute-start | bytes 200 | tf_op jit(solution)/shard_map/ppermute | solution.py:396
  132.3 3.6 %collective-permute-start.38 = (f32[8,2]{1,0:T(8,128)S(1)}, f32[8,2]{1,0:T(8,128)S(1)}, u32[]{:S(2)}, u32[]{:S(2)}) collective-permute-start(f32[8,2]{1,0:T(8,128)S(1)} %get-tuple-element.100.refs_0_), channel_id=1, source_target_pairs={{0,16},{4,20},{8,24},{12,28},{16,0},{20,4},{24,8},{28,12},{1,17},{... | collective-permute-start | bytes 200 | tf_op jit(solution)/shard_map/ppermute | solution.py:396
  133.3 3.6 %collective-permute-start.37 = (f32[8,2]{1,0:T(8,128)S(1)}, f32[8,2]{1,0:T(8,128)S(1)}, u32[]{:S(2)}, u32[]{:S(2)}) collective-permute-start(f32[8,2]{1,0:T(8,128)S(1)} %get-tuple-element.100.refs_0_), channel_id=1, source_target_pairs={{0,8},{4,12},{8,0},{12,4},{16,24},{20,28},{24,16},{28,20},{1,9},{5... | collective-permute-start | bytes 200 | tf_op jit(solution)/shard_map/ppermute | solution.py:396
  137.0 1.2 collective-permute-start.40
  142.0 5.4 %collective-permute-start.43 = (f32[8,2]{1,0:T(8,128)S(1)}, f32[8,2]{1,0:T(8,128)S(1)}, u32[]{:S(2)}, u32[]{:S(2)}) collective-permute-start(f32[8,2]{1,0:T(8,128)S(1)} %merge.3.refs_0_), channel_id=1, source_target_pairs={{0,3},{1,2},{2,1},{3,0},{4,7},{5,6},{6,5},{7,4},{8,11},{9,10},{10,... | collective-permute-start | bytes 200 | tf_op jit(solution)/shard_map/ppermute | solution.py:396
  143.9 4.5 %collective-permute-start.42 = (f32[8,2]{1,0:T(8,128)S(1)}, f32[8,2]{1,0:T(8,128)S(1)}, u32[]{:S(2)}, u32[]{:S(2)}) collective-permute-start(f32[8,2]{1,0:T(8,128)S(1)} %merge.3.refs_0_), channel_id=1, source_target_pairs={{0,2},{1,3},{2,0},{3,1},{4,6},{5,7},{6,4},{7,5},{8,10},{9,11},{10,... | collective-permute-start | bytes 200 | tf_op jit(solution)/shard_map/ppermute | solution.py:396
  143.9 4.5 %collective-permute-start.41 = (f32[8,2]{1,0:T(8,128)S(1)}, f32[8,2]{1,0:T(8,128)S(1)}, u32[]{:S(2)}, u32[]{:S(2)}) collective-permute-start(f32[8,2]{1,0:T(8,128)S(1)} %merge.3.refs_0_), channel_id=1, source_target_pairs={{0,1},{1,0},{2,3},{3,2},{4,5},{5,4},{6,7},{7,6},{8,9},{9,8},{10,11... | collective-permute-start | bytes 200 | tf_op jit(solution)/shard_map/ppermute | solution.py:396
  (7 other events, 24.8 us)

commit v9 on v8

--- a/solution.py
+++ b/solution.py
@@ -623,7 +623,10 @@
     )(*tables, *[head_weight] * streams)
     stats = merge(*exchange_all(stats, "req", n_req, 2, merge))
     stats = merge(stats, lax.ppermute(stats, "req", xor_pairs(n_req, 1)))
-    stats = exchange_all(after(stats, others), "row", n_row, 1, merge)
+    later = after(stats, others)
+    stats = [stats, lax.ppermute(stats, "row", xor_pairs(n_row, 1))] + [
+        lax.ppermute(later, "row", xor_pairs(n_row, mask)) for mask in range(2, n_row)
+    ]
     logprobs = pl.pallas_call(
         logprobs_kernel,
         out_shape=jax.ShapeDtypeStruct(logits.shape, jnp.float32),

time: 150 us -> 150 us (level)
    ppermute x9 -> x6, starting transfers between devices: 11.5 us -> 7.6 us  [exchange_all(): lax.ppermute(value, axis, xor_pairs(size, bit * index))]
    ppermute x0 -> x3, waiting for transfers between devices: none -> 3.56 us  [the longest x2 3.56 us: on_device(): lax.ppermute(later, 'row', xor_pairs(n_row, mask))]
    ppermute x0 -> x3, starting transfers between devices: none -> 2.43 us  [the longest x2 1.54 us: on_device(): lax.ppermute(later, 'row', xor_pairs(n_row, mask))]
    ppermute x1, waiting for transfers between devices: 2.06 us -> 0.01 us  [on_device(): got = after(lax.ppermute(send, 'row', xor_pairs(n_row, 1)), share)]
    ppermute x1, starting transfers between devices: 0.23 us -> 1.74 us  [on_device(): pair = lax.ppermute(share, 'req', xor_pairs(n_req, 1))]
    ppermute x9 -> x6, waiting for transfers between devices: 6.64 us -> 5.54 us  [exchange_all(): lax.ppermute(value, axis, xor_pairs(size, bit * index))]
  transfers between devices with their start and end apart: 44 -> 44, of which waited for: 23 -> 22; matrix products, arithmetic and copies ran while one was open for 8% -> 8% of each run, Pallas kernels for 21% -> 21%
where the time goes in v9:
time: 150 us
  starting transfers between devices  54.3 us (36%)
  waiting for transfers between devices  46.7 us (31%)
  Pallas kernels  32.6 us (22%)
  local copies, waits for them, and re-layouts  8 us (5%)
  other arithmetic  5.79 us (4%)
  between operations  2.39 us (2%)
    ppermute x18, waiting for transfers between devices, send(): return lax.ppermute(array, 'req', xor_pairs(self.size, mask))  18.3 us
    ppermute x18, starting transfers between devices, send(): return lax.ppermute(array, 'req', xor_pairs(self.size, mask))  11.3 us
    ppermute x1, waiting for transfers between devices, on_device(): across = lax.ppermute(cached[1], 'row', xor_pairs(n_row, 2))  9.42 us
    pallas_call x1, Pallas kernels, on_device(): pl.pallas_call(functools.partial(qkv_kernel, n_row, layout, block_rows),...  9.09 us
    pallas_call x1, Pallas kernels, on_device(): pl.pallas_call(functools.partial(attention_kernel, n_row), out_shape=(jax...  7.8 us
    ppermute x3, starting transfers between devices, gather_line(): up = lax.ppermute(up, 'row', up_pairs(size, 1, step - 1))  7.78 us
    pallas_call x1, Pallas kernels, on_device(): pl.pallas_call(functools.partial(head_kernel, streams), grid=(vocab // (w...  7.67 us
    ppermute x6, starting transfers between devices, exchange_all(): lax.ppermute(value, axis, xor_pairs(size, bit * index))  7.6 us
  transfers between devices with their start and end apart: 44, of which 22 were waited for; matrix products, arithmetic and copies ran while one was open for 8% of the time, Pallas kernels for 21%

profile of v9, /device:TPU:0, one launch (start us, length us, event | category | flops | bytes accessed | tf_op | source)
XLA Modules:
  0.0 149.8 jit_solution(16135156245703529872)
XLA Ops:
  0.6 1.1 copy-done
  2.6 1.3 collective-permute-start.1
  4.0 6.4 %collective-permute-start = (bf16[128,2304]{1,0:T(8,128)(2,1)S(1)}, bf16[128,2304]{1,0:T(8,128)(2,1)}, u32[]{:S(2)}, u32[]{:S(2)}) collective-permute-start(bf16[128,2304]{1,0:T(8,128)(2,1)S(1)} %norm.1.refs_0_), channel_id=1, source_target_pairs={{0,1},{1,2},{2,3},{4,5},{5,6},{6,7},{8,9},{9,10},{10,11},{12,13},{... | collective-permute-start | bytes 1769480 | tf_op jit(solution)/shard_map/ppermute | solution.py:106
  10.3 2.0 %concatenate.31.refs_7_ = bf16[288,1728]{1,0:T(8,128)(2,1)S(1)} concatenate(bf16[288,576]{1,0:T(8,128)(2,1)S(1)} %copy-done.7, bf16[288,64]{1,0:T(8,128)(2,1)S(1)} %slice-done, bf16[288,512]{1,0:T(8,128)(2,1)S(1)} %slice-done.1, bf16[288,576]{1,0:T(8,128)(2,1)} %param.20), dimensions={1} | concatenate | bytes 1990656 | tf_op jit(solution)/shard_map/concatenate | solution.py:455
  12.4 2.0 %collective-permute-start.6 = (bf16[288,1728]{1,0:T(8,128)(2,1)S(1)}, bf16[288,1728]{1,0:T(8,128)(2,1)S(1)}, u32[]{:S(2)}, u32[]{:S(2)}) collective-permute-start(bf16[288,1728]{1,0:T(8,128)(2,1)S(1)} %concatenate.31.refs_7_), channel_id=1, source_target_pairs={{0,16},{4,20},{8,24},{12,28},{16,0},{20,4},{24,8},{28,12},{1,17},{... | collective-permute-start | bytes 2985992 | tf_op jit(solution)/shard_map/ppermute | solution.py:64
  14.4 1.5 collective-permute-start.5
  17.4 3.0 %dynamic-slice_bitcast_fusion = (bf16[128,576]{1,0:T(8,128)(2,1)}, bf16[128,576]{1,0:T(8,128)(2,1)}, bf16[128,576]{1,0:T(8,128)(2,1)}, bf16[128,576]{1,0:T(8,128...) fusion(bf16[1,128,2304]{2,1,0:T(8,128)(2,1)} %param.16, ...), kind=kLoop, calls=%fused_computation.11 | loop fusion | bytes 2359312 | tf_op jit(solution)/shard_map/dynamic_slice | solution.py:461
  21.2 1.0 pad_maximum_fusion.4
  22.2 1.0 pad_maximum_fusion.2
  24.1 1.3 collective-permute-start.3
  25.4 1.0 fusion.1
  26.9 9.8 %collective-permute-done.6.refs_11_ = bf16[288,1728]{1,0:T(8,128)(2,1)S(1)} collective-permute-done((bf16[288,1728]{1,0:T(8,128)(2,1)S(1)}, bf16[288,1728]{1,0:T(8,128)(2,1)S(1)}, u32[]{:S(2)}, u32[]{:S(2)}) %collective-permute-start.6) | collective-permute-done | bytes 995360 | tf_op jit(solution)/shard_map/ppermute | solution.py:64
  36.7 1.5 %collective-permute-done.5.refs_9_ = bf16[288,1728]{1,0:T(8,128)(2,1)} collective-permute-done((bf16[288,1728]{1,0:T(8,128)(2,1)S(1)}, bf16[288,1728]{1,0:T(8,128)(2,1)}, u32[]{:S(2)}, u32[]{:S(2)}) %collective-permute-start.5) | collective-permute-done | bytes 995360 | tf_op jit(solution)/shard_map/ppermute | solution.py:64
  38.2 1.1 slice.20
  39.3 1.6 %collective-permute-start.7 = (bf16[144,1728]{1,0:T(8,128)(2,1)S(1)}, bf16[144,1728]{1,0:T(8,128)(2,1)S(1)}, u32[]{:S(2)}, u32[]{:S(2)}) collective-permute-start(bf16[144,1728]{1,0:T(8,128)(2,1)S(1)} %slice.21), channel_id=1, source_target_pairs={{0,8},{4,12},{8,0},{12,4},{16,24},{20,28},{24,16},{28,20},{1,9},{5... | collective-permute-start | bytes 1493000 | tf_op jit(solution)/shard_map/ppermute | solution.py:64
  41.4 1.2 pad_maximum_fusion.refs_0_
  43.3 1.3 collective-permute-start.15
  44.6 6.0 %collective-permute-start.13 = (bf16[256,576]{1,0:T(8,128)(2,1)S(1)}, bf16[256,576]{1,0:T(8,128)(2,1)S(1)}, u32[]{:S(2)}, u32[]{:S(2)}) collective-permute-start(bf16[256,576]{1,0:T(8,128)(2,1)S(1)} %pad_maximum_fusion.3), channel_id=1, source_target_pairs={{0,2},{1,3},{2,0},{3,1},{4,6},{5,7},{6,4},{7,5},{8,10},{9,11},{10,... | collective-permute-start | bytes 884744 | tf_op jit(solution)/shard_map/ppermute | solution.py:485
  51.1 1.7 %collective-permute-done.8.refs_15_ = bf16[144,1728]{1,0:T(8,128)(2,1)S(1)} collective-permute-done((bf16[144,1728]{1,0:T(8,128)(2,1)S(1)}, bf16[144,1728]{1,0:T(8,128)(2,1)S(1)}, u32[]{:S(2)}, u32[]{:S(2)}) %collective-permute-start.8) | collective-permute-done | bytes 497696 | tf_op jit(solution)/shard_map/ppermute | solution.py:64
  53.6 9.4 %collective-permute-done.13.refs_2_ = bf16[256,576]{1,0:T(8,128)(2,1)S(1)} collective-permute-done((bf16[256,576]{1,0:T(8,128)(2,1)S(1)}, bf16[256,576]{1,0:T(8,128)(2,1)S(1)}, u32[]{:S(2)}, u32[]{:S(2)}) %collective-permute-start.13) | collective-permute-done | bytes 294944 | tf_op jit(solution)/shard_map/ppermute | solution.py:485
  63.5 1.5 collective-permute-done.15.refs_6_
  65.0 1.5 %collective-permute-done.10.refs_4_ = bf16[288,1152]{1,0:T(8,128)(2,1)S(1)} collective-permute-done((bf16[288,1152]{1,0:T(8,128)(2,1)S(1)}, bf16[288,1152]{1,0:T(8,128)(2,1)S(1)}, u32[]{:S(2)}, u32[]{:S(2)}) %collective-permute-start.10) | collective-permute-done | bytes 663584 | tf_op jit(solution)/shard_map/ppermute | solution.py:64
  67.1 2.2 %collective-permute-done.21.refs_14_ = bf16[144,1728]{1,0:T(8,128)(2,1)S(1)} collective-permute-done((bf16[144,1728]{1,0:T(8,128)(2,1)S(1)}, bf16[144,1728]{1,0:T(8,128)(2,1)S(1)}, u32[]{:S(2)}, u32[]{:S(2)}) %collective-permute-start.21) | collective-permute-done | bytes 497696 | tf_op jit(solution)/shard_map/ppermute | solution.py:64
  70.1 5.6 %collective-permute-start.17 = (bf16[256,576]{1,0:T(8,128)(2,1)S(1)}, bf16[256,576]{1,0:T(8,128)(2,1)S(1)}, u32[]{:S(2)}, u32[]{:S(2)}) collective-permute-start(bf16[256,576]{1,0:T(8,128)(2,1)S(1)} %pad_maximum_fusion.4), channel_id=1, source_target_pairs={{0,3},{1,2},{2,1},{3,0},{4,7},{5,6},{6,5},{7,4},{8,11},{9,10},{10,... | collective-permute-start | bytes 884744 | tf_op jit(solution)/shard_map/ppermute | solution.py:490
  75.7 1.5 collective-permute-start.11
  77.2 1.5 %collective-permute-start.12 = (bf16[144,1152]{1,0:T(8,128)(2,1)S(1)}, bf16[144,1152]{1,0:T(8,128)(2,1)S(1)}, u32[]{:S(2)}, u32[]{:S(2)}) collective-permute-start(bf16[144,1152]{1,0:T(8,128)(2,1)S(1)} %slice.22), channel_id=1, source_target_pairs={{0,16},{4,20},{8,24},{12,28},{16,0},{20,4},{24,8},{28,12},{1,17},{... | collective-permute-start | bytes 995336 | tf_op jit(solution)/shard_map/ppermute | solution.py:64
  78.7 9.1 %qkv.1.refs_4_ = bf16[512,1728]{1,0:T(8,128)(2,1)S(1)} custom-call(s32[4]{0:T(128)S(1)} %pad_add_fusion.scalars, bf16[128,2304]{1,0:T(8,128)(2,1)S(1)} %norm.1.refs_0_, bf16[128,2304]{1,0:T(8,128)(2,1)} %collective-permute-done.refs_1_, bf16[128,2304]{1,0:T(8,128)(2,1)S(1)} %collective-permute-done.2.refs_2_, ...), custom_call_target="tpu_custom_call" | custom-call | flops 4076863488 | bytes 14680064 | tf_op jit(solution)/shard_map/qkv/pallas_call | solution.py:496
  87.8 2.3 %collective-permute-done.17.refs_3_ = bf16[256,576]{1,0:T(8,128)(2,1)S(1)} collective-permute-done((bf16[256,576]{1,0:T(8,128)(2,1)S(1)}, bf16[256,576]{1,0:T(8,128)(2,1)S(1)}, u32[]{:S(2)}, u32[]{:S(2)}) %collective-permute-start.17) | collective-permute-done | bytes 294944 | tf_op jit(solution)/shard_map/ppermute | solution.py:490
  91.2 7.8 %attention.1 = (bf16[256,576]{1,0:T(8,128)(2,1)S(1)}, bf16[256,576]{1,0:T(8,128)(2,1)S(1)}, bf16[16,576]{1,0:T(8,128)(2,1)S(1)}) custom-call(s32[4]{0:T(128)S(1)} %pad_add_fusion.scalars, bf16[256,576]{1,0:T(8,128)(2,1)S(1)} %pad_maximum_fusion.1.refs_0_, bf16[256,576]{1,0:T(8,128)(2,1)S(1)} %collective-permute-done.16.refs_1_, ...), custom_call_target="tpu_custom_call" | custom-call | flops 905969664 | bytes 4194304 | tf_op jit(solution)/shard_map/attention/pallas_call | solution.py:519
  99.9 1.9 %last_row.1 = f32[2,2304]{1,0:T(2,128)S(1)} custom-call(s32[4]{0:T(128)S(1)} %pad_add_fusion.scalars, bf16[288,1152]{1,0:T(8,128)(2,1)S(1)} %pad_maximum_fusion.refs_0_, bf16[288,1152]{1,0:T(8,128)(2,1)S(1)} %collective-permute-done.23.refs_1_, bf16[288,1152]{1,0:T(8,128)(2,1)S(1)} %collective-permute-done.9.refs_2_, ...), custom_call_target="tpu_custom_call" | custom-call | tf_op jit(solution)/shard_map/last_row/pallas_call | solution.py:544
  101.8 1.7 %collective-permute-start.29 = (f32[2,2304]{1,0:T(2,128)S(1)}, f32[2,2304]{1,0:T(2,128)S(1)}, u32[]{:S(2)}, u32[]{:S(2)}) collective-permute-start(f32[2,2304]{1,0:T(2,128)S(1)} %last_row.1), channel_id=1, source_target_pairs={{0,4},{4,0},{8,12},{12,8},{16,20},{20,16},{24,28},{28,24},{1,5},{5... | collective-permute-start | bytes 55304 | tf_op jit(solution)/shard_map/ppermute | solution.py:558
  104.3 2.7 %collective-permute-start.32 = (f32[2,2304]{1,0:T(2,128)S(1)}, f32[2,2304]{1,0:T(2,128)S(1)}, u32[]{:S(2)}, u32[]{:S(2)}) collective-permute-start(f32[2,2304]{1,0:T(2,128)S(1)} %add.38.refs_0_), channel_id=1, source_target_pairs={{0,3},{1,2},{2,1},{3,0},{4,7},{5,6},{6,5},{7,4},{8,11},{9,10},{10,... | collective-permute-start | bytes 55304 | tf_op jit(solution)/shard_map/ppermute | solution.py:561
  107.2 1.6 %collective-permute-start.30 = (f32[2,2304]{1,0:T(2,128)S(1)}, f32[2,2304]{1,0:T(2,128)S(1)}, u32[]{:S(2)}, u32[]{:S(2)}) collective-permute-start(f32[2,2304]{1,0:T(2,128)S(1)} %add.38.refs_0_), channel_id=1, source_target_pairs={{0,1},{1,0},{2,3},{3,2},{4,5},{5,4},{6,7},{7,6},{8,9},{9,8},{10,11... | collective-permute-start | bytes 55304 | tf_op jit(solution)/shard_map/ppermute | solution.py:561
  108.8 4.3 %project.1 = (f32[128,2304]{1,0:T(8,128)S(1)}, bf16[128,2304]{1,0:T(8,128)(2,1)S(1)}) custom-call(s32[4]{0:T(128)S(1)} %pad_add_fusion.scalars, bf16[288,1152]{1,0:T(8,128)(2,1)S(1)} %pad_maximum_fusion.refs_0_, bf16[288,1152]{1,0:T(8,128)(2,1)S(1)} %collective-permute-done.23.refs_1_, bf16[288,1152]{1,0:T(8,128)(2,1)S(1)} %collective-permute-done.9.refs_2_, ...), custom_call_target="tpu_custom_call" | custom-call | flops 1358954496 | bytes 8388608 | tf_op jit(solution)/shard_map/project/pallas_call | solution.py:565
  113.2 1.9 %collective-permute-start.33 = (bf16[128,2304]{1,0:T(8,128)(2,1)S(1)}, bf16[128,2304]{1,0:T(8,128)(2,1)S(1)}, u32[]{:S(2)}, u32[]{:S(2)}) collective-permute-start(bf16[128,2304]{1,0:T(8,128)(2,1)S(1)} %get-tuple-element.94), channel_id=1, source_target_pairs={{0,2},{1,3},{2,0},{3,1},{4,6},{5,7},{6,4},{7,5},{8,10},{9,11},{10,... | collective-permute-start | bytes 1769480 | tf_op jit(solution)/shard_map/ppermute | solution.py:584
  115.7 3.4 %collective-permute-start.36 = (bf16[8,2304]{1,0:T(8,128)(2,1)S(1)}, bf16[8,2304]{1,0:T(8,128)(2,1)S(1)}, u32[]{:S(2)}, u32[]{:S(2)}) collective-permute-start(bf16[8,2304]{1,0:T(8,128)(2,1)S(1)} %final_rows.1.refs_0_), channel_id=1, source_target_pairs={{0,24},{4,28},{8,16},{12,20},{16,8},{20,12},{24,0},{28,4},{1,25},{... | collective-permute-start | bytes 110600 | tf_op jit(solution)/shard_map/ppermute | solution.py:396
  119.8 1.6 %collective-permute-done.36.refs_3_ = bf16[8,2304]{1,0:T(8,128)(2,1)S(1)} collective-permute-done((bf16[8,2304]{1,0:T(8,128)(2,1)S(1)}, bf16[8,2304]{1,0:T(8,128)(2,1)S(1)}, u32[]{:S(2)}, u32[]{:S(2)}) %collective-permute-start.36) | collective-permute-done | bytes 36896 | tf_op jit(solution)/shard_map/ppermute | solution.py:396
  121.4 1.7 %collective-permute-done.35.refs_2_ = bf16[8,2304]{1,0:T(8,128)(2,1)S(1)} collective-permute-done((bf16[8,2304]{1,0:T(8,128)(2,1)S(1)}, bf16[8,2304]{1,0:T(8,128)(2,1)S(1)}, u32[]{:S(2)}, u32[]{:S(2)}) %collective-permute-start.35) | collective-permute-done | bytes 36896 | tf_op jit(solution)/shard_map/ppermute | solution.py:396
  123.6 7.7 %head.1 = (f32[8,3840]{1,0:T(8,128)S(1)}, f32[8,2]{1,0:T(8,128)S(1)}) custom-call(bf16[8,2304]{1,0:T(8,128)(2,1)S(1)} %final_rows.1.refs_0_, bf16[8,2304]{1,0:T(8,128)(2,1)S(1)} %collective-permute-done.34.refs_1_, bf16[8,2304]{1,0:T(8,128)(2,1)S(1)} %collective-permute-done.35.refs_2_, bf16[8,2304]{1,0:T(8,128)(2,1)S(1)} %collective-permute-done.36.refs_3_, ...), custom_call_target="tpu_custom_call" | custom-call | tf_op jit(solution)/shard_map/head/pallas_call | solution.py:605
  131.3 1.5 %collective-permute-start.39 = (f32[8,2]{1,0:T(8,128)S(1)}, f32[8,2]{1,0:T(8,128)S(1)}, u32[]{:S(2)}, u32[]{:S(2)}) collective-permute-start(f32[8,2]{1,0:T(8,128)S(1)} %get-tuple-element.100.refs_0_), channel_id=1, source_target_pairs={{0,24},{4,28},{8,16},{12,20},{16,8},{20,12},{24,0},{28,4},{1,25},{... | collective-permute-start | bytes 200 | tf_op jit(solution)/shard_map/ppermute | solution.py:396
  132.9 1.9 %collective-permute-start.37 = (f32[8,2]{1,0:T(8,128)S(1)}, f32[8,2]{1,0:T(8,128)S(1)}, u32[]{:S(2)}, u32[]{:S(2)}) collective-permute-start(f32[8,2]{1,0:T(8,128)S(1)} %get-tuple-element.100.refs_0_), channel_id=1, source_target_pairs={{0,8},{4,12},{8,0},{12,4},{16,24},{20,28},{24,16},{28,20},{1,9},{5... | collective-permute-start | bytes 200 | tf_op jit(solution)/shard_map/ppermute | solution.py:396
  134.8 1.0 collective-permute-done.39.refs_3_
  136.6 1.2 collective-permute-done.40.refs_1_
  137.9 0.9 collective-permute-start.41
  138.7 4.2 %collective-permute-done.33 = bf16[128,2304]{1,0:T(8,128)(2,1)S(1)} collective-permute-done((bf16[128,2304]{1,0:T(8,128)(2,1)S(1)}, bf16[128,2304]{1,0:T(8,128)(2,1)S(1)}, u32[]{:S(2)}, u32[]{:S(2)}) %collective-permute-start.33) | collective-permute-done | bytes 589856 | tf_op jit(solution)/shard_map/ppermute | solution.py:584
  142.9 1.5 %collective-permute-start.43 = (f32[8,2]{1,0:T(8,128)S(1)}, f32[8,2]{1,0:T(8,128)S(1)}, u32[]{:S(2)}, u32[]{:S(2)}) collective-permute-start(f32[8,2]{1,0:T(8,128)S(1)} %merge.3.refs_0_), channel_id=1, source_target_pairs={{0,3},{1,2},{2,1},{3,0},{4,7},{5,6},{6,5},{7,4},{8,11},{9,10},{10,... | collective-permute-start | bytes 200 | tf_op jit(solution)/shard_map/ppermute | solution.py:628
  144.5 0.9 fusion
  145.4 2.9 %collective-permute-done.43.refs_3_ = f32[8,2]{1,0:T(8,128)S(1)} collective-permute-done((f32[8,2]{1,0:T(8,128)S(1)}, f32[8,2]{1,0:T(8,128)S(1)}, u32[]{:S(2)}, u32[]{:S(2)}) %collective-permute-start.43) | collective-permute-done | bytes 96 | tf_op jit(solution)/shard_map/ppermute | solution.py:628
  (90 shorter events, 14.7 us)
Async XLA Ops:
  2.4 7.9 %slice-start.1 = ((bf16[288,576]{1,0:T(8,128)(2,1)}), bf16[288,512]{1,0:T(8,128)(2,1)S(1)}, s32[]{:S(2)}) async-start(bf16[288,576]{1,0:T(8,128)(2,1)} %param.19), calls=%async_computation.1 | async-start | bytes 589824 | tf_op jit(solution)/shard_map/slice | solution.py:455
  2.4 7.9 %copy-start.7 = (bf16[288,576]{1,0:T(8,128)(2,1)S(1)}, bf16[288,576]{1,0:T(8,128)(2,1)}, u32[]{:S(2)}) copy-start(bf16[288,576]{1,0:T(8,128)(2,1)} %param.18) | copy-start | bytes 995332
  2.6 20.7 %collective-permute-start.1 = (bf16[128,2304]{1,0:T(8,128)(2,1)S(1)}, bf16[128,2304]{1,0:T(8,128)(2,1)S(1)}, u32[]{:S(2)}, u32[]{:S(2)}) collective-permute-start(bf16[128,2304]{1,0:T(8,128)(2,1)S(1)} %norm.1.refs_0_), channel_id=1, source_target_pairs={{1,0},{2,1},{3,2},{5,4},{6,5},{7,6},{9,8},{10,9},{11,10},{13,12},{... | collective-permute-start | bytes 1769480 | tf_op jit(solution)/shard_map/ppermute | solution.py:107
  4.0 19.4 %collective-permute-start = (bf16[128,2304]{1,0:T(8,128)(2,1)S(1)}, bf16[128,2304]{1,0:T(8,128)(2,1)}, u32[]{:S(2)}, u32[]{:S(2)}) collective-permute-start(bf16[128,2304]{1,0:T(8,128)(2,1)S(1)} %norm.1.refs_0_), channel_id=1, source_target_pairs={{0,1},{1,2},{2,3},{4,5},{5,6},{6,7},{8,9},{9,10},{10,11},{12,13},{... | collective-permute-start | bytes 1769480 | tf_op jit(solution)/shard_map/ppermute | solution.py:106
  12.4 24.3 %collective-permute-start.6 = (bf16[288,1728]{1,0:T(8,128)(2,1)S(1)}, bf16[288,1728]{1,0:T(8,128)(2,1)S(1)}, u32[]{:S(2)}, u32[]{:S(2)}) collective-permute-start(bf16[288,1728]{1,0:T(8,128)(2,1)S(1)} %concatenate.31.refs_7_), channel_id=1, source_target_pairs={{0,16},{4,20},{8,24},{12,28},{16,0},{20,4},{24,8},{28,12},{1,17},{... | collective-permute-start | bytes 2985992 | tf_op jit(solution)/shard_map/ppermute | solution.py:64
  14.4 23.8 %collective-permute-start.5 = (bf16[288,1728]{1,0:T(8,128)(2,1)S(1)}, bf16[288,1728]{1,0:T(8,128)(2,1)}, u32[]{:S(2)}, u32[]{:S(2)}) collective-permute-start(bf16[288,1728]{1,0:T(8,128)(2,1)S(1)} %concatenate.31.refs_7_), channel_id=1, source_target_pairs={{0,8},{4,12},{8,0},{12,4},{16,24},{20,28},{24,16},{28,20},{1,9},{5... | collective-permute-start | bytes 2985992 | tf_op jit(solution)/shard_map/ppermute | solution.py:64
  15.9 25.5 %collective-permute-start.4 = (bf16[288,576]{1,0:T(8,128)(2,1)}, bf16[288,576]{1,0:T(8,128)(2,1)}, u32[]{:S(2)}, u32[]{:S(2)}) collective-permute-start(bf16[288,576]{1,0:T(8,128)(2,1)} %bitcast.27), channel_id=1, source_target_pairs={{0,1},{1,0},{2,3},{3,2},{4,5},{5,4},{6,7},{7,6},{8,9},{9,8},{10,11... | collective-permute-start | bytes 995336 | tf_op jit(solution)/shard_map/ppermute | solution.py:473
  23.4 19.2 %collective-permute-start.2 = (bf16[128,2304]{1,0:T(8,128)(2,1)}, bf16[128,2304]{1,0:T(8,128)(2,1)S(1)}, u32[]{:S(2)}, u32[]{:S(2)}) collective-permute-start(bf16[128,2304]{1,0:T(8,128)(2,1)} %collective-permute-done.refs_1_), channel_id=1, source_target_pairs={{1,2},{2,3},{5,6},{6,7},{9,10},{10,11},{13,14},{14,15},{17,18},{18... | collective-permute-start | bytes 1769480 | tf_op jit(solution)/shard_map/ppermute | solution.py:106
  24.1 18.5 %collective-permute-start.3 = (bf16[128,2304]{1,0:T(8,128)(2,1)S(1)}, bf16[128,2304]{1,0:T(8,128)(2,1)S(1)}, u32[]{:S(2)}, u32[]{:S(2)}) collective-permute-start(bf16[128,2304]{1,0:T(8,128)(2,1)S(1)} %collective-permute-done.1.refs_4_), channel_id=1, source_target_pairs={{1,0},{2,1},{5,4},{6,5},{9,8},{10,9},{13,12},{14,13},{17,16},{18,1... | collective-permute-start | bytes 1769480 | tf_op jit(solution)/shard_map/ppermute | solution.py:107
  26.9 14.5 %copy-start.8 = (bf16[576,288]{0,1:T(8,128)(2,1)S(1)}, bf16[576,288]{0,1:T(8,128)(2,1)}, u32[]{:S(2)}) copy-start(bf16[576,288]{0,1:T(8,128)(2,1)} %param.21) | copy-start | bytes 995332
  39.3 11.8 %collective-permute-start.7 = (bf16[144,1728]{1,0:T(8,128)(2,1)S(1)}, bf16[144,1728]{1,0:T(8,128)(2,1)S(1)}, u32[]{:S(2)}, u32[]{:S(2)}) collective-permute-start(bf16[144,1728]{1,0:T(8,128)(2,1)S(1)} %slice.21), channel_id=1, source_target_pairs={{0,8},{4,12},{8,0},{12,4},{16,24},{20,28},{24,16},{28,20},{1,9},{5... | collective-permute-start | bytes 1493000 | tf_op jit(solution)/shard_map/ppermute | solution.py:64
  40.9 11.9 %collective-permute-start.8 = (bf16[144,1728]{1,0:T(8,128)(2,1)S(1)}, bf16[144,1728]{1,0:T(8,128)(2,1)S(1)}, u32[]{:S(2)}, u32[]{:S(2)}) collective-permute-start(bf16[144,1728]{1,0:T(8,128)(2,1)S(1)} %slice.20), channel_id=1, source_target_pairs={{0,16},{4,20},{8,24},{12,28},{16,0},{20,4},{24,8},{28,12},{1,17},{... | collective-permute-start | bytes 1493000 | tf_op jit(solution)/shard_map/ppermute | solution.py:64
  42.6 20.4 %collective-permute-start.14 = (bf16[128,2304]{1,0:T(8,128)(2,1)S(1)}, bf16[128,2304]{1,0:T(8,128)(2,1)S(1)}, u32[]{:S(2)}, u32[]{:S(2)}) collective-permute-start(bf16[128,2304]{1,0:T(8,128)(2,1)S(1)} %collective-permute-done.2.refs_2_), channel_id=1, source_target_pairs={{2,3},{6,7},{10,11},{14,15},{18,19},{22,23},{26,27},{30,31}} | collective-permute-start | bytes 1769480 | tf_op jit(solution)/shard_map/ppermute | solution.py:106
  43.3 21.7 %collective-permute-start.15 = (bf16[128,2304]{1,0:T(8,128)(2,1)S(1)}, bf16[128,2304]{1,0:T(8,128)(2,1)S(1)}, u32[]{:S(2)}, u32[]{:S(2)}) collective-permute-start(bf16[128,2304]{1,0:T(8,128)(2,1)S(1)} %collective-permute-done.3.refs_5_), channel_id=1, source_target_pairs={{1,0},{5,4},{9,8},{13,12},{17,16},{21,20},{25,24},{29,28}} | collective-permute-start | bytes 1769480 | tf_op jit(solution)/shard_map/ppermute | solution.py:107
  44.6 18.4 %collective-permute-start.13 = (bf16[256,576]{1,0:T(8,128)(2,1)S(1)}, bf16[256,576]{1,0:T(8,128)(2,1)S(1)}, u32[]{:S(2)}, u32[]{:S(2)}) collective-permute-start(bf16[256,576]{1,0:T(8,128)(2,1)S(1)} %pad_maximum_fusion.3), channel_id=1, source_target_pairs={{0,2},{1,3},{2,0},{3,1},{4,6},{5,7},{6,4},{7,5},{8,10},{9,11},{10,... | collective-permute-start | bytes 884744 | tf_op jit(solution)/shard_map/ppermute | solution.py:485
  52.8 13.7 %collective-permute-start.10 = (bf16[288,1152]{1,0:T(8,128)(2,1)S(1)}, bf16[288,1152]{1,0:T(8,128)(2,1)S(1)}, u32[]{:S(2)}, u32[]{:S(2)}) collective-permute-start(bf16[288,1152]{1,0:T(8,128)(2,1)S(1)} %pad_maximum_fusion.refs_0_), channel_id=1, source_target_pairs={{0,16},{4,20},{8,24},{12,28},{16,0},{20,4},{24,8},{28,12},{1,17},{... | collective-permute-start | bytes 1990664 | tf_op jit(solution)/shard_map/ppermute | solution.py:64
  52.9 13.8 %collective-permute-start.9 = (bf16[288,1152]{1,0:T(8,128)(2,1)S(1)}, bf16[288,1152]{1,0:T(8,128)(2,1)S(1)}, u32[]{:S(2)}, u32[]{:S(2)}) collective-permute-start(bf16[288,1152]{1,0:T(8,128)(2,1)S(1)} %pad_maximum_fusion.refs_0_), channel_id=1, source_target_pairs={{0,8},{4,12},{8,0},{12,4},{16,24},{20,28},{24,16},{28,20},{1,9},{5... | collective-permute-start | bytes 1990664 | tf_op jit(solution)/shard_map/ppermute | solution.py:64
  63.0 12.7 %collective-permute-start.18 = (bf16[288,1728]{1,0:T(8,128)(2,1)S(1)}, bf16[288,1728]{1,0:T(8,128)(2,1)S(1)}, u32[]{:S(2)}, u32[]{:S(2)}) collective-permute-start(bf16[288,1728]{1,0:T(8,128)(2,1)S(1)} %concatenate.31.refs_7_), channel_id=1, source_target_pairs={{0,4},{4,0},{8,12},{12,8},{16,20},{20,16},{24,28},{28,24},{1,5},{5... | collective-permute-start | bytes 2985992 | tf_op jit(solution)/shard_map/ppermute | solution.py:64
  63.0 14.2 %collective-permute-start.19 = (bf16[288,1728]{1,0:T(8,128)(2,1)}, bf16[288,1728]{1,0:T(8,128)(2,1)S(1)}, u32[]{:S(2)}, u32[]{:S(2)}) collective-permute-start(bf16[288,1728]{1,0:T(8,128)(2,1)} %collective-permute-done.5.refs_9_), channel_id=1, source_target_pairs={{0,4},{4,0},{8,12},{12,8},{16,20},{20,16},{24,28},{28,24},{1,5},{5... | collective-permute-start | bytes 2985992 | tf_op jit(solution)/shard_map/ppermute | solution.py:64
  65.0 13.7 %collective-permute-start.20 = (bf16[288,1728]{1,0:T(8,128)(2,1)S(1)}, bf16[288,1728]{1,0:T(8,128)(2,1)S(1)}, u32[]{:S(2)}, u32[]{:S(2)}) collective-permute-start(bf16[288,1728]{1,0:T(8,128)(2,1)S(1)} %collective-permute-done.6.refs_11_), channel_id=1, source_target_pairs={{0,4},{4,0},{8,12},{12,8},{16,20},{20,16},{24,28},{28,24},{1,5},{5... | collective-permute-start | bytes 2985992 | tf_op jit(solution)/shard_map/ppermute | solution.py:64
  66.5 2.8 %collective-permute-start.21 = (bf16[144,1728]{1,0:T(8,128)(2,1)S(1)}, bf16[144,1728]{1,0:T(8,128)(2,1)S(1)}, u32[]{:S(2)}, u32[]{:S(2)}) collective-permute-start(bf16[144,1728]{1,0:T(8,128)(2,1)S(1)} %collective-permute-done.7.refs_13_), channel_id=1, source_target_pairs={{0,4},{4,0},{8,12},{12,8},{16,20},{20,16},{24,28},{28,24},{1,5},{5... | collective-permute-start | bytes 1493000 | tf_op jit(solution)/shard_map/ppermute | solution.py:64
  66.7 3.4 %collective-permute-start.22 = (bf16[144,1728]{1,0:T(8,128)(2,1)S(1)}, bf16[144,1728]{1,0:T(8,128)(2,1)S(1)}, u32[]{:S(2)}, u32[]{:S(2)}) collective-permute-start(bf16[144,1728]{1,0:T(8,128)(2,1)S(1)} %collective-permute-done.8.refs_15_), channel_id=1, source_target_pairs={{0,4},{4,0},{8,12},{12,8},{16,20},{20,16},{24,28},{28,24},{1,5},{5... | collective-permute-start | bytes 1493000 | tf_op jit(solution)/shard_map/ppermute | solution.py:64
  69.4 18.5 %collective-permute-start.16 = (bf16[256,576]{1,0:T(8,128)(2,1)S(1)}, bf16[256,576]{1,0:T(8,128)(2,1)S(1)}, u32[]{:S(2)}, u32[]{:S(2)}) collective-permute-start(bf16[256,576]{1,0:T(8,128)(2,1)S(1)} %pad_maximum_fusion.2), channel_id=1, source_target_pairs={{0,1},{1,0},{2,3},{3,2},{4,5},{5,4},{6,7},{7,6},{8,9},{9,8},{10,11... | collective-permute-start | bytes 884744 | tf_op jit(solution)/shard_map/ppermute | solution.py:488
  70.1 20.0 %collective-permute-start.17 = (bf16[256,576]{1,0:T(8,128)(2,1)S(1)}, bf16[256,576]{1,0:T(8,128)(2,1)S(1)}, u32[]{:S(2)}, u32[]{:S(2)}) collective-permute-start(bf16[256,576]{1,0:T(8,128)(2,1)S(1)} %pad_maximum_fusion.4), channel_id=1, source_target_pairs={{0,3},{1,2},{2,1},{3,0},{4,7},{5,6},{6,5},{7,4},{8,11},{9,10},{10,... | collective-permute-start | bytes 884744 | tf_op jit(solution)/shard_map/ppermute | solution.py:490
  75.7 14.4 %collective-permute-start.11 = (bf16[144,1152]{1,0:T(8,128)(2,1)S(1)}, bf16[144,1152]{1,0:T(8,128)(2,1)S(1)}, u32[]{:S(2)}, u32[]{:S(2)}) collective-permute-start(bf16[144,1152]{1,0:T(8,128)(2,1)S(1)} %slice.23), channel_id=1, source_target_pairs={{0,8},{4,12},{8,0},{12,4},{16,24},{20,28},{24,16},{28,20},{1,9},{5... | collective-permute-start | bytes 995336 | tf_op jit(solution)/shard_map/ppermute | solution.py:64
  77.2 12.9 %collective-permute-start.12 = (bf16[144,1152]{1,0:T(8,128)(2,1)S(1)}, bf16[144,1152]{1,0:T(8,128)(2,1)S(1)}, u32[]{:S(2)}, u32[]{:S(2)}) collective-permute-start(bf16[144,1152]{1,0:T(8,128)(2,1)S(1)} %slice.22), channel_id=1, source_target_pairs={{0,16},{4,20},{8,24},{12,28},{16,0},{20,4},{24,8},{28,12},{1,17},{... | collective-permute-start | bytes 995336 | tf_op jit(solution)/shard_map/ppermute | solution.py:64
  87.8 12.0 %copy-start.1 = (bf16[1,128,2304]{2,1,0:T(8,128)(2,1)S(1)}, bf16[1,128,2304]{2,1,0:T(8,128)(2,1)}, u32[]{:S(2)}) copy-start(bf16[1,128,2304]{2,1,0:T(8,128)(2,1)} %param.12) | copy-start | bytes 1769476
  90.1 9.7 %collective-permute-start.23 = (bf16[288,1152]{1,0:T(8,128)(2,1)S(1)}, bf16[288,1152]{1,0:T(8,128)(2,1)S(1)}, u32[]{:S(2)}, u32[]{:S(2)}) collective-permute-start(bf16[288,1152]{1,0:T(8,128)(2,1)S(1)} %pad_maximum_fusion.refs_0_), channel_id=1, source_target_pairs={{0,4},{4,0},{8,12},{12,8},{16,20},{20,16},{24,28},{28,24},{1,5},{5... | collective-permute-start | bytes 1990664 | tf_op jit(solution)/shard_map/ppermute | solution.py:64
  90.1 9.7 %collective-permute-start.24 = (bf16[288,1152]{1,0:T(8,128)(2,1)S(1)}, bf16[288,1152]{1,0:T(8,128)(2,1)S(1)}, u32[]{:S(2)}, u32[]{:S(2)}) collective-permute-start(bf16[288,1152]{1,0:T(8,128)(2,1)S(1)} %collective-permute-done.9.refs_2_), channel_id=1, source_target_pairs={{0,4},{4,0},{8,12},{12,8},{16,20},{20,16},{24,28},{28,24},{1,5},{5... | collective-permute-start | bytes 1990664 | tf_op jit(solution)/shard_map/ppermute | solution.py:64
  90.6 9.2 %collective-permute-start.25 = (bf16[288,1152]{1,0:T(8,128)(2,1)S(1)}, bf16[288,1152]{1,0:T(8,128)(2,1)S(1)}, u32[]{:S(2)}, u32[]{:S(2)}) collective-permute-start(bf16[288,1152]{1,0:T(8,128)(2,1)S(1)} %collective-permute-done.10.refs_4_), channel_id=1, source_target_pairs={{0,4},{4,0},{8,12},{12,8},{16,20},{20,16},{24,28},{28,24},{1,5},{5... | collective-permute-start | bytes 1990664 | tf_op jit(solution)/shard_map/ppermute | solution.py:64
  90.7 8.3 %collective-permute-start.26 = (bf16[144,1152]{1,0:T(8,128)(2,1)S(1)}, bf16[144,1152]{1,0:T(8,128)(2,1)S(1)}, u32[]{:S(2)}, u32[]{:S(2)}) collective-permute-start(bf16[144,1152]{1,0:T(8,128)(2,1)S(1)} %collective-permute-done.11.refs_6_), channel_id=1, source_target_pairs={{0,4},{4,0},{8,12},{12,8},{16,20},{20,16},{24,28},{28,24},{1,5},{5... | collective-permute-start | bytes 995336 | tf_op jit(solution)/shard_map/ppermute | solution.py:64
  91.1 8.7 %collective-permute-start.27 = (bf16[144,1152]{1,0:T(8,128)(2,1)S(1)}, bf16[144,1152]{1,0:T(8,128)(2,1)S(1)}, u32[]{:S(2)}, u32[]{:S(2)}) collective-permute-start(bf16[144,1152]{1,0:T(8,128)(2,1)S(1)} %collective-permute-done.12.refs_8_), channel_id=1, source_target_pairs={{0,4},{4,0},{8,12},{12,8},{16,20},{20,16},{24,28},{28,24},{1,5},{5... | collective-permute-start | bytes 995336 | tf_op jit(solution)/shard_map/ppermute | solution.py:64
  99.0 9.8 %collective-permute-start.28 = (bf16[256,576]{1,0:T(8,128)(2,1)S(1)}, bf16[256,576]{1,0:T(8,128)(2,1)S(1)}, u32[]{:S(2)}, u32[]{:S(2)}) collective-permute-start(bf16[256,576]{1,0:T(8,128)(2,1)S(1)} %get-tuple-element.89), channel_id=1, source_target_pairs={{0,1},{1,0},{2,3},{3,2},{4,5},{5,4},{6,7},{7,6},{8,9},{9,8},{10,11... | collective-permute-start | bytes 884744 | tf_op jit(solution)/shard_map/ppermute | solution.py:564
  101.8 2.6 %collective-permute-start.29 = (f32[2,2304]{1,0:T(2,128)S(1)}, f32[2,2304]{1,0:T(2,128)S(1)}, u32[]{:S(2)}, u32[]{:S(2)}) collective-permute-start(f32[2,2304]{1,0:T(2,128)S(1)} %last_row.1), channel_id=1, source_target_pairs={{0,4},{4,0},{8,12},{12,8},{16,20},{20,16},{24,28},{28,24},{1,5},{5... | collective-permute-start | bytes 55304 | tf_op jit(solution)/shard_map/ppermute | solution.py:558
  104.3 8.8 %collective-permute-start.32 = (f32[2,2304]{1,0:T(2,128)S(1)}, f32[2,2304]{1,0:T(2,128)S(1)}, u32[]{:S(2)}, u32[]{:S(2)}) collective-permute-start(f32[2,2304]{1,0:T(2,128)S(1)} %add.38.refs_0_), channel_id=1, source_target_pairs={{0,3},{1,2},{2,1},{3,0},{4,7},{5,6},{6,5},{7,4},{8,11},{9,10},{10,... | collective-permute-start | bytes 55304 | tf_op jit(solution)/shard_map/ppermute | solution.py:561
  107.0 6.1 %collective-permute-start.31 = (f32[2,2304]{1,0:T(2,128)S(1)}, f32[2,2304]{1,0:T(2,128)S(1)}, u32[]{:S(2)}, u32[]{:S(2)}) collective-permute-start(f32[2,2304]{1,0:T(2,128)S(1)} %add.38.refs_0_), channel_id=1, source_target_pairs={{0,2},{1,3},{2,0},{3,1},{4,6},{5,7},{6,4},{7,5},{8,10},{9,11},{10,... | collective-permute-start | bytes 55304 | tf_op jit(solution)/shard_map/ppermute | solution.py:561
  107.2 6.0 %collective-permute-start.30 = (f32[2,2304]{1,0:T(2,128)S(1)}, f32[2,2304]{1,0:T(2,128)S(1)}, u32[]{:S(2)}, u32[]{:S(2)}) collective-permute-start(f32[2,2304]{1,0:T(2,128)S(1)} %add.38.refs_0_), channel_id=1, source_target_pairs={{0,1},{1,0},{2,3},{3,2},{4,5},{5,4},{6,7},{7,6},{8,9},{9,8},{10,11... | collective-permute-start | bytes 55304 | tf_op jit(solution)/shard_map/ppermute | solution.py:561
  113.2 29.8 %collective-permute-start.33 = (bf16[128,2304]{1,0:T(8,128)(2,1)S(1)}, bf16[128,2304]{1,0:T(8,128)(2,1)S(1)}, u32[]{:S(2)}, u32[]{:S(2)}) collective-permute-start(bf16[128,2304]{1,0:T(8,128)(2,1)S(1)} %get-tuple-element.94), channel_id=1, source_target_pairs={{0,2},{1,3},{2,0},{3,1},{4,6},{5,7},{6,4},{7,5},{8,10},{9,11},{10,... | collective-permute-start | bytes 1769480 | tf_op jit(solution)/shard_map/ppermute | solution.py:584
  115.7 5.7 %collective-permute-start.36 = (bf16[8,2304]{1,0:T(8,128)(2,1)S(1)}, bf16[8,2304]{1,0:T(8,128)(2,1)S(1)}, u32[]{:S(2)}, u32[]{:S(2)}) collective-permute-start(bf16[8,2304]{1,0:T(8,128)(2,1)S(1)} %final_rows.1.refs_0_), channel_id=1, source_target_pairs={{0,24},{4,28},{8,16},{12,20},{16,8},{20,12},{24,0},{28,4},{1,25},{... | collective-permute-start | bytes 110600 | tf_op jit(solution)/shard_map/ppermute | solution.py:396
  119.1 4.0 %collective-permute-start.35 = (bf16[8,2304]{1,0:T(8,128)(2,1)S(1)}, bf16[8,2304]{1,0:T(8,128)(2,1)S(1)}, u32[]{:S(2)}, u32[]{:S(2)}) collective-permute-start(bf16[8,2304]{1,0:T(8,128)(2,1)S(1)} %final_rows.1.refs_0_), channel_id=1, source_target_pairs={{0,16},{4,20},{8,24},{12,28},{16,0},{20,4},{24,8},{28,12},{1,17},{... | collective-permute-start | bytes 110600 | tf_op jit(solution)/shard_map/ppermute | solution.py:396
  119.6 4.0 %collective-permute-start.34 = (bf16[8,2304]{1,0:T(8,128)(2,1)S(1)}, bf16[8,2304]{1,0:T(8,128)(2,1)S(1)}, u32[]{:S(2)}, u32[]{:S(2)}) collective-permute-start(bf16[8,2304]{1,0:T(8,128)(2,1)S(1)} %final_rows.1.refs_0_), channel_id=1, source_target_pairs={{0,8},{4,12},{8,0},{12,4},{16,24},{20,28},{24,16},{28,20},{1,9},{5... | collective-permute-start | bytes 110600 | tf_op jit(solution)/shard_map/ppermute | solution.py:396
  131.3 4.6 %collective-permute-start.39 = (f32[8,2]{1,0:T(8,128)S(1)}, f32[8,2]{1,0:T(8,128)S(1)}, u32[]{:S(2)}, u32[]{:S(2)}) collective-permute-start(f32[8,2]{1,0:T(8,128)S(1)} %get-tuple-element.100.refs_0_), channel_id=1, source_target_pairs={{0,24},{4,28},{8,16},{12,20},{16,8},{20,12},{24,0},{28,4},{1,25},{... | collective-permute-start | bytes 200 | tf_op jit(solution)/shard_map/ppermute | solution.py:396
  132.8 3.6 %collective-permute-start.38 = (f32[8,2]{1,0:T(8,128)S(1)}, f32[8,2]{1,0:T(8,128)S(1)}, u32[]{:S(2)}, u32[]{:S(2)}) collective-permute-start(f32[8,2]{1,0:T(8,128)S(1)} %get-tuple-element.100.refs_0_), channel_id=1, source_target_pairs={{0,16},{4,20},{8,24},{12,28},{16,0},{20,4},{24,8},{28,12},{1,17},{... | collective-permute-start | bytes 200 | tf_op jit(solution)/shard_map/ppermute | solution.py:396
  132.9 3.6 %collective-permute-start.37 = (f32[8,2]{1,0:T(8,128)S(1)}, f32[8,2]{1,0:T(8,128)S(1)}, u32[]{:S(2)}, u32[]{:S(2)}) collective-permute-start(f32[8,2]{1,0:T(8,128)S(1)} %get-tuple-element.100.refs_0_), channel_id=1, source_target_pairs={{0,8},{4,12},{8,0},{12,4},{16,24},{20,28},{24,16},{28,20},{1,9},{5... | collective-permute-start | bytes 200 | tf_op jit(solution)/shard_map/ppermute | solution.py:396
  136.6 1.2 collective-permute-start.40
  137.9 7.6 %collective-permute-start.41 = (f32[8,2]{1,0:T(8,128)S(1)}, f32[8,2]{1,0:T(8,128)S(1)}, u32[]{:S(2)}, u32[]{:S(2)}) collective-permute-start(f32[8,2]{1,0:T(8,128)S(1)} %merge.3.refs_0_), channel_id=1, source_target_pairs={{0,1},{1,0},{2,3},{3,2},{4,5},{5,4},{6,7},{7,6},{8,9},{9,8},{10,11... | collective-permute-start | bytes 200 | tf_op jit(solution)/shard_map/ppermute | solution.py:627
  142.9 5.4 %collective-permute-start.43 = (f32[8,2]{1,0:T(8,128)S(1)}, f32[8,2]{1,0:T(8,128)S(1)}, u32[]{:S(2)}, u32[]{:S(2)}) collective-permute-start(f32[8,2]{1,0:T(8,128)S(1)} %merge.3.refs_0_), channel_id=1, source_target_pairs={{0,3},{1,2},{2,1},{3,0},{4,7},{5,6},{6,5},{7,4},{8,11},{9,10},{10,... | collective-permute-start | bytes 200 | tf_op jit(solution)/shard_map/ppermute | solution.py:628
  144.5 4.5 %collective-permute-start.42 = (f32[8,2]{1,0:T(8,128)S(1)}, f32[8,2]{1,0:T(8,128)S(1)}, u32[]{:S(2)}, u32[]{:S(2)}) collective-permute-start(f32[8,2]{1,0:T(8,128)S(1)} %merge.3.refs_0_), channel_id=1, source_target_pairs={{0,2},{1,3},{2,0},{3,1},{4,6},{5,7},{6,4},{7,5},{8,10},{9,11},{10,... | collective-permute-start | bytes 200 | tf_op jit(solution)/shard_map/ppermute | solution.py:628
  (7 other events, 24.6 us)
